TPU v7x, 512 devices: a whole 4x8x8 slice. The times are simulated.
512 devices in a mesh: dp: 16 (over x, y_lo), seq: 32 (over y_hi, z, core).
Axes of the slice: x: 4, y: 8 (y_hi: 2, y_lo: 4; y = y_hi * 4 + y_lo), z: 8, core: 2. Of those that a mesh axis runs over, the one named last changes fastest.
Arguments:
- hidden_in: bfloat16 [16, 4096, 4096], P('dp', 'seq'), may hold values from -6 to 6
- queries: bfloat16 [16, 4096, 1024], P('dp', 'seq'), may hold values from -6 to 6
- out_grad: bfloat16 [16, 4096, 1024], P('dp', 'seq'), may hold values from -16 to 16
- kv_weight: bfloat16 [4096, 256], P('dp'), may hold values from -0.09375 to 0.09375
- block_pos: int32 [16, 32], P('dp'), may hold values from 0 to 31, each once within a row
- precision: int32 [16, 32, 2], P('dp', 'seq'), may hold values from 2 to 8, as said below
Outputs:
- query_grad: bfloat16 [16, 4096, 1024], P('dp', 'seq')
- kv_grad: bfloat16 [16, 4096, 256], P('dp', 'seq')
- input_grad: bfloat16 [16, 4096, 4096], P('dp', 'seq')
- weight_grad: float32 [4096, 256], P('dp')
Inputs may be any that keep to these rules, and one draw needn't show every extreme that they name: `block_pos`: each sequence's row names every block position 0 to 31 once. `precision`: every entry is 2, 4 or 8.
All inputs are finite; a program needn't handle non-finite values.
Results may differ from a plain program's by a relative error of at most 0.017.
Values may be sent and summed in bfloat16 or wider, within the bound.
No kernel may reach another device: no remote copies, remote signals or barrier semaphores. Data moves between devices by JAX's collectives and lax.ppermute only.
A program may use at most 64 MiB of HBM per device.

v0:
```python
import math

import jax
import jax.numpy as jnp
from jax import lax
from jax.sharding import PartitionSpec as P

QH = 8
HD = 128
BLOCK = 128


EPSILON = 1e-06


def shifted(value, axis, steps):
    count = lax.axis_size(axis)
    pairs = [(source, (source + steps) % count) for source in range(count)]
    return lax.ppermute(value, axis, pairs)


def frequencies(size):
    expo = jnp.arange(0, size, 2).astype(jnp.float32) / size
    base = 1.0 / jnp.power(jnp.float32(500000.0), expo)
    wavelen = 2.0 * math.pi / base
    mixing = (8192.0 / wavelen - 1.0) / 3.0
    blended = (1.0 - mixing) * base / 8.0 + mixing * base
    return jnp.where(wavelen < 2048.0, base, jnp.where(wavelen > 8192.0, base / 8.0, blended))


def rotate(values, cosine, sine_part):
    half = values.shape[1] // 2
    first, second = (values[:, :half], values[:, half:])
    return jnp.concatenate(
        [first * cosine - second * sine_part, second * cosine + first * sine_part], axis=1
    )


def rotate_back(grads, cosine, sine_part):
    half = grads.shape[1] // 2
    first, second = (grads[:, :half], grads[:, half:])
    return jnp.concatenate(
        [first * cosine + second * sine_part, second * cosine - first * sine_part], axis=1
    )


def softstep(scaled):
    return scaled - jnp.sin(2.0 * math.pi * scaled) / (2.0 * math.pi)


def quantize(values, bits_here):
    nblocks = bits_here.shape[0]
    grouped = values.reshape(nblocks, values.shape[0] // nblocks, values.shape[1])
    largest = jnp.max(jnp.abs(grouped), axis=1, keepdims=True)
    levels = (lax.shift_left(jnp.ones_like(bits_here), bits_here - 1) - 1).astype(jnp.float32)
    level_step = (largest + EPSILON) / levels[:, None, None]
    return (level_step * softstep(grouped / level_step)).reshape(values.shape)


def dot_rows(left, right):
    return lax.dot_general(
        left, right, (((0,), (0,)), ((), ())), preferred_element_type=jnp.float32
    )


def dot_cols(left, right):
    return lax.dot_general(
        left, right, (((1,), (1,)), ((), ())), preferred_element_type=jnp.float32
    )


def body(hidden_in, queries, out_grad, kv_weight, block_pos, precision):
    tokens_here = hidden_in.shape[1]
    score_scale = 1.0 / math.sqrt(HD)
    cycle_size = lax.axis_size("seq")
    group_count = lax.axis_size("dp")
    grad_scale = 1.0 / math.sqrt(group_count * cycle_size * tokens_here)
    self_index = lax.axis_index("seq")
    weight = lax.all_gather(kv_weight, "dp", axis=0, tiled=True)
    x_rows = hidden_in[0]
    projected = jnp.dot(x_rows, weight, preferred_element_type=jnp.float32)
    offsets = jnp.arange(BLOCK, dtype=jnp.int32)
    all_pos = (block_pos[0][:, None] * BLOCK + offsets[None, :]).reshape(-1)
    my_pos = lax.dynamic_slice_in_dim(all_pos, self_index * tokens_here, tokens_here)
    inv_freq = frequencies(HD)
    angles = my_pos.astype(jnp.float32)[:, None] * inv_freq[None, :]
    cosine = jnp.cos(angles)
    sine_part = jnp.sin(angles)
    key_quant = quantize(rotate(projected[:, :HD], cosine, sine_part), precision[0, :, 0])
    value_quant = quantize(projected[:, HD:], precision[0, :, 1])
    stacked = jnp.concatenate([key_quant, value_quant], axis=1).astype(jnp.bfloat16)
    q_rows = queries[0].reshape(tokens_here * QH, HD)
    dout_rows = out_grad[0].reshape(tokens_here * QH, HD)
    row_pos = jnp.repeat(my_pos, QH)
    top_pos = jnp.max(my_pos)
    row_count = tokens_here * QH
    arrived = lax.all_gather(stacked, "seq", axis=0, tiled=True)
    numerator = jnp.zeros((row_count, HD), jnp.float32)
    row_total = jnp.zeros((row_count,), jnp.float32)
    key_count = arrived.shape[0]
    sub_rows = math.gcd(key_count, 512)

    def key_step(partial_value, step_index):
        key_block = lax.dynamic_slice_in_dim(arrived, step_index * sub_rows, sub_rows)
        block_places = lax.dynamic_slice_in_dim(all_pos, step_index * sub_rows, sub_rows)

        def key_compute_pair(sums):
            scores = dot_cols(q_rows, key_block[:, :HD]) * score_scale
            exponent = jnp.where(block_places[None, :] <= row_pos[:, None], jnp.exp(scores), 0.0)
            added = jnp.dot(
                exponent.astype(jnp.bfloat16), key_block[:, HD:], preferred_element_type=jnp.float32
            )
            return (sums[0] + added, sums[1] + jnp.sum(exponent, axis=1))

        def key_nothing(sums):
            return sums

        partial_value = lax.cond(
            jnp.min(block_places) <= top_pos, key_compute_pair, key_nothing, partial_value
        )
        return (partial_value, None)

    (numerator, row_total), _ = lax.scan(
        key_step, (numerator, row_total), jnp.arange(key_count // sub_rows)
    )
    numerator, row_total, kv_store = (numerator, row_total, arrived)
    attended = numerator / row_total[:, None]
    row_delta = jnp.sum(dout_rows.astype(jnp.float32) * attended, axis=1)
    log_total = jnp.log(row_total)

    def backward_block(source):
        key_block = lax.dynamic_slice_in_dim(kv_store, source * tokens_here, tokens_here)
        block_places = lax.dynamic_slice_in_dim(all_pos, source * tokens_here, tokens_here)

        def backward_compute_pair(unused):
            scores = dot_cols(q_rows, key_block[:, :HD]) * score_scale
            visible = block_places[None, :] <= row_pos[:, None]
            probs = jnp.where(visible, jnp.exp(scores - log_total[:, None]), 0.0)
            probs_low = probs.astype(jnp.bfloat16)
            value_grad = dot_rows(probs_low, dout_rows)
            prob_grad = dot_cols(dout_rows, key_block[:, HD:])
            score_grad = (probs * (prob_grad - row_delta[:, None])).astype(jnp.bfloat16)
            dq_add = jnp.dot(score_grad, key_block[:, :HD], preferred_element_type=jnp.float32)
            key_grad = dot_rows(score_grad, q_rows)
            return (dq_add, jnp.concatenate([key_grad, value_grad], axis=1))

        def backward_nothing(unused):
            return (
                jnp.zeros((row_count, HD), jnp.float32),
                jnp.zeros((tokens_here, 2 * HD), jnp.float32),
            )

        return lax.cond(
            jnp.min(block_places) <= top_pos, backward_compute_pair, backward_nothing, source
        )

    dq_sum = jnp.zeros((row_count, HD), jnp.float32)
    empty_grads = jnp.zeros((tokens_here, 2 * HD), jnp.float32)

    def pass_along(carried):
        return shifted(carried, "seq", 1)

    def cycle_turn(turn_index, running):
        dq_run, carried = running
        dq_add, kv_add = backward_block((self_index - turn_index) % cycle_size)
        return (dq_run + dq_add, pass_along(carried + kv_add))

    dq_sum, carried = lax.fori_loop(0, cycle_size - 1, cycle_turn, (dq_sum, empty_grads))
    dq_add, kv_add = backward_block((self_index + 1) % cycle_size)
    dq_sum = dq_sum + dq_add
    carried = pass_along(carried + kv_add)
    key_part = rotate_back(carried[:, :HD] * score_scale, cosine, sine_part)
    proj_grad = jnp.concatenate([key_part, carried[:, HD:]], axis=1).astype(jnp.bfloat16)
    query_grad = (dq_sum * score_scale).astype(jnp.bfloat16).reshape(1, tokens_here, QH * HD)
    input_grad = dot_cols(proj_grad, weight).astype(jnp.bfloat16)[None]
    grad_share = lax.psum_scatter(
        dot_rows(x_rows, proj_grad), "dp", scatter_dimension=0, tiled=True
    )
    weight_grad = lax.psum(grad_share, "seq")
    weight_grad = weight_grad * grad_scale
    return (query_grad, proj_grad[None], input_grad, weight_grad)


def solution(mesh):
    in_specs = (
        P("dp", "seq", None),
        P("dp", "seq", None),
        P("dp", "seq", None),
        P("dp", None),
        P("dp", None),
        P("dp", "seq", None),
    )
    out_specs = (P("dp", "seq", None), P("dp", "seq", None), P("dp", "seq", None), P("dp", None))
    return jax.shard_map(body, mesh=mesh, in_specs=in_specs, out_specs=out_specs, check_vma=False)
```

profile of v0, /device:TPU:1, one launch (start us, length us, event | category | flops | bytes accessed | tf_op | source)
XLA Modules:
  0.0 1278.3 jit_solution(13609477339443352745)
XLA Ops:
  12.1 84.0 %all-gather.3.cloned.1.call-done = bf16[4096,256]{1,0:T(8,128)(2,1)} async-done(((bf16[256,256]{1,0:T(8,128)(2,1)}), bf16[4096,256]{1,0:T(8,128)(2,1)}) %all-gather.3.cloned.1.call-update) | async-done | bytes 2097168 | tf_op jit(solution)/shard_map/all_gather | solution.py:79
  102.0 97.4 %all-gather.5.cloned.1.call-done = bf16[4096,256]{1,0:T(8,128)(2,1)} async-done(((bf16[128,256]{1,0:T(8,128)(2,1)}), bf16[4096,256]{1,0:T(8,128)(2,1)}) %all-gather.5.cloned.1.call-update) | async-done | bytes 2097168 | tf_op jit(solution)/shard_map/all_gather | solution.py:97
  199.4 53.2 %while.31 = (s32[]{:T(128)}, f32[1024,128]{1,0:T(8,128)S(1)}, f32[1024]{0:T(1024)S(1)}, s32[8]{0:T(128)S(1)}, s32[4096]{0:T(1024)S(1)}, /*index=5*/s32[]{:T(128)...) while((s32[]{:T(128)}, f32[1024,128]{1,0:T(8,128)S(1)}, ...), condition=%wide.region_8.9_spmd.clone, body=%wide.region_3.8_spmd.clone.sunk | while | flops 271188480 | bytes 3710789 | solution.py:123
  253.0 543.3 %while.32 = (s32[]{:T(128)}, f32[1024,128]{1,0:T(8,128)S(1)}, f32[128,256]{0,1:T(8,128)S(1)}, s32[]{:T(128)}, s32[4096]{0:T(1024)S(1)}, /*index=5*/s32[]{:T(128)...) while((s32[]{:T(128)}, f32[1024,128]{1,0:T(8,128)S(1)}, ...), condition=%wide.region_14.15_spmd.clone, body=%wide.region_10.14_spmd.clone.sunk | while | flops 169148560 | bytes 6942708 | solution.py:168
  302.8 10.2 collective-permute-done
  339.3 10.2 collective-permute-done
  357.6 11.4 collective-permute-done
  389.3 12.5 collective-permute-done
  409.9 10.2 collective-permute-done
  428.2 10.2 collective-permute-done
  460.9 14.1 %collective-permute-done = f32[128,256]{0,1:T(8,128)S(1)} collective-permute-done((f32[128,256]{0,1:T(8,128)S(1)}, f32[128,256]{0,1:T(8,128)S(1)}, u32[]{:S(2)}, u32[]{:S(2)}) %collective-permute-start) | collective-permute-done | bytes 131104 | tf_op jit(solution)/shard_map/while/body/eval_jaxpr/ppermute | solution.py:19
  501.3 10.2 collective-permute-done
  515.7 14.1 %collective-permute-done = f32[128,256]{0,1:T(8,128)S(1)} collective-permute-done((f32[128,256]{0,1:T(8,128)S(1)}, f32[128,256]{0,1:T(8,128)S(1)}, u32[]{:S(2)}, u32[]{:S(2)}) %collective-permute-start) | collective-permute-done | bytes 131104 | tf_op jit(solution)/shard_map/while/body/eval_jaxpr/ppermute | solution.py:19
  534.0 14.1 %collective-permute-done = f32[128,256]{0,1:T(8,128)S(1)} collective-permute-done((f32[128,256]{0,1:T(8,128)S(1)}, f32[128,256]{0,1:T(8,128)S(1)}, u32[]{:S(2)}, u32[]{:S(2)}) %collective-permute-start) | collective-permute-done | bytes 131104 | tf_op jit(solution)/shard_map/while/body/eval_jaxpr/ppermute | solution.py:19
  552.3 14.1 %collective-permute-done = f32[128,256]{0,1:T(8,128)S(1)} collective-permute-done((f32[128,256]{0,1:T(8,128)S(1)}, f32[128,256]{0,1:T(8,128)S(1)}, u32[]{:S(2)}, u32[]{:S(2)}) %collective-permute-start) | collective-permute-done | bytes 131104 | tf_op jit(solution)/shard_map/while/body/eval_jaxpr/ppermute | solution.py:19
  570.6 14.1 %collective-permute-done = f32[128,256]{0,1:T(8,128)S(1)} collective-permute-done((f32[128,256]{0,1:T(8,128)S(1)}, f32[128,256]{0,1:T(8,128)S(1)}, u32[]{:S(2)}, u32[]{:S(2)}) %collective-permute-start) | collective-permute-done | bytes 131104 | tf_op jit(solution)/shard_map/while/body/eval_jaxpr/ppermute | solution.py:19
  610.9 10.2 collective-permute-done
  643.7 14.1 %collective-permute-done = f32[128,256]{0,1:T(8,128)S(1)} collective-permute-done((f32[128,256]{0,1:T(8,128)S(1)}, f32[128,256]{0,1:T(8,128)S(1)}, u32[]{:S(2)}, u32[]{:S(2)}) %collective-permute-start) | collective-permute-done | bytes 131104 | tf_op jit(solution)/shard_map/while/body/eval_jaxpr/ppermute | solution.py:19
  661.9 14.1 %collective-permute-done = f32[128,256]{0,1:T(8,128)S(1)} collective-permute-done((f32[128,256]{0,1:T(8,128)S(1)}, f32[128,256]{0,1:T(8,128)S(1)}, u32[]{:S(2)}, u32[]{:S(2)}) %collective-permute-start) | collective-permute-done | bytes 131104 | tf_op jit(solution)/shard_map/while/body/eval_jaxpr/ppermute | solution.py:19
  696.3 12.4 collective-permute-done
  749.5 14.1 %collective-permute-done = f32[128,256]{0,1:T(8,128)S(1)} collective-permute-done((f32[128,256]{0,1:T(8,128)S(1)}, f32[128,256]{0,1:T(8,128)S(1)}, u32[]{:S(2)}, u32[]{:S(2)}) %collective-permute-start) | collective-permute-done | bytes 131104 | tf_op jit(solution)/shard_map/while/body/eval_jaxpr/ppermute | solution.py:19
  798.4 14.3 %collective-permute-done.1 = f32[128,256]{1,0:T(8,128)S(1)} collective-permute-done((f32[128,256]{1,0:T(8,128)S(1)}, f32[128,256]{1,0:T(8,128)S(1)}, u32[]{:S(2)}, u32[]{:S(2)}) %collective-permute-start.1) | collective-permute-done | bytes 131104 | tf_op jit(solution)/shard_map/ppermute | solution.py:19
  816.8 109.3 %reduce-scatter.2.cloned.1.call-done = f32[256,256]{0,1:T(8,128)} async-done(((f32[4096,256]{0,1:T(8,128)}), f32[256,256]{0,1:T(8,128)}) %reduce-scatter.2.cloned.1.call-update) | async-done | bytes 262160 | tf_op jit(solution)/shard_map/reduce_scatter | solution.py:176
  930.2 339.7 %all-reduce.2.cloned.1.call-done = f32[256,256]{0,1:T(8,128)} async-done(((f32[256,256]{0,1:T(8,128)}), f32[256,256]{0,1:T(8,128)}) %all-reduce.2.cloned.1.call-update) | async-done | bytes 262160 | tf_op jit(solution)/shard_map/psum | solution.py:179
  (457 shorter events, 443.7 us)
Async XLA Ops:
  7.2 88.8 %all-gather.3.cloned.1.call-start = ((), (), s32[]{:S(2)}) async-start(), calls=%async_computation.1 | async-start | bytes 2228224 | tf_op jit(solution)/shard_map/all_gather | solution.py:79
  7.9 191.5 %all-gather.5.cloned.1.call-start = ((), (), s32[]{:S(2)}) async-start(), calls=%async_computation.2 | async-start | bytes 2162688 | tf_op jit(solution)/shard_map/all_gather | solution.py:97
  99.7 826.4 %reduce-scatter.2.cloned.1.call-start = ((), (), s32[]{:S(2)}) async-start(), calls=%async_computation.3 | async-start | bytes 4456448 | tf_op jit(solution)/shard_map/reduce_scatter | solution.py:176
  278.8 15.9 %collective-permute-start = (f32[128,256]{0,1:T(8,128)S(1)}, f32[128,256]{0,1:T(8,128)S(1)}, u32[]{:S(2)}, u32[]{:S(2)}) collective-permute-start(f32[128,256]{0,1:T(8,128)S(1)} %add.210), channel_id=1, source_target_pairs={{0,1},{1,2},{2,3},{3,4},{4,5},{5,6},{6,7},{7,8},{8,9},{9,10},{10,1... | collective-permute-start | bytes 393224 | tf_op jit(solution)/shard_map/while/body/eval_jaxpr/ppermute | solution.py:19
  300.7 12.3 collective-permute-start
  337.2 12.3 collective-permute-start
  355.5 13.5 %collective-permute-start = (f32[128,256]{0,1:T(8,128)S(1)}, f32[128,256]{0,1:T(8,128)S(1)}, u32[]{:S(2)}, u32[]{:S(2)}) collective-permute-start(f32[128,256]{0,1:T(8,128)S(1)} %add.210), channel_id=1, source_target_pairs={{0,1},{1,2},{2,3},{3,4},{4,5},{5,6},{6,7},{7,8},{8,9},{9,10},{10,1... | collective-permute-start | bytes 393224 | tf_op jit(solution)/shard_map/while/body/eval_jaxpr/ppermute | solution.py:19
  385.7 16.1 %collective-permute-start = (f32[128,256]{0,1:T(8,128)S(1)}, f32[128,256]{0,1:T(8,128)S(1)}, u32[]{:S(2)}, u32[]{:S(2)}) collective-permute-start(f32[128,256]{0,1:T(8,128)S(1)} %add.210), channel_id=1, source_target_pairs={{0,1},{1,2},{2,3},{3,4},{4,5},{5,6},{6,7},{7,8},{8,9},{9,10},{10,1... | collective-permute-start | bytes 393224 | tf_op jit(solution)/shard_map/while/body/eval_jaxpr/ppermute | solution.py:19
  407.8 12.3 collective-permute-start
  426.1 12.3 collective-permute-start
  458.8 16.1 %collective-permute-start = (f32[128,256]{0,1:T(8,128)S(1)}, f32[128,256]{0,1:T(8,128)S(1)}, u32[]{:S(2)}, u32[]{:S(2)}) collective-permute-start(f32[128,256]{0,1:T(8,128)S(1)} %add.210), channel_id=1, source_target_pairs={{0,1},{1,2},{2,3},{3,4},{4,5},{5,6},{6,7},{7,8},{8,9},{9,10},{10,1... | collective-permute-start | bytes 393224 | tf_op jit(solution)/shard_map/while/body/eval_jaxpr/ppermute | solution.py:19
  499.2 12.3 collective-permute-start
  513.6 16.1 %collective-permute-start = (f32[128,256]{0,1:T(8,128)S(1)}, f32[128,256]{0,1:T(8,128)S(1)}, u32[]{:S(2)}, u32[]{:S(2)}) collective-permute-start(f32[128,256]{0,1:T(8,128)S(1)} %add.210), channel_id=1, source_target_pairs={{0,1},{1,2},{2,3},{3,4},{4,5},{5,6},{6,7},{7,8},{8,9},{9,10},{10,1... | collective-permute-start | bytes 393224 | tf_op jit(solution)/shard_map/while/body/eval_jaxpr/ppermute | solution.py:19
  531.9 16.1 %collective-permute-start = (f32[128,256]{0,1:T(8,128)S(1)}, f32[128,256]{0,1:T(8,128)S(1)}, u32[]{:S(2)}, u32[]{:S(2)}) collective-permute-start(f32[128,256]{0,1:T(8,128)S(1)} %add.210), channel_id=1, source_target_pairs={{0,1},{1,2},{2,3},{3,4},{4,5},{5,6},{6,7},{7,8},{8,9},{9,10},{10,1... | collective-permute-start | bytes 393224 | tf_op jit(solution)/shard_map/while/body/eval_jaxpr/ppermute | solution.py:19
  550.2 16.1 %collective-permute-start = (f32[128,256]{0,1:T(8,128)S(1)}, f32[128,256]{0,1:T(8,128)S(1)}, u32[]{:S(2)}, u32[]{:S(2)}) collective-permute-start(f32[128,256]{0,1:T(8,128)S(1)} %add.210), channel_id=1, source_target_pairs={{0,1},{1,2},{2,3},{3,4},{4,5},{5,6},{6,7},{7,8},{8,9},{9,10},{10,1... | collective-permute-start | bytes 393224 | tf_op jit(solution)/shard_map/while/body/eval_jaxpr/ppermute | solution.py:19
  568.5 16.1 %collective-permute-start = (f32[128,256]{0,1:T(8,128)S(1)}, f32[128,256]{0,1:T(8,128)S(1)}, u32[]{:S(2)}, u32[]{:S(2)}) collective-permute-start(f32[128,256]{0,1:T(8,128)S(1)} %add.210), channel_id=1, source_target_pairs={{0,1},{1,2},{2,3},{3,4},{4,5},{5,6},{6,7},{7,8},{8,9},{9,10},{10,1... | collective-permute-start | bytes 393224 | tf_op jit(solution)/shard_map/while/body/eval_jaxpr/ppermute | solution.py:19
  608.9 12.3 collective-permute-start
  641.6 16.1 %collective-permute-start = (f32[128,256]{0,1:T(8,128)S(1)}, f32[128,256]{0,1:T(8,128)S(1)}, u32[]{:S(2)}, u32[]{:S(2)}) collective-permute-start(f32[128,256]{0,1:T(8,128)S(1)} %add.210), channel_id=1, source_target_pairs={{0,1},{1,2},{2,3},{3,4},{4,5},{5,6},{6,7},{7,8},{8,9},{9,10},{10,1... | collective-permute-start | bytes 393224 | tf_op jit(solution)/shard_map/while/body/eval_jaxpr/ppermute | solution.py:19
  659.9 16.1 %collective-permute-start = (f32[128,256]{0,1:T(8,128)S(1)}, f32[128,256]{0,1:T(8,128)S(1)}, u32[]{:S(2)}, u32[]{:S(2)}) collective-permute-start(f32[128,256]{0,1:T(8,128)S(1)} %add.210), channel_id=1, source_target_pairs={{0,1},{1,2},{2,3},{3,4},{4,5},{5,6},{6,7},{7,8},{8,9},{9,10},{10,1... | collective-permute-start | bytes 393224 | tf_op jit(solution)/shard_map/while/body/eval_jaxpr/ppermute | solution.py:19
  692.6 16.1 %collective-permute-start = (f32[128,256]{0,1:T(8,128)S(1)}, f32[128,256]{0,1:T(8,128)S(1)}, u32[]{:S(2)}, u32[]{:S(2)}) collective-permute-start(f32[128,256]{0,1:T(8,128)S(1)} %add.210), channel_id=1, source_target_pairs={{0,1},{1,2},{2,3},{3,4},{4,5},{5,6},{6,7},{7,8},{8,9},{9,10},{10,1... | collective-permute-start | bytes 393224 | tf_op jit(solution)/shard_map/while/body/eval_jaxpr/ppermute | solution.py:19
  714.7 12.3 collective-permute-start
  747.4 16.1 %collective-permute-start = (f32[128,256]{0,1:T(8,128)S(1)}, f32[128,256]{0,1:T(8,128)S(1)}, u32[]{:S(2)}, u32[]{:S(2)}) collective-permute-start(f32[128,256]{0,1:T(8,128)S(1)} %add.210), channel_id=1, source_target_pairs={{0,1},{1,2},{2,3},{3,4},{4,5},{5,6},{6,7},{7,8},{8,9},{9,10},{10,1... | collective-permute-start | bytes 393224 | tf_op jit(solution)/shard_map/while/body/eval_jaxpr/ppermute | solution.py:19
  796.5 16.2 %collective-permute-start.1 = (f32[128,256]{1,0:T(8,128)S(1)}, f32[128,256]{1,0:T(8,128)S(1)}, u32[]{:S(2)}, u32[]{:S(2)}) collective-permute-start(f32[128,256]{1,0:T(8,128)S(1)} %add.172), channel_id=1, source_target_pairs={{0,1},{1,2},{2,3},{3,4},{4,5},{5,6},{6,7},{7,8},{8,9},{9,10},{10,1... | collective-permute-start | bytes 393224 | tf_op jit(solution)/shard_map/ppermute | solution.py:19
  815.8 454.1 %all-reduce.2.cloned.1.call-start = ((), (), s32[]{:S(2)}) async-start(), calls=%async_computation.4 | async-start | bytes 524288 | tf_op jit(solution)/shard_map/psum | solution.py:179
  (15 other events, 399.3 us)
Sparse Core Ops, SparseCore 0:
  10.1 85.8 all-gather.2
  100.0 99.3 all-gather.4
  816.0 110.1 reduce-scatter.1
  928.9 341.0 all-reduce.1
where the time goes:
time: 1290 us; the launch traced here: 1280 us
  waiting for transfers between devices  972 us (75%)
  matrix products  98.5 us (8%)
  starting transfers between devices  78.9 us (6%)
  loops' own time  60.4 us (5%)
  other arithmetic  39.1 us (3%)
  between operations  16.5 us (1%)
  local copies, waits for them, and re-layouts  13.2 us (1%)
    ppermute x32, waiting for transfers between devices, shifted(): return lax.ppermute(value, axis, pairs)  341 us
    psum x1, waiting for transfers between devices, body(): weight_grad = lax.psum(grad_share, 'seq')  340 us
    reduce_scatter x1, waiting for transfers between devices, body(): lax.psum_scatter(dot_rows(x_rows, proj_grad), 'dp', scatter_dimension=0,...  109 us
    all_gather x1, waiting for transfers between devices, body(): arrived = lax.all_gather(stacked, 'seq', axis=0, tiled=True)  97.4 us
    all_gather x1, waiting for transfers between devices, body(): weight = lax.all_gather(kv_weight, 'dp', axis=0, tiled=True)  84 us
    ppermute x32, starting transfers between devices, shifted(): return lax.ppermute(value, axis, pairs)  78.7 us
    dot_general x45, matrix products, dot_cols(): lax.dot_general(left, right, (((1,), (1,)), ((), ())), preferred_element_...  53.2 us
    another operation x1, loops' own time, body(): lax.fori_loop(0, cycle_size - 1, cycle_turn, (dq_sum, empty_grads))  42.6 us
  transfers between devices with their start and end apart: 36, of which 36 were waited for; matrix products, arithmetic and copies ran while one was open for 1% of the time, Pallas kernels for 0%

commit v1 on v0

v1 whole, which is shorter than its diff:
```python
import functools
import math

import jax
import jax.numpy as jnp
from jax import lax
from jax.experimental import pallas as pl
from jax.experimental.pallas import tpu as pltpu
from jax.sharding import PartitionSpec as P

QH = 8
HD = 128
BLOCK = 128
TILE_BLOCKS = 4

EPSILON = 1e-06
LOG2E = math.log2(math.e)


def frequencies(size):
    expo = jnp.arange(0, size, 2).astype(jnp.float32) / size
    base = 1.0 / jnp.power(jnp.float32(500000.0), expo)
    wavelen = 2.0 * math.pi / base
    mixing = (8192.0 / wavelen - 1.0) / 3.0
    blended = (1.0 - mixing) * base / 8.0 + mixing * base
    return jnp.where(wavelen < 2048.0, base, jnp.where(wavelen > 8192.0, base / 8.0, blended))


def rotate(values, cosine, sine_part):
    half = values.shape[1] // 2
    first, second = (values[:, :half], values[:, half:])
    return jnp.concatenate(
        [first * cosine - second * sine_part, second * cosine + first * sine_part], axis=1
    )


def rotate_back(grads, cosine, sine_part):
    half = grads.shape[1] // 2
    first, second = (grads[:, :half], grads[:, half:])
    return jnp.concatenate(
        [first * cosine + second * sine_part, second * cosine - first * sine_part], axis=1
    )


def softstep(scaled):
    return scaled - jnp.sin(2.0 * math.pi * scaled) / (2.0 * math.pi)


def quantize(values, bits_here):
    nblocks = bits_here.shape[0]
    grouped = values.reshape(nblocks, values.shape[0] // nblocks, values.shape[1])
    largest = jnp.max(jnp.abs(grouped), axis=1, keepdims=True)
    levels = (lax.shift_left(jnp.ones_like(bits_here), bits_here - 1) - 1).astype(jnp.float32)
    level_step = (largest + EPSILON) / levels[:, None, None]
    return (level_step * softstep(grouped / level_step)).reshape(values.shape)


def dot_rows(left, right):
    return lax.dot_general(
        left, right, (((0,), (0,)), ((), ())), preferred_element_type=jnp.float32
    )


def dot_cols(left, right):
    return lax.dot_general(
        left, right, (((1,), (1,)), ((), ())), preferred_element_type=jnp.float32
    )


def dot(left, right):
    return jnp.dot(left, right, preferred_element_type=jnp.float32)


def attention_kernel(
    order_ref, place_ref, near_ref, far_ref, q_ref, g_ref,
    dq_ref, near_grad_ref, far_grad_ref,
    exp_store, prob_store, top_store, q_cols, g_cols, q_rows, g_rows, dq_cols,
):
    side = near_ref.shape[0]
    blocks = 2 * side
    rows = QH * BLOCK
    span = TILE_BLOCKS * BLOCK
    score_scale = LOG2E / math.sqrt(HD)
    place = place_ref[0]
    tiles = lax.div(place + TILE_BLOCKS, TILE_BLOCKS)

    for head in range(QH):
        part = pl.ds(head * HD, HD)
        q_cols[:, part] = q_ref[:, part].T
        g_cols[:, part] = g_ref[:, part].T
        q_rows[part, :] = q_ref[:, part]
        g_rows[part, :] = g_ref[:, part]
    dq_cols[...] = jnp.zeros_like(dq_cols)

    def gathered(tile):
        found = []
        for step in range(TILE_BLOCKS):
            slot = order_ref[tile * TILE_BLOCKS + step]
            near = near_ref[jnp.minimum(slot, side - 1)]
            far = far_ref[jnp.maximum(slot - side, 0)]
            found.append(jnp.where(slot < side, near, far))
        return jnp.concatenate(found, axis=0)

    def folded(values):
        return jnp.sum(values.reshape(span // 8, 8, rows), axis=0)

    def forward(tile, sums, masked):
        total, weighted, top = sums
        keys = gathered(tile)
        scores = dot(keys[:, :HD], q_cols[...]) * score_scale
        if masked:
            key_at = tile * span + lax.broadcasted_iota(jnp.int32, (span, rows), 0)
            row_at = place * BLOCK + lax.rem(
                lax.broadcasted_iota(jnp.int32, (span, rows), 1), BLOCK
            )
            visible = key_at <= row_at
            scores = jnp.where(visible, scores, -jnp.inf)
        highest = jnp.maximum(top, jnp.max(scores, axis=0, keepdims=True))
        shrink = jnp.exp2(top - highest)
        exponent = jnp.exp2(scores - highest)
        prob_grad = dot(keys[:, HD:], g_cols[...])
        exp_store[tile] = exponent
        prob_store[tile] = prob_grad
        top_store[tile] = highest
        total = total * shrink + folded(exponent)
        weighted = weighted * shrink + folded(exponent * prob_grad)
        return (total, weighted, highest)

    empty = jnp.zeros((8, rows), jnp.float32)
    start = forward(tiles - 1, (empty, empty, jnp.full((1, rows), -1e30, jnp.float32)), True)
    total, weighted, top = lax.fori_loop(
        0, tiles - 1, lambda tile, sums: forward(tile, sums, False), start
    )
    inverse = 1.0 / jnp.sum(total, axis=0, keepdims=True)
    row_delta = jnp.sum(weighted, axis=0, keepdims=True) * inverse

    def store(slot, value):
        @pl.when(slot < side)
        def _():
            near_grad_ref[slot] = value

        @pl.when(slot >= side)
        def _():
            far_grad_ref[slot - side] = value

    @pl.loop(0, tiles)
    def _(tile):
        keys = gathered(tile)[:, :HD]
        factor = jnp.exp2(top_store[tile] - top) * inverse
        probs = exp_store[tile] * factor
        score_grad = (probs * (prob_store[tile] - row_delta)).astype(jnp.bfloat16)
        value_grad = dot(probs.astype(jnp.bfloat16), g_rows[...])
        key_grad = dot(score_grad, q_rows[...])
        dq_cols[...] += dot(keys.T, score_grad)
        grads = jnp.concatenate([key_grad, value_grad], axis=1).astype(jnp.bfloat16)
        for step in range(TILE_BLOCKS):
            store(
                order_ref[tile * TILE_BLOCKS + step], grads[step * BLOCK : (step + 1) * BLOCK]
            )

    @pl.loop(tiles * TILE_BLOCKS, blocks)
    def _(place_at):
        store(order_ref[place_at], jnp.zeros((BLOCK, 2 * HD), jnp.bfloat16))

    for head in range(QH):
        part = pl.ds(head * HD, HD)
        dq_ref[:, part] = (dq_cols[:, part].T * (1.0 / math.sqrt(HD))).astype(jnp.bfloat16)


def attention_backward(order, place, near, far, queries, out_grad):
    tokens = queries.shape[0]
    rows = QH * tokens
    blocks = 2 * near.shape[0]
    tiles = blocks // TILE_BLOCKS
    span = TILE_BLOCKS * BLOCK
    smem = pl.BlockSpec(memory_space=pltpu.SMEM)
    vmem = pl.BlockSpec(memory_space=pltpu.VMEM)
    return pl.pallas_call(
        attention_kernel,
        out_shape=(
            jax.ShapeDtypeStruct(queries.shape, jnp.bfloat16),
            jax.ShapeDtypeStruct(near.shape, jnp.bfloat16),
            jax.ShapeDtypeStruct(far.shape, jnp.bfloat16),
        ),
        in_specs=[smem, smem, vmem, vmem, vmem, vmem],
        out_specs=(vmem, vmem, vmem),
        scratch_shapes=[
            pltpu.VMEM((tiles, span, rows), jnp.float32),
            pltpu.VMEM((tiles, span, rows), jnp.float32),
            pltpu.VMEM((tiles, 1, rows), jnp.float32),
            pltpu.VMEM((HD, rows), jnp.bfloat16),
            pltpu.VMEM((HD, rows), jnp.bfloat16),
            pltpu.VMEM((rows, HD), jnp.bfloat16),
            pltpu.VMEM((rows, HD), jnp.bfloat16),
            pltpu.VMEM((HD, rows), jnp.float32),
        ],
        compiler_params=pltpu.CompilerParams(vmem_limit_bytes=56 * 1024 * 1024),
        name="attention_backward",
    )(order, place, near, far, queries, out_grad)


def spread(value, axis, groups=None):
    count = lax.axis_size(axis) if groups is None else len(groups[0])
    copies = lax.optimization_barrier(jnp.broadcast_to(value[None], (count, *value.shape)))
    return lax.all_to_all(copies, axis, 0, 0, axis_index_groups=groups)


def added(value, axis, groups=None):
    arrived = lax.all_to_all(value, axis, 0, 0, axis_index_groups=groups)
    return jnp.sum(arrived.astype(jnp.float32), axis=0)


def body(hidden_in, queries, out_grad, kv_weight, block_pos, precision):
    score_scale = 1.0 / math.sqrt(HD)
    tokens = hidden_in.shape[1]
    width = hidden_in.shape[2]
    seq_count = lax.axis_size("seq")
    dp_count = lax.axis_size("dp")
    chips = seq_count // 2
    grad_scale = 1.0 / math.sqrt(dp_count * seq_count * tokens)
    self_index = lax.axis_index("seq")
    core = lax.rem(self_index, 2)
    is_first = core == 0
    same_core = [[2 * chip + side for chip in range(chips)] for side in range(2)]
    swap = [(source, source ^ 1) for source in range(seq_count)]

    def swapped(value):
        return lax.ppermute(value, "seq", swap)

    x_rows = hidden_in[0]
    places = block_pos[0]
    place = lax.dynamic_slice_in_dim(places, self_index, 1)
    by_core = places.reshape(chips, 2)
    slot_places = jnp.where(
        is_first,
        jnp.concatenate([by_core[:, 0], by_core[:, 1]]),
        jnp.concatenate([by_core[:, 1], by_core[:, 0]]),
    )
    slots = jnp.arange(seq_count, dtype=jnp.int32)
    order = jnp.sum(
        jnp.where(slot_places[None, :] == slots[:, None], slots[None, :], 0), axis=1
    ).astype(jnp.int32)
    my_pos = place * BLOCK + jnp.arange(tokens, dtype=jnp.int32)
    angles = my_pos.astype(jnp.float32)[:, None] * frequencies(HD)[None, :]
    cosine = jnp.cos(angles)
    sine_part = jnp.sin(angles)

    with jax.named_scope("weight_gather"):
        half = jnp.where(is_first, kv_weight[:, :HD], kv_weight[:, HD:])
        near_weight = spread(half, "dp").reshape(width, HD)
        far_weight = swapped(near_weight)
    with jax.named_scope("projection"):
        near_raw = dot(x_rows, near_weight)
        far_raw = dot(x_rows, far_weight)
        raw_keys = jnp.where(is_first, near_raw, far_raw)
        raw_values = jnp.where(is_first, far_raw, near_raw)
        key_quant = quantize(rotate(raw_keys, cosine, sine_part), precision[0, :, 0])
        value_quant = quantize(raw_values, precision[0, :, 1])
        stacked = jnp.concatenate([key_quant, value_quant], axis=1).astype(jnp.bfloat16)
    with jax.named_scope("kv_gather"):
        near = spread(stacked, "seq", same_core)
        far = swapped(near)
    with jax.named_scope("attention"):
        query_grad, near_grad, far_grad = attention_backward(
            order, place, near, far, queries[0], out_grad[0]
        )
    with jax.named_scope("kv_reduce"):
        pair = near_grad.astype(jnp.float32) + swapped(far_grad).astype(jnp.float32)
        carried = added(pair.astype(jnp.bfloat16), "seq", same_core)
    with jax.named_scope("projection_grad"):
        key_part = rotate_back(carried[:, :HD] * score_scale, cosine, sine_part)
        proj_grad = jnp.concatenate([key_part, carried[:, HD:]], axis=1).astype(jnp.bfloat16)
    with jax.named_scope("weight_grad"):
        share = dot_rows(x_rows, proj_grad).reshape(dp_count, 2, width // dp_count // 2, 2 * HD)
        kept = jnp.where(is_first, share[:, 0], share[:, 1])
        given = jnp.where(is_first, share[:, 1], share[:, 0]).astype(jnp.bfloat16)
        pair_share = kept + swapped(given).astype(jnp.float32)
        group_sum = added(pair_share.astype(jnp.bfloat16), "dp")
        piece = group_sum.shape[0] // chips
        chip_sum = added(
            group_sum.astype(jnp.bfloat16).reshape(chips, piece, 2 * HD), "seq", same_core
        )
        gathered = spread(chip_sum * grad_scale, "seq")
        weight_grad = (
            gathered.reshape(chips, 2, piece, 2 * HD)
            .transpose(1, 0, 2, 3)
            .reshape(width // dp_count, 2 * HD)
        )
    with jax.named_scope("input_grad"):
        key_weight = jnp.where(is_first, near_weight, far_weight)
        value_weight = jnp.where(is_first, far_weight, near_weight)
        weight = jnp.concatenate([key_weight, value_weight], axis=1)
        input_grad = dot_cols(proj_grad, weight).astype(jnp.bfloat16)
    return (query_grad[None], proj_grad[None], input_grad[None], weight_grad)


def solution(mesh):
    in_specs = (
        P("dp", "seq", None),
        P("dp", "seq", None),
        P("dp", "seq", None),
        P("dp", None),
        P("dp", None),
        P("dp", "seq", None),
    )
    out_specs = (P("dp", "seq", None), P("dp", "seq", None), P("dp", "seq", None), P("dp", None))
    return jax.shard_map(body, mesh=mesh, in_specs=in_specs, out_specs=out_specs, check_vma=False)
```

time: 1290 us -> 264 us (0.20)
  waiting for transfers between devices: 972 us -> 11.6 us
  blocking collectives: 0 us -> 168 us
  matrix products: 98.5 us -> 7.1 us
  loops' own time: 60.4 us -> 0 us
  starting transfers between devices: 78.9 us -> 21.6 us
  other arithmetic: 39.1 us -> 9.71 us
  local copies, waits for them, and re-layouts: 13.2 us -> 33 us
  between operations: 16.5 us -> 2.98 us
    psum x1 -> x0, waiting for transfers between devices: 340 us -> none  [body(): weight_grad = lax.psum(grad_share, 'seq')]
    ppermute x32 -> x4, waiting for transfers between devices: 341 us -> 4.84 us  [swapped(): return lax.ppermute(value, 'seq', swap)]
    all_gather x2 -> x0, waiting for transfers between devices: 181 us -> none  [the longest x1 97.4 us: body(): arrived = lax.all_gather(stacked, 'seq', axis=0, tiled=True)]
    all_to_all x0 -> x5, blocking collectives: none -> 168 us  [the longest x3 91.1 us: added(): arrived = lax.all_to_all(value, axis, 0, 0, axis_index_groups=groups)]
    reduce_scatter x1 -> x0, waiting for transfers between devices: 109 us -> none  [body(): lax.psum_scatter(dot_rows(x_rows, proj_grad), 'dp', scatter_dimension=0,...]
    ppermute x32 -> x4, starting transfers between devices: 78.7 us -> 15 us  [swapped(): return lax.ppermute(value, 'seq', swap)]
    another operation x42 -> x0, loops' own time: 60.4 us -> none  [the longest x1 42.6 us: body(): lax.fori_loop(0, cycle_size - 1, cycle_turn, (dq_sum, empty_grads))]
    dot_general x45 -> x1, matrix products: 53.2 us -> 3.39 us  [dot_cols(): lax.dot_general(left, right, (((1,), (1,)), ((), ())), preferred_element_...]
  transfers between devices with their start and end apart: 36 -> 5, of which waited for: 36 -> 4; matrix products, arithmetic and copies ran while one was open for 1% -> 4% of each run, Pallas kernels for 0% -> 0%
where the time goes in v1:
time: 264 us; the launch traced here: 263 us
  blocking collectives  168 us (64%)
  local copies, waits for them, and re-layouts  33 us (12%)
  starting transfers between devices  21.6 us (8%)
  waiting for transfers between devices  11.6 us (4%)
  other arithmetic  9.71 us (4%)
  Pallas kernels  9.53 us (4%)
  matrix products  7.1 us (3%)
  between operations  2.98 us (1%)
    all_to_all x3, blocking collectives, added(): arrived = lax.all_to_all(value, axis, 0, 0, axis_index_groups=groups)  91.1 us
    all_to_all x2, blocking collectives, spread(): return lax.all_to_all(copies, axis, 0, 0, axis_index_groups=groups)  76.5 us
    ppermute x4, starting transfers between devices, swapped(): return lax.ppermute(value, 'seq', swap)  15 us
    unnamed x32, local copies, waits for them, and re-layouts  12.2 us
    slice x1, local copies, waits for them, and re-layouts, body(): kept = jnp.where(is_first, share[:, 0], share[:, 1])  9.74 us
    pallas_call x1, Pallas kernels, attention_backward(): pl.pallas_call(attention_kernel, out_shape=(jax.ShapeDtypeStruct(queries....  9.53 us
    all_to_all x1, waiting for transfers between devices, spread(): return lax.all_to_all(copies, axis, 0, 0, axis_index_groups=groups)  6.81 us
    all_to_all x1, starting transfers between devices, spread(): return lax.all_to_all(copies, axis, 0, 0, axis_index_groups=groups)  6.63 us
  transfers between devices with their start and end apart: 5, of which 4 were waited for; matrix products, arithmetic and copies ran while one was open for 4% of the time, Pallas kernels for 0%

profile of v1, /device:TPU:1, one launch (start us, length us, event | category | flops | bytes accessed | tf_op | source)
XLA Modules:
  0.0 263.2 jit_solution(9305712108072032144)
XLA Ops:
  1.8 34.7 %all_to_all.30 = bf16[16,256,128]{2,1,0:T(8,128)(2,1)S(1)} all-to-all(bf16[16,256,128]{2,1,0:T(8,128)(2,1)S(1)} %broadcast_in_dim.24), channel_id=1, replica_groups=mesh['dp'=16,'seq'=32] {'dp'}, dimensions={0} | all-to-all | bytes 2097152 | tf_op jit(solution)/shard_map/weight_gather/all_to_all | solution.py:205
  36.6 3.7 %collective-permute-start = (bf16[4096,128]{1,0:T(8,128)(2,1)S(1)}, bf16[4096,128]{1,0:T(8,128)(2,1)S(1)}, u32[]{:S(2)}, u32[]{:S(2)}) collective-permute-start(bf16[4096,128]{1,0:T(8,128)(2,1)S(1)} %bitcast.57), channel_id=1, source_target_pairs={{0,1},{1,0},{2,3},{3,2},{4,5},{5,4},{6,7},{7,6},{8,9},{9,8},{10,11... | collective-permute-start | bytes 3145736 | tf_op jit(solution)/shard_map/weight_gather/ppermute | solution.py:228
  45.7 41.8 %all_to_all.31.near_ref = bf16[16,128,256]{2,1,0:T(8,128)(2,1)S(1)} all-to-all(bf16[16,128,256]{2,1,0:T(8,128)(2,1)S(1)} %broadcast_in_dim.25), channel_id=1, replica_groups={{0,2,4,6,8,10,12,14,16,18,20,22,24,26,28,30},{1,3,5,7,9,11,13,15,17,19,..., dimensions={0} | all-to-all | bytes 2097152 | tf_op jit(solution)/shard_map/kv_gather/all_to_all | solution.py:205
  87.4 3.0 %collective-permute-start.1 = (bf16[16,128,256]{2,1,0:T(8,128)(2,1)S(1)}, bf16[16,128,256]{2,1,0:T(8,128)(2,1)S(1)}, u32[]{:S(2)}, u32[]{:S(2)}) collective-permute-start(bf16[16,128,256]{2,1,0:T(8,128)(2,1)S(1)} %all_to_all.31.near_ref), channel_id=1, source_target_pairs={{0,1},{1,0},{2,3},{3,2},{4,5},{5,4},{6,7},{7,6},{8,9},{9,8},{10,11... | collective-permute-start | bytes 3145736 | tf_op jit(solution)/shard_map/kv_gather/ppermute | solution.py:228
  92.7 1.0 copy-done.7
  93.7 9.5 %attention_backward.1 = (bf16[128,1024]{1,0:T(8,128)(2,1)}, bf16[16,128,256]{2,1,0:T(8,128)(2,1)}, bf16[16,128,256]{2,1,0:T(8,128)(2,1)}) custom-call(s32[32]{0:T(128)} %select_reduce_fusion.order_ref, s32[1]{0:T(128)} %bitcast.place_ref, bf16[16,128,256]{2,1,0:T(8,128)(2,1)} %copy-done.6, bf16[16,128,256]{2,1,0:T(8,128)(2,1)} %copy-done.7, ...), custom_call_target="tpu_custom_call" | custom-call | tf_op jit(solution)/shard_map/attention/attention_backward/pallas_call | solution.py:178
  103.2 3.9 %collective-permute-start.2 = (bf16[16,128,256]{2,1,0:T(8,128)(2,1)}, bf16[16,128,256]{2,1,0:T(8,128)(2,1)S(1)}, u32[]{:S(2)}, u32[]{:S(2)}) collective-permute-start(bf16[16,128,256]{2,1,0:T(8,128)(2,1)} %get-tuple-element.9), channel_id=1, source_target_pairs={{0,1},{1,0},{2,3},{3,2},{4,5},{5,4},{6,7},{7,6},{8,9},{9,8},{10,11... | collective-permute-start | bytes 3145736 | tf_op jit(solution)/shard_map/kv_reduce/ppermute | solution.py:228
  107.1 2.5 collective-permute-done.2
  109.6 1.5 add_convert_fusion
  111.1 40.9 %all_to_all.32 = bf16[16,128,256]{2,1,0:T(8,128)(2,1)S(1)} all-to-all(bf16[16,128,256]{2,1,0:T(8,128)(2,1)S(1)} %add_convert_fusion), channel_id=1, replica_groups={{0,2,4,6,8,10,12,14,16,18,20,22,24,26,28,30},{1,3,5,7,9,11,13,15,17,19,..., dimensions={0} | all-to-all | bytes 2097152 | tf_op jit(solution)/shard_map/kv_reduce/all_to_all | solution.py:209
  152.8 2.8 %convolution_bitcast_fusion = f32[4096,256]{0,1:T(8,128)} fusion(bf16[1,128,4096]{2,1,0:T(8,128)(2,1)S(1)} %copy-done, bf16[128,128]{1,0:T(8,128)(2,1)S(1)} %slice.83, bf16[128,64]{1,0:T(8,128)(2,1)S(1)} %copy.39, bf16[128,64]{1,0:T(8,128)(2,1)S(1)} %copy.38), kind=kOutput, calls=%fused_computation | convolution fusion | flops 268632064 | bytes 5308416 | tf_op jit(solution)/shard_map/weight_grad/dot_general | solution.py:59
  155.6 6.6 %reshape.297 = f32[16,2,128,256]{2,1,0,3:T(2,128)} reshape(f32[4096,256]{0,1:T(8,128)} %convolution_bitcast_fusion) | data formatting | bytes 8388608 | tf_op jit(solution)/shard_map/weight_grad/reshape | solution.py:274
  162.2 9.7 %fusion.32 = (f32[16,1,128,256]{2,1,0,3:T(1,128)}, f32[16,1,128,256]{2,1,0,3:T(1,128)}) fusion(f32[16,2,128,256]{2,1,0,3:T(2,128)} %reshape.297), kind=kLoop, calls=%fused_computation.69 | loop fusion | bytes 8388608 | tf_op jit(solution)/shard_map/weight_grad/slice | solution.py:275
  171.9 4.6 %copy.44 = f32[16,1,128,256]{3,2,0,1:T(8,128)S(1)} copy(f32[16,1,128,256]{2,1,0,3:T(1,128)} %get-tuple-element.24) | data formatting | bytes 4194304
  176.5 6.0 %copy.45 = f32[16,1,128,256]{3,2,0,1:T(8,128)} copy(f32[16,1,128,256]{2,1,0,3:T(1,128)} %get-tuple-element.25) | data formatting | bytes 4194304
  182.8 4.4 %collective-permute-start.3 = (bf16[16,128,256]{2,1,0:T(8,128)(2,1)S(1)}, bf16[16,128,256]{2,1,0:T(8,128)(2,1)S(1)}, u32[]{:S(2)}, u32[]{:S(2)}) collective-permute-start(bf16[16,128,256]{2,1,0:T(8,128)(2,1)S(1)} %fusion.5), channel_id=1, source_target_pairs={{0,1},{1,0},{2,3},{3,2},{4,5},{5,4},{6,7},{7,6},{8,9},{9,8},{10,11... | collective-permute-start | bytes 3145736 | tf_op jit(solution)/shard_map/weight_grad/ppermute | solution.py:228
  187.2 2.3 collective-permute-done.3
  190.1 34.2 %all_to_all.33 = bf16[16,128,256]{2,1,0:T(8,128)(2,1)} all-to-all(bf16[16,128,256]{2,1,0:T(8,128)(2,1)S(1)} %fusion.4), channel_id=1, replica_groups=mesh['dp'=16,'seq'=32] {'dp'}, dimensions={0} | all-to-all | bytes 2097152 | tf_op jit(solution)/shard_map/weight_grad/all_to_all | solution.py:209
  224.2 1.4 reduce_sum.41
  225.6 16.1 %all_to_all.34 = bf16[16,8,256]{2,1,0:T(8,128)(2,1)S(1)} all-to-all(bf16[16,8,256]{2,1,0:T(8,128)(2,1)S(1)} %bitcast.64), channel_id=1, replica_groups={{0,2,4,6,8,10,12,14,16,18,20,22,24,26,28,30},{1,3,5,7,9,11,13,15,17,19,..., dimensions={0} | all-to-all | bytes 131072 | tf_op jit(solution)/shard_map/weight_grad/all_to_all | solution.py:209
  242.4 6.6 %all-to-all-start.5 = ((f32[32,8,256]{2,1,0:T(8,128)}), f32[32,8,256]{2,1,0:T(8,128)S(1)}, u32[]{:S(2)}, u32[]{:S(2)}) async-start(f32[32,8,256]{2,1,0:T(8,128)} %broadcast_in_dim.28), calls=%async_computation.5 | async-start | bytes 524288 | tf_op jit(solution)/shard_map/weight_grad/all_to_all | solution.py:205
  249.1 1.5 broadcast_select_fusion.1
  251.6 3.4 %fusion = bf16[1,128,4096]{2,1,0:T(8,128)(2,1)} fusion(bf16[4096,128]{1,0:T(8,128)(2,1)} %get-tuple-element.27, bf16[4096,128]{1,0:T(8,128)(2,1)} %get-tuple-element.26, bf16[128,128]{1,0:T(8,128)(2,1)} %copy-done.9, bf16[128,64]{1,0:T(8,128)(2,1)} %copy-done.11, bf16[128,64]{1,0:T(8,128)(2,1)} %copy-done.10), kind=kOutput, calls=%fused_computation.2 | convolution fusion | flops 273350656 | bytes 3211264 | tf_op jit(solution)/shard_map/input_grad/dot_general | solution.py:65
  255.7 6.8 %all-to-all-done.5 = f32[32,8,256]{2,1,0:T(8,128)S(1)} async-done(((f32[32,8,256]{2,1,0:T(8,128)}), f32[32,8,256]{2,1,0:T(8,128)S(1)}, u32[]{:S(2)}, u32[]{:S(2)}) %all-to-all-start.5) | async-done | bytes 262176 | tf_op jit(solution)/shard_map/weight_grad/all_to_all | solution.py:205
  (70 shorter events, 11.4 us)
Async XLA Ops:
  0.6 42.8 %copy-start = (bf16[1,128,4096]{2,1,0:T(8,128)(2,1)S(1)}, bf16[1,128,4096]{2,1,0:T(8,128)(2,1)}, u32[]{:S(2)}) copy-start(bf16[1,128,4096]{2,1,0:T(8,128)(2,1)} %param.6) | copy-start | bytes 3145732
  0.6 39.6 %copy-start.12 = (s32[1,1,2]{2,1,0:T(1,128)S(1)}, s32[1,1,2]{2,1,0:T(1,128)}, u32[]{:S(2)}) copy-start(s32[1,1,2]{2,1,0:T(1,128)} %param.11) | copy-start | bytes 28
  0.7 41.5 %copy-start.13 = (s32[1,32]{1,0:T(1,128)S(1)}, s32[1,32]{1,0:T(1,128)}, u32[]{:S(2)}) copy-start(s32[1,32]{1,0:T(1,128)} %param.10) | copy-start | bytes 388
  36.6 7.8 %copy-start.2 = (bf16[16,256,128]{2,1,0:T(8,128)(2,1)}, bf16[16,256,128]{2,1,0:T(8,128)(2,1)S(1)}, u32[]{:S(2)}) copy-start(bf16[16,256,128]{2,1,0:T(8,128)(2,1)S(1)} %all_to_all.30) | copy-start | bytes 3145732
  36.6 7.3 %collective-permute-start = (bf16[4096,128]{1,0:T(8,128)(2,1)S(1)}, bf16[4096,128]{1,0:T(8,128)(2,1)S(1)}, u32[]{:S(2)}, u32[]{:S(2)}) collective-permute-start(bf16[4096,128]{1,0:T(8,128)(2,1)S(1)} %bitcast.57), channel_id=1, source_target_pairs={{0,1},{1,0},{2,3},{3,2},{4,5},{5,4},{6,7},{7,6},{8,9},{9,8},{10,11... | collective-permute-start | bytes 3145736 | tf_op jit(solution)/shard_map/weight_gather/ppermute | solution.py:228
  43.9 1.7 copy-start.4
  87.4 5.3 %copy-start.6 = (bf16[16,128,256]{2,1,0:T(8,128)(2,1)}, bf16[16,128,256]{2,1,0:T(8,128)(2,1)S(1)}, u32[]{:S(2)}) copy-start(bf16[16,128,256]{2,1,0:T(8,128)(2,1)S(1)} %all_to_all.31.near_ref) | copy-start | bytes 3145732
  87.4 5.3 %collective-permute-start.1 = (bf16[16,128,256]{2,1,0:T(8,128)(2,1)S(1)}, bf16[16,128,256]{2,1,0:T(8,128)(2,1)S(1)}, u32[]{:S(2)}, u32[]{:S(2)}) collective-permute-start(bf16[16,128,256]{2,1,0:T(8,128)(2,1)S(1)} %all_to_all.31.near_ref), channel_id=1, source_target_pairs={{0,1},{1,0},{2,3},{3,2},{4,5},{5,4},{6,7},{7,6},{8,9},{9,8},{10,11... | collective-permute-start | bytes 3145736 | tf_op jit(solution)/shard_map/kv_gather/ppermute | solution.py:228
  92.7 1.0 copy-start.7
  103.2 6.4 %collective-permute-start.2 = (bf16[16,128,256]{2,1,0:T(8,128)(2,1)}, bf16[16,128,256]{2,1,0:T(8,128)(2,1)S(1)}, u32[]{:S(2)}, u32[]{:S(2)}) collective-permute-start(bf16[16,128,256]{2,1,0:T(8,128)(2,1)} %get-tuple-element.9), channel_id=1, source_target_pairs={{0,1},{1,0},{2,3},{3,2},{4,5},{5,4},{6,7},{7,6},{8,9},{9,8},{10,11... | collective-permute-start | bytes 3145736 | tf_op jit(solution)/shard_map/kv_reduce/ppermute | solution.py:228
  152.2 3.4 %copy-start.9 = (bf16[128,128]{1,0:T(8,128)(2,1)}, bf16[128,128]{1,0:T(8,128)(2,1)S(1)}, u32[]{:S(2)}) copy-start(bf16[128,128]{1,0:T(8,128)(2,1)S(1)} %slice.83) | copy-start | bytes 98308
  152.5 3.0 %copy-start.8 = (bf16[128,64]{0,1:T(8,128)(2,1)}, bf16[128,64]{0,1:T(8,128)(2,1)S(1)}, u32[]{:S(2)}) copy-start(bf16[128,64]{0,1:T(8,128)(2,1)S(1)} %get-tuple-element.31) | copy-start | bytes 49156
  152.7 2.9 %copy-start.10 = (bf16[128,64]{1,0:T(8,128)(2,1)}, bf16[128,64]{1,0:T(8,128)(2,1)S(1)}, u32[]{:S(2)}) copy-start(bf16[128,64]{1,0:T(8,128)(2,1)S(1)} %copy.38) | copy-start | bytes 49156
  152.8 2.8 %copy-start.11 = (bf16[128,64]{1,0:T(8,128)(2,1)}, bf16[128,64]{1,0:T(8,128)(2,1)S(1)}, u32[]{:S(2)}) copy-start(bf16[128,64]{1,0:T(8,128)(2,1)S(1)} %copy.39) | copy-start | bytes 49156
  182.5 7.0 %copy-start.1 = (f32[16,1,128,256]{3,2,0,1:T(8,128)S(1)}, f32[16,1,128,256]{3,2,0,1:T(8,128)}, u32[]{:S(2)}) copy-start(f32[16,1,128,256]{3,2,0,1:T(8,128)} %copy.45) | copy-start | bytes 6291460
  182.8 6.7 %collective-permute-start.3 = (bf16[16,128,256]{2,1,0:T(8,128)(2,1)S(1)}, bf16[16,128,256]{2,1,0:T(8,128)(2,1)S(1)}, u32[]{:S(2)}, u32[]{:S(2)}) collective-permute-start(bf16[16,128,256]{2,1,0:T(8,128)(2,1)S(1)} %fusion.5), channel_id=1, source_target_pairs={{0,1},{1,0},{2,3},{3,2},{4,5},{5,4},{6,7},{7,6},{8,9},{9,8},{10,11... | collective-permute-start | bytes 3145736 | tf_op jit(solution)/shard_map/weight_grad/ppermute | solution.py:228
  190.0 59.0 %copy-start.3 = (bf16[16,256,128]{2,1,0:T(8,128)(2,1)S(1)}, bf16[16,256,128]{2,1,0:T(8,128)(2,1)}, u32[]{:S(2)}) copy-start(bf16[16,256,128]{2,1,0:T(8,128)(2,1)} %copy-done.2) | copy-start | bytes 3145732
  190.0 59.0 %copy-start.5 = (bf16[4096,128]{1,0:T(8,128)(2,1)S(1)}, bf16[4096,128]{1,0:T(8,128)(2,1)}, u32[]{:S(2)}) copy-start(bf16[4096,128]{1,0:T(8,128)(2,1)} %copy-done.4) | copy-start | bytes 3145732
  242.4 20.1 %all-to-all-start.5 = ((f32[32,8,256]{2,1,0:T(8,128)}), f32[32,8,256]{2,1,0:T(8,128)S(1)}, u32[]{:S(2)}, u32[]{:S(2)}) async-start(f32[32,8,256]{2,1,0:T(8,128)} %broadcast_in_dim.28), calls=%async_computation.5 | async-start | bytes 524288 | tf_op jit(solution)/shard_map/weight_grad/all_to_all | solution.py:205

commit v2 on v1

--- a/solution.py
+++ b/solution.py
@@ -199,6 +199,31 @@
     )(order, place, near, far, queries, out_grad)
 
 
+def share_kernel(side_ref, x_ref, grad_ref, out_ref):
+    columns, groups, piece, _ = out_ref.shape
+    part = columns * piece
+    grads = grad_ref[...]
+    for group in range(groups):
+        start = pl.multiple_of((2 * group + side_ref[0]) * part, part)
+        chosen = x_ref[:, pl.ds(start, part)].T
+        share = dot(chosen, grads).astype(out_ref.dtype)
+        for column in range(columns):
+            out_ref[column, group] = share[column * piece : (column + 1) * piece]
+
+
+def weight_share(side, x_rows, proj_grad, columns, groups, kind):
+    piece = x_rows.shape[1] // groups // columns // 2
+    vmem = pl.BlockSpec(memory_space=pltpu.VMEM)
+    return pl.pallas_call(
+        share_kernel,
+        out_shape=jax.ShapeDtypeStruct((columns, groups, piece, proj_grad.shape[1]), kind),
+        in_specs=[pl.BlockSpec(memory_space=pltpu.SMEM), vmem, vmem],
+        out_specs=vmem,
+        compiler_params=pltpu.CompilerParams(vmem_limit_bytes=32 * 1024 * 1024),
+        name="weight_share",
+    )(side, x_rows, proj_grad)
+
+
 def spread(value, axis, groups=None):
     count = lax.axis_size(axis) if groups is None else len(groups[0])
     copies = lax.optimization_barrier(jnp.broadcast_to(value[None], (count, *value.shape)))
@@ -216,26 +241,41 @@
     width = hidden_in.shape[2]
     seq_count = lax.axis_size("seq")
     dp_count = lax.axis_size("dp")
-    chips = seq_count // 2
+    half_count = seq_count // 2
+    columns = half_count // 2
     grad_scale = 1.0 / math.sqrt(dp_count * seq_count * tokens)
     self_index = lax.axis_index("seq")
     core = lax.rem(self_index, 2)
     is_first = core == 0
-    same_core = [[2 * chip + side for chip in range(chips)] for side in range(2)]
+    in_low = self_index < half_count
+    column_groups = [
+        [start * half_count + 2 * column + side for column in range(columns)]
+        for start in range(2)
+        for side in range(2)
+    ]
+    row_count = math.gcd(dp_count, 4)
+    runs = [
+        [start + step for step in range(row_count)] for start in range(0, dp_count, row_count)
+    ]
+    strides = [
+        [start + step for step in range(0, dp_count, row_count)] for start in range(row_count)
+    ]
     swap = [(source, source ^ 1) for source in range(seq_count)]
+    cross = [(source, (source + half_count) % seq_count) for source in range(seq_count)]
 
     def swapped(value):
         return lax.ppermute(value, "seq", swap)
+
+    def crossed(value):
+        return lax.ppermute(value, "seq", cross)
 
     x_rows = hidden_in[0]
     places = block_pos[0]
     place = lax.dynamic_slice_in_dim(places, self_index, 1)
-    by_core = places.reshape(chips, 2)
-    slot_places = jnp.where(
-        is_first,
-        jnp.concatenate([by_core[:, 0], by_core[:, 1]]),
-        jnp.concatenate([by_core[:, 1], by_core[:, 0]]),
-    )
+    cube = places.reshape(2, columns, 2)
+    cube = jnp.where(in_low, cube, cube[::-1])
+    cube = jnp.where(is_first, cube, cube[:, :, ::-1])
+    slot_places = cube.transpose(2, 1, 0).reshape(-1)
     slots = jnp.arange(seq_count, dtype=jnp.int32)
     order = jnp.sum(
         jnp.where(slot_places[None, :] == slots[:, None], slots[None, :], 0), axis=1
@@ -247,7 +287,8 @@
 
     with jax.named_scope("weight_gather"):
         half = jnp.where(is_first, kv_weight[:, :HD], kv_weight[:, HD:])
-        near_weight = spread(half, "dp").reshape(width, HD)
+        run_weight = spread(half, "dp", runs)
+        near_weight = spread(run_weight, "dp", strides).reshape(width, HD)
         far_weight = swapped(near_weight)
     with jax.named_scope("projection"):
         near_raw = dot(x_rows, near_weight)
@@ -258,7 +299,8 @@
         value_quant = quantize(raw_values, precision[0, :, 1])
         stacked = jnp.concatenate([key_quant, value_quant], axis=1).astype(jnp.bfloat16)
     with jax.named_scope("kv_gather"):
-        near = spread(stacked, "seq", same_core)
+        both = jnp.stack([stacked, crossed(stacked)])
+        near = spread(both, "seq", column_groups).reshape(half_count, tokens, 2 * HD)
         far = swapped(near)
     with jax.named_scope("attention"):
         query_grad, near_grad, far_grad = attention_backward(
@@ -266,26 +308,29 @@
         )
     with jax.named_scope("kv_reduce"):
         pair = near_grad.astype(jnp.float32) + swapped(far_grad).astype(jnp.float32)
-        carried = added(pair.astype(jnp.bfloat16), "seq", same_core)
+        column_sum = added(
+            pair.astype(jnp.bfloat16).reshape(columns, 2, tokens, 2 * HD), "seq", column_groups
+        )
+        carried = column_sum[0] + crossed(column_sum[1].astype(jnp.bfloat16)).astype(jnp.float32)
     with jax.named_scope("projection_grad"):
         key_part = rotate_back(carried[:, :HD] * score_scale, cosine, sine_part)
         proj_grad = jnp.concatenate([key_part, carried[:, HD:]], axis=1).astype(jnp.bfloat16)
     with jax.named_scope("weight_grad"):
-        share = dot_rows(x_rows, proj_grad).reshape(dp_count, 2, width // dp_count // 2, 2 * HD)
-        kept = jnp.where(is_first, share[:, 0], share[:, 1])
-        given = jnp.where(is_first, share[:, 1], share[:, 0]).astype(jnp.bfloat16)
+        side = core.reshape(1).astype(jnp.int32)
+        given = weight_share(1 - side, x_rows, proj_grad, columns, dp_count, jnp.bfloat16)
+        kept = weight_share(side, x_rows, proj_grad, columns, dp_count, jnp.float32)
         pair_share = kept + swapped(given).astype(jnp.float32)
-        group_sum = added(pair_share.astype(jnp.bfloat16), "dp")
-        piece = group_sum.shape[0] // chips
-        chip_sum = added(
-            group_sum.astype(jnp.bfloat16).reshape(chips, piece, 2 * HD), "seq", same_core
-        )
-        gathered = spread(chip_sum * grad_scale, "seq")
+        column_share = added(pair_share.astype(jnp.bfloat16), "seq", column_groups)
+        group_share = added(column_share.astype(jnp.bfloat16), "dp")
+        gathered = spread(group_share.astype(jnp.bfloat16), "seq")
+        piece = group_share.shape[0]
         weight_grad = (
-            gathered.reshape(chips, 2, piece, 2 * HD)
+            jnp.sum(
+                gathered.reshape(2, columns, 2, piece, 2 * HD).astype(jnp.float32), axis=0
+            )
             .transpose(1, 0, 2, 3)
             .reshape(width // dp_count, 2 * HD)
-        )
+        ) * grad_scale
     with jax.named_scope("input_grad"):
         key_weight = jnp.where(is_first, near_weight, far_weight)
         value_weight = jnp.where(is_first, far_weight, near_weight)

time: 264 us -> 236 us (0.89)
  blocking collectives: 168 us -> 130 us
  local copies, waits for them, and re-layouts: 33 us -> 3.85 us
  starting transfers between devices: 21.6 us -> 42.6 us
  waiting for transfers between devices: 11.6 us -> 26.3 us
  Pallas kernels: 9.53 us -> 15.3 us
  matrix products: 7.1 us -> 3.85 us
    all_to_all x3 -> x2, blocking collectives: 91.1 us -> 65.4 us  [added(): arrived = lax.all_to_all(value, axis, 0, 0, axis_index_groups=groups)]
    ppermute x0 -> x2, starting transfers between devices: none -> 13.1 us  [crossed(): return lax.ppermute(value, 'seq', cross)]
    unnamed x32 -> x7, local copies, waits for them, and re-layouts: 12.2 us -> 0.53 us
    all_to_all x2 -> x3, blocking collectives: 76.5 us -> 64.9 us  [spread(): return lax.all_to_all(copies, axis, 0, 0, axis_index_groups=groups)]
    slice x3 -> x0, local copies, waits for them, and re-layouts: 9.93 us -> none  [the longest x1 9.74 us: body(): kept = jnp.where(is_first, share[:, 0], share[:, 1])]
    all_to_all x0 -> x1, starting transfers between devices: none -> 6.57 us  [added(): arrived = lax.all_to_all(value, axis, 0, 0, axis_index_groups=groups)]
    reshape x1 -> x0, local copies, waits for them, and re-layouts: 6.57 us -> none  [body(): dot_rows(x_rows, proj_grad)]
    all_to_all x0 -> x1, waiting for transfers between devices: none -> 6.06 us  [added(): arrived = lax.all_to_all(value, axis, 0, 0, axis_index_groups=groups)]
  transfers between devices with their start and end apart: 5 -> 8, of which waited for: 4 -> 7; matrix products, arithmetic and copies ran while one was open for 4% -> 4% of each run, Pallas kernels for 0% -> 0%
where the time goes in v2:
time: 236 us; the launch traced here: 234 us
  blocking collectives  130 us (55%)
  starting transfers between devices  42.6 us (18%)
  waiting for transfers between devices  26.3 us (11%)
  Pallas kernels  15.3 us (6%)
  other arithmetic  8.57 us (4%)
  local copies, waits for them, and re-layouts  3.85 us (2%)
  matrix products  3.85 us (2%)
  between operations  2.81 us (1%)
    all_to_all x2, blocking collectives, added(): arrived = lax.all_to_all(value, axis, 0, 0, axis_index_groups=groups)  65.4 us
    all_to_all x3, blocking collectives, spread(): return lax.all_to_all(copies, axis, 0, 0, axis_index_groups=groups)  64.9 us
    ppermute x4, starting transfers between devices, swapped(): return lax.ppermute(value, 'seq', swap)  16.1 us
    pallas_call x1, Pallas kernels, attention_backward(): pl.pallas_call(attention_kernel, out_shape=(jax.ShapeDtypeStruct(queries....  14.4 us
    ppermute x2, starting transfers between devices, crossed(): return lax.ppermute(value, 'seq', cross)  13.1 us
    all_to_all x1, waiting for transfers between devices, spread(): return lax.all_to_all(copies, axis, 0, 0, axis_index_groups=groups)  9.7 us
    all_to_all x1, starting transfers between devices, spread(): return lax.all_to_all(copies, axis, 0, 0, axis_index_groups=groups)  6.81 us
    all_to_all x1, starting transfers between devices, added(): arrived = lax.all_to_all(value, axis, 0, 0, axis_index_groups=groups)  6.57 us
  transfers between devices with their start and end apart: 8, of which 7 were waited for; matrix products, arithmetic and copies ran while one was open for 4% of the time, Pallas kernels for 0%

profile of v2, /device:TPU:1, one launch (start us, length us, event | category | flops | bytes accessed | tf_op | source)
XLA Modules:
  0.0 233.6 jit_solution(412709131763927827)
XLA Ops:
  0.6 0.9 slice_select_fusion
  1.6 11.3 %all_to_all.35 = bf16[4,256,128]{2,1,0:T(8,128)(2,1)S(1)} all-to-all(bf16[4,256,128]{2,1,0:T(8,128)(2,1)S(1)} %broadcast_in_dim.26), channel_id=1, replica_groups={{0,32,64,96},{128,160,192,224},{256,288,320,352},{384,416,448,480},{1,3..., dimensions={0} | all-to-all | bytes 524288 | tf_op jit(solution)/shard_map/weight_gather/all_to_all | solution.py:230
  13.1 16.6 %all_to_all.36 = bf16[4,4,256,128]{3,2,1,0:T(8,128)(2,1)S(1)} all-to-all(bf16[4,4,256,128]{3,2,1,0:T(8,128)(2,1)S(1)} %broadcast_in_dim.27), channel_id=1, replica_groups={{0,128,256,384},{32,160,288,416},{64,192,320,448},{96,224,352,480},{1,1..., dimensions={0} | all-to-all | bytes 2097152 | tf_op jit(solution)/shard_map/weight_gather/all_to_all | solution.py:230
  29.8 6.0 %collective-permute-start = (bf16[4096,128]{1,0:T(8,128)(2,1)S(1)}, bf16[4096,128]{1,0:T(8,128)(2,1)S(1)}, u32[]{:S(2)}, u32[]{:S(2)}) collective-permute-start(bf16[4096,128]{1,0:T(8,128)(2,1)S(1)} %bitcast.62), channel_id=1, source_target_pairs={{0,1},{1,0},{2,3},{3,2},{4,5},{5,4},{6,7},{7,6},{8,9},{9,8},{10,11... | collective-permute-start | bytes 3145736 | tf_op jit(solution)/shard_map/weight_gather/ppermute | solution.py:267
  40.7 5.6 %collective-permute-start.1 = (bf16[128,256]{1,0:T(8,128)(2,1)S(1)}, bf16[128,256]{1,0:T(8,128)(2,1)S(1)}, u32[]{:S(2)}, u32[]{:S(2)}) collective-permute-start(bf16[128,256]{1,0:T(8,128)(2,1)S(1)} %pad_maximum_fusion.1), channel_id=1, source_target_pairs={{0,16},{1,17},{2,18},{3,19},{4,20},{5,21},{6,22},{7,23},{8,24},{9,... | collective-permute-start | bytes 196616 | tf_op jit(solution)/shard_map/kv_gather/ppermute | solution.py:270
  46.3 3.9 %collective-permute-done.1 = bf16[128,256]{1,0:T(8,128)(2,1)S(1)} collective-permute-done((bf16[128,256]{1,0:T(8,128)(2,1)S(1)}, bf16[128,256]{1,0:T(8,128)(2,1)S(1)}, u32[]{:S(2)}, u32[]{:S(2)}) %collective-permute-start.1) | collective-permute-done | bytes 65568 | tf_op jit(solution)/shard_map/kv_gather/ppermute | solution.py:270
  50.4 36.9 %all_to_all.37 = bf16[8,2,128,256]{3,2,1,0:T(8,128)(2,1)} all-to-all(bf16[8,2,128,256]{3,2,1,0:T(8,128)(2,1)S(1)} %broadcast_in_dim.28), channel_id=1, replica_groups={{0,2,4,6,8,10,12,14},{1,3,5,7,9,11,13,15},{16,18,20,22,24,26,28,30},{17..., dimensions={0} | all-to-all | bytes 2097152 | tf_op jit(solution)/shard_map/kv_gather/all_to_all | solution.py:230
  87.3 4.6 %collective-permute-start.2 = (bf16[16,128,256]{2,1,0:T(8,128)(2,1)}, bf16[16,128,256]{2,1,0:T(8,128)(2,1)}, u32[]{:S(2)}, u32[]{:S(2)}) collective-permute-start(bf16[16,128,256]{2,1,0:T(8,128)(2,1)} %bitcast.14.near_ref), channel_id=1, source_target_pairs={{0,1},{1,0},{2,3},{3,2},{4,5},{5,4},{6,7},{7,6},{8,9},{9,8},{10,11... | collective-permute-start | bytes 3145736 | tf_op jit(solution)/shard_map/kv_gather/ppermute | solution.py:267
  94.5 14.4 %attention_backward.1 = (bf16[128,1024]{1,0:T(8,128)(2,1)}, bf16[16,128,256]{2,1,0:T(8,128)(2,1)}, bf16[16,128,256]{2,1,0:T(8,128)(2,1)}) custom-call(s32[32]{0:T(128)} %select_reduce_fusion.order_ref, s32[1]{0:T(128)} %bitcast.1.place_ref, bf16[16,128,256]{2,1,0:T(8,128)(2,1)} %bitcast.14.near_ref, bf16[16,128,256]{2,1,0:T(8,128)(2,1)} %collective-permute-done.2.far_ref, ...), custom_call_target="tpu_custom_call" | custom-call | tf_op jit(solution)/shard_map/attention/attention_backward/pallas_call | solution.py:178
  108.9 1.9 collective-permute-start.3
  110.8 2.8 %collective-permute-done.3 = bf16[16,128,256]{2,1,0:T(8,128)(2,1)S(1)} collective-permute-done((bf16[16,128,256]{2,1,0:T(8,128)(2,1)}, bf16[16,128,256]{2,1,0:T(8,128)(2,1)S(1)}, u32[]{:S(2)}, u32[]{:S(2)}) %collective-permute-start.3) | collective-permute-done | bytes 1048608 | tf_op jit(solution)/shard_map/kv_reduce/ppermute | solution.py:267
  113.6 1.5 add_convert_fusion.1
  115.2 33.8 %all_to_all.38 = bf16[8,2,128,256]{3,2,1,0:T(8,128)(2,1)S(1)} all-to-all(bf16[8,2,128,256]{3,2,1,0:T(8,128)(2,1)S(1)} %bitcast.64), channel_id=1, replica_groups={{0,2,4,6,8,10,12,14},{1,3,5,7,9,11,13,15},{16,18,20,22,24,26,28,30},{17..., dimensions={0} | all-to-all | bytes 2097152 | tf_op jit(solution)/shard_map/kv_reduce/all_to_all | solution.py:234
  149.1 7.5 %collective-permute-start.4 = (bf16[128,256]{1,0:T(8,128)(2,1)S(1)}, bf16[128,256]{1,0:T(8,128)(2,1)S(1)}, u32[]{:S(2)}, u32[]{:S(2)}) collective-permute-start(bf16[128,256]{1,0:T(8,128)(2,1)S(1)} %fusion.19), channel_id=1, source_target_pairs={{0,16},{1,17},{2,18},{3,19},{4,20},{5,21},{6,22},{7,23},{8,24},{9,... | collective-permute-start | bytes 196616 | tf_op jit(solution)/shard_map/kv_reduce/ppermute | solution.py:270
  156.7 1.6 collective-permute-done.4
  159.3 3.5 %collective-permute-start.5 = (bf16[8,16,16,256]{3,2,1,0:T(8,128)(2,1)S(1)}, bf16[8,16,16,256]{3,2,1,0:T(8,128)(2,1)S(1)}, u32[]{:S(2)}, u32[]{:S(2)}) collective-permute-start(bf16[8,16,16,256]{3,2,1,0:T(8,128)(2,1)S(1)} %weight_share.3), channel_id=1, source_target_pairs={{0,1},{1,0},{2,3},{3,2},{4,5},{5,4},{6,7},{7,6},{8,9},{9,8},{10,11... | collective-permute-start | bytes 3145736 | tf_op jit(solution)/shard_map/weight_grad/ppermute | solution.py:267
  163.3 1.8 collective-permute-done.5
  165.5 31.6 %all_to_all.39 = bf16[8,16,16,256]{3,2,1,0:T(8,128)(2,1)S(1)} all-to-all(bf16[8,16,16,256]{3,2,1,0:T(8,128)(2,1)S(1)} %add_convert_fusion), channel_id=1, replica_groups={{0,2,4,6,8,10,12,14},{1,3,5,7,9,11,13,15},{16,18,20,22,24,26,28,30},{17..., dimensions={0} | all-to-all | bytes 2097152 | tf_op jit(solution)/shard_map/weight_grad/all_to_all | solution.py:234
  197.9 6.6 %all-to-all-start.5 = ((bf16[16,16,256]{2,1,0:T(8,128)(2,1)}), bf16[16,16,256]{2,1,0:T(8,128)(2,1)S(1)}, u32[]{:S(2)}, u32[]{:S(2)}) async-start(bf16[16,16,256]{2,1,0:T(8,128)(2,1)} %reduce_sum.53), calls=%async_computation.5 | async-start | bytes 262144 | tf_op jit(solution)/shard_map/weight_grad/all_to_all | solution.py:234
  204.5 1.2 broadcast_select_fusion.1
  205.7 6.1 %all-to-all-done.5 = bf16[16,16,256]{2,1,0:T(8,128)(2,1)S(1)} async-done(((bf16[16,16,256]{2,1,0:T(8,128)(2,1)}), bf16[16,16,256]{2,1,0:T(8,128)(2,1)S(1)}, u32[]{:S(2)}, u32[]{:S(2)}) %all-to-all-start.5) | async-done | bytes 131104 | tf_op jit(solution)/shard_map/weight_grad/all_to_all | solution.py:234
  212.5 6.8 %all-to-all-start.6 = ((bf16[32,16,256]{2,1,0:T(8,128)(2,1)}), bf16[32,16,256]{2,1,0:T(8,128)(2,1)S(1)}, u32[]{:S(2)}, u32[]{:S(2)}) async-start(bf16[32,16,256]{2,1,0:T(8,128)(2,1)} %broadcast_in_dim.31), calls=%async_computation.6 | async-start | bytes 524288 | tf_op jit(solution)/shard_map/weight_grad/all_to_all | solution.py:230
  220.1 3.0 %fusion = bf16[1,128,4096]{2,1,0:T(8,128)(2,1)} fusion(bf16[128,256]{1,0:T(8,128)(2,1)S(1)} %pad_maximum_fusion.3.grad_ref, bf16[4096,128]{1,0:T(8,128)(2,1)} %get-tuple-element.11, bf16[4096,128]{1,0:T(8,128)(2,1)S(1)} %get-tuple-element.10), kind=kOutput, calls=%fused_computation.1 | convolution fusion | flops 273154048 | bytes 3211264 | tf_op jit(solution)/shard_map/input_grad/dot_general | solution.py:65
  223.1 9.7 %all-to-all-done.6 = bf16[32,16,256]{2,1,0:T(8,128)(2,1)S(1)} async-done(((bf16[32,16,256]{2,1,0:T(8,128)(2,1)}), bf16[32,16,256]{2,1,0:T(8,128)(2,1)S(1)}, u32[]{:S(2)}, u32[]{:S(2)}) %all-to-all-start.6) | async-done | bytes 262176 | tf_op jit(solution)/shard_map/weight_grad/all_to_all | solution.py:230
  (52 shorter events, 11.0 us)
Async XLA Ops:
  1.5 34.3 %copy-start.1 = (s32[1,1,2]{2,1,0:T(1,128)S(1)}, s32[1,1,2]{2,1,0:T(1,128)}, u32[]{:S(2)}) copy-start(s32[1,1,2]{2,1,0:T(1,128)} %param.11) | copy-start | bytes 28
  1.5 36.2 %copy-start.2 = (s32[1,32]{1,0:T(1,128)S(1)}, s32[1,32]{1,0:T(1,128)}, u32[]{:S(2)}) copy-start(s32[1,32]{1,0:T(1,128)} %param.10) | copy-start | bytes 388
  1.5 37.3 %copy-start = (bf16[1,128,4096]{2,1,0:T(8,128)(2,1)S(1)}, bf16[1,128,4096]{2,1,0:T(8,128)(2,1)}, u32[]{:S(2)}) copy-start(bf16[1,128,4096]{2,1,0:T(8,128)(2,1)} %param.6) | copy-start | bytes 3145732
  29.8 9.5 %collective-permute-start = (bf16[4096,128]{1,0:T(8,128)(2,1)S(1)}, bf16[4096,128]{1,0:T(8,128)(2,1)S(1)}, u32[]{:S(2)}, u32[]{:S(2)}) collective-permute-start(bf16[4096,128]{1,0:T(8,128)(2,1)S(1)} %bitcast.62), channel_id=1, source_target_pairs={{0,1},{1,0},{2,3},{3,2},{4,5},{5,4},{6,7},{7,6},{8,9},{9,8},{10,11... | collective-permute-start | bytes 3145736 | tf_op jit(solution)/shard_map/weight_gather/ppermute | solution.py:267
  40.7 9.5 %collective-permute-start.1 = (bf16[128,256]{1,0:T(8,128)(2,1)S(1)}, bf16[128,256]{1,0:T(8,128)(2,1)S(1)}, u32[]{:S(2)}, u32[]{:S(2)}) collective-permute-start(bf16[128,256]{1,0:T(8,128)(2,1)S(1)} %pad_maximum_fusion.1), channel_id=1, source_target_pairs={{0,16},{1,17},{2,18},{3,19},{4,20},{5,21},{6,22},{7,23},{8,24},{9,... | collective-permute-start | bytes 196616 | tf_op jit(solution)/shard_map/kv_gather/ppermute | solution.py:270
  87.3 7.2 %collective-permute-start.2 = (bf16[16,128,256]{2,1,0:T(8,128)(2,1)}, bf16[16,128,256]{2,1,0:T(8,128)(2,1)}, u32[]{:S(2)}, u32[]{:S(2)}) collective-permute-start(bf16[16,128,256]{2,1,0:T(8,128)(2,1)} %bitcast.14.near_ref), channel_id=1, source_target_pairs={{0,1},{1,0},{2,3},{3,2},{4,5},{5,4},{6,7},{7,6},{8,9},{9,8},{10,11... | collective-permute-start | bytes 3145736 | tf_op jit(solution)/shard_map/kv_gather/ppermute | solution.py:267
  108.9 4.8 %collective-permute-start.3 = (bf16[16,128,256]{2,1,0:T(8,128)(2,1)}, bf16[16,128,256]{2,1,0:T(8,128)(2,1)S(1)}, u32[]{:S(2)}, u32[]{:S(2)}) collective-permute-start(bf16[16,128,256]{2,1,0:T(8,128)(2,1)} %get-tuple-element.9), channel_id=1, source_target_pairs={{0,1},{1,0},{2,3},{3,2},{4,5},{5,4},{6,7},{7,6},{8,9},{9,8},{10,11... | collective-permute-start | bytes 3145736 | tf_op jit(solution)/shard_map/kv_reduce/ppermute | solution.py:267
  149.1 9.2 %collective-permute-start.4 = (bf16[128,256]{1,0:T(8,128)(2,1)S(1)}, bf16[128,256]{1,0:T(8,128)(2,1)S(1)}, u32[]{:S(2)}, u32[]{:S(2)}) collective-permute-start(bf16[128,256]{1,0:T(8,128)(2,1)S(1)} %fusion.19), channel_id=1, source_target_pairs={{0,16},{1,17},{2,18},{3,19},{4,20},{5,21},{6,22},{7,23},{8,24},{9,... | collective-permute-start | bytes 196616 | tf_op jit(solution)/shard_map/kv_reduce/ppermute | solution.py:270
  159.3 5.8 %collective-permute-start.5 = (bf16[8,16,16,256]{3,2,1,0:T(8,128)(2,1)S(1)}, bf16[8,16,16,256]{3,2,1,0:T(8,128)(2,1)S(1)}, u32[]{:S(2)}, u32[]{:S(2)}) collective-permute-start(bf16[8,16,16,256]{3,2,1,0:T(8,128)(2,1)S(1)} %weight_share.3), channel_id=1, source_target_pairs={{0,1},{1,0},{2,3},{3,2},{4,5},{5,4},{6,7},{7,6},{8,9},{9,8},{10,11... | collective-permute-start | bytes 3145736 | tf_op jit(solution)/shard_map/weight_grad/ppermute | solution.py:267
  197.9 13.8 %all-to-all-start.5 = ((bf16[16,16,256]{2,1,0:T(8,128)(2,1)}), bf16[16,16,256]{2,1,0:T(8,128)(2,1)S(1)}, u32[]{:S(2)}, u32[]{:S(2)}) async-start(bf16[16,16,256]{2,1,0:T(8,128)(2,1)} %reduce_sum.53), calls=%async_computation.5 | async-start | bytes 262144 | tf_op jit(solution)/shard_map/weight_grad/all_to_all | solution.py:234
  212.5 20.3 %all-to-all-start.6 = ((bf16[32,16,256]{2,1,0:T(8,128)(2,1)}), bf16[32,16,256]{2,1,0:T(8,128)(2,1)S(1)}, u32[]{:S(2)}, u32[]{:S(2)}) async-start(bf16[32,16,256]{2,1,0:T(8,128)(2,1)} %broadcast_in_dim.31), calls=%async_computation.6 | async-start | bytes 524288 | tf_op jit(solution)/shard_map/weight_grad/all_to_all | solution.py:230

commit v3 on v1

--- a/solution.py
+++ b/solution.py
@@ -199,6 +199,69 @@
     )(order, place, near, far, queries, out_grad)
 
 
+def turn_kernel(column_ref, x_ref, *rest):
+    outs, flipped = rest[:-1], rest[-1]
+    columns = len(outs)
+    width = x_ref.shape[1]
+    piece = BLOCK // columns
+    for block in range(width // BLOCK):
+        part = pl.ds(block * BLOCK, BLOCK)
+        flipped[part, :] = x_ref[:, part].T
+    for turn, out_ref in enumerate(outs):
+        column = lax.rem(column_ref[0] + turn, columns)
+        for block in range(width // BLOCK):
+            start = pl.multiple_of(block * BLOCK + column * piece, piece)
+            out_ref[block * piece : (block + 1) * piece, :] = flipped[pl.ds(start, piece), :]
+
+
+def column_pieces(column, x_rows, columns):
+    tokens, width = x_rows.shape
+    vmem = pl.BlockSpec(memory_space=pltpu.VMEM)
+    shape = jax.ShapeDtypeStruct((width // columns, tokens), x_rows.dtype)
+    return pl.pallas_call(
+        turn_kernel,
+        out_shape=(shape,) * columns,
+        in_specs=[pl.BlockSpec(memory_space=pltpu.SMEM), vmem],
+        out_specs=(vmem,) * columns,
+        scratch_shapes=[pltpu.VMEM((width, tokens), x_rows.dtype)],
+        compiler_params=pltpu.CompilerParams(vmem_limit_bytes=32 * 1024 * 1024),
+        name="column_pieces",
+    )(column, x_rows)
+
+
+def share_kernel(column_ref, side_ref, grads_ref, *rest):
+    pieces, (kept_ref, given_ref) = rest[:-2], rest[-2:]
+    columns = len(pieces)
+    groups, piece, _ = kept_ref.shape
+    share = jnp.zeros((pieces[0].shape[0], grads_ref.shape[2]), jnp.float32)
+    for turn, piece_ref in enumerate(pieces):
+        column = lax.rem(column_ref[0] + columns - turn, columns)
+        share += dot(piece_ref[...], grads_ref[column])
+    parts = share.reshape(groups, 2, piece, share.shape[1])
+    first = side_ref[0] == 0
+    kept_ref[...] = jnp.where(first, parts[:, 0], parts[:, 1])
+    given_ref[...] = jnp.where(first, parts[:, 1], parts[:, 0]).astype(jnp.bfloat16)
+
+
+def weight_share(column, side, grads, pieces, groups):
+    columns = len(pieces)
+    piece = pieces[0].shape[0] // groups // 2
+    smem = pl.BlockSpec(memory_space=pltpu.SMEM)
+    vmem = pl.BlockSpec(memory_space=pltpu.VMEM)
+    shape = (groups, piece, grads.shape[2])
+    return pl.pallas_call(
+        share_kernel,
+        out_shape=(
+            jax.ShapeDtypeStruct(shape, jnp.float32),
+            jax.ShapeDtypeStruct(shape, jnp.bfloat16),
+        ),
+        in_specs=[smem, smem] + [vmem] * (columns + 1),
+        out_specs=(vmem, vmem),
+        compiler_params=pltpu.CompilerParams(vmem_limit_bytes=32 * 1024 * 1024),
+        name="weight_share",
+    )(column, side, grads, *pieces)
+
+
 def spread(value, axis, groups=None):
     count = lax.axis_size(axis) if groups is None else len(groups[0])
     copies = lax.optimization_barrier(jnp.broadcast_to(value[None], (count, *value.shape)))
@@ -216,12 +279,40 @@
     width = hidden_in.shape[2]
     seq_count = lax.axis_size("seq")
     dp_count = lax.axis_size("dp")
-    chips = seq_count // 2
+    half_count = seq_count // 2
+    columns = half_count // 2
     grad_scale = 1.0 / math.sqrt(dp_count * seq_count * tokens)
     self_index = lax.axis_index("seq")
     core = lax.rem(self_index, 2)
     is_first = core == 0
-    same_core = [[2 * chip + side for chip in range(chips)] for side in range(2)]
+    column_groups = [
+        [start * half_count + 2 * column + side for column in range(columns)]
+        for start in range(2)
+        for side in range(2)
+    ]
+    plane_groups = [
+        [
+            group * seq_count + start * half_count + place_in
+            for group in range(dp_count)
+            for start in range(2)
+        ]
+        for place_in in range(half_count)
+    ]
+    half_groups = [
+        [start * half_count + place_in for place_in in range(half_count)] for start in range(2)
+    ]
+    turns = [
+        [
+            (
+                source,
+                source // half_count * half_count
+                + (source % half_count + 2 * turn) % half_count,
+            )
+            for source in range(seq_count)
+        ]
+        for turn in range(columns)
+    ]
+    same_core = [[2 * chip + side for chip in range(half_count)] for side in range(2)]
     swap = [(source, source ^ 1) for source in range(seq_count)]
 
     def swapped(value):
@@ -230,7 +321,7 @@
     x_rows = hidden_in[0]
     places = block_pos[0]
     place = lax.dynamic_slice_in_dim(places, self_index, 1)
-    by_core = places.reshape(chips, 2)
+    by_core = places.reshape(half_count, 2)
     slot_places = jnp.where(
         is_first,
         jnp.concatenate([by_core[:, 0], by_core[:, 1]]),
@@ -245,9 +336,18 @@
     cosine = jnp.cos(angles)
     sine_part = jnp.sin(angles)
 
+    with jax.named_scope("column_pieces"):
+        column = lax.rem(lax.div(self_index, 2), columns).reshape(1).astype(jnp.int32)
+        pieces = [
+            piece if turn == 0 else lax.ppermute(piece, "seq", turns[turn])
+            for turn, piece in enumerate(column_pieces(column, x_rows, columns))
+        ]
     with jax.named_scope("weight_gather"):
         half = jnp.where(is_first, kv_weight[:, :HD], kv_weight[:, HD:])
         near_weight = spread(half, "dp").reshape(width, HD)
+        near_weight, order, cosine, sine_part, *pieces = lax.optimization_barrier(
+            (near_weight, order, cosine, sine_part, *pieces)
+        )
         far_weight = swapped(near_weight)
     with jax.named_scope("projection"):
         near_raw = dot(x_rows, near_weight)
@@ -271,18 +371,20 @@
         key_part = rotate_back(carried[:, :HD] * score_scale, cosine, sine_part)
         proj_grad = jnp.concatenate([key_part, carried[:, HD:]], axis=1).astype(jnp.bfloat16)
     with jax.named_scope("weight_grad"):
-        share = dot_rows(x_rows, proj_grad).reshape(dp_count, 2, width // dp_count // 2, 2 * HD)
-        kept = jnp.where(is_first, share[:, 0], share[:, 1])
-        given = jnp.where(is_first, share[:, 1], share[:, 0]).astype(jnp.bfloat16)
+        side = core.reshape(1).astype(jnp.int32)
+        column_grads = spread(proj_grad, "seq", column_groups)
+        kept, given = weight_share(column, side, column_grads, pieces, dp_count)
         pair_share = kept + swapped(given).astype(jnp.float32)
-        group_sum = added(pair_share.astype(jnp.bfloat16), "dp")
-        piece = group_sum.shape[0] // chips
-        chip_sum = added(
-            group_sum.astype(jnp.bfloat16).reshape(chips, piece, 2 * HD), "seq", same_core
+        copies = jnp.broadcast_to(
+            pair_share.astype(jnp.bfloat16)[:, None], (dp_count, 2, *pair_share.shape[1:])
         )
-        gathered = spread(chip_sum * grad_scale, "seq")
+        whole_share = added(
+            copies.reshape(2 * dp_count, *pair_share.shape[1:]), ("dp", "seq"), plane_groups
+        )
+        gathered = spread(whole_share * grad_scale, "seq", half_groups)
+        piece = whole_share.shape[0]
         weight_grad = (
-            gathered.reshape(chips, 2, piece, 2 * HD)
+            gathered.reshape(columns, 2, piece, 2 * HD)
             .transpose(1, 0, 2, 3)
             .reshape(width // dp_count, 2 * HD)
         )

time: 264 us -> 236 us (0.89)
  blocking collectives: 168 us -> 93.4 us
  starting transfers between devices: 21.6 us -> 79.9 us
  local copies, waits for them, and re-layouts: 33 us -> 7.96 us
  waiting for transfers between devices: 11.6 us -> 32.3 us
  matrix products: 7.1 us -> 3.94 us
    all_to_all x3 -> x1, blocking collectives: 91.1 us -> 39.9 us  [added(): arrived = lax.all_to_all(value, axis, 0, 0, axis_index_groups=groups)]
    ppermute x0 -> x7, starting transfers between devices: none -> 31.6 us  [body(): lax.ppermute(piece, 'seq', turns[turn])]
    all_to_all x2, blocking collectives: 76.5 us -> 53.4 us  [spread(): return lax.all_to_all(copies, axis, 0, 0, axis_index_groups=groups)]
    all_to_all x0 -> x1, starting transfers between devices: none -> 14 us  [added(): arrived = lax.all_to_all(value, axis, 0, 0, axis_index_groups=groups)]
    unnamed x32 -> x18, local copies, waits for them, and re-layouts: 12.2 us -> 1.64 us
    slice x1 -> x0, local copies, waits for them, and re-layouts: 9.74 us -> none  [body(): kept = jnp.where(is_first, share[:, 0], share[:, 1])]
    ppermute x0 -> x7, waiting for transfers between devices: none -> 9.3 us  [body(): lax.ppermute(piece, 'seq', turns[turn])]
    all_to_all x1 -> x2, starting transfers between devices: 6.63 us -> 15.3 us  [spread(): return lax.all_to_all(copies, axis, 0, 0, axis_index_groups=groups)]
  transfers between devices with their start and end apart: 5 -> 14, of which waited for: 4 -> 7; matrix products, arithmetic and copies ran while one was open for 4% -> 4% of each run, Pallas kernels for 0% -> 0%
where the time goes in v3:
time: 236 us; the launch traced here: 235 us
  blocking collectives  93.4 us (40%)
  starting transfers between devices  79.9 us (34%)
  waiting for transfers between devices  32.3 us (14%)
  local copies, waits for them, and re-layouts  7.96 us (3%)
  Pallas kernels  7.54 us (3%)
  other arithmetic  7.26 us (3%)
  matrix products  3.94 us (2%)
  between operations  3.06 us (1%)
    all_to_all x2, blocking collectives, spread(): return lax.all_to_all(copies, axis, 0, 0, axis_index_groups=groups)  53.4 us
    all_to_all x1, blocking collectives, added(): arrived = lax.all_to_all(value, axis, 0, 0, axis_index_groups=groups)  39.9 us
    ppermute x7, starting transfers between devices, body(): lax.ppermute(piece, 'seq', turns[turn])  31.6 us
    ppermute x4, starting transfers between devices, swapped(): return lax.ppermute(value, 'seq', swap)  19 us
    all_to_all x2, starting transfers between devices, spread(): return lax.all_to_all(copies, axis, 0, 0, axis_index_groups=groups)  15.3 us
    all_to_all x1, starting transfers between devices, added(): arrived = lax.all_to_all(value, axis, 0, 0, axis_index_groups=groups)  14 us
    all_to_all x2, waiting for transfers between devices, spread(): return lax.all_to_all(copies, axis, 0, 0, axis_index_groups=groups)  9.34 us
    ppermute x7, waiting for transfers between devices, body(): lax.ppermute(piece, 'seq', turns[turn])  9.3 us
  transfers between devices with their start and end apart: 14, of which 7 were waited for; matrix products, arithmetic and copies ran while one was open for 4% of the time, Pallas kernels for 0%

profile of v3, /device:TPU:1, one launch (start us, length us, event | category | flops | bytes accessed | tf_op | source)
XLA Modules:
  0.0 235.3 jit_solution(14757599190796897354)
XLA Ops:
  2.7 8.2 %all-to-all-start = ((bf16[16,256,128]{2,1,0:T(8,128)(2,1)}), bf16[16,256,128]{2,1,0:T(8,128)(2,1)}, u32[]{:S(2)}, u32[]{:S(2)}) async-start(bf16[16,256,128]{2,1,0:T(8,128)(2,1)} %broadcast_in_dim.26), calls=%async_computation | async-start | bytes 2097152 | tf_op jit(solution)/shard_map/weight_gather/all_to_all | solution.py:268
  11.5 4.0 %collective-permute-start = (bf16[512,128]{1,0:T(8,128)(2,1)S(1)}, bf16[512,128]{1,0:T(8,128)(2,1)S(1)}, u32[]{:S(2)}, u32[]{:S(2)}) collective-permute-start(bf16[512,128]{1,0:T(8,128)(2,1)S(1)} %get-tuple-element.30), channel_id=1, source_target_pairs={{0,2},{1,3},{2,4},{3,5},{4,6},{5,7},{6,8},{7,9},{8,10},{9,11},{10,... | collective-permute-start | bytes 393224 | tf_op jit(solution)/shard_map/column_pieces/ppermute | solution.py:342
  15.5 5.8 %collective-permute-start.1 = (bf16[512,128]{1,0:T(8,128)(2,1)S(1)}, bf16[512,128]{1,0:T(8,128)(2,1)S(1)}, u32[]{:S(2)}, u32[]{:S(2)}) collective-permute-start(bf16[512,128]{1,0:T(8,128)(2,1)S(1)} %get-tuple-element.31), channel_id=1, source_target_pairs={{0,4},{1,5},{2,6},{3,7},{4,8},{5,9},{6,10},{7,11},{8,12},{9,13},{1... | collective-permute-start | bytes 393224 | tf_op jit(solution)/shard_map/column_pieces/ppermute | solution.py:342
  21.3 7.0 %collective-permute-start.2 = (bf16[512,128]{1,0:T(8,128)(2,1)S(1)}, bf16[512,128]{1,0:T(8,128)(2,1)S(1)}, u32[]{:S(2)}, u32[]{:S(2)}) collective-permute-start(bf16[512,128]{1,0:T(8,128)(2,1)S(1)} %get-tuple-element.32), channel_id=1, source_target_pairs={{0,6},{1,7},{2,8},{3,9},{4,10},{5,11},{6,12},{7,13},{8,14},{9,15},... | collective-permute-start | bytes 393224 | tf_op jit(solution)/shard_map/column_pieces/ppermute | solution.py:342
  28.4 2.8 %collective-permute-start.3 = (bf16[512,128]{1,0:T(8,128)(2,1)S(1)}, bf16[512,128]{1,0:T(8,128)(2,1)S(1)}, u32[]{:S(2)}, u32[]{:S(2)}) collective-permute-start(bf16[512,128]{1,0:T(8,128)(2,1)S(1)} %get-tuple-element.33), channel_id=1, source_target_pairs={{0,8},{1,9},{2,10},{3,11},{4,12},{5,13},{6,14},{7,15},{8,0},{9,1},... | collective-permute-start | bytes 393224 | tf_op jit(solution)/shard_map/column_pieces/ppermute | solution.py:342
  31.2 6.4 %collective-permute-start.4 = (bf16[512,128]{1,0:T(8,128)(2,1)S(1)}, bf16[512,128]{1,0:T(8,128)(2,1)S(1)}, u32[]{:S(2)}, u32[]{:S(2)}) collective-permute-start(bf16[512,128]{1,0:T(8,128)(2,1)S(1)} %get-tuple-element.34), channel_id=1, source_target_pairs={{0,10},{1,11},{2,12},{3,13},{4,14},{5,15},{6,0},{7,1},{8,2},{9,3},... | collective-permute-start | bytes 393224 | tf_op jit(solution)/shard_map/column_pieces/ppermute | solution.py:342
  40.6 3.4 %collective-permute-start.5 = (bf16[512,128]{1,0:T(8,128)(2,1)S(1)}, bf16[512,128]{1,0:T(8,128)(2,1)S(1)}, u32[]{:S(2)}, u32[]{:S(2)}) collective-permute-start(bf16[512,128]{1,0:T(8,128)(2,1)S(1)} %get-tuple-element.35), channel_id=1, source_target_pairs={{0,12},{1,13},{2,14},{3,15},{4,0},{5,1},{6,2},{7,3},{8,4},{9,5},{1... | collective-permute-start | bytes 393224 | tf_op jit(solution)/shard_map/column_pieces/ppermute | solution.py:342
  44.0 2.2 collective-permute-start.6
  47.0 9.0 %collective-permute-done.5.rest_6_ = bf16[512,128]{1,0:T(8,128)(2,1)S(1)} collective-permute-done((bf16[512,128]{1,0:T(8,128)(2,1)S(1)}, bf16[512,128]{1,0:T(8,128)(2,1)S(1)}, u32[]{:S(2)}, u32[]{:S(2)}) %collective-permute-start.5) | collective-permute-done | bytes 131104 | tf_op jit(solution)/shard_map/column_pieces/ppermute | solution.py:342
  56.2 3.3 %collective-permute-start.7 = (bf16[4096,128]{1,0:T(8,128)(2,1)}, bf16[4096,128]{1,0:T(8,128)(2,1)S(1)}, u32[]{:S(2)}, u32[]{:S(2)}) collective-permute-start(bf16[4096,128]{1,0:T(8,128)(2,1)} %bitcast), channel_id=1, source_target_pairs={{0,1},{1,0},{2,3},{3,2},{4,5},{5,4},{6,7},{7,6},{8,9},{9,8},{10,11... | collective-permute-start | bytes 3145736 | tf_op jit(solution)/shard_map/weight_gather/ppermute | solution.py:319
  64.7 31.2 %all_to_all.30.near_ref = bf16[16,128,256]{2,1,0:T(8,128)(2,1)S(1)} all-to-all(bf16[16,128,256]{2,1,0:T(8,128)(2,1)S(1)} %broadcast_in_dim.29), channel_id=1, replica_groups={{0,2,4,6,8,10,12,14,16,18,20,22,24,26,28,30},{1,3,5,7,9,11,13,15,17,19,..., dimensions={0} | all-to-all | bytes 2097152 | tf_op jit(solution)/shard_map/kv_gather/all_to_all | solution.py:268
  95.9 5.6 %collective-permute-start.8 = (bf16[16,128,256]{2,1,0:T(8,128)(2,1)S(1)}, bf16[16,128,256]{2,1,0:T(8,128)(2,1)S(1)}, u32[]{:S(2)}, u32[]{:S(2)}) collective-permute-start(bf16[16,128,256]{2,1,0:T(8,128)(2,1)S(1)} %all_to_all.30.near_ref), channel_id=1, source_target_pairs={{0,1},{1,0},{2,3},{3,2},{4,5},{5,4},{6,7},{7,6},{8,9},{9,8},{10,11... | collective-permute-start | bytes 3145736 | tf_op jit(solution)/shard_map/kv_gather/ppermute | solution.py:319
  101.5 2.3 collective-permute-done.8.far_ref
  104.8 6.3 %attention_backward.1 = (bf16[128,1024]{1,0:T(8,128)(2,1)}, bf16[16,128,256]{2,1,0:T(8,128)(2,1)}, bf16[16,128,256]{2,1,0:T(8,128)(2,1)}) custom-call(s32[32]{0:T(128)} %select_reduce_fusion.order_ref, s32[1]{0:T(128)} %bitcast.1.place_ref, bf16[16,128,256]{2,1,0:T(8,128)(2,1)} %copy-done.1, bf16[16,128,256]{2,1,0:T(8,128)(2,1)} %copy-done.2, ...), custom_call_target="tpu_custom_call" | custom-call | tf_op jit(solution)/shard_map/attention/attention_backward/pallas_call | solution.py:178
  111.0 5.6 %collective-permute-start.9 = (bf16[16,128,256]{2,1,0:T(8,128)(2,1)}, bf16[16,128,256]{2,1,0:T(8,128)(2,1)S(1)}, u32[]{:S(2)}, u32[]{:S(2)}) collective-permute-start(bf16[16,128,256]{2,1,0:T(8,128)(2,1)} %get-tuple-element.43), channel_id=1, source_target_pairs={{0,1},{1,0},{2,3},{3,2},{4,5},{5,4},{6,7},{7,6},{8,9},{9,8},{10,11... | collective-permute-start | bytes 3145736 | tf_op jit(solution)/shard_map/kv_reduce/ppermute | solution.py:319
  116.6 2.5 %collective-permute-done.9 = bf16[16,128,256]{2,1,0:T(8,128)(2,1)S(1)} collective-permute-done((bf16[16,128,256]{2,1,0:T(8,128)(2,1)}, bf16[16,128,256]{2,1,0:T(8,128)(2,1)S(1)}, u32[]{:S(2)}, u32[]{:S(2)}) %collective-permute-start.9) | collective-permute-done | bytes 1048608 | tf_op jit(solution)/shard_map/kv_reduce/ppermute | solution.py:319
  120.6 39.9 %all_to_all.31 = bf16[16,128,256]{2,1,0:T(8,128)(2,1)S(1)} all-to-all(bf16[16,128,256]{2,1,0:T(8,128)(2,1)S(1)} %add_convert_fusion), channel_id=1, replica_groups={{0,2,4,6,8,10,12,14,16,18,20,22,24,26,28,30},{1,3,5,7,9,11,13,15,17,19,..., dimensions={0} | all-to-all | bytes 2097152 | tf_op jit(solution)/shard_map/kv_reduce/all_to_all | solution.py:272
  161.3 22.2 %all_to_all.32.grads_ref = bf16[8,128,256]{2,1,0:T(8,128)(2,1)S(1)} all-to-all(bf16[8,128,256]{2,1,0:T(8,128)(2,1)S(1)} %broadcast_in_dim.32), channel_id=1, replica_groups={{0,2,4,6,8,10,12,14},{1,3,5,7,9,11,13,15},{16,18,20,22,24,26,28,30},{17..., dimensions={0} | all-to-all | bytes 1048576 | tf_op jit(solution)/shard_map/weight_grad/all_to_all | solution.py:268
  184.2 4.5 %collective-permute-start.10 = (bf16[16,16,256]{2,1,0:T(8,128)(2,1)S(1)}, bf16[16,16,256]{2,1,0:T(8,128)(2,1)S(1)}, u32[]{:S(2)}, u32[]{:S(2)}) collective-permute-start(bf16[16,16,256]{2,1,0:T(8,128)(2,1)S(1)} %get-tuple-element.53), channel_id=1, source_target_pairs={{0,1},{1,0},{2,3},{3,2},{4,5},{5,4},{6,7},{7,6},{8,9},{9,8},{10,11... | collective-permute-start | bytes 393224 | tf_op jit(solution)/shard_map/weight_grad/ppermute | solution.py:319
  190.5 14.0 %all-to-all-start.4 = ((bf16[32,16,256]{2,1,0:T(8,128)(2,1)}), bf16[32,16,256]{2,1,0:T(8,128)(2,1)S(1)}, u32[]{:S(2)}, u32[]{:S(2)}) async-start(bf16[32,16,256]{2,1,0:T(8,128)(2,1)} %bitcast.19), calls=%async_computation.4 | async-start | bytes 524288 | tf_op jit(solution)/shard_map/weight_grad/all_to_all | solution.py:272
  206.8 7.9 %all-to-all-done.4 = bf16[32,16,256]{2,1,0:T(8,128)(2,1)S(1)} async-done(((bf16[32,16,256]{2,1,0:T(8,128)(2,1)}), bf16[32,16,256]{2,1,0:T(8,128)(2,1)S(1)}, u32[]{:S(2)}, u32[]{:S(2)}) %all-to-all-start.4) | async-done | bytes 262176 | tf_op jit(solution)/shard_map/weight_grad/all_to_all | solution.py:272
  215.6 7.1 %all-to-all-start.5 = ((f32[16,16,256]{2,1,0:T(8,128)}), f32[16,16,256]{2,1,0:T(8,128)S(1)}, u32[]{:S(2)}, u32[]{:S(2)}) async-start(f32[16,16,256]{2,1,0:T(8,128)} %broadcast_in_dim.34), calls=%async_computation.5 | async-start | bytes 524288 | tf_op jit(solution)/shard_map/weight_grad/all_to_all | solution.py:268
  223.4 1.8 fusion
  225.2 9.3 %all-to-all-done.5 = f32[16,16,256]{2,1,0:T(8,128)S(1)} async-done(((f32[16,16,256]{2,1,0:T(8,128)}), f32[16,16,256]{2,1,0:T(8,128)S(1)}, u32[]{:S(2)}, u32[]{:S(2)}) %all-to-all-start.5) | async-done | bytes 262176 | tf_op jit(solution)/shard_map/weight_grad/all_to_all | solution.py:268
  (73 shorter events, 19.9 us)
Async XLA Ops:
  2.7 8.2 %copy-start = (bf16[1,128,4096]{2,1,0:T(8,128)(2,1)S(1)}, bf16[1,128,4096]{2,1,0:T(8,128)(2,1)}, u32[]{:S(2)}) copy-start(bf16[1,128,4096]{2,1,0:T(8,128)(2,1)} %param.6) | copy-start | bytes 3145732
  2.7 53.5 %all-to-all-start = ((bf16[16,256,128]{2,1,0:T(8,128)(2,1)}), bf16[16,256,128]{2,1,0:T(8,128)(2,1)}, u32[]{:S(2)}, u32[]{:S(2)}) async-start(bf16[16,256,128]{2,1,0:T(8,128)(2,1)} %broadcast_in_dim.26), calls=%async_computation | async-start | bytes 2097152 | tf_op jit(solution)/shard_map/weight_gather/all_to_all | solution.py:268
  10.9 26.7 %copy-start.7 = (s32[1,32]{1,0:T(1,128)S(1)}, s32[1,32]{1,0:T(1,128)}, u32[]{:S(2)}) copy-start(s32[1,32]{1,0:T(1,128)} %param.10) | copy-start | bytes 388
  10.9 48.7 %copy-start.6 = (s32[1,1,2]{2,1,0:T(1,128)S(1)}, s32[1,1,2]{2,1,0:T(1,128)}, u32[]{:S(2)}) copy-start(s32[1,1,2]{2,1,0:T(1,128)} %param.11) | copy-start | bytes 28
  11.5 29.1 %collective-permute-start = (bf16[512,128]{1,0:T(8,128)(2,1)S(1)}, bf16[512,128]{1,0:T(8,128)(2,1)S(1)}, u32[]{:S(2)}, u32[]{:S(2)}) collective-permute-start(bf16[512,128]{1,0:T(8,128)(2,1)S(1)} %get-tuple-element.30), channel_id=1, source_target_pairs={{0,2},{1,3},{2,4},{3,5},{4,6},{5,7},{6,8},{7,9},{8,10},{9,11},{10,... | collective-permute-start | bytes 393224 | tf_op jit(solution)/shard_map/column_pieces/ppermute | solution.py:342
  15.5 28.5 %collective-permute-start.1 = (bf16[512,128]{1,0:T(8,128)(2,1)S(1)}, bf16[512,128]{1,0:T(8,128)(2,1)S(1)}, u32[]{:S(2)}, u32[]{:S(2)}) collective-permute-start(bf16[512,128]{1,0:T(8,128)(2,1)S(1)} %get-tuple-element.31), channel_id=1, source_target_pairs={{0,4},{1,5},{2,6},{3,7},{4,8},{5,9},{6,10},{7,11},{8,12},{9,13},{1... | collective-permute-start | bytes 393224 | tf_op jit(solution)/shard_map/column_pieces/ppermute | solution.py:342
  21.3 25.6 %collective-permute-start.2 = (bf16[512,128]{1,0:T(8,128)(2,1)S(1)}, bf16[512,128]{1,0:T(8,128)(2,1)S(1)}, u32[]{:S(2)}, u32[]{:S(2)}) collective-permute-start(bf16[512,128]{1,0:T(8,128)(2,1)S(1)} %get-tuple-element.32), channel_id=1, source_target_pairs={{0,6},{1,7},{2,8},{3,9},{4,10},{5,11},{6,12},{7,13},{8,14},{9,15},... | collective-permute-start | bytes 393224 | tf_op jit(solution)/shard_map/column_pieces/ppermute | solution.py:342
  28.4 18.6 %collective-permute-start.3 = (bf16[512,128]{1,0:T(8,128)(2,1)S(1)}, bf16[512,128]{1,0:T(8,128)(2,1)S(1)}, u32[]{:S(2)}, u32[]{:S(2)}) collective-permute-start(bf16[512,128]{1,0:T(8,128)(2,1)S(1)} %get-tuple-element.33), channel_id=1, source_target_pairs={{0,8},{1,9},{2,10},{3,11},{4,12},{5,13},{6,14},{7,15},{8,0},{9,1},... | collective-permute-start | bytes 393224 | tf_op jit(solution)/shard_map/column_pieces/ppermute | solution.py:342
  31.2 15.7 %collective-permute-start.4 = (bf16[512,128]{1,0:T(8,128)(2,1)S(1)}, bf16[512,128]{1,0:T(8,128)(2,1)S(1)}, u32[]{:S(2)}, u32[]{:S(2)}) collective-permute-start(bf16[512,128]{1,0:T(8,128)(2,1)S(1)} %get-tuple-element.34), channel_id=1, source_target_pairs={{0,10},{1,11},{2,12},{3,13},{4,14},{5,15},{6,0},{7,1},{8,2},{9,3},... | collective-permute-start | bytes 393224 | tf_op jit(solution)/shard_map/column_pieces/ppermute | solution.py:342
  40.6 15.3 %collective-permute-start.5 = (bf16[512,128]{1,0:T(8,128)(2,1)S(1)}, bf16[512,128]{1,0:T(8,128)(2,1)S(1)}, u32[]{:S(2)}, u32[]{:S(2)}) collective-permute-start(bf16[512,128]{1,0:T(8,128)(2,1)S(1)} %get-tuple-element.35), channel_id=1, source_target_pairs={{0,12},{1,13},{2,14},{3,15},{4,0},{5,1},{6,2},{7,3},{8,4},{9,5},{1... | collective-permute-start | bytes 393224 | tf_op jit(solution)/shard_map/column_pieces/ppermute | solution.py:342
  44.0 12.2 %collective-permute-start.6 = (bf16[512,128]{1,0:T(8,128)(2,1)S(1)}, bf16[512,128]{1,0:T(8,128)(2,1)S(1)}, u32[]{:S(2)}, u32[]{:S(2)}) collective-permute-start(bf16[512,128]{1,0:T(8,128)(2,1)S(1)} %get-tuple-element.36), channel_id=1, source_target_pairs={{0,14},{1,15},{2,0},{3,1},{4,2},{5,3},{6,4},{7,5},{8,6},{9,7},{10,... | collective-permute-start | bytes 393224 | tf_op jit(solution)/shard_map/column_pieces/ppermute | solution.py:342
  56.2 6.9 %collective-permute-start.7 = (bf16[4096,128]{1,0:T(8,128)(2,1)}, bf16[4096,128]{1,0:T(8,128)(2,1)S(1)}, u32[]{:S(2)}, u32[]{:S(2)}) collective-permute-start(bf16[4096,128]{1,0:T(8,128)(2,1)} %bitcast), channel_id=1, source_target_pairs={{0,1},{1,0},{2,3},{3,2},{4,5},{5,4},{6,7},{7,6},{8,9},{9,8},{10,11... | collective-permute-start | bytes 3145736 | tf_op jit(solution)/shard_map/weight_gather/ppermute | solution.py:319
  95.9 7.9 %copy-start.1 = (bf16[16,128,256]{2,1,0:T(8,128)(2,1)}, bf16[16,128,256]{2,1,0:T(8,128)(2,1)S(1)}, u32[]{:S(2)}) copy-start(bf16[16,128,256]{2,1,0:T(8,128)(2,1)S(1)} %all_to_all.30.near_ref) | copy-start | bytes 3145732
  95.9 7.9 %collective-permute-start.8 = (bf16[16,128,256]{2,1,0:T(8,128)(2,1)S(1)}, bf16[16,128,256]{2,1,0:T(8,128)(2,1)S(1)}, u32[]{:S(2)}, u32[]{:S(2)}) collective-permute-start(bf16[16,128,256]{2,1,0:T(8,128)(2,1)S(1)} %all_to_all.30.near_ref), channel_id=1, source_target_pairs={{0,1},{1,0},{2,3},{3,2},{4,5},{5,4},{6,7},{7,6},{8,9},{9,8},{10,11... | collective-permute-start | bytes 3145736 | tf_op jit(solution)/shard_map/kv_gather/ppermute | solution.py:319
  103.8 1.0 copy-start.2
  111.0 8.1 %collective-permute-start.9 = (bf16[16,128,256]{2,1,0:T(8,128)(2,1)}, bf16[16,128,256]{2,1,0:T(8,128)(2,1)S(1)}, u32[]{:S(2)}, u32[]{:S(2)}) collective-permute-start(bf16[16,128,256]{2,1,0:T(8,128)(2,1)} %get-tuple-element.43), channel_id=1, source_target_pairs={{0,1},{1,0},{2,3},{3,2},{4,5},{5,4},{6,7},{7,6},{8,9},{9,8},{10,11... | collective-permute-start | bytes 3145736 | tf_op jit(solution)/shard_map/kv_reduce/ppermute | solution.py:319
  160.9 29.6 %copy-start.5 = (bf16[128,64]{0,1:T(8,128)(2,1)}, bf16[128,64]{0,1:T(8,128)(2,1)S(1)}, u32[]{:S(2)}) copy-start(bf16[128,64]{0,1:T(8,128)(2,1)S(1)} %get-tuple-element.71) | copy-start | bytes 49156
  161.2 23.0 %copy-start.3 = (bf16[128,256]{1,0:T(8,128)(2,1)}, bf16[128,256]{1,0:T(8,128)(2,1)S(1)}, u32[]{:S(2)}) copy-start(bf16[128,256]{1,0:T(8,128)(2,1)S(1)} %pad_maximum_fusion.2) | copy-start | bytes 196612
  184.2 5.5 %collective-permute-start.10 = (bf16[16,16,256]{2,1,0:T(8,128)(2,1)S(1)}, bf16[16,16,256]{2,1,0:T(8,128)(2,1)S(1)}, u32[]{:S(2)}, u32[]{:S(2)}) collective-permute-start(bf16[16,16,256]{2,1,0:T(8,128)(2,1)S(1)} %get-tuple-element.53), channel_id=1, source_target_pairs={{0,1},{1,0},{2,3},{3,2},{4,5},{5,4},{6,7},{7,6},{8,9},{9,8},{10,11... | collective-permute-start | bytes 393224 | tf_op jit(solution)/shard_map/weight_grad/ppermute | solution.py:319
  190.5 24.3 %all-to-all-start.4 = ((bf16[32,16,256]{2,1,0:T(8,128)(2,1)}), bf16[32,16,256]{2,1,0:T(8,128)(2,1)S(1)}, u32[]{:S(2)}, u32[]{:S(2)}) async-start(bf16[32,16,256]{2,1,0:T(8,128)(2,1)} %bitcast.19), calls=%async_computation.4 | async-start | bytes 524288 | tf_op jit(solution)/shard_map/weight_grad/all_to_all | solution.py:272
  205.8 17.6 %copy-start.4 = (bf16[128,256]{1,0:T(8,128)(2,1)S(1)}, bf16[128,256]{1,0:T(8,128)(2,1)}, u32[]{:S(2)}) copy-start(bf16[128,256]{1,0:T(8,128)(2,1)} %copy-done.3) | copy-start | bytes 196612
  215.6 19.0 %all-to-all-start.5 = ((f32[16,16,256]{2,1,0:T(8,128)}), f32[16,16,256]{2,1,0:T(8,128)S(1)}, u32[]{:S(2)}, u32[]{:S(2)}) async-start(f32[16,16,256]{2,1,0:T(8,128)} %broadcast_in_dim.34), calls=%async_computation.5 | async-start | bytes 524288 | tf_op jit(solution)/shard_map/weight_grad/all_to_all | solution.py:268

commit v4 on v1

v4 whole, which is shorter than its diff:
```python
import functools
import math

import jax
import jax.numpy as jnp
from jax import lax
from jax.experimental import pallas as pl
from jax.experimental.pallas import tpu as pltpu
from jax.sharding import PartitionSpec as P

QH = 8
HD = 128
BLOCK = 128
TILE_BLOCKS = 4

EPSILON = 1e-06
LOG2E = math.log2(math.e)


def frequencies(size):
    expo = jnp.arange(0, size, 2).astype(jnp.float32) / size
    base = 1.0 / jnp.power(jnp.float32(500000.0), expo)
    wavelen = 2.0 * math.pi / base
    mixing = (8192.0 / wavelen - 1.0) / 3.0
    blended = (1.0 - mixing) * base / 8.0 + mixing * base
    return jnp.where(wavelen < 2048.0, base, jnp.where(wavelen > 8192.0, base / 8.0, blended))


def softstep(scaled):
    return scaled - jnp.sin(2.0 * math.pi * (scaled - jnp.round(scaled))) / (2.0 * math.pi)


def dot_cols(left, right):
    return lax.dot_general(
        left, right, (((1,), (1,)), ((), ())), preferred_element_type=jnp.float32
    )


def dot(left, right):
    return jnp.dot(left, right, preferred_element_type=jnp.float32)


def attention_kernel(
    order_ref, place_ref, core_ref, near_ref, far_ref, q_ref, g_ref,
    dq_ref, near_grad_ref, far_grad_ref,
    exp_store, prob_store, top_store, q_cols, g_cols, q_rows, g_rows, dq_cols,
):
    blocks = near_ref.shape[0]
    rows = QH * BLOCK
    span = TILE_BLOCKS * BLOCK
    score_scale = LOG2E / math.sqrt(HD)
    place = place_ref[0]
    is_first = core_ref[0] == 0
    tiles = lax.div(place + TILE_BLOCKS, TILE_BLOCKS)

    for head in range(QH):
        part = pl.ds(head * HD, HD)
        q_cols[:, part] = q_ref[:, part].T
        g_cols[:, part] = g_ref[:, part].T
        q_rows[part, :] = q_ref[:, part]
        g_rows[part, :] = g_ref[:, part]
    dq_cols[...] = jnp.zeros_like(dq_cols)

    def gathered(tile):
        slots = [order_ref[tile * TILE_BLOCKS + step] for step in range(TILE_BLOCKS)]
        near = jnp.concatenate([near_ref[slot] for slot in slots], axis=0)
        far = jnp.concatenate([far_ref[slot] for slot in slots], axis=0)
        return jnp.where(is_first, near, far), jnp.where(is_first, far, near)

    def folded(values):
        return jnp.sum(values.reshape(span // 8, 8, rows), axis=0)

    def forward(tile, sums, masked):
        total, weighted, top = sums
        keys, values = gathered(tile)
        scores = dot(keys, q_cols[...]) * score_scale
        if masked:
            key_at = tile * span + lax.broadcasted_iota(jnp.int32, (span, rows), 0)
            row_at = place * BLOCK + lax.rem(
                lax.broadcasted_iota(jnp.int32, (span, rows), 1), BLOCK
            )
            visible = key_at <= row_at
            scores = jnp.where(visible, scores, -jnp.inf)
        highest = jnp.maximum(top, jnp.max(scores, axis=0, keepdims=True))
        shrink = jnp.exp2(top - highest)
        exponent = jnp.exp2(scores - highest)
        prob_grad = dot(values, g_cols[...])
        exp_store[tile] = exponent
        prob_store[tile] = prob_grad
        top_store[tile] = highest
        total = total * shrink + folded(exponent)
        weighted = weighted * shrink + folded(exponent * prob_grad)
        return (total, weighted, highest)

    empty = jnp.zeros((8, rows), jnp.float32)
    start = forward(tiles - 1, (empty, empty, jnp.full((1, rows), -1e30, jnp.float32)), True)
    total, weighted, top = lax.fori_loop(
        0, tiles - 1, lambda tile, sums: forward(tile, sums, False), start
    )
    inverse = 1.0 / jnp.sum(total, axis=0, keepdims=True)
    row_delta = jnp.sum(weighted, axis=0, keepdims=True) * inverse

    @pl.loop(0, tiles)
    def _(tile):
        keys, _ = gathered(tile)
        factor = jnp.exp2(top_store[tile] - top) * inverse
        probs = exp_store[tile] * factor
        score_grad = (probs * (prob_store[tile] - row_delta)).astype(jnp.bfloat16)
        value_grad = dot(probs.astype(jnp.bfloat16), g_rows[...]).astype(jnp.bfloat16)
        key_grad = dot(score_grad, q_rows[...]).astype(jnp.bfloat16)
        dq_cols[...] += dot(keys.T, score_grad)
        near_grad = jnp.where(is_first, key_grad, value_grad)
        far_grad = jnp.where(is_first, value_grad, key_grad)
        for step in range(TILE_BLOCKS):
            slot = order_ref[tile * TILE_BLOCKS + step]
            near_grad_ref[slot] = near_grad[step * BLOCK : (step + 1) * BLOCK]
            far_grad_ref[slot] = far_grad[step * BLOCK : (step + 1) * BLOCK]

    @pl.loop(tiles * TILE_BLOCKS, blocks)
    def _(place_at):
        slot = order_ref[place_at]
        near_grad_ref[slot] = jnp.zeros((BLOCK, HD), jnp.bfloat16)
        far_grad_ref[slot] = jnp.zeros((BLOCK, HD), jnp.bfloat16)

    for head in range(QH):
        part = pl.ds(head * HD, HD)
        dq_ref[:, part] = (dq_cols[:, part].T * (1.0 / math.sqrt(HD))).astype(jnp.bfloat16)


def attention_backward(order, place, core, near, far, queries, out_grad):
    tokens = queries.shape[0]
    rows = QH * tokens
    tiles = near.shape[0] // TILE_BLOCKS
    span = TILE_BLOCKS * BLOCK
    smem = pl.BlockSpec(memory_space=pltpu.SMEM)
    vmem = pl.BlockSpec(memory_space=pltpu.VMEM)
    return pl.pallas_call(
        attention_kernel,
        out_shape=(
            jax.ShapeDtypeStruct(queries.shape, jnp.bfloat16),
            jax.ShapeDtypeStruct(near.shape, jnp.bfloat16),
            jax.ShapeDtypeStruct(far.shape, jnp.bfloat16),
        ),
        in_specs=[smem, smem, smem, vmem, vmem, vmem, vmem],
        out_specs=(vmem, vmem, vmem),
        scratch_shapes=[
            pltpu.VMEM((tiles, span, rows), jnp.float32),
            pltpu.VMEM((tiles, span, rows), jnp.float32),
            pltpu.VMEM((tiles, 1, rows), jnp.float32),
            pltpu.VMEM((HD, rows), jnp.bfloat16),
            pltpu.VMEM((HD, rows), jnp.bfloat16),
            pltpu.VMEM((rows, HD), jnp.bfloat16),
            pltpu.VMEM((rows, HD), jnp.bfloat16),
            pltpu.VMEM((HD, rows), jnp.float32),
        ],
        compiler_params=pltpu.CompilerParams(vmem_limit_bytes=56 * 1024 * 1024),
        name="attention_backward",
    )(order, place, core, near, far, queries, out_grad)


def local_call(kernel, shapes, scalars, arrays, name, scratch=()):
    smem = pl.BlockSpec(memory_space=pltpu.SMEM)
    vmem = pl.BlockSpec(memory_space=pltpu.VMEM)
    return pl.pallas_call(
        kernel,
        out_shape=shapes,
        in_specs=[smem] * len(scalars) + [vmem] * len(arrays),
        out_specs=jax.tree.map(lambda _: vmem, shapes),
        scratch_shapes=scratch,
        compiler_params=pltpu.CompilerParams(vmem_limit_bytes=32 * 1024 * 1024),
        name=name,
    )(*scalars, *arrays)


def project_kernel(core_ref, levels_ref, own_ref, far_ref, weight_ref, cos_ref, sin_ref, out_ref):
    core = core_ref[0]
    weight = weight_ref[...]
    for distance, x_ref in enumerate((own_ref, far_ref)):
        at = core if distance == 0 else 1 - core
        raw = dot(x_ref[...], weight)
        turned = raw * cos_ref[at] + pltpu.roll(raw, HD // 2, 1) * sin_ref[at]
        largest = jnp.max(jnp.abs(turned), axis=0, keepdims=True)
        level_step = (largest + EPSILON) / levels_ref[distance]
        quantized = (level_step * softstep(turned / level_step)).astype(jnp.bfloat16)
        for copy in range(out_ref.shape[0]):
            out_ref[copy, at] = quantized


def settle_kernel(arrived_ref, cos_ref, sin_ref, out_ref):
    for at in range(2):
        grads = arrived_ref[0, at].astype(jnp.float32)
        for source in range(1, arrived_ref.shape[0]):
            grads += arrived_ref[source, at].astype(jnp.float32)
        turned = grads * cos_ref[at] - pltpu.roll(grads, HD // 2, 1) * sin_ref[at]
        turned = turned.astype(jnp.bfloat16)
        for copy in range(out_ref.shape[0]):
            out_ref[copy, at] = turned


def turn_kernel(x_ref, out_ref, flipped):
    columns, extent, _ = out_ref.shape
    piece = BLOCK // columns
    for block in range(extent // piece):
        part = pl.ds(block * BLOCK, BLOCK)
        flipped[...] = x_ref[:, part].T
        for column in range(columns):
            out_ref[column, block * piece : (block + 1) * piece, :] = flipped[
                column * piece : (column + 1) * piece, :
            ]


def share_kernel(core_ref, near_ref, far_ref, grads_ref, out_ref):
    core = core_ref[0]
    share = jnp.zeros(near_ref.shape[1:], jnp.float32)
    for column in range(near_ref.shape[0]):
        share += dot(near_ref[column], grads_ref[column, core])
        share += dot(far_ref[column], grads_ref[column, 1 - core])
    out_ref[...] = share.astype(out_ref.dtype).reshape(out_ref.shape)


def total_kernel(parts_ref, out_ref):
    total = parts_ref[0].astype(jnp.float32)
    for source in range(1, parts_ref.shape[0]):
        total += parts_ref[source].astype(jnp.float32)
    total = total.astype(out_ref.dtype)
    for copy in range(out_ref.shape[0]):
        out_ref[copy] = total


def assemble_kernel(grad_scale, parts_ref, out_ref):
    columns = parts_ref.shape[1]
    piece = parts_ref.shape[3] // 2
    for column in range(columns):
        for core in range(2):
            low = parts_ref[0, column, core].astype(jnp.float32)
            high = parts_ref[1, column, core].astype(jnp.float32)
            total = (low + high) * grad_scale
            for half in range(2):
                row = half * columns * piece + column * piece
                out_ref[row : row + piece, core * HD : (core + 1) * HD] = total[
                    half * piece : (half + 1) * piece
                ]


def body(hidden_in, queries, out_grad, kv_weight, block_pos, precision):
    score_scale = 1.0 / math.sqrt(HD)
    tokens = hidden_in.shape[1]
    width = hidden_in.shape[2]
    seq_count = lax.axis_size("seq")
    dp_count = lax.axis_size("dp")
    half_count = seq_count // 2
    columns = half_count // 2
    grad_scale = 1.0 / math.sqrt(dp_count * seq_count * tokens)
    self_index = lax.axis_index("seq")
    core_index = lax.rem(self_index, 2)
    core = core_index.reshape(1).astype(jnp.int32)
    is_first = core_index == 0
    column_groups = [
        [start * half_count + 2 * column + side for column in range(columns)]
        for start in range(2)
        for side in range(2)
    ]
    same_core = [[2 * chip + side for chip in range(half_count)] for side in range(2)]
    swap = [(source, source ^ 1) for source in range(seq_count)]

    def swapped(value):
        return lax.ppermute(value, "seq", swap)

    def exchanged(value, axis, groups=None):
        return lax.all_to_all(value, axis, 0, 0, axis_index_groups=groups)

    x_rows = hidden_in[0]
    places = block_pos[0]
    place = lax.dynamic_slice_in_dim(places, self_index, 1)
    slots = jnp.arange(seq_count, dtype=jnp.int32)
    order = jnp.sum(
        jnp.where(places[None, :] == slots[:, None], slots[None, :], 0), axis=1
    ).astype(jnp.int32)

    with jax.named_scope("rotation"):
        pair_places = lax.dynamic_slice_in_dim(places, self_index - core_index, 2)
        pair_pos = pair_places[:, None] * BLOCK + jnp.arange(tokens, dtype=jnp.int32)[None, :]
        freq = frequencies(HD)
        angles = pair_pos.astype(jnp.float32)[:, :, None] * jnp.concatenate([freq, freq])
        lane = jnp.arange(HD, dtype=jnp.int32)
        cosine = jnp.where(is_first, jnp.cos(angles), 1.0)
        sine_part = jnp.where(
            is_first, jnp.sin(angles) * jnp.where(lane < HD // 2, -1.0, 1.0), 0.0
        )
        back_scale = jnp.where(is_first, score_scale, 1.0)
        back_cosine = cosine * back_scale
        back_sine = sine_part * back_scale
        pair_bits = jnp.concatenate([precision[0], swapped(precision[0])])
        bits_here = jnp.where(is_first, pair_bits[:, 0], pair_bits[:, 1])
        levels = (lax.shift_left(jnp.ones_like(bits_here), bits_here - 1) - 1).astype(jnp.float32)
        x_far = swapped(x_rows)
        x_columns = local_call(
            turn_kernel,
            jax.ShapeDtypeStruct((columns, width // columns, tokens), x_rows.dtype),
            (),
            (x_rows,),
            "x_columns",
            (pltpu.VMEM((BLOCK, tokens), x_rows.dtype),),
        )
    with jax.named_scope("weight_gather"):
        half = jnp.where(is_first, kv_weight[:, :HD], kv_weight[:, HD:])
        copies = jnp.broadcast_to(half[None], (dp_count, *half.shape))
        near_weight = exchanged(lax.optimization_barrier(copies), "dp").reshape(width, HD)
        (
            near_weight, order, cosine, sine_part, back_cosine, back_sine, levels, x_far, x_columns
        ) = lax.optimization_barrier(
            (
                near_weight, order, cosine, sine_part, back_cosine, back_sine, levels, x_far,
                x_columns,
            )
        )
    with jax.named_scope("projection"):
        stacked = local_call(
            project_kernel,
            jax.ShapeDtypeStruct((half_count, 2, tokens, HD), jnp.bfloat16),
            (core, levels),
            (x_rows, x_far, near_weight, cosine, sine_part),
            "projection",
        )
    with jax.named_scope("kv_gather"):
        near = exchanged(stacked, "seq", same_core).reshape(seq_count, tokens, HD)
        near, x_columns = lax.optimization_barrier((near, x_columns))
        near_columns = exchanged(x_columns, "seq", column_groups)
        far = swapped(near)
    with jax.named_scope("attention"):
        query_grad, near_grad, far_grad = attention_backward(
            order, place, core, near, far, queries[0], out_grad[0]
        )
    with jax.named_scope("kv_reduce"):
        pair = near_grad.astype(jnp.float32) + swapped(far_grad).astype(jnp.float32)
        pair = pair.astype(jnp.bfloat16).reshape(half_count, 2, tokens, HD)
        pair, near_columns, near_weight = lax.optimization_barrier(
            (pair, near_columns, near_weight)
        )
        arrived = exchanged(pair, "seq", same_core)
        far_columns = swapped(near_columns)
        far_weight = swapped(near_weight)
    with jax.named_scope("projection_grad"):
        settled = local_call(
            settle_kernel,
            jax.ShapeDtypeStruct((columns, 2, tokens, HD), jnp.bfloat16),
            (),
            (arrived, back_cosine, back_sine),
            "projection_grad",
        )
    with jax.named_scope("weight_grad"):
        column_grads = exchanged(settled, "seq", column_groups)
        share = local_call(
            share_kernel,
            jax.ShapeDtypeStruct((dp_count, width // columns // dp_count, HD), jnp.bfloat16),
            (core,),
            (near_columns, far_columns, column_grads),
            "weight_share",
        )
        share_parts = exchanged(share, "dp")
        group_share = local_call(
            total_kernel,
            jax.ShapeDtypeStruct((seq_count, *share.shape[1:]), jnp.bfloat16),
            (),
            (share_parts,),
            "group_share",
        )
        gathered = exchanged(group_share, "seq")
        weight_grad = local_call(
            functools.partial(assemble_kernel, grad_scale),
            jax.ShapeDtypeStruct((width // dp_count, 2 * HD), jnp.float32),
            (),
            (gathered.reshape(2, columns, 2, *share.shape[1:]),),
            "weight_grad",
        )
    with jax.named_scope("input_grad"):
        both = settled[0]
        own = jnp.where(is_first, both[0], both[1])
        other = swapped(jnp.where(is_first, both[1], both[0]))
        proj_grad = jnp.concatenate(
            [jnp.where(is_first, own, other), jnp.where(is_first, other, own)], axis=1
        )
        input_grad = (dot_cols(own, near_weight) + dot_cols(other, far_weight)).astype(
            jnp.bfloat16
        )
    return (query_grad[None], proj_grad[None], input_grad[None], weight_grad)


def solution(mesh):
    in_specs = (
        P("dp", "seq", None),
        P("dp", "seq", None),
        P("dp", "seq", None),
        P("dp", None),
        P("dp", None),
        P("dp", "seq", None),
    )
    out_specs = (P("dp", "seq", None), P("dp", "seq", None), P("dp", "seq", None), P("dp", None))
    return jax.shard_map(body, mesh=mesh, in_specs=in_specs, out_specs=out_specs, check_vma=False)
```

time: 264 us -> 219 us (0.83)
  blocking collectives: 168 us -> 40.1 us
  waiting for transfers between devices: 11.6 us -> 72.2 us
  starting transfers between devices: 21.6 us -> 63 us
  local copies, waits for them, and re-layouts: 33 us -> 3.47 us
  Pallas kernels: 9.53 us -> 25 us
  matrix products: 7.1 us -> 3.84 us
    all_to_all x5 -> x1, blocking collectives: 168 us -> 40.1 us  [exchanged(): return lax.all_to_all(value, axis, 0, 0, axis_index_groups=groups)]
    all_to_all x1 -> x6, waiting for transfers between devices: 6.81 us -> 69.4 us  [exchanged(): return lax.all_to_all(value, axis, 0, 0, axis_index_groups=groups)]
    all_to_all x1 -> x6, starting transfers between devices: 6.63 us -> 40.6 us  [exchanged(): return lax.all_to_all(value, axis, 0, 0, axis_index_groups=groups)]
    unnamed x32 -> x12, local copies, waits for them, and re-layouts: 12.2 us -> 1.71 us
    slice x5 -> x0, local copies, waits for them, and re-layouts: 10.5 us -> none  [the longest x1 9.74 us: body(): kept = jnp.where(is_first, share[:, 0], share[:, 1])]
    pallas_call x1, Pallas kernels: 9.53 us -> 17.3 us  [attention_backward(): pl.pallas_call(attention_kernel, out_shape=(jax.ShapeDtypeStruct(queries....]
    pallas_call x0 -> x6, Pallas kernels: none -> 7.67 us  [local_call(): pl.pallas_call(kernel, out_shape=shapes, in_specs=[smem] * len(scalars) +...]
    ppermute x4 -> x7, starting transfers between devices: 15 us -> 22.4 us  [swapped(): return lax.ppermute(value, 'seq', swap)]
  transfers between devices with their start and end apart: 5 -> 13, of which waited for: 4 -> 7; matrix products, arithmetic and copies ran while one was open for 4% -> 5% of each run, Pallas kernels for 0% -> 10%
where the time goes in v4:
time: 219 us; the launch traced here: 216 us
  waiting for transfers between devices  72.2 us (33%)
  starting transfers between devices  63 us (29%)
  blocking collectives  40.1 us (18%)
  Pallas kernels  25 us (11%)
  other arithmetic  8.02 us (4%)
  matrix products  3.84 us (2%)
  local copies, waits for them, and re-layouts  3.47 us (2%)
    all_to_all x6, waiting for transfers between devices, exchanged(): return lax.all_to_all(value, axis, 0, 0, axis_index_groups=groups)  69.4 us
    all_to_all x6, starting transfers between devices, exchanged(): return lax.all_to_all(value, axis, 0, 0, axis_index_groups=groups)  40.6 us
    all_to_all x1, blocking collectives, exchanged(): return lax.all_to_all(value, axis, 0, 0, axis_index_groups=groups)  40.1 us
    ppermute x7, starting transfers between devices, swapped(): return lax.ppermute(value, 'seq', swap)  22.4 us
    pallas_call x1, Pallas kernels, attention_backward(): pl.pallas_call(attention_kernel, out_shape=(jax.ShapeDtypeStruct(queries....  17.3 us
    pallas_call x6, Pallas kernels, local_call(): pl.pallas_call(kernel, out_shape=shapes, in_specs=[smem] * len(scalars) +...  7.67 us
  transfers between devices with their start and end apart: 13, of which 7 were waited for; matrix products, arithmetic and copies ran while one was open for 5% of the time, Pallas kernels for 10%

profile of v4, /device:TPU:1, one launch (start us, length us, event | category | flops | bytes accessed | tf_op | source)
XLA Modules:
  0.0 216.4 jit_solution(865986735472202748)
XLA Ops:
  2.8 8.1 %all-to-all-start = ((bf16[16,256,128]{2,1,0:T(8,128)(2,1)}), bf16[16,256,128]{2,1,0:T(8,128)(2,1)S(1)}, u32[]{:S(2)}, u32[]{:S(2)}) async-start(bf16[16,256,128]{2,1,0:T(8,128)(2,1)} %broadcast_in_dim.49), calls=%async_computation | async-start | bytes 2097152 | tf_op jit(solution)/shard_map/weight_gather/all_to_all | solution.py:270
  10.9 4.5 %collective-permute-start = (s32[1,2]{1,0:T(1,128)S(1)}, s32[1,2]{1,0:T(1,128)S(1)}, u32[]{:S(2)}, u32[]{:S(2)}) collective-permute-start(s32[1,2]{1,0:T(1,128)S(1)} %bitcast.40), channel_id=1, source_target_pairs={{0,1},{1,0},{2,3},{3,2},{4,5},{5,4},{6,7},{7,6},{8,9},{9,8},{10,11... | collective-permute-start | bytes 32 | tf_op jit(solution)/shard_map/rotation/ppermute | solution.py:267
  15.4 1.9 collective-permute-start.1
  21.2 16.7 %all-to-all-done = bf16[16,256,128]{2,1,0:T(8,128)(2,1)S(1)} async-done(((bf16[16,256,128]{2,1,0:T(8,128)(2,1)}), bf16[16,256,128]{2,1,0:T(8,128)(2,1)S(1)}, u32[]{:S(2)}, u32[]{:S(2)}) %all-to-all-start) | async-done | bytes 1048608 | tf_op jit(solution)/shard_map/weight_gather/all_to_all | solution.py:270
  40.7 40.1 %all_to_all.35 = bf16[16,2,128,128]{3,2,1,0:T(8,128)(2,1)S(1)} all-to-all(bf16[16,2,128,128]{3,2,1,0:T(8,128)(2,1)S(1)} %projection.1), channel_id=1, replica_groups={{0,2,4,6,8,10,12,14,16,18,20,22,24,26,28,30},{1,3,5,7,9,11,13,15,17,19,..., dimensions={0} | all-to-all | bytes 2097152 | tf_op jit(solution)/shard_map/kv_gather/all_to_all | solution.py:270
  80.8 4.9 %collective-permute-start.2 = (bf16[32,128,128]{2,1,0:T(8,128)(2,1)S(1)}, bf16[32,128,128]{2,1,0:T(8,128)(2,1)}, u32[]{:S(2)}, u32[]{:S(2)}) collective-permute-start(bf16[32,128,128]{2,1,0:T(8,128)(2,1)S(1)} %bitcast.36), channel_id=1, source_target_pairs={{0,1},{1,0},{2,3},{3,2},{4,5},{5,4},{6,7},{7,6},{8,9},{9,8},{10,11... | collective-permute-start | bytes 3145736 | tf_op jit(solution)/shard_map/kv_gather/ppermute | solution.py:267
  85.7 3.6 %all-to-all-start.2 = ((bf16[8,512,128]{2,1,0:T(8,128)(2,1)}), bf16[8,512,128]{2,1,0:T(8,128)(2,1)S(1)}, u32[]{:S(2)}, u32[]{:S(2)}) async-start(bf16[8,512,128]{2,1,0:T(8,128)(2,1)} %x_columns.1), calls=%async_computation.2 | async-start | bytes 2097152 | tf_op jit(solution)/shard_map/kv_gather/all_to_all | solution.py:270
  89.9 17.3 %attention_backward.1 = (bf16[128,1024]{1,0:T(8,128)(2,1)}, bf16[32,128,128]{2,1,0:T(8,128)(2,1)}, bf16[32,128,128]{2,1,0:T(8,128)(2,1)}) custom-call(s32[32]{0:T(128)} %select_reduce_fusion.order_ref, s32[1]{0:T(128)} %bitcast.5.place_ref, s32[1]{0:T(128)} %bitcast.6.core_ref, bf16[32,128,128]{2,1,0:T(8,128)(2,1)} %bitcast.37, ...), custom_call_target="tpu_custom_call" | custom-call | tf_op jit(solution)/shard_map/attention/attention_backward/pallas_call | solution.py:137
  107.2 1.9 collective-permute-start.3
  109.1 2.8 %collective-permute-done.3 = bf16[32,128,128]{2,1,0:T(8,128)(2,1)S(1)} collective-permute-done((bf16[32,128,128]{2,1,0:T(8,128)(2,1)}, bf16[32,128,128]{2,1,0:T(8,128)(2,1)S(1)}, u32[]{:S(2)}, u32[]{:S(2)}) %collective-permute-start.3) | collective-permute-done | bytes 1048608 | tf_op jit(solution)/shard_map/kv_reduce/ppermute | solution.py:267
  112.0 2.6 %add_convert_fusion = bf16[32,128,128]{2,1,0:T(8,128)(2,1)} fusion(bf16[32,128,128]{2,1,0:T(8,128)(2,1)S(1)} %collective-permute-done.3, bf16[32,128,128]{2,1,0:T(8,128)(2,1)} %get-tuple-element.30), kind=kLoop, calls=%fused_computation.3 | loop fusion | flops 2097152 | bytes 3145728 | tf_op jit(solution)/shard_map/kv_reduce/convert_element_type | solution.py:336
  114.5 4.0 %all-to-all-done.2.near_ref = bf16[8,512,128]{2,1,0:T(8,128)(2,1)S(1)} async-done(((bf16[8,512,128]{2,1,0:T(8,128)(2,1)}), bf16[8,512,128]{2,1,0:T(8,128)(2,1)S(1)}, u32[]{:S(2)}, u32[]{:S(2)}) %all-to-all-start.2) | async-done | bytes 1048608 | tf_op jit(solution)/shard_map/kv_gather/all_to_all | solution.py:270
  118.5 4.7 %all-to-all-start.3 = ((bf16[16,2,128,128]{3,2,1,0:T(8,128)(2,1)}), bf16[16,2,128,128]{3,2,1,0:T(8,128)(2,1)S(1)}, u32[]{:S(2)}, u32[]{:S(2)}) async-start(bf16[16,2,128,128]{3,2,1,0:T(8,128)(2,1)} %bitcast.35), calls=%async_computation.3 | async-start | bytes 2097152 | tf_op jit(solution)/shard_map/kv_reduce/all_to_all | solution.py:270
  123.2 2.6 %collective-permute-start.6 = (bf16[8,512,128]{2,1,0:T(8,128)(2,1)S(1)}, bf16[8,512,128]{2,1,0:T(8,128)(2,1)}, u32[]{:S(2)}, u32[]{:S(2)}) collective-permute-start(bf16[8,512,128]{2,1,0:T(8,128)(2,1)S(1)} %all-to-all-done.2.near_ref), channel_id=1, source_target_pairs={{0,1},{1,0},{2,3},{3,2},{4,5},{5,4},{6,7},{7,6},{8,9},{9,8},{10,11... | collective-permute-start | bytes 3145736 | tf_op jit(solution)/shard_map/kv_reduce/ppermute | solution.py:267
  125.9 25.8 %all-to-all-done.3.arrived_ref = bf16[16,2,128,128]{3,2,1,0:T(8,128)(2,1)S(1)} async-done(((bf16[16,2,128,128]{3,2,1,0:T(8,128)(2,1)}), bf16[16,2,128,128]{3,2,1,0:T(8,128)(2,1)S(1)}, u32[]{:S(2)}, u32[]{:S(2)}) %all-to-all-start.3) | async-done | bytes 1048608 | tf_op jit(solution)/shard_map/kv_reduce/all_to_all | solution.py:270
  152.7 3.5 %all-to-all-start.4 = ((bf16[8,2,128,128]{3,2,1,0:T(8,128)(2,1)}), bf16[8,2,128,128]{3,2,1,0:T(8,128)(2,1)S(1)}, u32[]{:S(2)}, u32[]{:S(2)}) async-start(bf16[8,2,128,128]{3,2,1,0:T(8,128)(2,1)} %copy-done.1), calls=%async_computation.4 | async-start | bytes 1048576 | tf_op jit(solution)/shard_map/weight_grad/all_to_all | solution.py:270
  156.2 4.6 %collective-permute-start.5 = (bf16[4096,128]{1,0:T(8,128)(2,1)S(1)}, bf16[4096,128]{1,0:T(8,128)(2,1)}, u32[]{:S(2)}, u32[]{:S(2)}) collective-permute-start(bf16[4096,128]{1,0:T(8,128)(2,1)S(1)} %bitcast.29), channel_id=1, source_target_pairs={{0,1},{1,0},{2,3},{3,2},{4,5},{5,4},{6,7},{7,6},{8,9},{9,8},{10,11... | collective-permute-start | bytes 3145736 | tf_op jit(solution)/shard_map/kv_reduce/ppermute | solution.py:267
  163.5 7.4 %all-to-all-done.4.grads_ref = bf16[8,2,128,128]{3,2,1,0:T(8,128)(2,1)S(1)} async-done(((bf16[8,2,128,128]{3,2,1,0:T(8,128)(2,1)}), bf16[8,2,128,128]{3,2,1,0:T(8,128)(2,1)S(1)}, u32[]{:S(2)}, u32[]{:S(2)}) %all-to-all-start.4) | async-done | bytes 524320 | tf_op jit(solution)/shard_map/weight_grad/all_to_all | solution.py:270
  170.9 2.6 %weight_share.1 = bf16[16,32,128]{2,1,0:T(8,128)(2,1)} custom-call(s32[1]{0:T(128)} %bitcast.6.core_ref, bf16[8,512,128]{2,1,0:T(8,128)(2,1)S(1)} %all-to-all-done.2.near_ref, bf16[8,512,128]{2,1,0:T(8,128)(2,1)} %collective-permute-done.6.far_ref, bf16[8,2,128,128]{3,2,1,0:T(8,128)(2,1)S(1)} %all-to-all-done.4.grads_ref), custom_call_target="tpu_custom_call" | custom-call | tf_op jit(solution)/shard_map/weight_grad/weight_share/pallas_call | solution.py:164
  173.4 15.3 %all-to-all-start.5 = ((bf16[16,32,128]{2,1,0:T(8,128)(2,1)}), bf16[16,32,128]{2,1,0:T(8,128)(2,1)S(1)}, u32[]{:S(2)}, u32[]{:S(2)}) async-start(bf16[16,32,128]{2,1,0:T(8,128)(2,1)} %weight_share.1), calls=%async_computation.5 | async-start | bytes 262144 | tf_op jit(solution)/shard_map/weight_grad/all_to_all | solution.py:270
  189.9 6.1 %all-to-all-done.5.parts_ref = bf16[16,32,128]{2,1,0:T(8,128)(2,1)S(1)} async-done(((bf16[16,32,128]{2,1,0:T(8,128)(2,1)}), bf16[16,32,128]{2,1,0:T(8,128)(2,1)S(1)}, u32[]{:S(2)}, u32[]{:S(2)}) %all-to-all-start.5) | async-done | bytes 131104 | tf_op jit(solution)/shard_map/weight_grad/all_to_all | solution.py:270
  196.8 5.4 %all-to-all-start.6 = ((bf16[32,32,128]{2,1,0:T(8,128)(2,1)}), bf16[32,32,128]{2,1,0:T(8,128)(2,1)S(1)}, u32[]{:S(2)}, u32[]{:S(2)}) async-start(bf16[32,32,128]{2,1,0:T(8,128)(2,1)} %group_share.1), calls=%async_computation.6 | async-start | bytes 524288 | tf_op jit(solution)/shard_map/weight_grad/all_to_all | solution.py:270
  203.7 2.6 %fusion.1 = bf16[1,128,4096]{2,1,0:T(8,128)(2,1)} fusion(f32[128,4096]{1,0:T(8,128)S(1)} %fusion.5, bf16[128,128]{1,0:T(8,128)(2,1)S(1)} %collective-permute-done.4, bf16[4096,128]{1,0:T(8,128)(2,1)} %collective-permute-done.5), kind=kOutput, calls=%fused_computation.2 | convolution fusion | flops 135266304 | bytes 4227072 | tf_op jit(solution)/shard_map/input_grad/dot_general | solution.py:34
  206.3 9.4 %all-to-all-done.6 = bf16[32,32,128]{2,1,0:T(8,128)(2,1)S(1)} async-done(((bf16[32,32,128]{2,1,0:T(8,128)(2,1)}), bf16[32,32,128]{2,1,0:T(8,128)(2,1)S(1)}, u32[]{:S(2)}, u32[]{:S(2)}) %all-to-all-start.6) | async-done | bytes 262176 | tf_op jit(solution)/shard_map/weight_grad/all_to_all | solution.py:270
  (39 shorter events, 17.2 us)
Async XLA Ops:
  0.6 10.3 %copy-start.4 = (s32[1,1,2]{2,1,0:T(1,128)S(1)}, s32[1,1,2]{2,1,0:T(1,128)}, u32[]{:S(2)}) copy-start(s32[1,1,2]{2,1,0:T(1,128)} %param.11) | copy-start | bytes 28
  0.6 14.8 %copy-start = (bf16[1,128,4096]{2,1,0:T(8,128)(2,1)S(1)}, bf16[1,128,4096]{2,1,0:T(8,128)(2,1)}, u32[]{:S(2)}) copy-start(bf16[1,128,4096]{2,1,0:T(8,128)(2,1)} %param.6) | copy-start | bytes 3145732
  2.8 16.1 %copy-start.5 = (s32[1,32]{1,0:T(1,128)S(1)}, s32[1,32]{1,0:T(1,128)}, u32[]{:S(2)}) copy-start(s32[1,32]{1,0:T(1,128)} %param.10) | copy-start | bytes 388
  2.8 35.1 %all-to-all-start = ((bf16[16,256,128]{2,1,0:T(8,128)(2,1)}), bf16[16,256,128]{2,1,0:T(8,128)(2,1)S(1)}, u32[]{:S(2)}, u32[]{:S(2)}) async-start(bf16[16,256,128]{2,1,0:T(8,128)(2,1)} %broadcast_in_dim.49), calls=%async_computation | async-start | bytes 2097152 | tf_op jit(solution)/shard_map/weight_gather/all_to_all | solution.py:270
  10.9 10.0 %collective-permute-start = (s32[1,2]{1,0:T(1,128)S(1)}, s32[1,2]{1,0:T(1,128)S(1)}, u32[]{:S(2)}, u32[]{:S(2)}) collective-permute-start(s32[1,2]{1,0:T(1,128)S(1)} %bitcast.40), channel_id=1, source_target_pairs={{0,1},{1,0},{2,3},{3,2},{4,5},{5,4},{6,7},{7,6},{8,9},{9,8},{10,11... | collective-permute-start | bytes 32 | tf_op jit(solution)/shard_map/rotation/ppermute | solution.py:267
  15.4 5.7 %collective-permute-start.1 = (bf16[128,4096]{1,0:T(8,128)(2,1)S(1)}, bf16[128,4096]{1,0:T(8,128)(2,1)S(1)}, u32[]{:S(2)}, u32[]{:S(2)}) collective-permute-start(bf16[128,4096]{1,0:T(8,128)(2,1)S(1)} %bitcast.31), channel_id=1, source_target_pairs={{0,1},{1,0},{2,3},{3,2},{4,5},{5,4},{6,7},{7,6},{8,9},{9,8},{10,11... | collective-permute-start | bytes 3145736 | tf_op jit(solution)/shard_map/rotation/ppermute | solution.py:267
  37.9 0.9 copy-start.2
  80.8 9.1 %copy-start.3 = (bf16[16,2,128,128]{3,2,1,0:T(8,128)(2,1)}, bf16[16,2,128,128]{3,2,1,0:T(8,128)(2,1)S(1)}, u32[]{:S(2)}) copy-start(bf16[16,2,128,128]{3,2,1,0:T(8,128)(2,1)S(1)} %all_to_all.35) | copy-start | bytes 3145732
  80.8 9.1 %collective-permute-start.2 = (bf16[32,128,128]{2,1,0:T(8,128)(2,1)S(1)}, bf16[32,128,128]{2,1,0:T(8,128)(2,1)}, u32[]{:S(2)}, u32[]{:S(2)}) collective-permute-start(bf16[32,128,128]{2,1,0:T(8,128)(2,1)S(1)} %bitcast.36), channel_id=1, source_target_pairs={{0,1},{1,0},{2,3},{3,2},{4,5},{5,4},{6,7},{7,6},{8,9},{9,8},{10,11... | collective-permute-start | bytes 3145736 | tf_op jit(solution)/shard_map/kv_gather/ppermute | solution.py:267
  85.7 32.8 %all-to-all-start.2 = ((bf16[8,512,128]{2,1,0:T(8,128)(2,1)}), bf16[8,512,128]{2,1,0:T(8,128)(2,1)S(1)}, u32[]{:S(2)}, u32[]{:S(2)}) async-start(bf16[8,512,128]{2,1,0:T(8,128)(2,1)} %x_columns.1), calls=%async_computation.2 | async-start | bytes 2097152 | tf_op jit(solution)/shard_map/kv_gather/all_to_all | solution.py:270
  107.2 4.8 %collective-permute-start.3 = (bf16[32,128,128]{2,1,0:T(8,128)(2,1)}, bf16[32,128,128]{2,1,0:T(8,128)(2,1)S(1)}, u32[]{:S(2)}, u32[]{:S(2)}) collective-permute-start(bf16[32,128,128]{2,1,0:T(8,128)(2,1)} %get-tuple-element.31), channel_id=1, source_target_pairs={{0,1},{1,0},{2,3},{3,2},{4,5},{5,4},{6,7},{7,6},{8,9},{9,8},{10,11... | collective-permute-start | bytes 3145736 | tf_op jit(solution)/shard_map/kv_reduce/ppermute | solution.py:267
  118.5 33.1 %all-to-all-start.3 = ((bf16[16,2,128,128]{3,2,1,0:T(8,128)(2,1)}), bf16[16,2,128,128]{3,2,1,0:T(8,128)(2,1)S(1)}, u32[]{:S(2)}, u32[]{:S(2)}) async-start(bf16[16,2,128,128]{3,2,1,0:T(8,128)(2,1)} %bitcast.35), calls=%async_computation.3 | async-start | bytes 2097152 | tf_op jit(solution)/shard_map/kv_reduce/all_to_all | solution.py:270
  123.2 40.3 %collective-permute-start.6 = (bf16[8,512,128]{2,1,0:T(8,128)(2,1)S(1)}, bf16[8,512,128]{2,1,0:T(8,128)(2,1)}, u32[]{:S(2)}, u32[]{:S(2)}) collective-permute-start(bf16[8,512,128]{2,1,0:T(8,128)(2,1)S(1)} %all-to-all-done.2.near_ref), channel_id=1, source_target_pairs={{0,1},{1,0},{2,3},{3,2},{4,5},{5,4},{6,7},{7,6},{8,9},{9,8},{10,11... | collective-permute-start | bytes 3145736 | tf_op jit(solution)/shard_map/kv_reduce/ppermute | solution.py:267
  151.9 0.8 copy-start.1
  152.7 18.2 %all-to-all-start.4 = ((bf16[8,2,128,128]{3,2,1,0:T(8,128)(2,1)}), bf16[8,2,128,128]{3,2,1,0:T(8,128)(2,1)S(1)}, u32[]{:S(2)}, u32[]{:S(2)}) async-start(bf16[8,2,128,128]{3,2,1,0:T(8,128)(2,1)} %copy-done.1), calls=%async_computation.4 | async-start | bytes 1048576 | tf_op jit(solution)/shard_map/weight_grad/all_to_all | solution.py:270
  156.2 47.5 %collective-permute-start.5 = (bf16[4096,128]{1,0:T(8,128)(2,1)S(1)}, bf16[4096,128]{1,0:T(8,128)(2,1)}, u32[]{:S(2)}, u32[]{:S(2)}) collective-permute-start(bf16[4096,128]{1,0:T(8,128)(2,1)S(1)} %bitcast.29), channel_id=1, source_target_pairs={{0,1},{1,0},{2,3},{3,2},{4,5},{5,4},{6,7},{7,6},{8,9},{9,8},{10,11... | collective-permute-start | bytes 3145736 | tf_op jit(solution)/shard_map/kv_reduce/ppermute | solution.py:267
  161.6 40.7 %collective-permute-start.4 = (bf16[128,128]{1,0:T(8,128)(2,1)S(1)}, bf16[128,128]{1,0:T(8,128)(2,1)S(1)}, u32[]{:S(2)}, u32[]{:S(2)}) collective-permute-start(bf16[128,128]{1,0:T(8,128)(2,1)S(1)} %select_bitcast_fusion), channel_id=1, source_target_pairs={{0,1},{1,0},{2,3},{3,2},{4,5},{5,4},{6,7},{7,6},{8,9},{9,8},{10,11... | collective-permute-start | bytes 98312 | tf_op jit(solution)/shard_map/input_grad/ppermute | solution.py:267
  173.4 22.7 %all-to-all-start.5 = ((bf16[16,32,128]{2,1,0:T(8,128)(2,1)}), bf16[16,32,128]{2,1,0:T(8,128)(2,1)S(1)}, u32[]{:S(2)}, u32[]{:S(2)}) async-start(bf16[16,32,128]{2,1,0:T(8,128)(2,1)} %weight_share.1), calls=%async_computation.5 | async-start | bytes 262144 | tf_op jit(solution)/shard_map/weight_grad/all_to_all | solution.py:270
  196.8 18.9 %all-to-all-start.6 = ((bf16[32,32,128]{2,1,0:T(8,128)(2,1)}), bf16[32,32,128]{2,1,0:T(8,128)(2,1)S(1)}, u32[]{:S(2)}, u32[]{:S(2)}) async-start(bf16[32,32,128]{2,1,0:T(8,128)(2,1)} %group_share.1), calls=%async_computation.6 | async-start | bytes 524288 | tf_op jit(solution)/shard_map/weight_grad/all_to_all | solution.py:270

commit v5 on v4

--- a/solution.py
+++ b/solution.py
@@ -41,9 +41,9 @@
 
 
 def attention_kernel(
-    order_ref, place_ref, core_ref, near_ref, far_ref, q_ref, g_ref,
+    order_ref, place_ref, core_ref, near_ref, far_ref, q_cols, g_cols, q_rows, g_rows,
     dq_ref, near_grad_ref, far_grad_ref,
-    exp_store, prob_store, top_store, q_cols, g_cols, q_rows, g_rows, dq_cols,
+    exp_store, prob_store, top_store, dq_cols,
 ):
     blocks = near_ref.shape[0]
     rows = QH * BLOCK
@@ -53,12 +53,6 @@
     is_first = core_ref[0] == 0
     tiles = lax.div(place + TILE_BLOCKS, TILE_BLOCKS)
 
-    for head in range(QH):
-        part = pl.ds(head * HD, HD)
-        q_cols[:, part] = q_ref[:, part].T
-        g_cols[:, part] = g_ref[:, part].T
-        q_rows[part, :] = q_ref[:, part]
-        g_rows[part, :] = g_ref[:, part]
     dq_cols[...] = jnp.zeros_like(dq_cols)
 
     def gathered(tile):
@@ -127,9 +121,8 @@
         dq_ref[:, part] = (dq_cols[:, part].T * (1.0 / math.sqrt(HD))).astype(jnp.bfloat16)
 
 
-def attention_backward(order, place, core, near, far, queries, out_grad):
-    tokens = queries.shape[0]
-    rows = QH * tokens
+def attention_backward(order, place, core, near, far, columns_and_rows):
+    rows = columns_and_rows[0].shape[1]
     tiles = near.shape[0] // TILE_BLOCKS
     span = TILE_BLOCKS * BLOCK
     smem = pl.BlockSpec(memory_space=pltpu.SMEM)
@@ -137,25 +130,21 @@
     return pl.pallas_call(
         attention_kernel,
         out_shape=(
-            jax.ShapeDtypeStruct(queries.shape, jnp.bfloat16),
+            jax.ShapeDtypeStruct((rows // QH, QH * HD), jnp.bfloat16),
             jax.ShapeDtypeStruct(near.shape, jnp.bfloat16),
             jax.ShapeDtypeStruct(far.shape, jnp.bfloat16),
         ),
-        in_specs=[smem, smem, smem, vmem, vmem, vmem, vmem],
+        in_specs=[smem] * 3 + [vmem] * 6,
         out_specs=(vmem, vmem, vmem),
         scratch_shapes=[
             pltpu.VMEM((tiles, span, rows), jnp.float32),
             pltpu.VMEM((tiles, span, rows), jnp.float32),
             pltpu.VMEM((tiles, 1, rows), jnp.float32),
-            pltpu.VMEM((HD, rows), jnp.bfloat16),
-            pltpu.VMEM((HD, rows), jnp.bfloat16),
-            pltpu.VMEM((rows, HD), jnp.bfloat16),
-            pltpu.VMEM((rows, HD), jnp.bfloat16),
             pltpu.VMEM((HD, rows), jnp.float32),
         ],
         compiler_params=pltpu.CompilerParams(vmem_limit_bytes=56 * 1024 * 1024),
         name="attention_backward",
-    )(order, place, core, near, far, queries, out_grad)
+    )(order, place, core, near, far, *columns_and_rows)
 
 
 def local_call(kernel, shapes, scalars, arrays, name, scratch=()):
@@ -172,6 +161,22 @@
     )(*scalars, *arrays)
 
 
+def copies_kernel(core_ref, weight_ref, out_ref):
+    start = pl.multiple_of(core_ref[0] * HD, HD)
+    half = weight_ref[:, pl.ds(start, HD)]
+    for copy in range(out_ref.shape[0]):
+        out_ref[copy] = half
+
+
+def query_kernel(q_ref, g_ref, q_cols, g_cols, q_rows, g_rows):
+    for head in range(QH):
+        part = pl.ds(head * HD, HD)
+        q_cols[:, part] = q_ref[:, part].T
+        g_cols[:, part] = g_ref[:, part].T
+        q_rows[part, :] = q_ref[:, part]
+        g_rows[part, :] = g_ref[:, part]
+
+
 def project_kernel(core_ref, levels_ref, own_ref, far_ref, weight_ref, cos_ref, sin_ref, out_ref):
     core = core_ref[0]
     weight = weight_ref[...]
@@ -197,25 +202,34 @@
             out_ref[copy, at] = turned
 
 
-def turn_kernel(x_ref, out_ref, flipped):
-    columns, extent, _ = out_ref.shape
-    piece = BLOCK // columns
-    for block in range(extent // piece):
-        part = pl.ds(block * BLOCK, BLOCK)
-        flipped[...] = x_ref[:, part].T
-        for column in range(columns):
-            out_ref[column, block * piece : (block + 1) * piece, :] = flipped[
-                column * piece : (column + 1) * piece, :
-            ]
-
-
-def share_kernel(core_ref, near_ref, far_ref, grads_ref, out_ref):
+def turn_kernel(parity_ref, x_ref, keep_ref, *rest):
+    parity = parity_ref[0]
+    for group in range(keep_ref.shape[0] // BLOCK):
+        rows = slice(group * BLOCK, (group + 1) * BLOCK)
+        for out_ref, half in zip((keep_ref, *rest), (parity, 1 - parity)):
+            start = pl.multiple_of((2 * group + half) * BLOCK, BLOCK)
+            out_ref[rows, :] = x_ref[:, pl.ds(start, BLOCK)].T
+
+
+def turned_halves(parity, x_rows, count, name):
+    tokens, width = x_rows.shape
+    shape = jax.ShapeDtypeStruct((width // 2, tokens), x_rows.dtype)
+    return local_call(turn_kernel, (shape,) * count, (parity,), (x_rows,), name)
+
+
+def share_kernel(core_ref, *rest):
     core = core_ref[0]
-    share = jnp.zeros(near_ref.shape[1:], jnp.float32)
-    for column in range(near_ref.shape[0]):
-        share += dot(near_ref[column], grads_ref[column, core])
-        share += dot(far_ref[column], grads_ref[column, 1 - core])
-    out_ref[...] = share.astype(out_ref.dtype).reshape(out_ref.shape)
+    own_ref, own_far_ref, next_ref, next_far_ref, grads_ref, next_grads_ref, out_ref = rest
+    quads, groups, piece, _ = out_ref.shape
+    own = jnp.concatenate([grads_ref[core], grads_ref[1 - core]], axis=0)
+    beside = jnp.concatenate([next_grads_ref[core], next_grads_ref[1 - core]], axis=0)
+    for group in range(groups):
+        rows = slice(group * BLOCK, (group + 1) * BLOCK)
+        share = dot(jnp.concatenate([own_ref[rows, :], own_far_ref[rows, :]], axis=1), own)
+        share += dot(jnp.concatenate([next_ref[rows, :], next_far_ref[rows, :]], axis=1), beside)
+        share = share.astype(out_ref.dtype)
+        for quad in range(quads):
+            out_ref[quad, group] = share[quad * piece : (quad + 1) * piece]
 
 
 def total_kernel(parts_ref, out_ref):
@@ -228,18 +242,16 @@
 
 
 def assemble_kernel(grad_scale, parts_ref, out_ref):
-    columns = parts_ref.shape[1]
-    piece = parts_ref.shape[3] // 2
-    for column in range(columns):
-        for core in range(2):
-            low = parts_ref[0, column, core].astype(jnp.float32)
-            high = parts_ref[1, column, core].astype(jnp.float32)
-            total = (low + high) * grad_scale
-            for half in range(2):
-                row = half * columns * piece + column * piece
-                out_ref[row : row + piece, core * HD : (core + 1) * HD] = total[
-                    half * piece : (half + 1) * piece
-                ]
+    _, quads, _, _, piece, _ = parts_ref.shape
+    for quad in range(quads):
+        for parity in range(2):
+            for core in range(2):
+                low = parts_ref[0, quad, parity, core].astype(jnp.float32)
+                high = parts_ref[1, quad, parity, core].astype(jnp.float32)
+                row = parity * BLOCK + quad * piece
+                out_ref[row : row + piece, core * HD : (core + 1) * HD] = (
+                    low + high
+                ) * grad_scale
 
 
 def body(hidden_in, queries, out_grad, kv_weight, block_pos, precision):
@@ -255,16 +267,22 @@
     core_index = lax.rem(self_index, 2)
     core = core_index.reshape(1).astype(jnp.int32)
     is_first = core_index == 0
-    column_groups = [
-        [start * half_count + 2 * column + side for column in range(columns)]
+    quads = columns // 2
+    parity = lax.rem(lax.div(self_index, 2), 2).reshape(1).astype(jnp.int32)
+    quad_groups = [
+        [start * half_count + 4 * quad + side for quad in range(quads)]
         for start in range(2)
-        for side in range(2)
+        for side in range(4)
     ]
     same_core = [[2 * chip + side for chip in range(half_count)] for side in range(2)]
     swap = [(source, source ^ 1) for source in range(seq_count)]
+    beside = [(source, source ^ 2) for source in range(seq_count)]
 
     def swapped(value):
         return lax.ppermute(value, "seq", swap)
+
+    def passed(value):
+        return lax.ppermute(value, "seq", beside)
 
     def exchanged(value, axis, groups=None):
         return lax.all_to_all(value, axis, 0, 0, axis_index_groups=groups)
@@ -294,24 +312,25 @@
         bits_here = jnp.where(is_first, pair_bits[:, 0], pair_bits[:, 1])
         levels = (lax.shift_left(jnp.ones_like(bits_here), bits_here - 1) - 1).astype(jnp.float32)
         x_far = swapped(x_rows)
-        x_columns = local_call(
-            turn_kernel,
-            jax.ShapeDtypeStruct((columns, width // columns, tokens), x_rows.dtype),
-            (),
-            (x_rows,),
-            "x_columns",
-            (pltpu.VMEM((BLOCK, tokens), x_rows.dtype),),
-        )
+        own_half, given_half = turned_halves(parity, x_rows, 2, "own_halves")
+        next_half = passed(given_half)
+        (far_half,) = turned_halves(parity, x_far, 1, "far_half")
     with jax.named_scope("weight_gather"):
-        half = jnp.where(is_first, kv_weight[:, :HD], kv_weight[:, HD:])
-        copies = jnp.broadcast_to(half[None], (dp_count, *half.shape))
-        near_weight = exchanged(lax.optimization_barrier(copies), "dp").reshape(width, HD)
+        copies = local_call(
+            copies_kernel,
+            jax.ShapeDtypeStruct((dp_count, kv_weight.shape[0], HD), kv_weight.dtype),
+            (core,),
+            (kv_weight,),
+            "weight_copies",
+        )
+        near_weight = exchanged(copies, "dp").reshape(width, HD)
         (
-            near_weight, order, cosine, sine_part, back_cosine, back_sine, levels, x_far, x_columns
+            near_weight, order, cosine, sine_part, back_cosine, back_sine, levels, x_far,
+            own_half, next_half, far_half,
         ) = lax.optimization_barrier(
             (
                 near_weight, order, cosine, sine_part, back_cosine, back_sine, levels, x_far,
-                x_columns,
+                own_half, next_half, far_half,
             )
         )
     with jax.named_scope("projection"):
@@ -324,43 +343,60 @@
         )
     with jax.named_scope("kv_gather"):
         near = exchanged(stacked, "seq", same_core).reshape(seq_count, tokens, HD)
-        near, x_columns = lax.optimization_barrier((near, x_columns))
-        near_columns = exchanged(x_columns, "seq", column_groups)
+        columns_shape = jax.ShapeDtypeStruct((HD, QH * tokens), jnp.bfloat16)
+        rows_shape = jax.ShapeDtypeStruct((QH * tokens, HD), jnp.bfloat16)
+        columns_and_rows = local_call(
+            query_kernel,
+            (columns_shape, columns_shape, rows_shape, rows_shape),
+            (),
+            (queries[0], out_grad[0]),
+            "query_columns",
+        )
+        near, *columns_and_rows = lax.optimization_barrier((near, *columns_and_rows))
         far = swapped(near)
     with jax.named_scope("attention"):
         query_grad, near_grad, far_grad = attention_backward(
-            order, place, core, near, far, queries[0], out_grad[0]
+            order, place, core, near, far, columns_and_rows
         )
     with jax.named_scope("kv_reduce"):
         pair = near_grad.astype(jnp.float32) + swapped(far_grad).astype(jnp.float32)
         pair = pair.astype(jnp.bfloat16).reshape(half_count, 2, tokens, HD)
-        pair, near_columns, near_weight = lax.optimization_barrier(
-            (pair, near_columns, near_weight)
-        )
+        pair, next_half, near_weight = lax.optimization_barrier((pair, next_half, near_weight))
         arrived = exchanged(pair, "seq", same_core)
-        far_columns = swapped(near_columns)
+        next_far_half = swapped(next_half)
         far_weight = swapped(near_weight)
+        arrived, next_far_half, far_weight = lax.optimization_barrier(
+            (arrived, next_far_half, far_weight)
+        )
     with jax.named_scope("projection_grad"):
         settled = local_call(
             settle_kernel,
-            jax.ShapeDtypeStruct((columns, 2, tokens, HD), jnp.bfloat16),
+            jax.ShapeDtypeStruct((1, 2, tokens, HD), jnp.bfloat16),
             (),
             (arrived, back_cosine, back_sine),
             "projection_grad",
         )
     with jax.named_scope("weight_grad"):
-        column_grads = exchanged(settled, "seq", column_groups)
+        piece = BLOCK // quads
         share = local_call(
             share_kernel,
-            jax.ShapeDtypeStruct((dp_count, width // columns // dp_count, HD), jnp.bfloat16),
+            jax.ShapeDtypeStruct((quads, dp_count, piece, HD), jnp.bfloat16),
             (core,),
-            (near_columns, far_columns, column_grads),
+            (own_half, far_half, next_half, next_far_half, settled[0], passed(settled[0])),
             "weight_share",
         )
-        share_parts = exchanged(share, "dp")
+        quad_parts = exchanged(share, "seq", quad_groups)
+        (quad_share,) = local_call(
+            total_kernel,
+            (jax.ShapeDtypeStruct((1, dp_count, piece, HD), jnp.bfloat16),),
+            (),
+            (quad_parts,),
+            "quad_share",
+        )
+        share_parts = exchanged(quad_share[0], "dp")
         group_share = local_call(
             total_kernel,
-            jax.ShapeDtypeStruct((seq_count, *share.shape[1:]), jnp.bfloat16),
+            jax.ShapeDtypeStruct((seq_count, piece, HD), jnp.bfloat16),
             (),
             (share_parts,),
             "group_share",
@@ -370,7 +406,7 @@
             functools.partial(assemble_kernel, grad_scale),
             jax.ShapeDtypeStruct((width // dp_count, 2 * HD), jnp.float32),
             (),
-            (gathered.reshape(2, columns, 2, *share.shape[1:]),),
+            (gathered.reshape(2, quads, 2, 2, piece, HD),),
             "weight_grad",
         )
     with jax.named_scope("input_grad"):

time: 219 us -> 219 us (level)
  blocking collectives: 40.1 us -> 0 us
  waiting for transfers between devices: 72.2 us -> 92.3 us
  starting transfers between devices: 63 us -> 78.1 us
  local copies, waits for them, and re-layouts: 3.47 us -> 8.9 us
  other arithmetic: 8.02 us -> 5.54 us
    all_to_all x1 -> x0, blocking collectives: 40.1 us -> none  [exchanged(): return lax.all_to_all(value, axis, 0, 0, axis_index_groups=groups)]
    ppermute x0 -> x2, waiting for transfers between devices: none -> 12.3 us  [passed(): return lax.ppermute(value, 'seq', beside)]
    all_to_all x6, starting transfers between devices: 40.6 us -> 51.6 us  [exchanged(): return lax.all_to_all(value, axis, 0, 0, axis_index_groups=groups)]
    unnamed x12 -> x38, local copies, waits for them, and re-layouts: 1.71 us -> 8.25 us
    ppermute x0 -> x2, starting transfers between devices: none -> 4.52 us  [passed(): return lax.ppermute(value, 'seq', beside)]
    all_to_all x6, waiting for transfers between devices: 69.4 us -> 73.2 us  [exchanged(): return lax.all_to_all(value, axis, 0, 0, axis_index_groups=groups)]
    ppermute x7, waiting for transfers between devices: 2.85 us -> 6.68 us  [swapped(): return lax.ppermute(value, 'seq', swap)]
    pallas_call x6 -> x10, Pallas kernels: 7.67 us -> 9.57 us  [local_call(): pl.pallas_call(kernel, out_shape=shapes, in_specs=[smem] * len(scalars) +...]
  transfers between devices with their start and end apart: 13 -> 15, of which waited for: 7 -> 11; matrix products, arithmetic and copies ran while one was open for 5% -> 4% of each run, Pallas kernels for 10% -> 1%
where the time goes in v5:
time: 219 us; the launch traced here: 216 us
  waiting for transfers between devices  92.3 us (42%)
  starting transfers between devices  78.1 us (36%)
  Pallas kernels  25.3 us (12%)
  local copies, waits for them, and re-layouts  8.9 us (4%)
  other arithmetic  5.54 us (3%)
  matrix products  5.12 us (2%)
    all_to_all x6, waiting for transfers between devices, exchanged(): return lax.all_to_all(value, axis, 0, 0, axis_index_groups=groups)  73.2 us
    all_to_all x6, starting transfers between devices, exchanged(): return lax.all_to_all(value, axis, 0, 0, axis_index_groups=groups)  51.6 us
    ppermute x7, starting transfers between devices, swapped(): return lax.ppermute(value, 'seq', swap)  22 us
    pallas_call x1, Pallas kernels, attention_backward(): pl.pallas_call(attention_kernel, out_shape=(jax.ShapeDtypeStruct((rows //...  15.7 us
    ppermute x2, waiting for transfers between devices, passed(): return lax.ppermute(value, 'seq', beside)  12.3 us
    pallas_call x10, Pallas kernels, local_call(): pl.pallas_call(kernel, out_shape=shapes, in_specs=[smem] * len(scalars) +...  9.57 us
    unnamed x38, local copies, waits for them, and re-layouts  8.25 us
    ppermute x7, waiting for transfers between devices, swapped(): return lax.ppermute(value, 'seq', swap)  6.68 us
  transfers between devices with their start and end apart: 15, of which 11 were waited for; matrix products, arithmetic and copies ran while one was open for 4% of the time, Pallas kernels for 1%

profile of v5, /device:TPU:1, one launch (start us, length us, event | category | flops | bytes accessed | tf_op | source)
XLA Modules:
  0.0 216.1 jit_solution(15005793060946748803)
XLA Ops:
  2.8 8.0 %all-to-all-start = ((bf16[16,256,128]{2,1,0:T(8,128)(2,1)}), bf16[16,256,128]{2,1,0:T(8,128)(2,1)S(1)}, u32[]{:S(2)}, u32[]{:S(2)}) async-start(bf16[16,256,128]{2,1,0:T(8,128)(2,1)} %weight_copies.1), calls=%async_computation | async-start | bytes 2097152 | tf_op jit(solution)/shard_map/weight_gather/all_to_all | solution.py:288
  10.8 4.5 %collective-permute-start = (s32[1,2]{1,0:T(1,128)S(1)}, s32[1,2]{1,0:T(1,128)S(1)}, u32[]{:S(2)}, u32[]{:S(2)}) collective-permute-start(s32[1,2]{1,0:T(1,128)S(1)} %bitcast.45), channel_id=1, source_target_pairs={{0,1},{1,0},{2,3},{3,2},{4,5},{5,4},{6,7},{7,6},{8,9},{9,8},{10,11... | collective-permute-start | bytes 32 | tf_op jit(solution)/shard_map/rotation/ppermute | solution.py:282
  19.2 2.4 %collective-permute-start.2 = (bf16[2048,128]{1,0:T(8,128)(2,1)}, bf16[2048,128]{1,0:T(8,128)(2,1)}, u32[]{:S(2)}, u32[]{:S(2)}) collective-permute-start(bf16[2048,128]{1,0:T(8,128)(2,1)} %get-tuple-element.36), channel_id=1, source_target_pairs={{0,2},{1,3},{2,0},{3,1},{4,6},{5,7},{6,4},{7,5},{8,10},{9,11},{10,... | collective-permute-start | bytes 1572872 | tf_op jit(solution)/shard_map/rotation/ppermute | solution.py:285
  24.9 9.5 %collective-permute-done.2.rest_2_ = bf16[2048,128]{1,0:T(8,128)(2,1)} collective-permute-done((bf16[2048,128]{1,0:T(8,128)(2,1)}, bf16[2048,128]{1,0:T(8,128)(2,1)}, u32[]{:S(2)}, u32[]{:S(2)}) %collective-permute-start.2) | collective-permute-done | bytes 524320 | tf_op jit(solution)/shard_map/rotation/ppermute | solution.py:285
  34.4 3.4 %all-to-all-done = bf16[16,256,128]{2,1,0:T(8,128)(2,1)S(1)} async-done(((bf16[16,256,128]{2,1,0:T(8,128)(2,1)}), bf16[16,256,128]{2,1,0:T(8,128)(2,1)S(1)}, u32[]{:S(2)}, u32[]{:S(2)}) %all-to-all-start) | async-done | bytes 1048608 | tf_op jit(solution)/shard_map/weight_gather/all_to_all | solution.py:288
  40.6 12.9 %all-to-all-start.1 = ((bf16[16,2,128,128]{3,2,1,0:T(8,128)(2,1)}), bf16[16,2,128,128]{3,2,1,0:T(8,128)(2,1)S(1)}, u32[]{:S(2)}, u32[]{:S(2)}) async-start(bf16[16,2,128,128]{3,2,1,0:T(8,128)(2,1)} %copy-done.1), calls=%async_computation.1 | async-start | bytes 2097152 | tf_op jit(solution)/shard_map/kv_gather/all_to_all | solution.py:288
  56.6 24.9 %all-to-all-done.1 = bf16[16,2,128,128]{3,2,1,0:T(8,128)(2,1)S(1)} async-done(((bf16[16,2,128,128]{3,2,1,0:T(8,128)(2,1)}), bf16[16,2,128,128]{3,2,1,0:T(8,128)(2,1)S(1)}, u32[]{:S(2)}, u32[]{:S(2)}) %all-to-all-start.1) | async-done | bytes 1048608 | tf_op jit(solution)/shard_map/kv_gather/all_to_all | solution.py:288
  81.5 4.6 %collective-permute-start.3 = (bf16[32,128,128]{2,1,0:T(8,128)(2,1)S(1)}, bf16[32,128,128]{2,1,0:T(8,128)(2,1)}, u32[]{:S(2)}, u32[]{:S(2)}) collective-permute-start(bf16[32,128,128]{2,1,0:T(8,128)(2,1)S(1)} %bitcast.43), channel_id=1, source_target_pairs={{0,1},{1,0},{2,3},{3,2},{4,5},{5,4},{6,7},{7,6},{8,9},{9,8},{10,11... | collective-permute-start | bytes 3145736 | tf_op jit(solution)/shard_map/kv_gather/ppermute | solution.py:282
  88.5 15.7 %attention_backward.1 = (bf16[128,1024]{1,0:T(8,128)(2,1)}, bf16[32,128,128]{2,1,0:T(8,128)(2,1)}, bf16[32,128,128]{2,1,0:T(8,128)(2,1)}) custom-call(s32[32]{0:T(128)} %select_reduce_fusion.order_ref, s32[1]{0:T(128)} %bitcast.7.place_ref, s32[1]{0:T(128)} %bitcast.core_ref, bf16[32,128,128]{2,1,0:T(8,128)(2,1)} %bitcast.44, ...), custom_call_target="tpu_custom_call" | custom-call | tf_op jit(solution)/shard_map/attention/attention_backward/pallas_call | solution.py:130
  106.1 2.8 %collective-permute-done.4 = bf16[32,128,128]{2,1,0:T(8,128)(2,1)S(1)} collective-permute-done((bf16[32,128,128]{2,1,0:T(8,128)(2,1)}, bf16[32,128,128]{2,1,0:T(8,128)(2,1)S(1)}, u32[]{:S(2)}, u32[]{:S(2)}) %collective-permute-start.4) | collective-permute-done | bytes 1048608 | tf_op jit(solution)/shard_map/kv_reduce/ppermute | solution.py:282
  109.0 2.6 %add_convert_fusion = bf16[32,128,128]{2,1,0:T(8,128)(2,1)} fusion(bf16[32,128,128]{2,1,0:T(8,128)(2,1)S(1)} %collective-permute-done.4, bf16[32,128,128]{2,1,0:T(8,128)(2,1)} %get-tuple-element.53), kind=kLoop, calls=%fused_computation.3 | loop fusion | flops 2097152 | bytes 3145728 | tf_op jit(solution)/shard_map/kv_reduce/convert_element_type | solution.py:363
  111.6 7.4 %all-to-all-start.2 = ((bf16[16,2,128,128]{3,2,1,0:T(8,128)(2,1)}), bf16[16,2,128,128]{3,2,1,0:T(8,128)(2,1)S(1)}, u32[]{:S(2)}, u32[]{:S(2)}) async-start(bf16[16,2,128,128]{3,2,1,0:T(8,128)(2,1)} %bitcast.42), calls=%async_computation.2 | async-start | bytes 2097152 | tf_op jit(solution)/shard_map/kv_reduce/all_to_all | solution.py:288
  118.9 2.6 %collective-permute-start.6 = (bf16[4096,128]{1,0:T(8,128)(2,1)S(1)}, bf16[4096,128]{1,0:T(8,128)(2,1)}, u32[]{:S(2)}, u32[]{:S(2)}) collective-permute-start(bf16[4096,128]{1,0:T(8,128)(2,1)S(1)} %bitcast.32), channel_id=1, source_target_pairs={{0,1},{1,0},{2,3},{3,2},{4,5},{5,4},{6,7},{7,6},{8,9},{9,8},{10,11... | collective-permute-start | bytes 3145736 | tf_op jit(solution)/shard_map/kv_reduce/ppermute | solution.py:282
  126.3 22.4 %all-to-all-done.2.arrived_ref = bf16[16,2,128,128]{3,2,1,0:T(8,128)(2,1)S(1)} async-done(((bf16[16,2,128,128]{3,2,1,0:T(8,128)(2,1)}), bf16[16,2,128,128]{3,2,1,0:T(8,128)(2,1)S(1)}, u32[]{:S(2)}, u32[]{:S(2)}) %all-to-all-start.2) | async-done | bytes 1048608 | tf_op jit(solution)/shard_map/kv_reduce/all_to_all | solution.py:288
  151.1 2.9 %collective-permute-done.8.rest_5_ = bf16[2,128,128]{2,1,0:T(8,128)(2,1)S(1)} collective-permute-done((bf16[2,128,128]{2,1,0:T(8,128)(2,1)S(1)}, bf16[2,128,128]{2,1,0:T(8,128)(2,1)S(1)}, u32[]{:S(2)}, u32[]{:S(2)}) %collective-permute-start.8) | collective-permute-done | bytes 65568 | tf_op jit(solution)/shard_map/weight_grad/ppermute | solution.py:285
  155.0 2.5 %weight_share.1 = bf16[4,16,32,128]{3,2,1,0:T(8,128)(2,1)} custom-call(s32[1]{0:T(128)} %bitcast.core_ref, bf16[2048,128]{1,0:T(8,128)(2,1)S(1)} %copy-done.5, bf16[2048,128]{1,0:T(8,128)(2,1)S(1)} %copy-done.3, bf16[2048,128]{1,0:T(8,128)(2,1)} %collective-permute-done.2.rest_2_, bf16[2048,128]{1,0:T(8,128)(2,1)S(1)} %copy-done.7, ...), custom_call_target="tpu_custom_call" | custom-call | tf_op jit(solution)/shard_map/weight_grad/weight_share/pallas_call | solution.py:153
  157.5 4.1 %all-to-all-start.3 = ((bf16[4,16,32,128]{3,2,1,0:T(8,128)(2,1)}), bf16[4,16,32,128]{3,2,1,0:T(8,128)(2,1)S(1)}, u32[]{:S(2)}, u32[]{:S(2)}) async-start(bf16[4,16,32,128]{3,2,1,0:T(8,128)(2,1)} %weight_share.1), calls=%async_computation.3 | async-start | bytes 1048576 | tf_op jit(solution)/shard_map/weight_grad/all_to_all | solution.py:288
  161.7 4.6 %collective-permute-start.7 = (bf16[128,128]{1,0:T(8,128)(2,1)S(1)}, bf16[128,128]{1,0:T(8,128)(2,1)S(1)}, u32[]{:S(2)}, u32[]{:S(2)}) collective-permute-start(bf16[128,128]{1,0:T(8,128)(2,1)S(1)} %select_bitcast_fusion), channel_id=1, source_target_pairs={{0,1},{1,0},{2,3},{3,2},{4,5},{5,4},{6,7},{7,6},{8,9},{9,8},{10,11... | collective-permute-start | bytes 98312 | tf_op jit(solution)/shard_map/input_grad/ppermute | solution.py:282
  166.3 7.6 %all-to-all-done.3.parts_ref = bf16[4,16,32,128]{3,2,1,0:T(8,128)(2,1)S(1)} async-done(((bf16[4,16,32,128]{3,2,1,0:T(8,128)(2,1)}), bf16[4,16,32,128]{3,2,1,0:T(8,128)(2,1)S(1)}, u32[]{:S(2)}, u32[]{:S(2)}) %all-to-all-start.3) | async-done | bytes 524320 | tf_op jit(solution)/shard_map/weight_grad/all_to_all | solution.py:288
  174.7 11.5 %all-to-all-start.4 = ((bf16[16,32,128]{2,1,0:T(8,128)(2,1)}), bf16[16,32,128]{2,1,0:T(8,128)(2,1)S(1)}, u32[]{:S(2)}, u32[]{:S(2)}) async-start(bf16[16,32,128]{2,1,0:T(8,128)(2,1)} %bitcast.18), calls=%async_computation.4 | async-start | bytes 262144 | tf_op jit(solution)/shard_map/weight_grad/all_to_all | solution.py:288
  188.0 5.5 %all-to-all-done.4.parts_ref = bf16[16,32,128]{2,1,0:T(8,128)(2,1)S(1)} async-done(((bf16[16,32,128]{2,1,0:T(8,128)(2,1)}), bf16[16,32,128]{2,1,0:T(8,128)(2,1)S(1)}, u32[]{:S(2)}, u32[]{:S(2)}) %all-to-all-start.4) | async-done | bytes 131104 | tf_op jit(solution)/shard_map/weight_grad/all_to_all | solution.py:288
  194.2 7.7 %all-to-all-start.5 = ((bf16[32,32,128]{2,1,0:T(8,128)(2,1)}), bf16[32,32,128]{2,1,0:T(8,128)(2,1)S(1)}, u32[]{:S(2)}, u32[]{:S(2)}) async-start(bf16[32,32,128]{2,1,0:T(8,128)(2,1)} %group_share.1), calls=%async_computation.5 | async-start | bytes 524288 | tf_op jit(solution)/shard_map/weight_grad/all_to_all | solution.py:288
  202.6 3.3 %fusion.1 = bf16[1,128,4096]{2,1,0:T(8,128)(2,1)} fusion(f32[128,4096]{1,0:T(8,128)} %fusion.5, bf16[128,128]{1,0:T(8,128)(2,1)S(1)} %collective-permute-done.7, bf16[4096,128]{1,0:T(8,128)(2,1)} %collective-permute-done.6), kind=kOutput, calls=%fused_computation.2 | convolution fusion | flops 135266304 | bytes 4227072 | tf_op jit(solution)/shard_map/input_grad/dot_general | solution.py:34
  205.9 9.5 %all-to-all-done.5 = bf16[32,32,128]{2,1,0:T(8,128)(2,1)S(1)} async-done(((bf16[32,32,128]{2,1,0:T(8,128)(2,1)}), bf16[32,32,128]{2,1,0:T(8,128)(2,1)S(1)}, u32[]{:S(2)}, u32[]{:S(2)}) %all-to-all-start.5) | async-done | bytes 262176 | tf_op jit(solution)/shard_map/weight_grad/all_to_all | solution.py:288
  (70 shorter events, 32.4 us)
Async XLA Ops:
  0.6 14.7 %copy-start = (bf16[1,128,4096]{2,1,0:T(8,128)(2,1)S(1)}, bf16[1,128,4096]{2,1,0:T(8,128)(2,1)}, u32[]{:S(2)}) copy-start(bf16[1,128,4096]{2,1,0:T(8,128)(2,1)} %param.6) | copy-start | bytes 3145732
  1.6 9.2 %copy-start.17 = (s32[1,1,2]{2,1,0:T(1,128)S(1)}, s32[1,1,2]{2,1,0:T(1,128)}, u32[]{:S(2)}) copy-start(s32[1,1,2]{2,1,0:T(1,128)} %param.11) | copy-start | bytes 28
  1.6 20.0 %copy-start.18 = (s32[1,32]{1,0:T(1,128)S(1)}, s32[1,32]{1,0:T(1,128)}, u32[]{:S(2)}) copy-start(s32[1,32]{1,0:T(1,128)} %param.10) | copy-start | bytes 388
  2.8 34.9 %all-to-all-start = ((bf16[16,256,128]{2,1,0:T(8,128)(2,1)}), bf16[16,256,128]{2,1,0:T(8,128)(2,1)S(1)}, u32[]{:S(2)}, u32[]{:S(2)}) async-start(bf16[16,256,128]{2,1,0:T(8,128)(2,1)} %weight_copies.1), calls=%async_computation | async-start | bytes 2097152 | tf_op jit(solution)/shard_map/weight_gather/all_to_all | solution.py:288
  10.8 12.9 %collective-permute-start = (s32[1,2]{1,0:T(1,128)S(1)}, s32[1,2]{1,0:T(1,128)S(1)}, u32[]{:S(2)}, u32[]{:S(2)}) collective-permute-start(s32[1,2]{1,0:T(1,128)S(1)} %bitcast.45), channel_id=1, source_target_pairs={{0,1},{1,0},{2,3},{3,2},{4,5},{5,4},{6,7},{7,6},{8,9},{9,8},{10,11... | collective-permute-start | bytes 32 | tf_op jit(solution)/shard_map/rotation/ppermute | solution.py:282
  15.3 8.6 %collective-permute-start.1 = (bf16[128,4096]{1,0:T(8,128)(2,1)S(1)}, bf16[128,4096]{1,0:T(8,128)(2,1)S(1)}, u32[]{:S(2)}, u32[]{:S(2)}) collective-permute-start(bf16[128,4096]{1,0:T(8,128)(2,1)S(1)} %bitcast.34), channel_id=1, source_target_pairs={{0,1},{1,0},{2,3},{3,2},{4,5},{5,4},{6,7},{7,6},{8,9},{9,8},{10,11... | collective-permute-start | bytes 3145736 | tf_op jit(solution)/shard_map/rotation/ppermute | solution.py:282
  19.2 15.2 %collective-permute-start.2 = (bf16[2048,128]{1,0:T(8,128)(2,1)}, bf16[2048,128]{1,0:T(8,128)(2,1)}, u32[]{:S(2)}, u32[]{:S(2)}) collective-permute-start(bf16[2048,128]{1,0:T(8,128)(2,1)} %get-tuple-element.36), channel_id=1, source_target_pairs={{0,2},{1,3},{2,0},{3,1},{4,6},{5,7},{6,4},{7,5},{8,10},{9,11},{10,... | collective-permute-start | bytes 1572872 | tf_op jit(solution)/shard_map/rotation/ppermute | solution.py:285
  40.6 12.9 %copy-start.13 = (bf16[1,128,1024]{2,1,0:T(8,128)(2,1)S(1)}, bf16[1,128,1024]{2,1,0:T(8,128)(2,1)}, u32[]{:S(2)}) copy-start(bf16[1,128,1024]{2,1,0:T(8,128)(2,1)} %param.7) | copy-start | bytes 786436
  40.6 12.9 %copy-start.14 = (bf16[1,128,1024]{2,1,0:T(8,128)(2,1)S(1)}, bf16[1,128,1024]{2,1,0:T(8,128)(2,1)}, u32[]{:S(2)}) copy-start(bf16[1,128,1024]{2,1,0:T(8,128)(2,1)} %param.8) | copy-start | bytes 786436
  40.6 40.9 %all-to-all-start.1 = ((bf16[16,2,128,128]{3,2,1,0:T(8,128)(2,1)}), bf16[16,2,128,128]{3,2,1,0:T(8,128)(2,1)S(1)}, u32[]{:S(2)}, u32[]{:S(2)}) async-start(bf16[16,2,128,128]{3,2,1,0:T(8,128)(2,1)} %copy-done.1), calls=%async_computation.1 | async-start | bytes 2097152 | tf_op jit(solution)/shard_map/kv_gather/all_to_all | solution.py:288
  81.5 7.0 %copy-start.16 = (bf16[16,2,128,128]{3,2,1,0:T(8,128)(2,1)}, bf16[16,2,128,128]{3,2,1,0:T(8,128)(2,1)S(1)}, u32[]{:S(2)}) copy-start(bf16[16,2,128,128]{3,2,1,0:T(8,128)(2,1)S(1)} %all-to-all-done.1) | copy-start | bytes 3145732
  81.5 7.0 %collective-permute-start.3 = (bf16[32,128,128]{2,1,0:T(8,128)(2,1)S(1)}, bf16[32,128,128]{2,1,0:T(8,128)(2,1)}, u32[]{:S(2)}, u32[]{:S(2)}) collective-permute-start(bf16[32,128,128]{2,1,0:T(8,128)(2,1)S(1)} %bitcast.43), channel_id=1, source_target_pairs={{0,1},{1,0},{2,3},{3,2},{4,5},{5,4},{6,7},{7,6},{8,9},{9,8},{10,11... | collective-permute-start | bytes 3145736 | tf_op jit(solution)/shard_map/kv_gather/ppermute | solution.py:282
  104.2 4.8 %collective-permute-start.4 = (bf16[32,128,128]{2,1,0:T(8,128)(2,1)}, bf16[32,128,128]{2,1,0:T(8,128)(2,1)S(1)}, u32[]{:S(2)}, u32[]{:S(2)}) collective-permute-start(bf16[32,128,128]{2,1,0:T(8,128)(2,1)} %get-tuple-element.54), channel_id=1, source_target_pairs={{0,1},{1,0},{2,3},{3,2},{4,5},{5,4},{6,7},{7,6},{8,9},{9,8},{10,11... | collective-permute-start | bytes 3145736 | tf_op jit(solution)/shard_map/kv_reduce/ppermute | solution.py:282
  109.0 39.8 %copy-start.8 = (f32[2,128,128]{2,1,0:T(8,128)S(1)}, f32[2,128,128]{2,1,0:T(8,128)}, u32[]{:S(2)}) copy-start(f32[2,128,128]{2,1,0:T(8,128)} %get-tuple-element.60.cos_ref) | copy-start | bytes 393220
  111.6 42.4 %copy-start.3 = (bf16[2048,128]{1,0:T(8,128)(2,1)S(1)}, bf16[2048,128]{1,0:T(8,128)(2,1)}, u32[]{:S(2)}) copy-start(bf16[2048,128]{1,0:T(8,128)(2,1)} %copy-done.2) | copy-start | bytes 1572868
  111.6 42.4 %copy-start.5 = (bf16[2048,128]{1,0:T(8,128)(2,1)S(1)}, bf16[2048,128]{1,0:T(8,128)(2,1)}, u32[]{:S(2)}) copy-start(bf16[2048,128]{1,0:T(8,128)(2,1)} %copy-done.4) | copy-start | bytes 1572868
  111.6 37.2 %all-to-all-start.2 = ((bf16[16,2,128,128]{3,2,1,0:T(8,128)(2,1)}), bf16[16,2,128,128]{3,2,1,0:T(8,128)(2,1)S(1)}, u32[]{:S(2)}, u32[]{:S(2)}) async-start(bf16[16,2,128,128]{3,2,1,0:T(8,128)(2,1)} %bitcast.42), calls=%async_computation.2 | async-start | bytes 2097152 | tf_op jit(solution)/shard_map/kv_reduce/all_to_all | solution.py:288
  118.9 7.4 %collective-permute-start.6 = (bf16[4096,128]{1,0:T(8,128)(2,1)S(1)}, bf16[4096,128]{1,0:T(8,128)(2,1)}, u32[]{:S(2)}, u32[]{:S(2)}) collective-permute-start(bf16[4096,128]{1,0:T(8,128)(2,1)S(1)} %bitcast.32), channel_id=1, source_target_pairs={{0,1},{1,0},{2,3},{3,2},{4,5},{5,4},{6,7},{7,6},{8,9},{9,8},{10,11... | collective-permute-start | bytes 3145736 | tf_op jit(solution)/shard_map/kv_reduce/ppermute | solution.py:282
  121.5 4.0 %collective-permute-start.5 = (bf16[2048,128]{1,0:T(8,128)(2,1)}, bf16[2048,128]{1,0:T(8,128)(2,1)S(1)}, u32[]{:S(2)}, u32[]{:S(2)}) collective-permute-start(bf16[2048,128]{1,0:T(8,128)(2,1)} %collective-permute-done.2.rest_2_), channel_id=1, source_target_pairs={{0,1},{1,0},{2,3},{3,2},{4,5},{5,4},{6,7},{7,6},{8,9},{9,8},{10,11... | collective-permute-start | bytes 1572872 | tf_op jit(solution)/shard_map/kv_reduce/ppermute | solution.py:282
  148.9 5.0 %collective-permute-start.8 = (bf16[2,128,128]{2,1,0:T(8,128)(2,1)S(1)}, bf16[2,128,128]{2,1,0:T(8,128)(2,1)S(1)}, u32[]{:S(2)}, u32[]{:S(2)}) collective-permute-start(bf16[2,128,128]{2,1,0:T(8,128)(2,1)S(1)} %bitcast.37), channel_id=1, source_target_pairs={{0,2},{1,3},{2,0},{3,1},{4,6},{5,7},{6,4},{7,5},{8,10},{9,11},{10,... | collective-permute-start | bytes 196616 | tf_op jit(solution)/shard_map/weight_grad/ppermute | solution.py:285
  157.5 16.4 %all-to-all-start.3 = ((bf16[4,16,32,128]{3,2,1,0:T(8,128)(2,1)}), bf16[4,16,32,128]{3,2,1,0:T(8,128)(2,1)S(1)}, u32[]{:S(2)}, u32[]{:S(2)}) async-start(bf16[4,16,32,128]{3,2,1,0:T(8,128)(2,1)} %weight_share.1), calls=%async_computation.3 | async-start | bytes 1048576 | tf_op jit(solution)/shard_map/weight_grad/all_to_all | solution.py:288
  161.7 40.2 %collective-permute-start.7 = (bf16[128,128]{1,0:T(8,128)(2,1)S(1)}, bf16[128,128]{1,0:T(8,128)(2,1)S(1)}, u32[]{:S(2)}, u32[]{:S(2)}) collective-permute-start(bf16[128,128]{1,0:T(8,128)(2,1)S(1)} %select_bitcast_fusion), channel_id=1, source_target_pairs={{0,1},{1,0},{2,3},{3,2},{4,5},{5,4},{6,7},{7,6},{8,9},{9,8},{10,11... | collective-permute-start | bytes 98312 | tf_op jit(solution)/shard_map/input_grad/ppermute | solution.py:282
  174.7 18.8 %all-to-all-start.4 = ((bf16[16,32,128]{2,1,0:T(8,128)(2,1)}), bf16[16,32,128]{2,1,0:T(8,128)(2,1)S(1)}, u32[]{:S(2)}, u32[]{:S(2)}) async-start(bf16[16,32,128]{2,1,0:T(8,128)(2,1)} %bitcast.18), calls=%async_computation.4 | async-start | bytes 262144 | tf_op jit(solution)/shard_map/weight_grad/all_to_all | solution.py:288
  194.2 21.2 %all-to-all-start.5 = ((bf16[32,32,128]{2,1,0:T(8,128)(2,1)}), bf16[32,32,128]{2,1,0:T(8,128)(2,1)S(1)}, u32[]{:S(2)}, u32[]{:S(2)}) async-start(bf16[32,32,128]{2,1,0:T(8,128)(2,1)} %group_share.1), calls=%async_computation.5 | async-start | bytes 524288 | tf_op jit(solution)/shard_map/weight_grad/all_to_all | solution.py:288
  (10 other events, 8.2 us)

commit v6 on v5

--- a/solution.py
+++ b/solution.py
@@ -40,114 +40,145 @@
     return jnp.dot(left, right, preferred_element_type=jnp.float32)
 
 
-def attention_kernel(
-    order_ref, place_ref, core_ref, near_ref, far_ref, q_cols, g_cols, q_rows, g_rows,
-    dq_ref, near_grad_ref, far_grad_ref,
-    exp_store, prob_store, top_store, dq_cols,
-):
+def tile_of(plan_ref, core_ref, near_ref, far_ref, tile):
+    slots = [plan_ref[tile * TILE_BLOCKS + step] for step in range(TILE_BLOCKS)]
+    near = jnp.concatenate([near_ref[slot] for slot in slots], axis=0)
+    far = jnp.concatenate([far_ref[slot] for slot in slots], axis=0)
+    is_first = core_ref[0] == 0
+    return jnp.where(is_first, near, far), jnp.where(is_first, far, near)
+
+
+def tile_counts(plan_ref, blocks, group):
+    below = plan_ref[2 * blocks + 2 + group]
+    seen = below + 1 - group
+    return lax.div(below, TILE_BLOCKS), lax.div(seen + TILE_BLOCKS - 1, TILE_BLOCKS)
+
+
+def visible_in(plan_ref, blocks, group, tile, rows):
+    offsets = lax.broadcasted_iota(jnp.int32, (BLOCK, 1), 0)
+    key_at = jnp.concatenate(
+        [
+            plan_ref[blocks + tile * TILE_BLOCKS + step] * BLOCK + offsets
+            for step in range(TILE_BLOCKS)
+        ],
+        axis=0,
+    )
+    token = lax.rem(lax.broadcasted_iota(jnp.int32, (1, rows), 1), BLOCK)
+    return key_at <= plan_ref[2 * blocks + group] * BLOCK + token
+
+
+SCORE_SCALE = LOG2E / math.sqrt(HD)
+
+
+def totals_kernel(plan_ref, core_ref, near_ref, far_ref, *rest):
+    query_refs, out_ref = rest[:-1], rest[-1]
     blocks = near_ref.shape[0]
     rows = QH * BLOCK
     span = TILE_BLOCKS * BLOCK
-    score_scale = LOG2E / math.sqrt(HD)
-    place = place_ref[0]
-    is_first = core_ref[0] == 0
-    tiles = lax.div(place + TILE_BLOCKS, TILE_BLOCKS)
-
-    dq_cols[...] = jnp.zeros_like(dq_cols)
-
-    def gathered(tile):
-        slots = [order_ref[tile * TILE_BLOCKS + step] for step in range(TILE_BLOCKS)]
-        near = jnp.concatenate([near_ref[slot] for slot in slots], axis=0)
-        far = jnp.concatenate([far_ref[slot] for slot in slots], axis=0)
-        return jnp.where(is_first, near, far), jnp.where(is_first, far, near)
 
     def folded(values):
         return jnp.sum(values.reshape(span // 8, 8, rows), axis=0)
 
-    def forward(tile, sums, masked):
-        total, weighted, top = sums
-        keys, values = gathered(tile)
-        scores = dot(keys, q_cols[...]) * score_scale
-        if masked:
-            key_at = tile * span + lax.broadcasted_iota(jnp.int32, (span, rows), 0)
-            row_at = place * BLOCK + lax.rem(
-                lax.broadcasted_iota(jnp.int32, (span, rows), 1), BLOCK
-            )
-            visible = key_at <= row_at
-            scores = jnp.where(visible, scores, -jnp.inf)
-        highest = jnp.maximum(top, jnp.max(scores, axis=0, keepdims=True))
-        shrink = jnp.exp2(top - highest)
-        exponent = jnp.exp2(scores - highest)
-        prob_grad = dot(values, g_cols[...])
-        exp_store[tile] = exponent
-        prob_store[tile] = prob_grad
-        top_store[tile] = highest
-        total = total * shrink + folded(exponent)
-        weighted = weighted * shrink + folded(exponent * prob_grad)
-        return (total, weighted, highest)
-
-    empty = jnp.zeros((8, rows), jnp.float32)
-    start = forward(tiles - 1, (empty, empty, jnp.full((1, rows), -1e30, jnp.float32)), True)
-    total, weighted, top = lax.fori_loop(
-        0, tiles - 1, lambda tile, sums: forward(tile, sums, False), start
-    )
-    inverse = 1.0 / jnp.sum(total, axis=0, keepdims=True)
-    row_delta = jnp.sum(weighted, axis=0, keepdims=True) * inverse
-
-    @pl.loop(0, tiles)
+    for group in range(2):
+        q_cols, g_cols = query_refs[2 * group], query_refs[2 * group + 1]
+
+        def step(tile, sums, masked, q_cols=q_cols, g_cols=g_cols, group=group):
+            total, weighted, top = sums
+            keys, values = tile_of(plan_ref, core_ref, near_ref, far_ref, tile)
+            scores = dot(keys, q_cols[...]) * SCORE_SCALE
+            if masked:
+                visible = visible_in(plan_ref, blocks, group, tile, rows)
+                scores = jnp.where(visible, scores, -jnp.inf)
+            highest = jnp.maximum(top, jnp.max(scores, axis=0, keepdims=True))
+            shrink = jnp.exp2(top - highest)
+            exponent = jnp.exp2(scores - highest)
+            prob_grad = dot(values, g_cols[...])
+            total = total * shrink + folded(exponent)
+            weighted = weighted * shrink + folded(exponent * prob_grad)
+            return (total, weighted, highest)
+
+        full, tiles = tile_counts(plan_ref, blocks, group)
+        empty = jnp.zeros((8, rows), jnp.float32)
+        sums = (empty, empty, jnp.full((1, rows), -1e30, jnp.float32))
+        sums = lax.fori_loop(0, full, functools.partial(step, masked=False), sums)
+        total, weighted, top = lax.fori_loop(
+            full, tiles, functools.partial(step, masked=True), sums
+        )
+        out_ref[group, 0:1, :] = top
+        out_ref[group, 1:2, :] = jnp.sum(total, axis=0, keepdims=True)
+        out_ref[group, 2:3, :] = jnp.sum(weighted, axis=0, keepdims=True)
+
+
+def grads_kernel(plan_ref, core_ref, near_ref, far_ref, own_ref, other_ref, *rest):
+    query_refs, (dq_ref, dq_sent_ref, near_grad_ref, far_grad_ref) = rest[:8], rest[8:12]
+    key_sums, value_sums, dq_cols = rest[12:]
+    blocks = near_ref.shape[0]
+    rows = QH * BLOCK
+    is_first = core_ref[0] == 0
+    key_sums[...] = jnp.zeros_like(key_sums)
+    value_sums[...] = jnp.zeros_like(value_sums)
+
+    for group, out_ref in enumerate((dq_ref, dq_sent_ref)):
+        q_cols, g_cols, q_rows, g_rows = query_refs[4 * group : 4 * group + 4]
+        here, there = own_ref[group], other_ref[1 - group]
+        top = jnp.maximum(here[0:1], there[0:1])
+        here_part, there_part = jnp.exp2(here[0:1] - top), jnp.exp2(there[0:1] - top)
+        total = here[1:2] * here_part + there[1:2] * there_part
+        row_delta = (here[2:3] * here_part + there[2:3] * there_part) / total
+        log_total = top + jnp.log(total) * LOG2E
+        dq_cols[...] = jnp.zeros_like(dq_cols)
+
+        def step(
+            tile, carry, masked, group=group, q_cols=q_cols, g_cols=g_cols, q_rows=q_rows,
+            g_rows=g_rows, row_delta=row_delta, log_total=log_total,
+        ):
+            keys, values = tile_of(plan_ref, core_ref, near_ref, far_ref, tile)
+            probs = jnp.exp2(dot(keys, q_cols[...]) * SCORE_SCALE - log_total)
+            if masked:
+                probs = jnp.where(visible_in(plan_ref, blocks, group, tile, rows), probs, 0.0)
+            prob_grad = dot(values, g_cols[...])
+            score_grad = (probs * (prob_grad - row_delta)).astype(jnp.bfloat16)
+            value_sums[tile] += dot(probs.astype(jnp.bfloat16), g_rows[...])
+            key_sums[tile] += dot(score_grad, q_rows[...])
+            dq_cols[...] += dot(keys.T, score_grad)
+            return carry
+
+        full, tiles = tile_counts(plan_ref, blocks, group)
+        lax.fori_loop(0, full, functools.partial(step, masked=False), 0)
+        lax.fori_loop(full, tiles, functools.partial(step, masked=True), 0)
+        for head in range(QH):
+            part = pl.ds(head * HD, HD)
+            out_ref[:, part] = (dq_cols[:, part].T * (1.0 / math.sqrt(HD))).astype(out_ref.dtype)
+
+    @pl.loop(0, blocks // TILE_BLOCKS)
     def _(tile):
-        keys, _ = gathered(tile)
-        factor = jnp.exp2(top_store[tile] - top) * inverse
-        probs = exp_store[tile] * factor
-        score_grad = (probs * (prob_store[tile] - row_delta)).astype(jnp.bfloat16)
-        value_grad = dot(probs.astype(jnp.bfloat16), g_rows[...]).astype(jnp.bfloat16)
-        key_grad = dot(score_grad, q_rows[...]).astype(jnp.bfloat16)
-        dq_cols[...] += dot(keys.T, score_grad)
+        key_grad = key_sums[tile].astype(jnp.bfloat16)
+        value_grad = value_sums[tile].astype(jnp.bfloat16)
         near_grad = jnp.where(is_first, key_grad, value_grad)
         far_grad = jnp.where(is_first, value_grad, key_grad)
         for step in range(TILE_BLOCKS):
-            slot = order_ref[tile * TILE_BLOCKS + step]
+            slot = plan_ref[tile * TILE_BLOCKS + step]
             near_grad_ref[slot] = near_grad[step * BLOCK : (step + 1) * BLOCK]
             far_grad_ref[slot] = far_grad[step * BLOCK : (step + 1) * BLOCK]
 
-    @pl.loop(tiles * TILE_BLOCKS, blocks)
-    def _(place_at):
-        slot = order_ref[place_at]
-        near_grad_ref[slot] = jnp.zeros((BLOCK, HD), jnp.bfloat16)
-        far_grad_ref[slot] = jnp.zeros((BLOCK, HD), jnp.bfloat16)
-
+
+def copies_kernel(core_ref, weight_ref, out_ref):
+    start = pl.multiple_of(core_ref[0] * HD, HD)
+    half = weight_ref[:, pl.ds(start, HD)]
+    for copy in range(out_ref.shape[0]):
+        out_ref[copy] = half
+
+
+def query_kernel(q_ref, g_ref, q_cols, g_cols, q_rows, g_rows):
     for head in range(QH):
         part = pl.ds(head * HD, HD)
-        dq_ref[:, part] = (dq_cols[:, part].T * (1.0 / math.sqrt(HD))).astype(jnp.bfloat16)
-
-
-def attention_backward(order, place, core, near, far, columns_and_rows):
-    rows = columns_and_rows[0].shape[1]
-    tiles = near.shape[0] // TILE_BLOCKS
-    span = TILE_BLOCKS * BLOCK
-    smem = pl.BlockSpec(memory_space=pltpu.SMEM)
-    vmem = pl.BlockSpec(memory_space=pltpu.VMEM)
-    return pl.pallas_call(
-        attention_kernel,
-        out_shape=(
-            jax.ShapeDtypeStruct((rows // QH, QH * HD), jnp.bfloat16),
-            jax.ShapeDtypeStruct(near.shape, jnp.bfloat16),
-            jax.ShapeDtypeStruct(far.shape, jnp.bfloat16),
-        ),
-        in_specs=[smem] * 3 + [vmem] * 6,
-        out_specs=(vmem, vmem, vmem),
-        scratch_shapes=[
-            pltpu.VMEM((tiles, span, rows), jnp.float32),
-            pltpu.VMEM((tiles, span, rows), jnp.float32),
-            pltpu.VMEM((tiles, 1, rows), jnp.float32),
-            pltpu.VMEM((HD, rows), jnp.float32),
-        ],
-        compiler_params=pltpu.CompilerParams(vmem_limit_bytes=56 * 1024 * 1024),
-        name="attention_backward",
-    )(order, place, core, near, far, *columns_and_rows)
-
-
-def local_call(kernel, shapes, scalars, arrays, name, scratch=()):
+        q_cols[:, part] = q_ref[:, part].T
+        g_cols[:, part] = g_ref[:, part].T
+        q_rows[part, :] = q_ref[:, part]
+        g_rows[part, :] = g_ref[:, part]
+
+
+def local_call(kernel, shapes, scalars, arrays, name, scratch=(), limit=32):
     smem = pl.BlockSpec(memory_space=pltpu.SMEM)
     vmem = pl.BlockSpec(memory_space=pltpu.VMEM)
     return pl.pallas_call(
@@ -156,25 +187,9 @@
         in_specs=[smem] * len(scalars) + [vmem] * len(arrays),
         out_specs=jax.tree.map(lambda _: vmem, shapes),
         scratch_shapes=scratch,
-        compiler_params=pltpu.CompilerParams(vmem_limit_bytes=32 * 1024 * 1024),
+        compiler_params=pltpu.CompilerParams(vmem_limit_bytes=limit * 1024 * 1024),
         name=name,
     )(*scalars, *arrays)
-
-
-def copies_kernel(core_ref, weight_ref, out_ref):
-    start = pl.multiple_of(core_ref[0] * HD, HD)
-    half = weight_ref[:, pl.ds(start, HD)]
-    for copy in range(out_ref.shape[0]):
-        out_ref[copy] = half
-
-
-def query_kernel(q_ref, g_ref, q_cols, g_cols, q_rows, g_rows):
-    for head in range(QH):
-        part = pl.ds(head * HD, HD)
-        q_cols[:, part] = q_ref[:, part].T
-        g_cols[:, part] = g_ref[:, part].T
-        q_rows[part, :] = q_ref[:, part]
-        g_rows[part, :] = g_ref[:, part]
 
 
 def project_kernel(core_ref, levels_ref, own_ref, far_ref, weight_ref, cos_ref, sin_ref, out_ref):
@@ -274,13 +289,35 @@
         for start in range(2)
         for side in range(4)
     ]
-    same_core = [[2 * chip + side for chip in range(half_count)] for side in range(2)]
+    column_groups = [
+        [start * half_count + 2 * column + side for column in range(columns)]
+        for start in range(2)
+        for side in range(2)
+    ]
+    run = math.gcd(dp_count, 4)
+    runs = [[start + step for step in range(run)] for start in range(0, dp_count, run)]
+    strides = [[start + step for step in range(0, dp_count, run)] for start in range(run)]
     swap = [(source, source ^ 1) for source in range(seq_count)]
+    cross = [(source, (source + half_count) % seq_count) for source in range(seq_count)]
     beside = [(source, source ^ 2) for source in range(seq_count)]
 
     def swapped(value):
         return lax.ppermute(value, "seq", swap)
 
+    def crossed(value):
+        return lax.ppermute(value, "seq", cross)
+
+    def moved(value, steps):
+        pairs = []
+        for group in range(dp_count):
+            for member in range(seq_count):
+                high = member // half_count
+                place_y = (high * run + group % run + steps) % (2 * run)
+                target_group = group // run * run + place_y % run
+                target = place_y // run * half_count + member % half_count
+                pairs.append((group * seq_count + member, target_group * seq_count + target))
+        return lax.ppermute(value, ("dp", "seq"), pairs)
+
     def passed(value):
         return lax.ppermute(value, "seq", beside)
 
@@ -289,11 +326,21 @@
 
     x_rows = hidden_in[0]
     places = block_pos[0]
-    place = lax.dynamic_slice_in_dim(places, self_index, 1)
-    slots = jnp.arange(seq_count, dtype=jnp.int32)
-    order = jnp.sum(
-        jnp.where(places[None, :] == slots[:, None], slots[None, :], 0), axis=1
-    ).astype(jnp.int32)
+    half_places = lax.dynamic_slice_in_dim(
+        places, lax.div(self_index, half_count) * half_count, half_count
+    )
+    own_place = lax.dynamic_slice_in_dim(places, self_index, 1)
+    cross_place = lax.dynamic_slice_in_dim(
+        places, lax.rem(self_index + half_count, seq_count), 1
+    )
+    slots = jnp.arange(half_count, dtype=jnp.int32)
+    below = (half_places[None, :] < half_places[:, None]).astype(jnp.int32)
+    ranked = jnp.sum(below, axis=1)[None, :] == slots[:, None]
+    order = jnp.sum(jnp.where(ranked, slots[None, :], 0), axis=1)
+    ranked_places = jnp.sum(jnp.where(ranked, half_places[None, :], 0), axis=1)
+    group_places = jnp.concatenate([own_place, cross_place])
+    seen = jnp.sum((half_places[None, :] < group_places[:, None]).astype(jnp.int32), axis=1)
+    plan = jnp.concatenate([order, ranked_places, group_places, seen]).astype(jnp.int32)
 
     with jax.named_scope("rotation"):
         pair_places = lax.dynamic_slice_in_dim(places, self_index - core_index, 2)
@@ -318,56 +365,93 @@
     with jax.named_scope("weight_gather"):
         copies = local_call(
             copies_kernel,
-            jax.ShapeDtypeStruct((dp_count, kv_weight.shape[0], HD), kv_weight.dtype),
+            jax.ShapeDtypeStruct((run, kv_weight.shape[0], HD), kv_weight.dtype),
             (core,),
             (kv_weight,),
             "weight_copies",
         )
-        near_weight = exchanged(copies, "dp").reshape(width, HD)
+        run_weight = exchanged(copies, "dp", runs)
+        run_weight, q_start, g_start = lax.optimization_barrier(
+            (run_weight, queries[0], out_grad[0])
+        )
+        q_middle, g_middle = moved(q_start, run // 2), moved(g_start, -(run // 2))
+        copies = jnp.broadcast_to(run_weight[None], (dp_count // run, *run_weight.shape))
+        copies = lax.optimization_barrier(copies)
+        near_weight = exchanged(copies, "dp", strides).reshape(width, HD)
         (
-            near_weight, order, cosine, sine_part, back_cosine, back_sine, levels, x_far,
+            near_weight, q_middle, g_middle, plan, cosine, sine_part, back_cosine, back_sine, levels, x_far,
             own_half, next_half, far_half,
         ) = lax.optimization_barrier(
             (
-                near_weight, order, cosine, sine_part, back_cosine, back_sine, levels, x_far,
+                near_weight, q_middle, g_middle, plan, cosine, sine_part, back_cosine, back_sine, levels, x_far,
                 own_half, next_half, far_half,
             )
         )
     with jax.named_scope("projection"):
         stacked = local_call(
             project_kernel,
-            jax.ShapeDtypeStruct((half_count, 2, tokens, HD), jnp.bfloat16),
+            jax.ShapeDtypeStruct((columns, 2, tokens, HD), jnp.bfloat16),
             (core, levels),
             (x_rows, x_far, near_weight, cosine, sine_part),
             "projection",
         )
     with jax.named_scope("kv_gather"):
-        near = exchanged(stacked, "seq", same_core).reshape(seq_count, tokens, HD)
+        near = exchanged(stacked, "seq", column_groups).reshape(half_count, tokens, HD)
+        q_cross, g_cross = moved(q_middle, run // 2), moved(g_middle, -(run // 2))
         columns_shape = jax.ShapeDtypeStruct((HD, QH * tokens), jnp.bfloat16)
         rows_shape = jax.ShapeDtypeStruct((QH * tokens, HD), jnp.bfloat16)
-        columns_and_rows = local_call(
-            query_kernel,
-            (columns_shape, columns_shape, rows_shape, rows_shape),
-            (),
-            (queries[0], out_grad[0]),
-            "query_columns",
-        )
-        near, *columns_and_rows = lax.optimization_barrier((near, *columns_and_rows))
+        query_shapes = (columns_shape, columns_shape, rows_shape, rows_shape)
+        own_forms = local_call(
+            query_kernel, query_shapes, (), (queries[0], out_grad[0]), "own_query_forms"
+        )
+        cross_forms = local_call(
+            query_kernel, query_shapes, (), (q_cross, g_cross), "cross_query_forms"
+        )
+        near, own_forms, cross_forms = lax.optimization_barrier((near, own_forms, cross_forms))
         far = swapped(near)
     with jax.named_scope("attention"):
-        query_grad, near_grad, far_grad = attention_backward(
-            order, place, core, near, far, columns_and_rows
+        totals = local_call(
+            totals_kernel,
+            jax.ShapeDtypeStruct((2, 3, QH * tokens), jnp.float32),
+            (plan, core),
+            (near, far, *own_forms[:2], *cross_forms[:2]),
+            "attention_totals",
+            (),
+            48,
+        )
+        sum_tiles = (half_count // TILE_BLOCKS, TILE_BLOCKS * BLOCK, HD)
+        dq_own, dq_sent, near_grad, far_grad = local_call(
+            grads_kernel,
+            (
+                jax.ShapeDtypeStruct((tokens, QH * HD), jnp.float32),
+                jax.ShapeDtypeStruct((tokens, QH * HD), jnp.bfloat16),
+                jax.ShapeDtypeStruct(near.shape, jnp.bfloat16),
+                jax.ShapeDtypeStruct(near.shape, jnp.bfloat16),
+            ),
+            (plan, core),
+            (near, far, totals, crossed(totals), *own_forms, *cross_forms),
+            "attention_grads",
+            (
+                pltpu.VMEM(sum_tiles, jnp.float32),
+                pltpu.VMEM(sum_tiles, jnp.float32),
+                pltpu.VMEM((HD, QH * tokens), jnp.float32),
+            ),
+            48,
         )
     with jax.named_scope("kv_reduce"):
         pair = near_grad.astype(jnp.float32) + swapped(far_grad).astype(jnp.float32)
-        pair = pair.astype(jnp.bfloat16).reshape(half_count, 2, tokens, HD)
-        pair, next_half, near_weight = lax.optimization_barrier((pair, next_half, near_weight))
-        arrived = exchanged(pair, "seq", same_core)
+        pair = pair.astype(jnp.bfloat16).reshape(columns, 2, tokens, HD)
+        pair, next_half, near_weight, dq_sent = lax.optimization_barrier(
+            (pair, next_half, near_weight, dq_sent)
+        )
+        arrived = exchanged(pair, "seq", column_groups)
         next_far_half = swapped(next_half)
         far_weight = swapped(near_weight)
         arrived, next_far_half, far_weight = lax.optimization_barrier(
             (arrived, next_far_half, far_weight)
         )
+    with jax.named_scope("query_grad"):
+        query_grad = (dq_own + crossed(dq_sent).astype(jnp.float32)).astype(jnp.bfloat16)
     with jax.named_scope("projection_grad"):
         settled = local_call(
             settle_kernel,

time: 219 us -> 230 us (1.050)
  starting transfers between devices: 78.1 us -> 118 us
  waiting for transfers between devices: 92.3 us -> 54.1 us
  local copies, waits for them, and re-layouts: 8.9 us -> 17.2 us
  other arithmetic: 5.54 us -> 8.84 us
  Pallas kernels: 25.3 us -> 22.8 us
    all_to_all x6 -> x7, waiting for transfers between devices: 73.2 us -> 32.4 us  [exchanged(): return lax.all_to_all(value, axis, 0, 0, axis_index_groups=groups)]
    ppermute x0 -> x6, starting transfers between devices: none -> 28.4 us  [the longest x4 14.8 us: moved(): return lax.ppermute(value, ('dp', 'seq'), pairs)]
    pallas_call x1 -> x0, Pallas kernels: 15.7 us -> none  [attention_backward(): pl.pallas_call(attention_kernel, out_shape=(jax.ShapeDtypeStruct((rows //...]
    ppermute x0 -> x6, waiting for transfers between devices: none -> 13.8 us  [the longest x2 8.84 us: crossed(): return lax.ppermute(value, 'seq', cross)]
    pallas_call x10 -> x13, Pallas kernels: 9.57 us -> 22.8 us  [local_call(): pl.pallas_call(kernel, out_shape=shapes, in_specs=[smem] * len(scalars) +...]
    ppermute x7, starting transfers between devices: 22 us -> 34.5 us  [swapped(): return lax.ppermute(value, 'seq', swap)]
    ppermute x2, waiting for transfers between devices: 12.3 us -> 3.08 us  [passed(): return lax.ppermute(value, 'seq', beside)]
    unnamed x38 -> x46, local copies, waits for them, and re-layouts: 8.25 us -> 11.9 us
  transfers between devices with their start and end apart: 15 -> 22, of which waited for: 11 -> 12; matrix products, arithmetic and copies ran while one was open for 4% -> 8% of each run, Pallas kernels for 1% -> 2%
where the time goes in v6:
time: 230 us; the launch traced here: 227 us
  starting transfers between devices  118 us (51%)
  waiting for transfers between devices  54.1 us (24%)
  Pallas kernels  22.8 us (10%)
  local copies, waits for them, and re-layouts  17.2 us (7%)
  other arithmetic  8.84 us (4%)
  matrix products  5.11 us (2%)
    all_to_all x7, starting transfers between devices, exchanged(): return lax.all_to_all(value, axis, 0, 0, axis_index_groups=groups)  50.9 us
    ppermute x7, starting transfers between devices, swapped(): return lax.ppermute(value, 'seq', swap)  34.5 us
    all_to_all x7, waiting for transfers between devices, exchanged(): return lax.all_to_all(value, axis, 0, 0, axis_index_groups=groups)  32.4 us
    pallas_call x13, Pallas kernels, local_call(): pl.pallas_call(kernel, out_shape=shapes, in_specs=[smem] * len(scalars) +...  22.8 us
    ppermute x4, starting transfers between devices, moved(): return lax.ppermute(value, ('dp', 'seq'), pairs)  14.8 us
    ppermute x2, starting transfers between devices, crossed(): return lax.ppermute(value, 'seq', cross)  13.6 us
    unnamed x46, local copies, waits for them, and re-layouts  11.9 us
    ppermute x2, waiting for transfers between devices, crossed(): return lax.ppermute(value, 'seq', cross)  8.84 us
  transfers between devices with their start and end apart: 22, of which 12 were waited for; matrix products, arithmetic and copies ran while one was open for 8% of the time, Pallas kernels for 2%

profile of v6, /device:TPU:1, one launch (start us, length us, event | category | flops | bytes accessed | tf_op | source)
XLA Modules:
  0.0 226.8 jit_solution(15147328349028589676)
XLA Ops:
  0.6 8.8 %collective-permute-start.2 = (s32[1,2]{1,0:T(1,128)}, s32[1,2]{1,0:T(1,128)}, u32[]{:S(2)}, u32[]{:S(2)}) collective-permute-start(s32[1,2]{1,0:T(1,128)} %bitcast.51), channel_id=1, source_target_pairs={{0,1},{1,0},{2,3},{3,2},{4,5},{5,4},{6,7},{7,6},{8,9},{9,8},{10,11... | collective-permute-start | bytes 32 | tf_op jit(solution)/shard_map/rotation/ppermute | solution.py:305
  11.1 3.4 %all-to-all-start = ((bf16[4,256,128]{2,1,0:T(8,128)(2,1)}), bf16[4,256,128]{2,1,0:T(8,128)(2,1)S(1)}, u32[]{:S(2)}, u32[]{:S(2)}) async-start(bf16[4,256,128]{2,1,0:T(8,128)(2,1)} %weight_copies.1), calls=%async_computation | async-start | bytes 524288 | tf_op jit(solution)/shard_map/weight_gather/all_to_all | solution.py:325
  28.6 3.6 %all-to-all-start.1 = ((bf16[4,4,256,128]{3,2,1,0:T(8,128)(2,1)}), bf16[4,4,256,128]{3,2,1,0:T(8,128)(2,1)S(1)}, u32[]{:S(2)}, u32[]{:S(2)}) async-start(bf16[4,4,256,128]{3,2,1,0:T(8,128)(2,1)} %broadcast_in_dim.59), calls=%async_computation.1 | async-start | bytes 2097152 | tf_op jit(solution)/shard_map/weight_gather/all_to_all | solution.py:325
  33.5 4.5 %collective-permute-start = (bf16[128,1024]{1,0:T(8,128)(2,1)}, bf16[128,1024]{1,0:T(8,128)(2,1)}, u32[]{:S(2)}, u32[]{:S(2)}) collective-permute-start(bf16[128,1024]{1,0:T(8,128)(2,1)} %bitcast.46), channel_id=1, source_target_pairs={{0,64},{1,65},{2,66},{3,67},{4,68},{5,69},{6,70},{7,71},{8,72},{9,... | collective-permute-start | bytes 786440 | tf_op jit(solution)/shard_map/weight_gather/ppermute | solution.py:319
  45.5 3.9 %collective-permute-done.1 = bf16[128,1024]{1,0:T(8,128)(2,1)} collective-permute-done((bf16[128,1024]{1,0:T(8,128)(2,1)}, bf16[128,1024]{1,0:T(8,128)(2,1)}, u32[]{:S(2)}, u32[]{:S(2)}) %collective-permute-start.1) | collective-permute-done | bytes 262176 | tf_op jit(solution)/shard_map/weight_gather/ppermute | solution.py:319
  52.1 10.6 %all-to-all-start.2 = ((bf16[8,2,128,128]{3,2,1,0:T(8,128)(2,1)}), bf16[8,2,128,128]{3,2,1,0:T(8,128)(2,1)S(1)}, u32[]{:S(2)}, u32[]{:S(2)}) async-start(bf16[8,2,128,128]{3,2,1,0:T(8,128)(2,1)} %copy-done.2), calls=%async_computation.2 | async-start | bytes 1048576 | tf_op jit(solution)/shard_map/kv_gather/all_to_all | solution.py:325
  65.0 5.1 %collective-permute-start.6 = (bf16[128,1024]{1,0:T(8,128)(2,1)}, bf16[128,1024]{1,0:T(8,128)(2,1)S(1)}, u32[]{:S(2)}, u32[]{:S(2)}) collective-permute-start(bf16[128,1024]{1,0:T(8,128)(2,1)} %collective-permute-done.1), channel_id=1, source_target_pairs={{0,80},{1,81},{2,82},{3,83},{4,84},{5,85},{6,86},{7,87},{8,88},{9,... | collective-permute-start | bytes 786440 | tf_op jit(solution)/shard_map/kv_gather/ppermute | solution.py:319
  74.3 4.4 %all-to-all-done.2 = bf16[8,2,128,128]{3,2,1,0:T(8,128)(2,1)S(1)} async-done(((bf16[8,2,128,128]{3,2,1,0:T(8,128)(2,1)}), bf16[8,2,128,128]{3,2,1,0:T(8,128)(2,1)S(1)}, u32[]{:S(2)}, u32[]{:S(2)}) %all-to-all-start.2) | async-done | bytes 524320 | tf_op jit(solution)/shard_map/kv_gather/all_to_all | solution.py:325
  78.7 4.5 %collective-permute-start.7 = (bf16[16,128,128]{2,1,0:T(8,128)(2,1)S(1)}, bf16[16,128,128]{2,1,0:T(8,128)(2,1)S(1)}, u32[]{:S(2)}, u32[]{:S(2)}) collective-permute-start(bf16[16,128,128]{2,1,0:T(8,128)(2,1)S(1)} %bitcast.37), channel_id=1, source_target_pairs={{0,1},{1,0},{2,3},{3,2},{4,5},{5,4},{6,7},{7,6},{8,9},{9,8},{10,11... | collective-permute-start | bytes 1572872 | tf_op jit(solution)/shard_map/kv_gather/ppermute | solution.py:305
  84.8 4.8 %attention_totals.1.own_ref = f32[2,3,1024]{2,1,0:T(4,128)S(1)} custom-call(s32[36]{0:T(128)S(1)} %concatenate.17.plan_ref, s32[1]{0:T(128)} %bitcast.core_ref, bf16[16,128,128]{2,1,0:T(8,128)(2,1)S(1)} %bitcast.38, bf16[16,128,128]{2,1,0:T(8,128)(2,1)S(1)} %collective-permute-done.7.far_ref, bf16[128,1024]{1,0:T(8,128)(2,1)S(1)} %get-tuple-element.72.rest_0_, ...), custom_call_target="tpu_custom_call" | custom-call | tf_op jit(solution)/shard_map/attention/attention_totals/pallas_call | solution.py:184
  89.5 7.5 %collective-permute-start.8 = (f32[2,3,1024]{2,1,0:T(4,128)S(1)}, f32[2,3,1024]{2,1,0:T(4,128)S(1)}, u32[]{:S(2)}, u32[]{:S(2)}) collective-permute-start(f32[2,3,1024]{2,1,0:T(4,128)S(1)} %attention_totals.1.own_ref), channel_id=1, source_target_pairs={{0,16},{1,17},{2,18},{3,19},{4,20},{5,21},{6,22},{7,23},{8,24},{9,... | collective-permute-start | bytes 73736 | tf_op jit(solution)/shard_map/attention/ppermute | solution.py:308
  100.2 8.7 %attention_grads.1 = (f32[128,1024]{1,0:T(8,128)S(1)}, bf16[128,1024]{1,0:T(8,128)(2,1)S(1)}, bf16[16,128,128]{2,1,0:T(8,128)(2,1)S(1)}, bf16[16,128,128]{2,1,0:T(8,128)(2,1)S(1)}) custom-call(s32[36]{0:T(128)S(1)} %concatenate.17.plan_ref, s32[1]{0:T(128)} %bitcast.core_ref, bf16[16,128,128]{2,1,0:T(8,128)(2,1)S(1)} %bitcast.39, ...), custom_call_target="tpu_custom_call" | custom-call | tf_op jit(solution)/shard_map/attention/attention_grads/pallas_call | solution.py:184
  109.0 10.1 %collective-permute-start.9 = (bf16[16,128,128]{2,1,0:T(8,128)(2,1)S(1)}, bf16[16,128,128]{2,1,0:T(8,128)(2,1)S(1)}, u32[]{:S(2)}, u32[]{:S(2)}) collective-permute-start(bf16[16,128,128]{2,1,0:T(8,128)(2,1)S(1)} %get-tuple-element.82), channel_id=1, source_target_pairs={{0,1},{1,0},{2,3},{3,2},{4,5},{5,4},{6,7},{7,6},{8,9},{9,8},{10,11... | collective-permute-start | bytes 1572872 | tf_op jit(solution)/shard_map/kv_reduce/ppermute | solution.py:305
  123.8 6.0 %all-to-all-start.3 = ((bf16[8,2,128,128]{3,2,1,0:T(8,128)(2,1)}), bf16[8,2,128,128]{3,2,1,0:T(8,128)(2,1)S(1)}, u32[]{:S(2)}, u32[]{:S(2)}) async-start(bf16[8,2,128,128]{3,2,1,0:T(8,128)(2,1)} %bitcast.50), calls=%async_computation.3 | async-start | bytes 1048576 | tf_op jit(solution)/shard_map/kv_reduce/all_to_all | solution.py:325
  134.7 13.1 %all-to-all-done.3.arrived_ref = bf16[8,2,128,128]{3,2,1,0:T(8,128)(2,1)S(1)} async-done(((bf16[8,2,128,128]{3,2,1,0:T(8,128)(2,1)}), bf16[8,2,128,128]{3,2,1,0:T(8,128)(2,1)S(1)}, u32[]{:S(2)}, u32[]{:S(2)}) %all-to-all-start.3) | async-done | bytes 524320 | tf_op jit(solution)/shard_map/kv_reduce/all_to_all | solution.py:325
  157.6 3.5 %all-to-all-start.4 = ((bf16[4,16,32,128]{3,2,1,0:T(8,128)(2,1)}), bf16[4,16,32,128]{3,2,1,0:T(8,128)(2,1)S(1)}, u32[]{:S(2)}, u32[]{:S(2)}) async-start(bf16[4,16,32,128]{3,2,1,0:T(8,128)(2,1)} %weight_share.1), calls=%async_computation.4 | async-start | bytes 1048576 | tf_op jit(solution)/shard_map/weight_grad/all_to_all | solution.py:325
  161.1 6.1 %collective-permute-start.10 = (bf16[128,1024]{1,0:T(8,128)(2,1)S(1)}, bf16[128,1024]{1,0:T(8,128)(2,1)S(1)}, u32[]{:S(2)}, u32[]{:S(2)}) collective-permute-start(bf16[128,1024]{1,0:T(8,128)(2,1)S(1)} %copy-done.20), channel_id=1, source_target_pairs={{0,16},{1,17},{2,18},{3,19},{4,20},{5,21},{6,22},{7,23},{8,24},{9,... | collective-permute-start | bytes 786440 | tf_op jit(solution)/shard_map/query_grad/ppermute | solution.py:308
  167.2 7.6 %collective-permute-done.10 = bf16[128,1024]{1,0:T(8,128)(2,1)S(1)} collective-permute-done((bf16[128,1024]{1,0:T(8,128)(2,1)S(1)}, bf16[128,1024]{1,0:T(8,128)(2,1)S(1)}, u32[]{:S(2)}, u32[]{:S(2)}) %collective-permute-start.10) | collective-permute-done | bytes 262176 | tf_op jit(solution)/shard_map/query_grad/ppermute | solution.py:308
  175.6 4.6 %collective-permute-start.13 = (bf16[128,128]{1,0:T(8,128)(2,1)S(1)}, bf16[128,128]{1,0:T(8,128)(2,1)S(1)}, u32[]{:S(2)}, u32[]{:S(2)}) collective-permute-start(bf16[128,128]{1,0:T(8,128)(2,1)S(1)} %select_bitcast_fusion), channel_id=1, source_target_pairs={{0,1},{1,0},{2,3},{3,2},{4,5},{5,4},{6,7},{7,6},{8,9},{9,8},{10,11... | collective-permute-start | bytes 98312 | tf_op jit(solution)/shard_map/input_grad/ppermute | solution.py:305
  180.9 11.5 %all-to-all-start.5 = ((bf16[16,32,128]{2,1,0:T(8,128)(2,1)}), bf16[16,32,128]{2,1,0:T(8,128)(2,1)S(1)}, u32[]{:S(2)}, u32[]{:S(2)}) async-start(bf16[16,32,128]{2,1,0:T(8,128)(2,1)} %bitcast.19), calls=%async_computation.5 | async-start | bytes 262144 | tf_op jit(solution)/shard_map/weight_grad/all_to_all | solution.py:325
  194.2 5.5 %all-to-all-done.5.parts_ref = bf16[16,32,128]{2,1,0:T(8,128)(2,1)S(1)} async-done(((bf16[16,32,128]{2,1,0:T(8,128)(2,1)}), bf16[16,32,128]{2,1,0:T(8,128)(2,1)S(1)}, u32[]{:S(2)}, u32[]{:S(2)}) %all-to-all-start.5) | async-done | bytes 131104 | tf_op jit(solution)/shard_map/weight_grad/all_to_all | solution.py:325
  200.4 12.2 %all-to-all-start.6 = ((bf16[32,32,128]{2,1,0:T(8,128)(2,1)}), bf16[32,32,128]{2,1,0:T(8,128)(2,1)S(1)}, u32[]{:S(2)}, u32[]{:S(2)}) async-start(bf16[32,32,128]{2,1,0:T(8,128)(2,1)} %group_share.1), calls=%async_computation.6 | async-start | bytes 524288 | tf_op jit(solution)/shard_map/weight_grad/all_to_all | solution.py:325
  213.3 3.3 %fusion.1 = bf16[1,128,4096]{2,1,0:T(8,128)(2,1)} fusion(f32[128,4096]{1,0:T(8,128)} %fusion.6, bf16[128,128]{1,0:T(8,128)(2,1)S(1)} %collective-permute-done.13, bf16[4096,128]{1,0:T(8,128)(2,1)} %collective-permute-done.12), kind=kOutput, calls=%fused_computation.2 | convolution fusion | flops 135266304 | bytes 4227072 | tf_op jit(solution)/shard_map/input_grad/dot_general | solution.py:34
  216.6 9.4 %all-to-all-done.6 = bf16[32,32,128]{2,1,0:T(8,128)(2,1)S(1)} async-done(((bf16[32,32,128]{2,1,0:T(8,128)(2,1)}), bf16[32,32,128]{2,1,0:T(8,128)(2,1)S(1)}, u32[]{:S(2)}, u32[]{:S(2)}) %all-to-all-start.6) | async-done | bytes 262176 | tf_op jit(solution)/shard_map/weight_grad/all_to_all | solution.py:325
  (101 shorter events, 63.0 us)
Async XLA Ops:
  0.6 43.1 %collective-permute-start.2 = (s32[1,2]{1,0:T(1,128)}, s32[1,2]{1,0:T(1,128)}, u32[]{:S(2)}, u32[]{:S(2)}) collective-permute-start(s32[1,2]{1,0:T(1,128)} %bitcast.51), channel_id=1, source_target_pairs={{0,1},{1,0},{2,3},{3,2},{4,5},{5,4},{6,7},{7,6},{8,9},{9,8},{10,11... | collective-permute-start | bytes 32 | tf_op jit(solution)/shard_map/rotation/ppermute | solution.py:305
  11.1 16.3 %all-to-all-start = ((bf16[4,256,128]{2,1,0:T(8,128)(2,1)}), bf16[4,256,128]{2,1,0:T(8,128)(2,1)S(1)}, u32[]{:S(2)}, u32[]{:S(2)}) async-start(bf16[4,256,128]{2,1,0:T(8,128)(2,1)} %weight_copies.1), calls=%async_computation | async-start | bytes 524288 | tf_op jit(solution)/shard_map/weight_gather/all_to_all | solution.py:325
  14.5 30.0 %collective-permute-start.3 = (bf16[128,4096]{1,0:T(8,128)(2,1)}, bf16[128,4096]{1,0:T(8,128)(2,1)S(1)}, u32[]{:S(2)}, u32[]{:S(2)}) collective-permute-start(bf16[128,4096]{1,0:T(8,128)(2,1)} %bitcast.40), channel_id=1, source_target_pairs={{0,1},{1,0},{2,3},{3,2},{4,5},{5,4},{6,7},{7,6},{8,9},{9,8},{10,11... | collective-permute-start | bytes 3145736 | tf_op jit(solution)/shard_map/rotation/ppermute | solution.py:305
  19.6 25.9 %collective-permute-start.4 = (bf16[2048,128]{1,0:T(8,128)(2,1)}, bf16[2048,128]{1,0:T(8,128)(2,1)}, u32[]{:S(2)}, u32[]{:S(2)}) collective-permute-start(bf16[2048,128]{1,0:T(8,128)(2,1)} %get-tuple-element.54), channel_id=1, source_target_pairs={{0,2},{1,3},{2,0},{3,1},{4,6},{5,7},{6,4},{7,5},{8,10},{9,11},{10,... | collective-permute-start | bytes 1572872 | tf_op jit(solution)/shard_map/rotation/ppermute | solution.py:322
  28.6 20.9 %all-to-all-start.1 = ((bf16[4,4,256,128]{3,2,1,0:T(8,128)(2,1)}), bf16[4,4,256,128]{3,2,1,0:T(8,128)(2,1)S(1)}, u32[]{:S(2)}, u32[]{:S(2)}) async-start(bf16[4,4,256,128]{3,2,1,0:T(8,128)(2,1)} %broadcast_in_dim.59), calls=%async_computation.1 | async-start | bytes 2097152 | tf_op jit(solution)/shard_map/weight_gather/all_to_all | solution.py:325
  33.5 12.0 %collective-permute-start = (bf16[128,1024]{1,0:T(8,128)(2,1)}, bf16[128,1024]{1,0:T(8,128)(2,1)}, u32[]{:S(2)}, u32[]{:S(2)}) collective-permute-start(bf16[128,1024]{1,0:T(8,128)(2,1)} %bitcast.46), channel_id=1, source_target_pairs={{0,64},{1,65},{2,66},{3,67},{4,68},{5,69},{6,70},{7,71},{8,72},{9,... | collective-permute-start | bytes 786440 | tf_op jit(solution)/shard_map/weight_gather/ppermute | solution.py:319
  38.0 11.4 %collective-permute-start.1 = (bf16[128,1024]{1,0:T(8,128)(2,1)}, bf16[128,1024]{1,0:T(8,128)(2,1)}, u32[]{:S(2)}, u32[]{:S(2)}) collective-permute-start(bf16[128,1024]{1,0:T(8,128)(2,1)} %bitcast.48), channel_id=1, source_target_pairs={{0,80},{1,81},{2,82},{3,83},{4,84},{5,85},{6,86},{7,87},{8,88},{9,... | collective-permute-start | bytes 786440 | tf_op jit(solution)/shard_map/weight_gather/ppermute | solution.py:319
  52.1 26.6 %all-to-all-start.2 = ((bf16[8,2,128,128]{3,2,1,0:T(8,128)(2,1)}), bf16[8,2,128,128]{3,2,1,0:T(8,128)(2,1)S(1)}, u32[]{:S(2)}, u32[]{:S(2)}) async-start(bf16[8,2,128,128]{3,2,1,0:T(8,128)(2,1)} %copy-done.2), calls=%async_computation.2 | async-start | bytes 1048576 | tf_op jit(solution)/shard_map/kv_gather/all_to_all | solution.py:325
  62.7 11.2 %collective-permute-start.5 = (bf16[128,1024]{1,0:T(8,128)(2,1)}, bf16[128,1024]{1,0:T(8,128)(2,1)S(1)}, u32[]{:S(2)}, u32[]{:S(2)}) collective-permute-start(bf16[128,1024]{1,0:T(8,128)(2,1)} %collective-permute-done), channel_id=1, source_target_pairs={{0,64},{1,65},{2,66},{3,67},{4,68},{5,69},{6,70},{7,71},{8,72},{9,... | collective-permute-start | bytes 786440 | tf_op jit(solution)/shard_map/kv_gather/ppermute | solution.py:319
  65.0 9.0 %collective-permute-start.6 = (bf16[128,1024]{1,0:T(8,128)(2,1)}, bf16[128,1024]{1,0:T(8,128)(2,1)S(1)}, u32[]{:S(2)}, u32[]{:S(2)}) collective-permute-start(bf16[128,1024]{1,0:T(8,128)(2,1)} %collective-permute-done.1), channel_id=1, source_target_pairs={{0,80},{1,81},{2,82},{3,83},{4,84},{5,85},{6,86},{7,87},{8,88},{9,... | collective-permute-start | bytes 786440 | tf_op jit(solution)/shard_map/kv_gather/ppermute | solution.py:319
  78.7 6.1 %collective-permute-start.7 = (bf16[16,128,128]{2,1,0:T(8,128)(2,1)S(1)}, bf16[16,128,128]{2,1,0:T(8,128)(2,1)S(1)}, u32[]{:S(2)}, u32[]{:S(2)}) collective-permute-start(bf16[16,128,128]{2,1,0:T(8,128)(2,1)S(1)} %bitcast.37), channel_id=1, source_target_pairs={{0,1},{1,0},{2,3},{3,2},{4,5},{5,4},{6,7},{7,6},{8,9},{9,8},{10,11... | collective-permute-start | bytes 1572872 | tf_op jit(solution)/shard_map/kv_gather/ppermute | solution.py:305
  89.5 8.8 %collective-permute-start.8 = (f32[2,3,1024]{2,1,0:T(4,128)S(1)}, f32[2,3,1024]{2,1,0:T(4,128)S(1)}, u32[]{:S(2)}, u32[]{:S(2)}) collective-permute-start(f32[2,3,1024]{2,1,0:T(4,128)S(1)} %attention_totals.1.own_ref), channel_id=1, source_target_pairs={{0,16},{1,17},{2,18},{3,19},{4,20},{5,21},{6,22},{7,23},{8,24},{9,... | collective-permute-start | bytes 73736 | tf_op jit(solution)/shard_map/attention/ppermute | solution.py:308
  108.9 38.9 %copy-start.9 = (f32[2,128,128]{2,1,0:T(8,128)S(1)}, f32[2,128,128]{2,1,0:T(8,128)}, u32[]{:S(2)}) copy-start(f32[2,128,128]{2,1,0:T(8,128)} %get-tuple-element.90.cos_ref) | copy-start | bytes 393220
  108.9 44.0 %copy-start.4 = (bf16[2048,128]{1,0:T(8,128)(2,1)S(1)}, bf16[2048,128]{1,0:T(8,128)(2,1)}, u32[]{:S(2)}) copy-start(bf16[2048,128]{1,0:T(8,128)(2,1)} %copy-done.3) | copy-start | bytes 1572868
  109.0 11.6 %collective-permute-start.9 = (bf16[16,128,128]{2,1,0:T(8,128)(2,1)S(1)}, bf16[16,128,128]{2,1,0:T(8,128)(2,1)S(1)}, u32[]{:S(2)}, u32[]{:S(2)}) collective-permute-start(bf16[16,128,128]{2,1,0:T(8,128)(2,1)S(1)} %get-tuple-element.82), channel_id=1, source_target_pairs={{0,1},{1,0},{2,3},{3,2},{4,5},{5,4},{6,7},{7,6},{8,9},{9,8},{10,11... | collective-permute-start | bytes 1572872 | tf_op jit(solution)/shard_map/kv_reduce/ppermute | solution.py:305
  121.5 26.3 %collective-permute-start.12 = (bf16[4096,128]{1,0:T(8,128)(2,1)S(1)}, bf16[4096,128]{1,0:T(8,128)(2,1)}, u32[]{:S(2)}, u32[]{:S(2)}) collective-permute-start(bf16[4096,128]{1,0:T(8,128)(2,1)S(1)} %bitcast.35), channel_id=1, source_target_pairs={{0,1},{1,0},{2,3},{3,2},{4,5},{5,4},{6,7},{7,6},{8,9},{9,8},{10,11... | collective-permute-start | bytes 3145736 | tf_op jit(solution)/shard_map/kv_reduce/ppermute | solution.py:305
  123.8 24.0 %all-to-all-start.3 = ((bf16[8,2,128,128]{3,2,1,0:T(8,128)(2,1)}), bf16[8,2,128,128]{3,2,1,0:T(8,128)(2,1)S(1)}, u32[]{:S(2)}, u32[]{:S(2)}) async-start(bf16[8,2,128,128]{3,2,1,0:T(8,128)(2,1)} %bitcast.50), calls=%async_computation.3 | async-start | bytes 1048576 | tf_op jit(solution)/shard_map/kv_reduce/all_to_all | solution.py:325
  129.8 4.1 %collective-permute-start.11 = (bf16[2048,128]{1,0:T(8,128)(2,1)}, bf16[2048,128]{1,0:T(8,128)(2,1)S(1)}, u32[]{:S(2)}, u32[]{:S(2)}) collective-permute-start(bf16[2048,128]{1,0:T(8,128)(2,1)} %collective-permute-done.4.rest_2_), channel_id=1, source_target_pairs={{0,1},{1,0},{2,3},{3,2},{4,5},{5,4},{6,7},{7,6},{8,9},{9,8},{10,11... | collective-permute-start | bytes 1572872 | tf_op jit(solution)/shard_map/kv_reduce/ppermute | solution.py:305
  147.9 5.0 %collective-permute-start.14 = (bf16[2,128,128]{2,1,0:T(8,128)(2,1)S(1)}, bf16[2,128,128]{2,1,0:T(8,128)(2,1)S(1)}, u32[]{:S(2)}, u32[]{:S(2)}) collective-permute-start(bf16[2,128,128]{2,1,0:T(8,128)(2,1)S(1)} %bitcast.43), channel_id=1, source_target_pairs={{0,2},{1,3},{2,0},{3,1},{4,6},{5,7},{6,4},{7,5},{8,10},{9,11},{10,... | collective-permute-start | bytes 196616 | tf_op jit(solution)/shard_map/weight_grad/ppermute | solution.py:322
  157.6 22.5 %all-to-all-start.4 = ((bf16[4,16,32,128]{3,2,1,0:T(8,128)(2,1)}), bf16[4,16,32,128]{3,2,1,0:T(8,128)(2,1)S(1)}, u32[]{:S(2)}, u32[]{:S(2)}) async-start(bf16[4,16,32,128]{3,2,1,0:T(8,128)(2,1)} %weight_share.1), calls=%async_computation.4 | async-start | bytes 1048576 | tf_op jit(solution)/shard_map/weight_grad/all_to_all | solution.py:325
  161.1 13.7 %collective-permute-start.10 = (bf16[128,1024]{1,0:T(8,128)(2,1)S(1)}, bf16[128,1024]{1,0:T(8,128)(2,1)S(1)}, u32[]{:S(2)}, u32[]{:S(2)}) collective-permute-start(bf16[128,1024]{1,0:T(8,128)(2,1)S(1)} %copy-done.20), channel_id=1, source_target_pairs={{0,16},{1,17},{2,18},{3,19},{4,20},{5,21},{6,22},{7,23},{8,24},{9,... | collective-permute-start | bytes 786440 | tf_op jit(solution)/shard_map/query_grad/ppermute | solution.py:308
  175.6 37.1 %collective-permute-start.13 = (bf16[128,128]{1,0:T(8,128)(2,1)S(1)}, bf16[128,128]{1,0:T(8,128)(2,1)S(1)}, u32[]{:S(2)}, u32[]{:S(2)}) collective-permute-start(bf16[128,128]{1,0:T(8,128)(2,1)S(1)} %select_bitcast_fusion), channel_id=1, source_target_pairs={{0,1},{1,0},{2,3},{3,2},{4,5},{5,4},{6,7},{7,6},{8,9},{9,8},{10,11... | collective-permute-start | bytes 98312 | tf_op jit(solution)/shard_map/input_grad/ppermute | solution.py:305
  180.9 18.8 %all-to-all-start.5 = ((bf16[16,32,128]{2,1,0:T(8,128)(2,1)}), bf16[16,32,128]{2,1,0:T(8,128)(2,1)S(1)}, u32[]{:S(2)}, u32[]{:S(2)}) async-start(bf16[16,32,128]{2,1,0:T(8,128)(2,1)} %bitcast.19), calls=%async_computation.5 | async-start | bytes 262144 | tf_op jit(solution)/shard_map/weight_grad/all_to_all | solution.py:325
  200.4 25.7 %all-to-all-start.6 = ((bf16[32,32,128]{2,1,0:T(8,128)(2,1)}), bf16[32,32,128]{2,1,0:T(8,128)(2,1)S(1)}, u32[]{:S(2)}, u32[]{:S(2)}) async-start(bf16[32,32,128]{2,1,0:T(8,128)(2,1)} %group_share.1), calls=%async_computation.6 | async-start | bytes 524288 | tf_op jit(solution)/shard_map/weight_grad/all_to_all | solution.py:325
  (21 other events, 153.9 us)

commit v7 on v6

--- a/solution.py
+++ b/solution.py
@@ -3,6 +3,7 @@
 
 import jax
 import jax.numpy as jnp
+import numpy as np
 from jax import lax
 from jax.experimental import pallas as pl
 from jax.experimental.pallas import tpu as pltpu
@@ -18,12 +19,13 @@
 
 
 def frequencies(size):
-    expo = jnp.arange(0, size, 2).astype(jnp.float32) / size
-    base = 1.0 / jnp.power(jnp.float32(500000.0), expo)
-    wavelen = 2.0 * math.pi / base
-    mixing = (8192.0 / wavelen - 1.0) / 3.0
+    expo = np.arange(0, size, 2).astype(np.float32) / np.float32(size)
+    base = np.float32(1.0) / np.power(np.float32(500000.0), expo)
+    wavelen = np.float32(2.0 * math.pi) / base
+    mixing = (np.float32(8192.0) / wavelen - np.float32(1.0)) / np.float32(3.0)
     blended = (1.0 - mixing) * base / 8.0 + mixing * base
-    return jnp.where(wavelen < 2048.0, base, jnp.where(wavelen > 8192.0, base / 8.0, blended))
+    slow = np.where(wavelen > 8192.0, base / 8.0, blended)
+    return np.where(wavelen < 2048.0, base, slow).astype(np.float32)
 
 
 def softstep(scaled):
@@ -38,6 +40,42 @@
 
 def dot(left, right):
     return jnp.dot(left, right, preferred_element_type=jnp.float32)
+
+
+def plan_kernel(index_ref, places_ref, plan_ref, slot_at):
+    blocks = slot_at.shape[0]
+    half = blocks // 2
+    me = index_ref[0]
+    start = lax.div(me, half) * half
+    for place in range(blocks):
+        slot_at[place] = -1
+    for slot in range(half):
+        slot_at[places_ref[start + slot]] = slot
+    own = places_ref[me]
+    cross = places_ref[lax.rem(me + half, blocks)]
+
+    def visit(place, counts):
+        rank, below_own, below_cross = counts
+        slot = slot_at[place]
+        found = slot >= 0
+
+        @pl.when(found)
+        def _():
+            plan_ref[rank] = slot
+            plan_ref[half + rank] = place
+
+        one = jnp.where(found, 1, 0)
+        return (
+            rank + one,
+            below_own + jnp.where(place < own, one, 0),
+            below_cross + jnp.where(place < cross, one, 0),
+        )
+
+    _, below_own, below_cross = lax.fori_loop(0, blocks, visit, (0, 0, 0))
+    plan_ref[2 * half] = own
+    plan_ref[2 * half + 1] = cross
+    plan_ref[2 * half + 2] = below_own
+    plan_ref[2 * half + 3] = below_cross
 
 
 def tile_of(plan_ref, core_ref, near_ref, far_ref, tile):
@@ -192,29 +230,40 @@
     )(*scalars, *arrays)
 
 
-def project_kernel(core_ref, levels_ref, own_ref, far_ref, weight_ref, cos_ref, sin_ref, out_ref):
+def turning(core_ref, cos_ref, sin_ref, at):
+    is_first = core_ref[0] == 0
+    first_half = lax.broadcasted_iota(jnp.int32, (1, HD), 1) < HD // 2
+    sine_part = jnp.where(first_half, -sin_ref[at], sin_ref[at])
+    return jnp.where(is_first, cos_ref[at], 1.0), jnp.where(is_first, sine_part, 0.0)
+
+
+def project_kernel(
+    core_ref, own_bits_ref, far_bits_ref, own_ref, far_ref, weight_ref, cos_ref, sin_ref, out_ref
+):
     core = core_ref[0]
     weight = weight_ref[...]
-    for distance, x_ref in enumerate((own_ref, far_ref)):
-        at = core if distance == 0 else 1 - core
+    for x_ref, bits_ref, at in ((own_ref, own_bits_ref, core), (far_ref, far_bits_ref, 1 - core)):
         raw = dot(x_ref[...], weight)
-        turned = raw * cos_ref[at] + pltpu.roll(raw, HD // 2, 1) * sin_ref[at]
+        cosine, sine_part = turning(core_ref, cos_ref, sin_ref, at)
+        turned = raw * cosine + pltpu.roll(raw, HD // 2, 1) * sine_part
         largest = jnp.max(jnp.abs(turned), axis=0, keepdims=True)
-        level_step = (largest + EPSILON) / levels_ref[distance]
+        levels = (lax.shift_left(jnp.int32(1), bits_ref[core] - 1) - 1).astype(jnp.float32)
+        level_step = (largest + EPSILON) / levels
         quantized = (level_step * softstep(turned / level_step)).astype(jnp.bfloat16)
         for copy in range(out_ref.shape[0]):
             out_ref[copy, at] = quantized
 
 
-def settle_kernel(arrived_ref, cos_ref, sin_ref, out_ref):
+def settle_kernel(core_ref, arrived_ref, cos_ref, sin_ref, out_ref):
+    scale = jnp.where(core_ref[0] == 0, 1.0 / math.sqrt(HD), 1.0)
     for at in range(2):
         grads = arrived_ref[0, at].astype(jnp.float32)
         for source in range(1, arrived_ref.shape[0]):
             grads += arrived_ref[source, at].astype(jnp.float32)
-        turned = grads * cos_ref[at] - pltpu.roll(grads, HD // 2, 1) * sin_ref[at]
-        turned = turned.astype(jnp.bfloat16)
-        for copy in range(out_ref.shape[0]):
-            out_ref[copy, at] = turned
+        cosine, sine_part = turning(core_ref, cos_ref, sin_ref, at)
+        grads = grads * scale
+        turned = grads * cosine - pltpu.roll(grads, HD // 2, 1) * sine_part
+        out_ref[0, at] = turned.astype(jnp.bfloat16)
 
 
 def turn_kernel(parity_ref, x_ref, keep_ref, *rest):
@@ -270,7 +319,6 @@
 
 
 def body(hidden_in, queries, out_grad, kv_weight, block_pos, precision):
-    score_scale = 1.0 / math.sqrt(HD)
     tokens = hidden_in.shape[1]
     width = hidden_in.shape[2]
     seq_count = lax.axis_size("seq")
@@ -326,38 +374,24 @@
 
     x_rows = hidden_in[0]
     places = block_pos[0]
-    half_places = lax.dynamic_slice_in_dim(
-        places, lax.div(self_index, half_count) * half_count, half_count
-    )
-    own_place = lax.dynamic_slice_in_dim(places, self_index, 1)
-    cross_place = lax.dynamic_slice_in_dim(
-        places, lax.rem(self_index + half_count, seq_count), 1
-    )
-    slots = jnp.arange(half_count, dtype=jnp.int32)
-    below = (half_places[None, :] < half_places[:, None]).astype(jnp.int32)
-    ranked = jnp.sum(below, axis=1)[None, :] == slots[:, None]
-    order = jnp.sum(jnp.where(ranked, slots[None, :], 0), axis=1)
-    ranked_places = jnp.sum(jnp.where(ranked, half_places[None, :], 0), axis=1)
-    group_places = jnp.concatenate([own_place, cross_place])
-    seen = jnp.sum((half_places[None, :] < group_places[:, None]).astype(jnp.int32), axis=1)
-    plan = jnp.concatenate([order, ranked_places, group_places, seen]).astype(jnp.int32)
+    index = self_index.reshape(1).astype(jnp.int32)
+    smem = pl.BlockSpec(memory_space=pltpu.SMEM)
 
     with jax.named_scope("rotation"):
         pair_places = lax.dynamic_slice_in_dim(places, self_index - core_index, 2)
         pair_pos = pair_places[:, None] * BLOCK + jnp.arange(tokens, dtype=jnp.int32)[None, :]
         freq = frequencies(HD)
-        angles = pair_pos.astype(jnp.float32)[:, :, None] * jnp.concatenate([freq, freq])
-        lane = jnp.arange(HD, dtype=jnp.int32)
-        cosine = jnp.where(is_first, jnp.cos(angles), 1.0)
-        sine_part = jnp.where(
-            is_first, jnp.sin(angles) * jnp.where(lane < HD // 2, -1.0, 1.0), 0.0
-        )
-        back_scale = jnp.where(is_first, score_scale, 1.0)
-        back_cosine = cosine * back_scale
-        back_sine = sine_part * back_scale
-        pair_bits = jnp.concatenate([precision[0], swapped(precision[0])])
-        bits_here = jnp.where(is_first, pair_bits[:, 0], pair_bits[:, 1])
-        levels = (lax.shift_left(jnp.ones_like(bits_here), bits_here - 1) - 1).astype(jnp.float32)
+        angles = pair_pos.astype(jnp.float32)[:, :, None] * np.concatenate([freq, freq])
+        cosine = jnp.cos(angles)
+        sine_part = jnp.sin(angles)
+        plan = pl.pallas_call(
+            plan_kernel,
+            out_shape=jax.ShapeDtypeStruct((2 * half_count + 4,), jnp.int32),
+            in_specs=[smem, smem],
+            out_specs=smem,
+            scratch_shapes=[pltpu.SMEM((seq_count,), jnp.int32)],
+            name="block_plan",
+        )(index, places)
         x_far = swapped(x_rows)
         own_half, given_half = turned_halves(parity, x_rows, 2, "own_halves")
         next_half = passed(given_half)
@@ -371,19 +405,20 @@
             "weight_copies",
         )
         run_weight = exchanged(copies, "dp", runs)
-        run_weight, q_start, g_start = lax.optimization_barrier(
-            (run_weight, queries[0], out_grad[0])
-        )
+        run_weight, q_start, g_start, own_bits = lax.optimization_barrier(
+            (run_weight, queries[0], out_grad[0], precision.reshape(2))
+        )
+        far_bits = swapped(own_bits)
         q_middle, g_middle = moved(q_start, run // 2), moved(g_start, -(run // 2))
         copies = jnp.broadcast_to(run_weight[None], (dp_count // run, *run_weight.shape))
         copies = lax.optimization_barrier(copies)
         near_weight = exchanged(copies, "dp", strides).reshape(width, HD)
         (
-            near_weight, q_middle, g_middle, plan, cosine, sine_part, back_cosine, back_sine, levels, x_far,
-            own_half, next_half, far_half,
+            near_weight, q_middle, g_middle, plan, cosine, sine_part, far_bits, x_far, own_half,
+            next_half, far_half,
         ) = lax.optimization_barrier(
             (
-                near_weight, q_middle, g_middle, plan, cosine, sine_part, back_cosine, back_sine, levels, x_far,
+                near_weight, q_middle, g_middle, plan, cosine, sine_part, far_bits, x_far,
                 own_half, next_half, far_half,
             )
         )
@@ -391,12 +426,17 @@
         stacked = local_call(
             project_kernel,
             jax.ShapeDtypeStruct((columns, 2, tokens, HD), jnp.bfloat16),
-            (core, levels),
+            (core, own_bits, far_bits),
             (x_rows, x_far, near_weight, cosine, sine_part),
             "projection",
         )
     with jax.named_scope("kv_gather"):
+        stacked, late_weight, late_half = lax.optimization_barrier(
+            (stacked, near_weight, next_half)
+        )
         near = exchanged(stacked, "seq", column_groups).reshape(half_count, tokens, HD)
+        next_far_half = swapped(late_half)
+        far_weight = swapped(late_weight)
         q_cross, g_cross = moved(q_middle, run // 2), moved(g_middle, -(run // 2))
         columns_shape = jax.ShapeDtypeStruct((HD, QH * tokens), jnp.bfloat16)
         rows_shape = jax.ShapeDtypeStruct((QH * tokens, HD), jnp.bfloat16)
@@ -407,7 +447,9 @@
         cross_forms = local_call(
             query_kernel, query_shapes, (), (q_cross, g_cross), "cross_query_forms"
         )
-        near, own_forms, cross_forms = lax.optimization_barrier((near, own_forms, cross_forms))
+        near, own_forms, cross_forms, next_far_half, far_weight = lax.optimization_barrier(
+            (near, own_forms, cross_forms, next_far_half, far_weight)
+        )
         far = swapped(near)
     with jax.named_scope("attention"):
         totals = local_call(
@@ -441,23 +483,17 @@
     with jax.named_scope("kv_reduce"):
         pair = near_grad.astype(jnp.float32) + swapped(far_grad).astype(jnp.float32)
         pair = pair.astype(jnp.bfloat16).reshape(columns, 2, tokens, HD)
-        pair, next_half, near_weight, dq_sent = lax.optimization_barrier(
-            (pair, next_half, near_weight, dq_sent)
-        )
         arrived = exchanged(pair, "seq", column_groups)
-        next_far_half = swapped(next_half)
-        far_weight = swapped(near_weight)
-        arrived, next_far_half, far_weight = lax.optimization_barrier(
-            (arrived, next_far_half, far_weight)
-        )
+        arrived, dq_middle = lax.optimization_barrier((arrived, moved(dq_sent, run // 2)))
     with jax.named_scope("query_grad"):
-        query_grad = (dq_own + crossed(dq_sent).astype(jnp.float32)).astype(jnp.bfloat16)
+        dq_back = moved(dq_middle, run // 2)
+        query_grad = (dq_own + dq_back.astype(jnp.float32)).astype(jnp.bfloat16)
     with jax.named_scope("projection_grad"):
         settled = local_call(
             settle_kernel,
             jax.ShapeDtypeStruct((1, 2, tokens, HD), jnp.bfloat16),
-            (),
-            (arrived, back_cosine, back_sine),
+            (core,),
+            (arrived, cosine, sine_part),
             "projection_grad",
         )
     with jax.named_scope("weight_grad"):

time: 230 us -> 217 us (0.943)
  starting transfers between devices: 118 us -> 98.7 us
  Pallas kernels: 22.8 us -> 32 us
  waiting for transfers between devices: 54.1 us -> 63.1 us
  local copies, waits for them, and re-layouts: 17.2 us -> 10.2 us
  other arithmetic: 8.84 us -> 3.03 us
    ppermute x4 -> x6, waiting for transfers between devices: 4.96 us -> 27.9 us  [moved(): return lax.ppermute(value, ('dp', 'seq'), pairs)]
    ppermute x2 -> x1, starting transfers between devices: 13.6 us -> 1.92 us  [crossed(): return lax.ppermute(value, 'seq', cross)]
    all_to_all x7, waiting for transfers between devices: 32.4 us -> 22.1 us  [exchanged(): return lax.all_to_all(value, axis, 0, 0, axis_index_groups=groups)]
    ppermute x7, starting transfers between devices: 34.5 us -> 26.2 us  [swapped(): return lax.ppermute(value, 'seq', swap)]
    pallas_call x13, Pallas kernels: 22.8 us -> 30.5 us  [local_call(): pl.pallas_call(kernel, out_shape=shapes, in_specs=[smem] * len(scalars) +...]
    all_to_all x7, starting transfers between devices: 50.9 us -> 46.1 us  [exchanged(): return lax.all_to_all(value, axis, 0, 0, axis_index_groups=groups)]
    ppermute x4 -> x6, starting transfers between devices: 14.8 us -> 18.6 us  [moved(): return lax.ppermute(value, ('dp', 'seq'), pairs)]
    unnamed x46 -> x44, local copies, waits for them, and re-layouts: 11.9 us -> 8.99 us
  transfers between devices with their start and end apart: 22 -> 23, of which waited for: 12 -> 12; matrix products, arithmetic and copies ran while one was open for 8% -> 4% of each run, Pallas kernels for 2% -> 3%
where the time goes in v7:
time: 217 us; the launch traced here: 214 us
  starting transfers between devices  98.7 us (45%)
  waiting for transfers between devices  63.1 us (29%)
  Pallas kernels  32 us (15%)
  local copies, waits for them, and re-layouts  10.2 us (5%)
  matrix products  6.01 us (3%)
  other arithmetic  3.03 us (1%)
    all_to_all x7, starting transfers between devices, exchanged(): return lax.all_to_all(value, axis, 0, 0, axis_index_groups=groups)  46.1 us
    pallas_call x13, Pallas kernels, local_call(): pl.pallas_call(kernel, out_shape=shapes, in_specs=[smem] * len(scalars) +...  30.5 us
    ppermute x6, waiting for transfers between devices, moved(): return lax.ppermute(value, ('dp', 'seq'), pairs)  27.9 us
    ppermute x7, starting transfers between devices, swapped(): return lax.ppermute(value, 'seq', swap)  26.2 us
    all_to_all x7, waiting for transfers between devices, exchanged(): return lax.all_to_all(value, axis, 0, 0, axis_index_groups=groups)  22.1 us
    ppermute x6, starting transfers between devices, moved(): return lax.ppermute(value, ('dp', 'seq'), pairs)  18.6 us
    unnamed x44, local copies, waits for them, and re-layouts  8.99 us
    ppermute x1, waiting for transfers between devices, crossed(): return lax.ppermute(value, 'seq', cross)  6.64 us
  transfers between devices with their start and end apart: 23, of which 12 were waited for; matrix products, arithmetic and copies ran while one was open for 4% of the time, Pallas kernels for 3%

profile of v7, /device:TPU:1, one launch (start us, length us, event | category | flops | bytes accessed | tf_op | source)
XLA Modules:
  0.0 214.1 jit_solution(12391367372745221703)
XLA Ops:
  2.3 5.4 %all-to-all-start = ((bf16[4,256,128]{2,1,0:T(8,128)(2,1)}), bf16[4,256,128]{2,1,0:T(8,128)(2,1)S(1)}, u32[]{:S(2)}, u32[]{:S(2)}) async-start(bf16[4,256,128]{2,1,0:T(8,128)(2,1)} %weight_copies.1), calls=%async_computation | async-start | bytes 524288 | tf_op jit(solution)/shard_map/weight_gather/all_to_all | solution.py:373
  7.7 6.8 %collective-permute-start.3 = (bf16[128,4096]{1,0:T(8,128)(2,1)}, bf16[128,4096]{1,0:T(8,128)(2,1)S(1)}, u32[]{:S(2)}, u32[]{:S(2)}) collective-permute-start(bf16[128,4096]{1,0:T(8,128)(2,1)} %bitcast.38), channel_id=1, source_target_pairs={{0,1},{1,0},{2,3},{3,2},{4,5},{5,4},{6,7},{7,6},{8,9},{9,8},{10,11... | collective-permute-start | bytes 3145736 | tf_op jit(solution)/shard_map/rotation/ppermute | solution.py:353
  15.7 4.7 %all-to-all-start.1 = ((bf16[4,4,256,128]{3,2,1,0:T(8,128)(2,1)}), bf16[4,4,256,128]{3,2,1,0:T(8,128)(2,1)S(1)}, u32[]{:S(2)}, u32[]{:S(2)}) async-start(bf16[4,4,256,128]{3,2,1,0:T(8,128)(2,1)} %broadcast_in_dim.8), calls=%async_computation.1 | async-start | bytes 2097152 | tf_op jit(solution)/shard_map/weight_gather/all_to_all | solution.py:373
  22.4 4.0 %collective-permute-start.4 = (bf16[2048,128]{1,0:T(8,128)(2,1)}, bf16[2048,128]{1,0:T(8,128)(2,1)}, u32[]{:S(2)}, u32[]{:S(2)}) collective-permute-start(bf16[2048,128]{1,0:T(8,128)(2,1)} %get-tuple-element.54), channel_id=1, source_target_pairs={{0,2},{1,3},{2,0},{3,1},{4,6},{5,7},{6,4},{7,5},{8,10},{9,11},{10,... | collective-permute-start | bytes 1572872 | tf_op jit(solution)/shard_map/rotation/ppermute | solution.py:370
  28.4 5.5 %collective-permute-start.1 = (bf16[128,1024]{1,0:T(8,128)(2,1)}, bf16[128,1024]{1,0:T(8,128)(2,1)}, u32[]{:S(2)}, u32[]{:S(2)}) collective-permute-start(bf16[128,1024]{1,0:T(8,128)(2,1)} %bitcast.2.g_ref), channel_id=1, source_target_pairs={{0,80},{1,81},{2,82},{3,83},{4,84},{5,85},{6,86},{7,87},{8,88},{9,... | collective-permute-start | bytes 786440 | tf_op jit(solution)/shard_map/weight_gather/ppermute | solution.py:367
  36.1 5.3 %collective-permute-start.2 = (s32[2]{0:T(128)S(1)}, s32[2]{0:T(128)S(1)}, u32[]{:S(2)}, u32[]{:S(2)}) collective-permute-start(s32[2]{0:T(128)S(1)} %bitcast.44), channel_id=1, source_target_pairs={{0,1},{1,0},{2,3},{3,2},{4,5},{5,4},{6,7},{7,6},{8,9},{9,8},{10,11... | collective-permute-start | bytes 32 | tf_op jit(solution)/shard_map/weight_gather/ppermute | solution.py:353
  42.5 4.8 %collective-permute-done.1 = bf16[128,1024]{1,0:T(8,128)(2,1)} collective-permute-done((bf16[128,1024]{1,0:T(8,128)(2,1)}, bf16[128,1024]{1,0:T(8,128)(2,1)}, u32[]{:S(2)}, u32[]{:S(2)}) %collective-permute-start.1) | collective-permute-done | bytes 262176 | tf_op jit(solution)/shard_map/weight_gather/ppermute | solution.py:367
  52.5 9.1 %all-to-all-start.2 = ((bf16[8,2,128,128]{3,2,1,0:T(8,128)(2,1)}), bf16[8,2,128,128]{3,2,1,0:T(8,128)(2,1)S(1)}, u32[]{:S(2)}, u32[]{:S(2)}) async-start(bf16[8,2,128,128]{3,2,1,0:T(8,128)(2,1)} %copy-done.1), calls=%async_computation.2 | async-start | bytes 1048576 | tf_op jit(solution)/shard_map/kv_gather/all_to_all | solution.py:373
  63.9 5.5 %collective-permute-start.5 = (bf16[128,1024]{1,0:T(8,128)(2,1)}, bf16[128,1024]{1,0:T(8,128)(2,1)S(1)}, u32[]{:S(2)}, u32[]{:S(2)}) collective-permute-start(bf16[128,1024]{1,0:T(8,128)(2,1)} %collective-permute-done), channel_id=1, source_target_pairs={{0,64},{1,65},{2,66},{3,67},{4,68},{5,69},{6,70},{7,71},{8,72},{9,... | collective-permute-start | bytes 786440 | tf_op jit(solution)/shard_map/kv_gather/ppermute | solution.py:367
  74.0 4.9 %collective-permute-done.5.q_ref = bf16[128,1024]{1,0:T(8,128)(2,1)S(1)} collective-permute-done((bf16[128,1024]{1,0:T(8,128)(2,1)}, bf16[128,1024]{1,0:T(8,128)(2,1)S(1)}, u32[]{:S(2)}, u32[]{:S(2)}) %collective-permute-start.5) | collective-permute-done | bytes 262176 | tf_op jit(solution)/shard_map/kv_gather/ppermute | solution.py:367
  78.9 4.5 %collective-permute-done.6.g_ref = bf16[128,1024]{1,0:T(8,128)(2,1)S(1)} collective-permute-done((bf16[128,1024]{1,0:T(8,128)(2,1)}, bf16[128,1024]{1,0:T(8,128)(2,1)S(1)}, u32[]{:S(2)}, u32[]{:S(2)}) %collective-permute-start.6) | collective-permute-done | bytes 262176 | tf_op jit(solution)/shard_map/kv_gather/ppermute | solution.py:367
  89.9 7.2 %attention_totals.1.own_ref = f32[2,3,1024]{2,1,0:T(4,128)S(1)} custom-call(s32[36]{0:T(128)S(1)} %copy-done.17, s32[1]{0:T(128)} %bitcast.core_ref, bf16[16,128,128]{2,1,0:T(8,128)(2,1)S(1)} %bitcast.36, bf16[16,128,128]{2,1,0:T(8,128)(2,1)S(1)} %collective-permute-done.9.far_ref, bf16[128,1024]{1,0:T(8,128)(2,1)S(1)} %get-tuple-element.76.rest_0_, ...), custom_call_target="tpu_custom_call" | custom-call | tf_op jit(solution)/shard_map/attention/attention_totals/pallas_call | solution.py:222
  99.1 6.6 %collective-permute-done.10.other_ref = f32[2,3,1024]{2,1,0:T(4,128)S(1)} collective-permute-done((f32[2,3,1024]{2,1,0:T(4,128)S(1)}, f32[2,3,1024]{2,1,0:T(4,128)S(1)}, u32[]{:S(2)}, u32[]{:S(2)}) %collective-permute-start.10) | collective-permute-done | bytes 24608 | tf_op jit(solution)/shard_map/attention/ppermute | solution.py:356
  105.8 12.9 %attention_grads.1 = (f32[128,1024]{1,0:T(8,128)S(1)}, bf16[128,1024]{1,0:T(8,128)(2,1)S(1)}, bf16[16,128,128]{2,1,0:T(8,128)(2,1)S(1)}, bf16[16,128,128]{2,1,0:T(8,128)(2,1)S(1)}) custom-call(s32[36]{0:T(128)S(1)} %copy-done.17, s32[1]{0:T(128)} %bitcast.core_ref, bf16[16,128,128]{2,1,0:T(8,128)(2,1)S(1)} %bitcast.37, ...), custom_call_target="tpu_custom_call" | custom-call | tf_op jit(solution)/shard_map/attention/attention_grads/pallas_call | solution.py:222
  123.6 7.4 %all-to-all-start.3 = ((bf16[8,2,128,128]{3,2,1,0:T(8,128)(2,1)}), bf16[8,2,128,128]{3,2,1,0:T(8,128)(2,1)S(1)}, u32[]{:S(2)}, u32[]{:S(2)}) async-start(bf16[8,2,128,128]{3,2,1,0:T(8,128)(2,1)} %bitcast.11), calls=%async_computation.3 | async-start | bytes 1048576 | tf_op jit(solution)/shard_map/kv_reduce/all_to_all | solution.py:373
  132.8 13.6 %collective-permute-done.12 = bf16[128,1024]{1,0:T(8,128)(2,1)S(1)} collective-permute-done((bf16[128,1024]{1,0:T(8,128)(2,1)}, bf16[128,1024]{1,0:T(8,128)(2,1)S(1)}, u32[]{:S(2)}, u32[]{:S(2)}) %collective-permute-start.12) | collective-permute-done | bytes 262176 | tf_op jit(solution)/shard_map/kv_reduce/ppermute | solution.py:367
  151.0 3.1 %collective-permute-done.15.rest_5_ = bf16[2,128,128]{2,1,0:T(8,128)(2,1)S(1)} collective-permute-done((bf16[2,128,128]{2,1,0:T(8,128)(2,1)S(1)}, bf16[2,128,128]{2,1,0:T(8,128)(2,1)S(1)}, u32[]{:S(2)}, u32[]{:S(2)}) %collective-permute-start.15) | collective-permute-done | bytes 65568 | tf_op jit(solution)/shard_map/weight_grad/ppermute | solution.py:370
  158.7 4.2 %all-to-all-start.4 = ((bf16[4,16,32,128]{3,2,1,0:T(8,128)(2,1)}), bf16[4,16,32,128]{3,2,1,0:T(8,128)(2,1)S(1)}, u32[]{:S(2)}, u32[]{:S(2)}) async-start(bf16[4,16,32,128]{3,2,1,0:T(8,128)(2,1)} %weight_share.1), calls=%async_computation.4 | async-start | bytes 1048576 | tf_op jit(solution)/shard_map/weight_grad/all_to_all | solution.py:373
  162.8 4.8 %collective-permute-start.14 = (bf16[128,128]{1,0:T(8,128)(2,1)S(1)}, bf16[128,128]{1,0:T(8,128)(2,1)S(1)}, u32[]{:S(2)}, u32[]{:S(2)}) collective-permute-start(bf16[128,128]{1,0:T(8,128)(2,1)S(1)} %select_bitcast_fusion), channel_id=1, source_target_pairs={{0,1},{1,0},{2,3},{3,2},{4,5},{5,4},{6,7},{7,6},{8,9},{9,8},{10,11... | collective-permute-start | bytes 98312 | tf_op jit(solution)/shard_map/input_grad/ppermute | solution.py:353
  169.6 6.4 %all-to-all-done.4.parts_ref = bf16[4,16,32,128]{3,2,1,0:T(8,128)(2,1)S(1)} async-done(((bf16[4,16,32,128]{3,2,1,0:T(8,128)(2,1)}), bf16[4,16,32,128]{3,2,1,0:T(8,128)(2,1)S(1)}, u32[]{:S(2)}, u32[]{:S(2)}) %all-to-all-start.4) | async-done | bytes 524320 | tf_op jit(solution)/shard_map/weight_grad/all_to_all | solution.py:373
  176.7 5.7 %all-to-all-start.5 = ((bf16[16,32,128]{2,1,0:T(8,128)(2,1)}), bf16[16,32,128]{2,1,0:T(8,128)(2,1)S(1)}, u32[]{:S(2)}, u32[]{:S(2)}) async-start(bf16[16,32,128]{2,1,0:T(8,128)(2,1)} %bitcast.18), calls=%async_computation.5 | async-start | bytes 262144 | tf_op jit(solution)/shard_map/weight_grad/all_to_all | solution.py:373
  185.5 4.2 %all-to-all-done.5.parts_ref = bf16[16,32,128]{2,1,0:T(8,128)(2,1)S(1)} async-done(((bf16[16,32,128]{2,1,0:T(8,128)(2,1)}), bf16[16,32,128]{2,1,0:T(8,128)(2,1)S(1)}, u32[]{:S(2)}, u32[]{:S(2)}) %all-to-all-start.5) | async-done | bytes 131104 | tf_op jit(solution)/shard_map/weight_grad/all_to_all | solution.py:373
  190.4 9.5 %all-to-all-start.6 = ((bf16[32,32,128]{2,1,0:T(8,128)(2,1)}), bf16[32,32,128]{2,1,0:T(8,128)(2,1)S(1)}, u32[]{:S(2)}, u32[]{:S(2)}) async-start(bf16[32,32,128]{2,1,0:T(8,128)(2,1)} %group_share.1), calls=%async_computation.6 | async-start | bytes 524288 | tf_op jit(solution)/shard_map/weight_grad/all_to_all | solution.py:373
  204.3 9.0 %all-to-all-done.6 = bf16[32,32,128]{2,1,0:T(8,128)(2,1)S(1)} async-done(((bf16[32,32,128]{2,1,0:T(8,128)(2,1)}), bf16[32,32,128]{2,1,0:T(8,128)(2,1)S(1)}, u32[]{:S(2)}, u32[]{:S(2)}) %all-to-all-start.6) | async-done | bytes 262176 | tf_op jit(solution)/shard_map/weight_grad/all_to_all | solution.py:373
  (91 shorter events, 57.8 us)
Async XLA Ops:
  2.3 12.2 %all-to-all-start = ((bf16[4,256,128]{2,1,0:T(8,128)(2,1)}), bf16[4,256,128]{2,1,0:T(8,128)(2,1)S(1)}, u32[]{:S(2)}, u32[]{:S(2)}) async-start(bf16[4,256,128]{2,1,0:T(8,128)(2,1)} %weight_copies.1), calls=%async_computation | async-start | bytes 524288 | tf_op jit(solution)/shard_map/weight_gather/all_to_all | solution.py:373
  7.7 33.7 %collective-permute-start.3 = (bf16[128,4096]{1,0:T(8,128)(2,1)}, bf16[128,4096]{1,0:T(8,128)(2,1)S(1)}, u32[]{:S(2)}, u32[]{:S(2)}) collective-permute-start(bf16[128,4096]{1,0:T(8,128)(2,1)} %bitcast.38), channel_id=1, source_target_pairs={{0,1},{1,0},{2,3},{3,2},{4,5},{5,4},{6,7},{7,6},{8,9},{9,8},{10,11... | collective-permute-start | bytes 3145736 | tf_op jit(solution)/shard_map/rotation/ppermute | solution.py:353
  15.7 31.6 %all-to-all-start.1 = ((bf16[4,4,256,128]{3,2,1,0:T(8,128)(2,1)}), bf16[4,4,256,128]{3,2,1,0:T(8,128)(2,1)S(1)}, u32[]{:S(2)}, u32[]{:S(2)}) async-start(bf16[4,4,256,128]{3,2,1,0:T(8,128)(2,1)} %broadcast_in_dim.8), calls=%async_computation.1 | async-start | bytes 2097152 | tf_op jit(solution)/shard_map/weight_gather/all_to_all | solution.py:373
  22.4 20.1 %collective-permute-start.4 = (bf16[2048,128]{1,0:T(8,128)(2,1)}, bf16[2048,128]{1,0:T(8,128)(2,1)}, u32[]{:S(2)}, u32[]{:S(2)}) collective-permute-start(bf16[2048,128]{1,0:T(8,128)(2,1)} %get-tuple-element.54), channel_id=1, source_target_pairs={{0,2},{1,3},{2,0},{3,1},{4,6},{5,7},{6,4},{7,5},{8,10},{9,11},{10,... | collective-permute-start | bytes 1572872 | tf_op jit(solution)/shard_map/rotation/ppermute | solution.py:370
  26.5 16.0 %collective-permute-start = (bf16[128,1024]{1,0:T(8,128)(2,1)}, bf16[128,1024]{1,0:T(8,128)(2,1)}, u32[]{:S(2)}, u32[]{:S(2)}) collective-permute-start(bf16[128,1024]{1,0:T(8,128)(2,1)} %bitcast.1.q_ref), channel_id=1, source_target_pairs={{0,64},{1,65},{2,66},{3,67},{4,68},{5,69},{6,70},{7,71},{8,72},{9,... | collective-permute-start | bytes 786440 | tf_op jit(solution)/shard_map/weight_gather/ppermute | solution.py:367
  28.4 18.9 %collective-permute-start.1 = (bf16[128,1024]{1,0:T(8,128)(2,1)}, bf16[128,1024]{1,0:T(8,128)(2,1)}, u32[]{:S(2)}, u32[]{:S(2)}) collective-permute-start(bf16[128,1024]{1,0:T(8,128)(2,1)} %bitcast.2.g_ref), channel_id=1, source_target_pairs={{0,80},{1,81},{2,82},{3,83},{4,84},{5,85},{6,86},{7,87},{8,88},{9,... | collective-permute-start | bytes 786440 | tf_op jit(solution)/shard_map/weight_gather/ppermute | solution.py:367
  36.1 6.4 %collective-permute-start.2 = (s32[2]{0:T(128)S(1)}, s32[2]{0:T(128)S(1)}, u32[]{:S(2)}, u32[]{:S(2)}) collective-permute-start(s32[2]{0:T(128)S(1)} %bitcast.44), channel_id=1, source_target_pairs={{0,1},{1,0},{2,3},{3,2},{4,5},{5,4},{6,7},{7,6},{8,9},{9,8},{10,11... | collective-permute-start | bytes 32 | tf_op jit(solution)/shard_map/weight_gather/ppermute | solution.py:353
  47.3 42.6 %copy-start.17 = (s32[36]{0:T(128)S(1)}, s32[36]{0:T(128)}, u32[]{:S(2)}) copy-start(s32[36]{0:T(128)} %block_plan.1.plan_ref) | copy-start | bytes 436
  50.0 35.9 %collective-permute-start.8 = (bf16[4096,128]{1,0:T(8,128)(2,1)S(1)}, bf16[4096,128]{1,0:T(8,128)(2,1)}, u32[]{:S(2)}, u32[]{:S(2)}) collective-permute-start(bf16[4096,128]{1,0:T(8,128)(2,1)S(1)} %bitcast.33), channel_id=1, source_target_pairs={{0,1},{1,0},{2,3},{3,2},{4,5},{5,4},{6,7},{7,6},{8,9},{9,8},{10,11... | collective-permute-start | bytes 3145736 | tf_op jit(solution)/shard_map/kv_gather/ppermute | solution.py:353
  52.5 33.3 %all-to-all-start.2 = ((bf16[8,2,128,128]{3,2,1,0:T(8,128)(2,1)}), bf16[8,2,128,128]{3,2,1,0:T(8,128)(2,1)S(1)}, u32[]{:S(2)}, u32[]{:S(2)}) async-start(bf16[8,2,128,128]{3,2,1,0:T(8,128)(2,1)} %copy-done.1), calls=%async_computation.2 | async-start | bytes 1048576 | tf_op jit(solution)/shard_map/kv_gather/all_to_all | solution.py:373
  61.7 23.4 %collective-permute-start.7 = (bf16[2048,128]{1,0:T(8,128)(2,1)}, bf16[2048,128]{1,0:T(8,128)(2,1)S(1)}, u32[]{:S(2)}, u32[]{:S(2)}) collective-permute-start(bf16[2048,128]{1,0:T(8,128)(2,1)} %collective-permute-done.4.rest_2_), channel_id=1, source_target_pairs={{0,1},{1,0},{2,3},{3,2},{4,5},{5,4},{6,7},{7,6},{8,9},{9,8},{10,11... | collective-permute-start | bytes 1572872 | tf_op jit(solution)/shard_map/kv_gather/ppermute | solution.py:353
  63.9 15.0 %collective-permute-start.5 = (bf16[128,1024]{1,0:T(8,128)(2,1)}, bf16[128,1024]{1,0:T(8,128)(2,1)S(1)}, u32[]{:S(2)}, u32[]{:S(2)}) collective-permute-start(bf16[128,1024]{1,0:T(8,128)(2,1)} %collective-permute-done), channel_id=1, source_target_pairs={{0,64},{1,65},{2,66},{3,67},{4,68},{5,69},{6,70},{7,71},{8,72},{9,... | collective-permute-start | bytes 786440 | tf_op jit(solution)/shard_map/kv_gather/ppermute | solution.py:367
  69.4 14.1 %collective-permute-start.6 = (bf16[128,1024]{1,0:T(8,128)(2,1)}, bf16[128,1024]{1,0:T(8,128)(2,1)S(1)}, u32[]{:S(2)}, u32[]{:S(2)}) collective-permute-start(bf16[128,1024]{1,0:T(8,128)(2,1)} %collective-permute-done.1), channel_id=1, source_target_pairs={{0,80},{1,81},{2,82},{3,83},{4,84},{5,85},{6,86},{7,87},{8,88},{9,... | collective-permute-start | bytes 786440 | tf_op jit(solution)/shard_map/kv_gather/ppermute | solution.py:367
  85.9 4.1 %collective-permute-start.9 = (bf16[16,128,128]{2,1,0:T(8,128)(2,1)S(1)}, bf16[16,128,128]{2,1,0:T(8,128)(2,1)S(1)}, u32[]{:S(2)}, u32[]{:S(2)}) collective-permute-start(bf16[16,128,128]{2,1,0:T(8,128)(2,1)S(1)} %bitcast.35), channel_id=1, source_target_pairs={{0,1},{1,0},{2,3},{3,2},{4,5},{5,4},{6,7},{7,6},{8,9},{9,8},{10,11... | collective-permute-start | bytes 1572872 | tf_op jit(solution)/shard_map/kv_gather/ppermute | solution.py:353
  97.2 8.6 %collective-permute-start.10 = (f32[2,3,1024]{2,1,0:T(4,128)S(1)}, f32[2,3,1024]{2,1,0:T(4,128)S(1)}, u32[]{:S(2)}, u32[]{:S(2)}) collective-permute-start(f32[2,3,1024]{2,1,0:T(4,128)S(1)} %attention_totals.1.own_ref), channel_id=1, source_target_pairs={{0,16},{1,17},{2,18},{3,19},{4,20},{5,21},{6,22},{7,23},{8,24},{9,... | collective-permute-start | bytes 73736 | tf_op jit(solution)/shard_map/attention/ppermute | solution.py:356
  118.7 3.9 %collective-permute-start.11 = (bf16[16,128,128]{2,1,0:T(8,128)(2,1)S(1)}, bf16[16,128,128]{2,1,0:T(8,128)(2,1)S(1)}, u32[]{:S(2)}, u32[]{:S(2)}) collective-permute-start(bf16[16,128,128]{2,1,0:T(8,128)(2,1)S(1)} %get-tuple-element.86), channel_id=1, source_target_pairs={{0,1},{1,0},{2,3},{3,2},{4,5},{5,4},{6,7},{7,6},{8,9},{9,8},{10,11... | collective-permute-start | bytes 1572872 | tf_op jit(solution)/shard_map/kv_reduce/ppermute | solution.py:353
  123.6 25.3 %all-to-all-start.3 = ((bf16[8,2,128,128]{3,2,1,0:T(8,128)(2,1)}), bf16[8,2,128,128]{3,2,1,0:T(8,128)(2,1)S(1)}, u32[]{:S(2)}, u32[]{:S(2)}) async-start(bf16[8,2,128,128]{3,2,1,0:T(8,128)(2,1)} %bitcast.11), calls=%async_computation.3 | async-start | bytes 1048576 | tf_op jit(solution)/shard_map/kv_reduce/all_to_all | solution.py:373
  130.9 15.5 %collective-permute-start.12 = (bf16[128,1024]{1,0:T(8,128)(2,1)}, bf16[128,1024]{1,0:T(8,128)(2,1)S(1)}, u32[]{:S(2)}, u32[]{:S(2)}) collective-permute-start(bf16[128,1024]{1,0:T(8,128)(2,1)} %copy-done.19), channel_id=1, source_target_pairs={{0,64},{1,65},{2,66},{3,67},{4,68},{5,69},{6,70},{7,71},{8,72},{9,... | collective-permute-start | bytes 786440 | tf_op jit(solution)/shard_map/kv_reduce/ppermute | solution.py:367
  149.0 5.0 %collective-permute-start.15 = (bf16[2,128,128]{2,1,0:T(8,128)(2,1)S(1)}, bf16[2,128,128]{2,1,0:T(8,128)(2,1)S(1)}, u32[]{:S(2)}, u32[]{:S(2)}) collective-permute-start(bf16[2,128,128]{2,1,0:T(8,128)(2,1)S(1)} %bitcast.41), channel_id=1, source_target_pairs={{0,2},{1,3},{2,0},{3,1},{4,6},{5,7},{6,4},{7,5},{8,10},{9,11},{10,... | collective-permute-start | bytes 196616 | tf_op jit(solution)/shard_map/weight_grad/ppermute | solution.py:370
  158.7 17.3 %all-to-all-start.4 = ((bf16[4,16,32,128]{3,2,1,0:T(8,128)(2,1)}), bf16[4,16,32,128]{3,2,1,0:T(8,128)(2,1)S(1)}, u32[]{:S(2)}, u32[]{:S(2)}) async-start(bf16[4,16,32,128]{3,2,1,0:T(8,128)(2,1)} %weight_share.1), calls=%async_computation.4 | async-start | bytes 1048576 | tf_op jit(solution)/shard_map/weight_grad/all_to_all | solution.py:373
  162.8 19.6 %collective-permute-start.14 = (bf16[128,128]{1,0:T(8,128)(2,1)S(1)}, bf16[128,128]{1,0:T(8,128)(2,1)S(1)}, u32[]{:S(2)}, u32[]{:S(2)}) collective-permute-start(bf16[128,128]{1,0:T(8,128)(2,1)S(1)} %select_bitcast_fusion), channel_id=1, source_target_pairs={{0,1},{1,0},{2,3},{3,2},{4,5},{5,4},{6,7},{7,6},{8,9},{9,8},{10,11... | collective-permute-start | bytes 98312 | tf_op jit(solution)/shard_map/input_grad/ppermute | solution.py:353
  167.6 36.0 %collective-permute-start.13 = (bf16[128,1024]{1,0:T(8,128)(2,1)S(1)}, bf16[128,1024]{1,0:T(8,128)(2,1)S(1)}, u32[]{:S(2)}, u32[]{:S(2)}) collective-permute-start(bf16[128,1024]{1,0:T(8,128)(2,1)S(1)} %collective-permute-done.12), channel_id=1, source_target_pairs={{0,64},{1,65},{2,66},{3,67},{4,68},{5,69},{6,70},{7,71},{8,72},{9,... | collective-permute-start | bytes 786440 | tf_op jit(solution)/shard_map/query_grad/ppermute | solution.py:367
  176.7 13.0 %all-to-all-start.5 = ((bf16[16,32,128]{2,1,0:T(8,128)(2,1)}), bf16[16,32,128]{2,1,0:T(8,128)(2,1)S(1)}, u32[]{:S(2)}, u32[]{:S(2)}) async-start(bf16[16,32,128]{2,1,0:T(8,128)(2,1)} %bitcast.18), calls=%async_computation.5 | async-start | bytes 262144 | tf_op jit(solution)/shard_map/weight_grad/all_to_all | solution.py:373
  190.4 23.0 %all-to-all-start.6 = ((bf16[32,32,128]{2,1,0:T(8,128)(2,1)}), bf16[32,32,128]{2,1,0:T(8,128)(2,1)S(1)}, u32[]{:S(2)}, u32[]{:S(2)}) async-start(bf16[32,32,128]{2,1,0:T(8,128)(2,1)} %group_share.1), calls=%async_computation.6 | async-start | bytes 524288 | tf_op jit(solution)/shard_map/weight_grad/all_to_all | solution.py:373
  (21 other events, 202.2 us)

commit v8 on v7

--- a/solution.py
+++ b/solution.py
@@ -393,9 +393,6 @@
             name="block_plan",
         )(index, places)
         x_far = swapped(x_rows)
-        own_half, given_half = turned_halves(parity, x_rows, 2, "own_halves")
-        next_half = passed(given_half)
-        (far_half,) = turned_halves(parity, x_far, 1, "far_half")
     with jax.named_scope("weight_gather"):
         copies = local_call(
             copies_kernel,
@@ -413,13 +410,9 @@
         copies = jnp.broadcast_to(run_weight[None], (dp_count // run, *run_weight.shape))
         copies = lax.optimization_barrier(copies)
         near_weight = exchanged(copies, "dp", strides).reshape(width, HD)
-        (
-            near_weight, q_middle, g_middle, plan, cosine, sine_part, far_bits, x_far, own_half,
-            next_half, far_half,
-        ) = lax.optimization_barrier(
-            (
-                near_weight, q_middle, g_middle, plan, cosine, sine_part, far_bits, x_far,
-                own_half, next_half, far_half,
+        near_weight, q_middle, g_middle, plan, cosine, sine_part, far_bits, x_far = (
+            lax.optimization_barrier(
+                (near_weight, q_middle, g_middle, plan, cosine, sine_part, far_bits, x_far)
             )
         )
     with jax.named_scope("projection"):
@@ -431,12 +424,13 @@
             "projection",
         )
     with jax.named_scope("kv_gather"):
-        stacked, late_weight, late_half = lax.optimization_barrier(
-            (stacked, near_weight, next_half)
-        )
+        stacked, x_late, x_far_late, late_weight = lax.optimization_barrier(
+            (stacked, x_rows, x_far, near_weight)
+        )
+        far_weight = swapped(late_weight)
         near = exchanged(stacked, "seq", column_groups).reshape(half_count, tokens, HD)
-        next_far_half = swapped(late_half)
-        far_weight = swapped(late_weight)
+        own_half, given_half = turned_halves(parity, x_late, 2, "own_halves")
+        (far_half,) = turned_halves(parity, x_far_late, 1, "far_half")
         q_cross, g_cross = moved(q_middle, run // 2), moved(g_middle, -(run // 2))
         columns_shape = jax.ShapeDtypeStruct((HD, QH * tokens), jnp.bfloat16)
         rows_shape = jax.ShapeDtypeStruct((QH * tokens, HD), jnp.bfloat16)
@@ -447,8 +441,10 @@
         cross_forms = local_call(
             query_kernel, query_shapes, (), (q_cross, g_cross), "cross_query_forms"
         )
-        near, own_forms, cross_forms, next_far_half, far_weight = lax.optimization_barrier(
-            (near, own_forms, cross_forms, next_far_half, far_weight)
+        near, own_forms, cross_forms, own_half, given_half, far_half, far_weight = (
+            lax.optimization_barrier(
+                (near, own_forms, cross_forms, own_half, given_half, far_half, far_weight)
+            )
         )
         far = swapped(near)
     with jax.named_scope("attention"):
@@ -461,6 +457,9 @@
             (),
             48,
         )
+        totals, given_half = lax.optimization_barrier((totals, given_half))
+        other_totals = crossed(totals)
+        next_half = passed(given_half)
         sum_tiles = (half_count // TILE_BLOCKS, TILE_BLOCKS * BLOCK, HD)
         dq_own, dq_sent, near_grad, far_grad = local_call(
             grads_kernel,
@@ -471,7 +470,7 @@
                 jax.ShapeDtypeStruct(near.shape, jnp.bfloat16),
             ),
             (plan, core),
-            (near, far, totals, crossed(totals), *own_forms, *cross_forms),
+            (near, far, totals, other_totals, *own_forms, *cross_forms),
             "attention_grads",
             (
                 pltpu.VMEM(sum_tiles, jnp.float32),
@@ -481,13 +480,15 @@
             48,
         )
     with jax.named_scope("kv_reduce"):
+        near_grad, far_grad, next_half = lax.optimization_barrier(
+            (near_grad, far_grad, next_half)
+        )
         pair = near_grad.astype(jnp.float32) + swapped(far_grad).astype(jnp.float32)
         pair = pair.astype(jnp.bfloat16).reshape(columns, 2, tokens, HD)
+        pair, next_half, dq_sent = lax.optimization_barrier((pair, next_half, dq_sent))
         arrived = exchanged(pair, "seq", column_groups)
-        arrived, dq_middle = lax.optimization_barrier((arrived, moved(dq_sent, run // 2)))
-    with jax.named_scope("query_grad"):
-        dq_back = moved(dq_middle, run // 2)
-        query_grad = (dq_own + dq_back.astype(jnp.float32)).astype(jnp.bfloat16)
+        next_far_half = swapped(next_half)
+        dq_middle = moved(dq_sent, run // 2)
     with jax.named_scope("projection_grad"):
         settled = local_call(
             settle_kernel,
@@ -497,15 +498,20 @@
             "projection_grad",
         )
     with jax.named_scope("weight_grad"):
+        next_grads, next_far_half, dq_middle = lax.optimization_barrier(
+            (passed(settled[0]), next_far_half, dq_middle)
+        )
         piece = BLOCK // quads
         share = local_call(
             share_kernel,
             jax.ShapeDtypeStruct((quads, dp_count, piece, HD), jnp.bfloat16),
             (core,),
-            (own_half, far_half, next_half, next_far_half, settled[0], passed(settled[0])),
+            (own_half, far_half, next_half, next_far_half, settled[0], next_grads),
             "weight_share",
         )
         quad_parts = exchanged(share, "seq", quad_groups)
+        dq_back = moved(dq_middle, run // 2)
+        quad_parts, dq_back = lax.optimization_barrier((quad_parts, dq_back))
         (quad_share,) = local_call(
             total_kernel,
             (jax.ShapeDtypeStruct((1, dp_count, piece, HD), jnp.bfloat16),),
@@ -529,6 +535,8 @@
             (gathered.reshape(2, quads, 2, 2, piece, HD),),
             "weight_grad",
         )
+    with jax.named_scope("query_grad"):
+        query_grad = (dq_own + dq_back.astype(jnp.float32)).astype(jnp.bfloat16)
     with jax.named_scope("input_grad"):
         both = settled[0]
         own = jnp.where(is_first, both[0], both[1])

time: 217 us -> 215 us (level)
  starting transfers between devices: 98.7 us -> 108 us
  Pallas kernels: 32 us -> 27.4 us
  waiting for transfers between devices: 63.1 us -> 59 us
  local copies, waits for them, and re-layouts: 10.2 us -> 7.68 us
    ppermute x6, waiting for transfers between devices: 27.9 us -> 18.6 us  [moved(): return lax.ppermute(value, ('dp', 'seq'), pairs)]
    all_to_all x7, starting transfers between devices: 46.1 us -> 52.1 us  [exchanged(): return lax.all_to_all(value, axis, 0, 0, axis_index_groups=groups)]
    all_to_all x7, waiting for transfers between devices: 22.1 us -> 27.4 us  [exchanged(): return lax.all_to_all(value, axis, 0, 0, axis_index_groups=groups)]
    pallas_call x13, Pallas kernels: 30.5 us -> 25.8 us  [local_call(): pl.pallas_call(kernel, out_shape=shapes, in_specs=[smem] * len(scalars) +...]
    ppermute x7, starting transfers between devices: 26.2 us -> 30.6 us  [swapped(): return lax.ppermute(value, 'seq', swap)]
    unnamed x44 -> x54, local copies, waits for them, and re-layouts: 8.99 us -> 6.51 us
  transfers between devices with their start and end apart: 23 -> 23, of which waited for: 12 -> 13; matrix products, arithmetic and copies ran while one was open for 4% -> 4% of each run, Pallas kernels for 3% -> 7%
where the time goes in v8:
time: 215 us; the launch traced here: 212 us
  starting transfers between devices  108 us (50%)
  waiting for transfers between devices  59 us (27%)
  Pallas kernels  27.4 us (13%)
  local copies, waits for them, and re-layouts  7.68 us (4%)
  matrix products  6.08 us (3%)
  other arithmetic  3.03 us (1%)
    all_to_all x7, starting transfers between devices, exchanged(): return lax.all_to_all(value, axis, 0, 0, axis_index_groups=groups)  52.1 us
    ppermute x7, starting transfers between devices, swapped(): return lax.ppermute(value, 'seq', swap)  30.6 us
    all_to_all x7, waiting for transfers between devices, exchanged(): return lax.all_to_all(value, axis, 0, 0, axis_index_groups=groups)  27.4 us
    pallas_call x13, Pallas kernels, local_call(): pl.pallas_call(kernel, out_shape=shapes, in_specs=[smem] * len(scalars) +...  25.8 us
    ppermute x6, starting transfers between devices, moved(): return lax.ppermute(value, ('dp', 'seq'), pairs)  18.6 us
    ppermute x6, waiting for transfers between devices, moved(): return lax.ppermute(value, ('dp', 'seq'), pairs)  18.6 us
    unnamed x54, local copies, waits for them, and re-layouts  6.51 us
    ppermute x1, waiting for transfers between devices, crossed(): return lax.ppermute(value, 'seq', cross)  6.14 us
  transfers between devices with their start and end apart: 23, of which 13 were waited for; matrix products, arithmetic and copies ran while one was open for 4% of the time, Pallas kernels for 7%

profile of v8, /device:TPU:1, one launch (start us, length us, event | category | flops | bytes accessed | tf_op | source)
XLA Modules:
  0.0 211.9 jit_solution(17689047982363002697)
XLA Ops:
  2.3 5.6 %all-to-all-start = ((bf16[4,256,128]{2,1,0:T(8,128)(2,1)}), bf16[4,256,128]{2,1,0:T(8,128)(2,1)S(1)}, u32[]{:S(2)}, u32[]{:S(2)}) async-start(bf16[4,256,128]{2,1,0:T(8,128)(2,1)} %weight_copies.1), calls=%async_computation | async-start | bytes 524288 | tf_op jit(solution)/shard_map/weight_gather/all_to_all | solution.py:373
  7.9 6.8 %collective-permute-start.3 = (bf16[128,4096]{1,0:T(8,128)(2,1)}, bf16[128,4096]{1,0:T(8,128)(2,1)}, u32[]{:S(2)}, u32[]{:S(2)}) collective-permute-start(bf16[128,4096]{1,0:T(8,128)(2,1)} %bitcast.38), channel_id=1, source_target_pairs={{0,1},{1,0},{2,3},{3,2},{4,5},{5,4},{6,7},{7,6},{8,9},{9,8},{10,11... | collective-permute-start | bytes 3145736 | tf_op jit(solution)/shard_map/rotation/ppermute | solution.py:353
  15.8 4.8 %all-to-all-start.1 = ((bf16[4,4,256,128]{3,2,1,0:T(8,128)(2,1)}), bf16[4,4,256,128]{3,2,1,0:T(8,128)(2,1)S(1)}, u32[]{:S(2)}, u32[]{:S(2)}) async-start(bf16[4,4,256,128]{3,2,1,0:T(8,128)(2,1)} %broadcast_in_dim.8), calls=%async_computation.1 | async-start | bytes 2097152 | tf_op jit(solution)/shard_map/weight_gather/all_to_all | solution.py:373
  20.7 3.3 %collective-permute-start = (bf16[128,1024]{1,0:T(8,128)(2,1)S(1)}, bf16[128,1024]{1,0:T(8,128)(2,1)}, u32[]{:S(2)}, u32[]{:S(2)}) collective-permute-start(bf16[128,1024]{1,0:T(8,128)(2,1)S(1)} %bitcast.44), channel_id=1, source_target_pairs={{0,64},{1,65},{2,66},{3,67},{4,68},{5,69},{6,70},{7,71},{8,72},{9,... | collective-permute-start | bytes 786440 | tf_op jit(solution)/shard_map/weight_gather/ppermute | solution.py:367
  24.0 4.1 %collective-permute-start.1 = (bf16[128,1024]{1,0:T(8,128)(2,1)S(1)}, bf16[128,1024]{1,0:T(8,128)(2,1)}, u32[]{:S(2)}, u32[]{:S(2)}) collective-permute-start(bf16[128,1024]{1,0:T(8,128)(2,1)S(1)} %bitcast.46), channel_id=1, source_target_pairs={{0,80},{1,81},{2,82},{3,83},{4,84},{5,85},{6,86},{7,87},{8,88},{9,... | collective-permute-start | bytes 786440 | tf_op jit(solution)/shard_map/weight_gather/ppermute | solution.py:367
  30.3 6.0 %collective-permute-start.2 = (s32[2]{0:T(128)S(1)}, s32[2]{0:T(128)S(1)}, u32[]{:S(2)}, u32[]{:S(2)}) collective-permute-start(s32[2]{0:T(128)S(1)} %bitcast.48), channel_id=1, source_target_pairs={{0,1},{1,0},{2,3},{3,2},{4,5},{5,4},{6,7},{7,6},{8,9},{9,8},{10,11... | collective-permute-start | bytes 32 | tf_op jit(solution)/shard_map/weight_gather/ppermute | solution.py:353
  37.2 4.0 %collective-permute-done.1 = bf16[128,1024]{1,0:T(8,128)(2,1)} collective-permute-done((bf16[128,1024]{1,0:T(8,128)(2,1)S(1)}, bf16[128,1024]{1,0:T(8,128)(2,1)}, u32[]{:S(2)}, u32[]{:S(2)}) %collective-permute-start.1) | collective-permute-done | bytes 262176 | tf_op jit(solution)/shard_map/weight_gather/ppermute | solution.py:367
  41.2 3.3 %projection.1 = bf16[8,2,128,128]{3,2,1,0:T(8,128)(2,1)} custom-call(s32[1]{0:T(128)} %bitcast.core_ref, s32[2]{0:T(128)S(1)} %bitcast.49, s32[2]{0:T(128)S(1)} %collective-permute-done.2.far_bits_ref, bf16[128,4096]{1,0:T(8,128)(2,1)S(1)} %bitcast.39, bf16[128,4096]{1,0:T(8,128)(2,1)} %collective-permute-done.3.far_ref.x_ref, ...), custom_call_target="tpu_custom_call" | custom-call | tf_op jit(solution)/shard_map/projection/projection/pallas_call | solution.py:222
  47.3 10.0 %all-to-all-start.2 = ((bf16[8,2,128,128]{3,2,1,0:T(8,128)(2,1)}), bf16[8,2,128,128]{3,2,1,0:T(8,128)(2,1)S(1)}, u32[]{:S(2)}, u32[]{:S(2)}) async-start(bf16[8,2,128,128]{3,2,1,0:T(8,128)(2,1)} %projection.1), calls=%async_computation.2 | async-start | bytes 1048576 | tf_op jit(solution)/shard_map/kv_gather/all_to_all | solution.py:373
  57.3 5.5 %collective-permute-start.4 = (bf16[128,1024]{1,0:T(8,128)(2,1)}, bf16[128,1024]{1,0:T(8,128)(2,1)}, u32[]{:S(2)}, u32[]{:S(2)}) collective-permute-start(bf16[128,1024]{1,0:T(8,128)(2,1)} %collective-permute-done), channel_id=1, source_target_pairs={{0,64},{1,65},{2,66},{3,67},{4,68},{5,69},{6,70},{7,71},{8,72},{9,... | collective-permute-start | bytes 786440 | tf_op jit(solution)/shard_map/kv_gather/ppermute | solution.py:367
  72.4 4.7 %collective-permute-done.5.g_ref = bf16[128,1024]{1,0:T(8,128)(2,1)} collective-permute-done((bf16[128,1024]{1,0:T(8,128)(2,1)}, bf16[128,1024]{1,0:T(8,128)(2,1)}, u32[]{:S(2)}, u32[]{:S(2)}) %collective-permute-start.5) | collective-permute-done | bytes 262176 | tf_op jit(solution)/shard_map/kv_gather/ppermute | solution.py:367
  84.0 4.8 %attention_totals.1.own_ref = f32[2,3,1024]{2,1,0:T(4,128)S(1)} custom-call(s32[36]{0:T(128)S(1)} %copy-done.20, s32[1]{0:T(128)} %bitcast.core_ref, bf16[16,128,128]{2,1,0:T(8,128)(2,1)S(1)} %bitcast.36, bf16[16,128,128]{2,1,0:T(8,128)(2,1)S(1)} %collective-permute-done.7.far_ref, bf16[128,1024]{1,0:T(8,128)(2,1)S(1)} %get-tuple-element.87.rest_0_, ...), custom_call_target="tpu_custom_call" | custom-call | tf_op jit(solution)/shard_map/attention/attention_totals/pallas_call | solution.py:222
  93.2 6.1 %collective-permute-done.8.other_ref = f32[2,3,1024]{2,1,0:T(4,128)S(1)} collective-permute-done((f32[2,3,1024]{2,1,0:T(4,128)S(1)}, f32[2,3,1024]{2,1,0:T(4,128)S(1)}, u32[]{:S(2)}, u32[]{:S(2)}) %collective-permute-start.8) | collective-permute-done | bytes 24608 | tf_op jit(solution)/shard_map/attention/ppermute | solution.py:356
  99.3 8.6 %attention_grads.1 = (f32[128,1024]{1,0:T(8,128)S(1)}, bf16[128,1024]{1,0:T(8,128)(2,1)S(1)}, bf16[16,128,128]{2,1,0:T(8,128)(2,1)S(1)}, bf16[16,128,128]{2,1,0:T(8,128)(2,1)S(1)}) custom-call(s32[36]{0:T(128)S(1)} %copy-done.20, s32[1]{0:T(128)} %bitcast.core_ref, bf16[16,128,128]{2,1,0:T(8,128)(2,1)S(1)} %bitcast.37, ...), custom_call_target="tpu_custom_call" | custom-call | tf_op jit(solution)/shard_map/attention/attention_grads/pallas_call | solution.py:222
  108.0 6.4 %collective-permute-start.10 = (bf16[16,128,128]{2,1,0:T(8,128)(2,1)S(1)}, bf16[16,128,128]{2,1,0:T(8,128)(2,1)S(1)}, u32[]{:S(2)}, u32[]{:S(2)}) collective-permute-start(bf16[16,128,128]{2,1,0:T(8,128)(2,1)S(1)} %get-tuple-element.104), channel_id=1, source_target_pairs={{0,1},{1,0},{2,3},{3,2},{4,5},{5,4},{6,7},{7,6},{8,9},{9,8},{10,11... | collective-permute-start | bytes 1572872 | tf_op jit(solution)/shard_map/kv_reduce/ppermute | solution.py:353
  116.8 8.7 %all-to-all-start.3 = ((bf16[8,2,128,128]{3,2,1,0:T(8,128)(2,1)}), bf16[8,2,128,128]{3,2,1,0:T(8,128)(2,1)S(1)}, u32[]{:S(2)}, u32[]{:S(2)}) async-start(bf16[8,2,128,128]{3,2,1,0:T(8,128)(2,1)} %bitcast.50), calls=%async_computation.3 | async-start | bytes 1048576 | tf_op jit(solution)/shard_map/kv_reduce/all_to_all | solution.py:373
  130.0 13.5 %all-to-all-done.3.arrived_ref = bf16[8,2,128,128]{3,2,1,0:T(8,128)(2,1)S(1)} async-done(((bf16[8,2,128,128]{3,2,1,0:T(8,128)(2,1)}), bf16[8,2,128,128]{3,2,1,0:T(8,128)(2,1)S(1)}, u32[]{:S(2)}, u32[]{:S(2)}) %all-to-all-start.3) | async-done | bytes 524320 | tf_op jit(solution)/shard_map/kv_reduce/all_to_all | solution.py:373
  151.2 3.5 %all-to-all-start.4 = ((bf16[4,16,32,128]{3,2,1,0:T(8,128)(2,1)}), bf16[4,16,32,128]{3,2,1,0:T(8,128)(2,1)S(1)}, u32[]{:S(2)}, u32[]{:S(2)}) async-start(bf16[4,16,32,128]{3,2,1,0:T(8,128)(2,1)} %weight_share.1), calls=%async_computation.4 | async-start | bytes 1048576 | tf_op jit(solution)/shard_map/weight_grad/all_to_all | solution.py:373
  156.6 3.6 %collective-permute-start.15 = (bf16[128,128]{1,0:T(8,128)(2,1)S(1)}, bf16[128,128]{1,0:T(8,128)(2,1)S(1)}, u32[]{:S(2)}, u32[]{:S(2)}) collective-permute-start(bf16[128,128]{1,0:T(8,128)(2,1)S(1)} %select_bitcast_fusion), channel_id=1, source_target_pairs={{0,1},{1,0},{2,3},{3,2},{4,5},{5,4},{6,7},{7,6},{8,9},{9,8},{10,11... | collective-permute-start | bytes 98312 | tf_op jit(solution)/shard_map/input_grad/ppermute | solution.py:353
  160.2 8.5 %collective-permute-done.14 = bf16[128,1024]{1,0:T(8,128)(2,1)S(1)} collective-permute-done((bf16[128,1024]{1,0:T(8,128)(2,1)}, bf16[128,1024]{1,0:T(8,128)(2,1)S(1)}, u32[]{:S(2)}, u32[]{:S(2)}) %collective-permute-start.14) | collective-permute-done | bytes 262176 | tf_op jit(solution)/shard_map/weight_grad/ppermute | solution.py:367
  170.1 6.7 %all-to-all-start.5 = ((bf16[16,32,128]{2,1,0:T(8,128)(2,1)}), bf16[16,32,128]{2,1,0:T(8,128)(2,1)S(1)}, u32[]{:S(2)}, u32[]{:S(2)}) async-start(bf16[16,32,128]{2,1,0:T(8,128)(2,1)} %bitcast.18), calls=%async_computation.5 | async-start | bytes 262144 | tf_op jit(solution)/shard_map/weight_grad/all_to_all | solution.py:373
  179.8 4.2 %all-to-all-done.5.parts_ref = bf16[16,32,128]{2,1,0:T(8,128)(2,1)S(1)} async-done(((bf16[16,32,128]{2,1,0:T(8,128)(2,1)}), bf16[16,32,128]{2,1,0:T(8,128)(2,1)S(1)}, u32[]{:S(2)}, u32[]{:S(2)}) %all-to-all-start.5) | async-done | bytes 131104 | tf_op jit(solution)/shard_map/weight_grad/all_to_all | solution.py:373
  184.8 13.0 %all-to-all-start.6 = ((bf16[32,32,128]{2,1,0:T(8,128)(2,1)}), bf16[32,32,128]{2,1,0:T(8,128)(2,1)S(1)}, u32[]{:S(2)}, u32[]{:S(2)}) async-start(bf16[32,32,128]{2,1,0:T(8,128)(2,1)} %group_share.1), calls=%async_computation.6 | async-start | bytes 524288 | tf_op jit(solution)/shard_map/weight_grad/all_to_all | solution.py:373
  202.2 9.0 %all-to-all-done.6 = bf16[32,32,128]{2,1,0:T(8,128)(2,1)S(1)} async-done(((bf16[32,32,128]{2,1,0:T(8,128)(2,1)}), bf16[32,32,128]{2,1,0:T(8,128)(2,1)S(1)}, u32[]{:S(2)}, u32[]{:S(2)}) %all-to-all-start.6) | async-done | bytes 262176 | tf_op jit(solution)/shard_map/weight_grad/all_to_all | solution.py:373
  (101 shorter events, 56.4 us)
Async XLA Ops:
  2.3 12.3 %all-to-all-start = ((bf16[4,256,128]{2,1,0:T(8,128)(2,1)}), bf16[4,256,128]{2,1,0:T(8,128)(2,1)S(1)}, u32[]{:S(2)}, u32[]{:S(2)}) async-start(bf16[4,256,128]{2,1,0:T(8,128)(2,1)} %weight_copies.1), calls=%async_computation | async-start | bytes 524288 | tf_op jit(solution)/shard_map/weight_gather/all_to_all | solution.py:373
  7.9 33.3 %collective-permute-start.3 = (bf16[128,4096]{1,0:T(8,128)(2,1)}, bf16[128,4096]{1,0:T(8,128)(2,1)}, u32[]{:S(2)}, u32[]{:S(2)}) collective-permute-start(bf16[128,4096]{1,0:T(8,128)(2,1)} %bitcast.38), channel_id=1, source_target_pairs={{0,1},{1,0},{2,3},{3,2},{4,5},{5,4},{6,7},{7,6},{8,9},{9,8},{10,11... | collective-permute-start | bytes 3145736 | tf_op jit(solution)/shard_map/rotation/ppermute | solution.py:353
  15.8 25.4 %all-to-all-start.1 = ((bf16[4,4,256,128]{3,2,1,0:T(8,128)(2,1)}), bf16[4,4,256,128]{3,2,1,0:T(8,128)(2,1)S(1)}, u32[]{:S(2)}, u32[]{:S(2)}) async-start(bf16[4,4,256,128]{3,2,1,0:T(8,128)(2,1)} %broadcast_in_dim.8), calls=%async_computation.1 | async-start | bytes 2097152 | tf_op jit(solution)/shard_map/weight_gather/all_to_all | solution.py:373
  20.7 16.5 %collective-permute-start = (bf16[128,1024]{1,0:T(8,128)(2,1)S(1)}, bf16[128,1024]{1,0:T(8,128)(2,1)}, u32[]{:S(2)}, u32[]{:S(2)}) collective-permute-start(bf16[128,1024]{1,0:T(8,128)(2,1)S(1)} %bitcast.44), channel_id=1, source_target_pairs={{0,64},{1,65},{2,66},{3,67},{4,68},{5,69},{6,70},{7,71},{8,72},{9,... | collective-permute-start | bytes 786440 | tf_op jit(solution)/shard_map/weight_gather/ppermute | solution.py:367
  24.0 17.2 %collective-permute-start.1 = (bf16[128,1024]{1,0:T(8,128)(2,1)S(1)}, bf16[128,1024]{1,0:T(8,128)(2,1)}, u32[]{:S(2)}, u32[]{:S(2)}) collective-permute-start(bf16[128,1024]{1,0:T(8,128)(2,1)S(1)} %bitcast.46), channel_id=1, source_target_pairs={{0,80},{1,81},{2,82},{3,83},{4,84},{5,85},{6,86},{7,87},{8,88},{9,... | collective-permute-start | bytes 786440 | tf_op jit(solution)/shard_map/weight_gather/ppermute | solution.py:367
  30.3 6.8 %collective-permute-start.2 = (s32[2]{0:T(128)S(1)}, s32[2]{0:T(128)S(1)}, u32[]{:S(2)}, u32[]{:S(2)}) collective-permute-start(s32[2]{0:T(128)S(1)} %bitcast.48), channel_id=1, source_target_pairs={{0,1},{1,0},{2,3},{3,2},{4,5},{5,4},{6,7},{7,6},{8,9},{9,8},{10,11... | collective-permute-start | bytes 32 | tf_op jit(solution)/shard_map/weight_gather/ppermute | solution.py:353
  44.5 35.4 %collective-permute-start.6 = (bf16[4096,128]{1,0:T(8,128)(2,1)S(1)}, bf16[4096,128]{1,0:T(8,128)(2,1)}, u32[]{:S(2)}, u32[]{:S(2)}) collective-permute-start(bf16[4096,128]{1,0:T(8,128)(2,1)S(1)} %bitcast.33), channel_id=1, source_target_pairs={{0,1},{1,0},{2,3},{3,2},{4,5},{5,4},{6,7},{7,6},{8,9},{9,8},{10,11... | collective-permute-start | bytes 3145736 | tf_op jit(solution)/shard_map/kv_gather/ppermute | solution.py:353
  47.3 32.6 %all-to-all-start.2 = ((bf16[8,2,128,128]{3,2,1,0:T(8,128)(2,1)}), bf16[8,2,128,128]{3,2,1,0:T(8,128)(2,1)S(1)}, u32[]{:S(2)}, u32[]{:S(2)}) async-start(bf16[8,2,128,128]{3,2,1,0:T(8,128)(2,1)} %projection.1), calls=%async_computation.2 | async-start | bytes 1048576 | tf_op jit(solution)/shard_map/kv_gather/all_to_all | solution.py:373
  57.3 15.1 %collective-permute-start.4 = (bf16[128,1024]{1,0:T(8,128)(2,1)}, bf16[128,1024]{1,0:T(8,128)(2,1)}, u32[]{:S(2)}, u32[]{:S(2)}) collective-permute-start(bf16[128,1024]{1,0:T(8,128)(2,1)} %collective-permute-done), channel_id=1, source_target_pairs={{0,64},{1,65},{2,66},{3,67},{4,68},{5,69},{6,70},{7,71},{8,72},{9,... | collective-permute-start | bytes 786440 | tf_op jit(solution)/shard_map/kv_gather/ppermute | solution.py:367
  62.8 14.4 %collective-permute-start.5 = (bf16[128,1024]{1,0:T(8,128)(2,1)}, bf16[128,1024]{1,0:T(8,128)(2,1)}, u32[]{:S(2)}, u32[]{:S(2)}) collective-permute-start(bf16[128,1024]{1,0:T(8,128)(2,1)} %collective-permute-done.1), channel_id=1, source_target_pairs={{0,80},{1,81},{2,82},{3,83},{4,84},{5,85},{6,86},{7,87},{8,88},{9,... | collective-permute-start | bytes 786440 | tf_op jit(solution)/shard_map/kv_gather/ppermute | solution.py:367
  80.0 4.1 %collective-permute-start.7 = (bf16[16,128,128]{2,1,0:T(8,128)(2,1)S(1)}, bf16[16,128,128]{2,1,0:T(8,128)(2,1)S(1)}, u32[]{:S(2)}, u32[]{:S(2)}) collective-permute-start(bf16[16,128,128]{2,1,0:T(8,128)(2,1)S(1)} %bitcast.35), channel_id=1, source_target_pairs={{0,1},{1,0},{2,3},{3,2},{4,5},{5,4},{6,7},{7,6},{8,9},{9,8},{10,11... | collective-permute-start | bytes 1572872 | tf_op jit(solution)/shard_map/kv_gather/ppermute | solution.py:353
  88.8 19.2 %collective-permute-start.9 = (bf16[2048,128]{1,0:T(8,128)(2,1)S(1)}, bf16[2048,128]{1,0:T(8,128)(2,1)S(1)}, u32[]{:S(2)}, u32[]{:S(2)}) collective-permute-start(bf16[2048,128]{1,0:T(8,128)(2,1)S(1)} %copy-done.23), channel_id=1, source_target_pairs={{0,2},{1,3},{2,0},{3,1},{4,6},{5,7},{6,4},{7,5},{8,10},{9,11},{10,... | collective-permute-start | bytes 1572872 | tf_op jit(solution)/shard_map/attention/ppermute | solution.py:370
  90.7 8.6 %collective-permute-start.8 = (f32[2,3,1024]{2,1,0:T(4,128)S(1)}, f32[2,3,1024]{2,1,0:T(4,128)S(1)}, u32[]{:S(2)}, u32[]{:S(2)}) collective-permute-start(f32[2,3,1024]{2,1,0:T(4,128)S(1)} %attention_totals.1.own_ref), channel_id=1, source_target_pairs={{0,16},{1,17},{2,18},{3,19},{4,20},{5,21},{6,22},{7,23},{8,24},{9,... | collective-permute-start | bytes 73736 | tf_op jit(solution)/shard_map/attention/ppermute | solution.py:356
  108.0 40.6 %copy-start.4 = (bf16[2048,128]{1,0:T(8,128)(2,1)S(1)}, bf16[2048,128]{1,0:T(8,128)(2,1)}, u32[]{:S(2)}) copy-start(bf16[2048,128]{1,0:T(8,128)(2,1)} %copy-done.3) | copy-start | bytes 1572868
  108.0 7.9 %collective-permute-start.10 = (bf16[16,128,128]{2,1,0:T(8,128)(2,1)S(1)}, bf16[16,128,128]{2,1,0:T(8,128)(2,1)S(1)}, u32[]{:S(2)}, u32[]{:S(2)}) collective-permute-start(bf16[16,128,128]{2,1,0:T(8,128)(2,1)S(1)} %get-tuple-element.104), channel_id=1, source_target_pairs={{0,1},{1,0},{2,3},{3,2},{4,5},{5,4},{6,7},{7,6},{8,9},{9,8},{10,11... | collective-permute-start | bytes 1572872 | tf_op jit(solution)/shard_map/kv_reduce/ppermute | solution.py:353
  116.8 26.6 %all-to-all-start.3 = ((bf16[8,2,128,128]{3,2,1,0:T(8,128)(2,1)}), bf16[8,2,128,128]{3,2,1,0:T(8,128)(2,1)S(1)}, u32[]{:S(2)}, u32[]{:S(2)}) async-start(bf16[8,2,128,128]{3,2,1,0:T(8,128)(2,1)} %bitcast.50), calls=%async_computation.3 | async-start | bytes 1048576 | tf_op jit(solution)/shard_map/kv_reduce/all_to_all | solution.py:373
  125.5 20.0 %collective-permute-start.12 = (bf16[2048,128]{1,0:T(8,128)(2,1)}, bf16[2048,128]{1,0:T(8,128)(2,1)}, u32[]{:S(2)}, u32[]{:S(2)}) collective-permute-start(bf16[2048,128]{1,0:T(8,128)(2,1)} %copy-done.5), channel_id=1, source_target_pairs={{0,1},{1,0},{2,3},{3,2},{4,5},{5,4},{6,7},{7,6},{8,9},{9,8},{10,11... | collective-permute-start | bytes 1572872 | tf_op jit(solution)/shard_map/kv_reduce/ppermute | solution.py:353
  128.1 17.5 %collective-permute-start.13 = (bf16[128,1024]{1,0:T(8,128)(2,1)}, bf16[128,1024]{1,0:T(8,128)(2,1)}, u32[]{:S(2)}, u32[]{:S(2)}) collective-permute-start(bf16[128,1024]{1,0:T(8,128)(2,1)} %copy-done.24), channel_id=1, source_target_pairs={{0,64},{1,65},{2,66},{3,67},{4,68},{5,69},{6,70},{7,71},{8,72},{9,... | collective-permute-start | bytes 786440 | tf_op jit(solution)/shard_map/kv_reduce/ppermute | solution.py:367
  143.6 5.0 %collective-permute-start.11 = (bf16[2,128,128]{2,1,0:T(8,128)(2,1)S(1)}, bf16[2,128,128]{2,1,0:T(8,128)(2,1)S(1)}, u32[]{:S(2)}, u32[]{:S(2)}) collective-permute-start(bf16[2,128,128]{2,1,0:T(8,128)(2,1)S(1)} %bitcast.41), channel_id=1, source_target_pairs={{0,2},{1,3},{2,0},{3,1},{4,6},{5,7},{6,4},{7,5},{8,10},{9,11},{10,... | collective-permute-start | bytes 196616 | tf_op jit(solution)/shard_map/weight_grad/ppermute | solution.py:370
  151.2 18.2 %all-to-all-start.4 = ((bf16[4,16,32,128]{3,2,1,0:T(8,128)(2,1)}), bf16[4,16,32,128]{3,2,1,0:T(8,128)(2,1)S(1)}, u32[]{:S(2)}, u32[]{:S(2)}) async-start(bf16[4,16,32,128]{3,2,1,0:T(8,128)(2,1)} %weight_share.1), calls=%async_computation.4 | async-start | bytes 1048576 | tf_op jit(solution)/shard_map/weight_grad/all_to_all | solution.py:373
  154.6 14.0 %collective-permute-start.14 = (bf16[128,1024]{1,0:T(8,128)(2,1)}, bf16[128,1024]{1,0:T(8,128)(2,1)S(1)}, u32[]{:S(2)}, u32[]{:S(2)}) collective-permute-start(bf16[128,1024]{1,0:T(8,128)(2,1)} %collective-permute-done.13), channel_id=1, source_target_pairs={{0,64},{1,65},{2,66},{3,67},{4,68},{5,69},{6,70},{7,71},{8,72},{9,... | collective-permute-start | bytes 786440 | tf_op jit(solution)/shard_map/weight_grad/ppermute | solution.py:367
  156.6 20.2 %collective-permute-start.15 = (bf16[128,128]{1,0:T(8,128)(2,1)S(1)}, bf16[128,128]{1,0:T(8,128)(2,1)S(1)}, u32[]{:S(2)}, u32[]{:S(2)}) collective-permute-start(bf16[128,128]{1,0:T(8,128)(2,1)S(1)} %select_bitcast_fusion), channel_id=1, source_target_pairs={{0,1},{1,0},{2,3},{3,2},{4,5},{5,4},{6,7},{7,6},{8,9},{9,8},{10,11... | collective-permute-start | bytes 98312 | tf_op jit(solution)/shard_map/input_grad/ppermute | solution.py:353
  170.1 14.0 %all-to-all-start.5 = ((bf16[16,32,128]{2,1,0:T(8,128)(2,1)}), bf16[16,32,128]{2,1,0:T(8,128)(2,1)S(1)}, u32[]{:S(2)}, u32[]{:S(2)}) async-start(bf16[16,32,128]{2,1,0:T(8,128)(2,1)} %bitcast.18), calls=%async_computation.5 | async-start | bytes 262144 | tf_op jit(solution)/shard_map/weight_grad/all_to_all | solution.py:373
  184.8 26.5 %all-to-all-start.6 = ((bf16[32,32,128]{2,1,0:T(8,128)(2,1)}), bf16[32,32,128]{2,1,0:T(8,128)(2,1)S(1)}, u32[]{:S(2)}, u32[]{:S(2)}) async-start(bf16[32,32,128]{2,1,0:T(8,128)(2,1)} %group_share.1), calls=%async_computation.6 | async-start | bytes 524288 | tf_op jit(solution)/shard_map/weight_grad/all_to_all | solution.py:373
  (26 other events, 339.8 us)

commit v9 on v8

--- a/solution.py
+++ b/solution.py
@@ -296,6 +296,12 @@
             out_ref[quad, group] = share[quad * piece : (quad + 1) * piece]
 
 
+def sum_kernel(here_ref, there_ref, out_ref):
+    total = here_ref[...].astype(jnp.float32) + there_ref[...].astype(jnp.float32)
+    for copy in range(out_ref.shape[0]):
+        out_ref[copy] = total.astype(out_ref.dtype)
+
+
 def total_kernel(parts_ref, out_ref):
     total = parts_ref[0].astype(jnp.float32)
     for source in range(1, parts_ref.shape[0]):
@@ -305,17 +311,15 @@
         out_ref[copy] = total
 
 
-def assemble_kernel(grad_scale, parts_ref, out_ref):
-    _, quads, _, _, piece, _ = parts_ref.shape
-    for quad in range(quads):
-        for parity in range(2):
-            for core in range(2):
-                low = parts_ref[0, quad, parity, core].astype(jnp.float32)
-                high = parts_ref[1, quad, parity, core].astype(jnp.float32)
-                row = parity * BLOCK + quad * piece
-                out_ref[row : row + piece, core * HD : (core + 1) * HD] = (
-                    low + high
-                ) * grad_scale
+def assemble_kernel(grad_scale, core_ref, near_ref, far_ref, out_ref):
+    columns, piece, _ = near_ref.shape
+    is_first = core_ref[0] == 0
+    for column in range(columns):
+        row = column % 2 * BLOCK + column // 2 * piece
+        near = near_ref[column].astype(jnp.float32) * grad_scale
+        far = far_ref[column].astype(jnp.float32) * grad_scale
+        out_ref[row : row + piece, :HD] = jnp.where(is_first, near, far)
+        out_ref[row : row + piece, HD:] = jnp.where(is_first, far, near)
 
 
 def body(hidden_in, queries, out_grad, kv_weight, block_pos, precision):
@@ -431,6 +435,7 @@
         near = exchanged(stacked, "seq", column_groups).reshape(half_count, tokens, HD)
         own_half, given_half = turned_halves(parity, x_late, 2, "own_halves")
         (far_half,) = turned_halves(parity, x_far_late, 1, "far_half")
+        next_half = passed(given_half)
         q_cross, g_cross = moved(q_middle, run // 2), moved(g_middle, -(run // 2))
         columns_shape = jax.ShapeDtypeStruct((HD, QH * tokens), jnp.bfloat16)
         rows_shape = jax.ShapeDtypeStruct((QH * tokens, HD), jnp.bfloat16)
@@ -441,9 +446,9 @@
         cross_forms = local_call(
             query_kernel, query_shapes, (), (q_cross, g_cross), "cross_query_forms"
         )
-        near, own_forms, cross_forms, own_half, given_half, far_half, far_weight = (
+        near, own_forms, cross_forms, own_half, next_half, far_half, far_weight = (
             lax.optimization_barrier(
-                (near, own_forms, cross_forms, own_half, given_half, far_half, far_weight)
+                (near, own_forms, cross_forms, own_half, next_half, far_half, far_weight)
             )
         )
         far = swapped(near)
@@ -457,9 +462,7 @@
             (),
             48,
         )
-        totals, given_half = lax.optimization_barrier((totals, given_half))
         other_totals = crossed(totals)
-        next_half = passed(given_half)
         sum_tiles = (half_count // TILE_BLOCKS, TILE_BLOCKS * BLOCK, HD)
         dq_own, dq_sent, near_grad, far_grad = local_call(
             grads_kernel,
@@ -480,9 +483,6 @@
             48,
         )
     with jax.named_scope("kv_reduce"):
-        near_grad, far_grad, next_half = lax.optimization_barrier(
-            (near_grad, far_grad, next_half)
-        )
         pair = near_grad.astype(jnp.float32) + swapped(far_grad).astype(jnp.float32)
         pair = pair.astype(jnp.bfloat16).reshape(columns, 2, tokens, HD)
         pair, next_half, dq_sent = lax.optimization_barrier((pair, next_half, dq_sent))
@@ -520,19 +520,26 @@
             "quad_share",
         )
         share_parts = exchanged(quad_share[0], "dp")
-        group_share = local_call(
+        (group_share,) = local_call(
             total_kernel,
-            jax.ShapeDtypeStruct((seq_count, piece, HD), jnp.bfloat16),
+            (jax.ShapeDtypeStruct((1, piece, HD), jnp.bfloat16),),
             (),
             (share_parts,),
             "group_share",
         )
-        gathered = exchanged(group_share, "seq")
+        whole_share = local_call(
+            sum_kernel,
+            jax.ShapeDtypeStruct((columns, piece, HD), jnp.bfloat16),
+            (),
+            (group_share[0], crossed(group_share[0])),
+            "whole_share",
+        )
+        near_parts = exchanged(whole_share, "seq", column_groups)
         weight_grad = local_call(
             functools.partial(assemble_kernel, grad_scale),
             jax.ShapeDtypeStruct((width // dp_count, 2 * HD), jnp.float32),
-            (),
-            (gathered.reshape(2, quads, 2, 2, piece, HD),),
+            (core,),
+            (near_parts, swapped(near_parts)),
             "weight_grad",
         )
     with jax.named_scope("query_grad"):

time: 215 us -> 218 us (1.014)
  starting transfers between devices: 108 us -> 118 us
  waiting for transfers between devices: 59 us -> 56.3 us
    ppermute x1 -> x2, starting transfers between devices: 2.46 us -> 7.63 us  [crossed(): return lax.ppermute(value, 'seq', cross)]
    ppermute x6, starting transfers between devices: 18.6 us -> 22.7 us  [moved(): return lax.ppermute(value, ('dp', 'seq'), pairs)]
    all_to_all x7, starting transfers between devices: 52.1 us -> 48.4 us  [exchanged(): return lax.all_to_all(value, axis, 0, 0, axis_index_groups=groups)]
    ppermute x7 -> x8, starting transfers between devices: 30.6 us -> 34.2 us  [swapped(): return lax.ppermute(value, 'seq', swap)]
    all_to_all x7, waiting for transfers between devices: 27.4 us -> 24 us  [exchanged(): return lax.all_to_all(value, axis, 0, 0, axis_index_groups=groups)]
    unnamed x54 -> x46, local copies, waits for them, and re-layouts: 6.51 us -> 4.53 us
    pallas_call x13 -> x14, Pallas kernels: 25.8 us -> 24.8 us  [local_call(): pl.pallas_call(kernel, out_shape=shapes, in_specs=[smem] * len(scalars) +...]
    ppermute x1 -> x2, waiting for transfers between devices: 6.14 us -> 6.37 us  [crossed(): return lax.ppermute(value, 'seq', cross)]
  transfers between devices with their start and end apart: 23 -> 25, of which waited for: 13 -> 15; matrix products, arithmetic and copies ran while one was open for 4% -> 4% of each run, Pallas kernels for 7% -> 2%
where the time goes in v9:
time: 218 us; the launch traced here: 217 us
  starting transfers between devices  118 us (54%)
  waiting for transfers between devices  56.3 us (26%)
  Pallas kernels  26.4 us (12%)
  matrix products  6.01 us (3%)
  local copies, waits for them, and re-layouts  5.7 us (3%)
  other arithmetic  3.03 us (1%)
    all_to_all x7, starting transfers between devices, exchanged(): return lax.all_to_all(value, axis, 0, 0, axis_index_groups=groups)  48.4 us
    ppermute x8, starting transfers between devices, swapped(): return lax.ppermute(value, 'seq', swap)  34.2 us
    pallas_call x14, Pallas kernels, local_call(): pl.pallas_call(kernel, out_shape=shapes, in_specs=[smem] * len(scalars) +...  24.8 us
    all_to_all x7, waiting for transfers between devices, exchanged(): return lax.all_to_all(value, axis, 0, 0, axis_index_groups=groups)  24 us
    ppermute x6, starting transfers between devices, moved(): return lax.ppermute(value, ('dp', 'seq'), pairs)  22.7 us
    ppermute x6, waiting for transfers between devices, moved(): return lax.ppermute(value, ('dp', 'seq'), pairs)  18.5 us
    ppermute x2, starting transfers between devices, crossed(): return lax.ppermute(value, 'seq', cross)  7.63 us
    ppermute x2, waiting for transfers between devices, crossed(): return lax.ppermute(value, 'seq', cross)  6.37 us
  transfers between devices with their start and end apart: 25, of which 15 were waited for; matrix products, arithmetic and copies ran while one was open for 4% of the time, Pallas kernels for 2%

profile of v9, /device:TPU:1, one launch (start us, length us, event | category | flops | bytes accessed | tf_op | source)
XLA Modules:
  0.0 216.7 jit_solution(12501472254512108888)
XLA Ops:
  2.3 5.6 %all-to-all-start = ((bf16[4,256,128]{2,1,0:T(8,128)(2,1)}), bf16[4,256,128]{2,1,0:T(8,128)(2,1)S(1)}, u32[]{:S(2)}, u32[]{:S(2)}) async-start(bf16[4,256,128]{2,1,0:T(8,128)(2,1)} %weight_copies.1), calls=%async_computation | async-start | bytes 524288 | tf_op jit(solution)/shard_map/weight_gather/all_to_all | solution.py:377
  7.9 6.8 %collective-permute-start.3 = (bf16[128,4096]{1,0:T(8,128)(2,1)}, bf16[128,4096]{1,0:T(8,128)(2,1)}, u32[]{:S(2)}, u32[]{:S(2)}) collective-permute-start(bf16[128,4096]{1,0:T(8,128)(2,1)} %bitcast.38), channel_id=1, source_target_pairs={{0,1},{1,0},{2,3},{3,2},{4,5},{5,4},{6,7},{7,6},{8,9},{9,8},{10,11... | collective-permute-start | bytes 3145736 | tf_op jit(solution)/shard_map/rotation/ppermute | solution.py:357
  15.8 4.8 %all-to-all-start.1 = ((bf16[4,4,256,128]{3,2,1,0:T(8,128)(2,1)}), bf16[4,4,256,128]{3,2,1,0:T(8,128)(2,1)S(1)}, u32[]{:S(2)}, u32[]{:S(2)}) async-start(bf16[4,4,256,128]{3,2,1,0:T(8,128)(2,1)} %broadcast_in_dim.8), calls=%async_computation.1 | async-start | bytes 2097152 | tf_op jit(solution)/shard_map/weight_gather/all_to_all | solution.py:377
  24.0 4.1 %collective-permute-start.1 = (bf16[128,1024]{1,0:T(8,128)(2,1)S(1)}, bf16[128,1024]{1,0:T(8,128)(2,1)S(1)}, u32[]{:S(2)}, u32[]{:S(2)}) collective-permute-start(bf16[128,1024]{1,0:T(8,128)(2,1)S(1)} %bitcast.45), channel_id=1, source_target_pairs={{0,80},{1,81},{2,82},{3,83},{4,84},{5,85},{6,86},{7,87},{8,88},{9,... | collective-permute-start | bytes 786440 | tf_op jit(solution)/shard_map/weight_gather/ppermute | solution.py:371
  30.3 6.0 %collective-permute-start.2 = (s32[2]{0:T(128)S(1)}, s32[2]{0:T(128)S(1)}, u32[]{:S(2)}, u32[]{:S(2)}) collective-permute-start(s32[2]{0:T(128)S(1)} %bitcast.49), channel_id=1, source_target_pairs={{0,1},{1,0},{2,3},{3,2},{4,5},{5,4},{6,7},{7,6},{8,9},{9,8},{10,11... | collective-permute-start | bytes 32 | tf_op jit(solution)/shard_map/weight_gather/ppermute | solution.py:357
  37.2 3.9 %collective-permute-done.1 = bf16[128,1024]{1,0:T(8,128)(2,1)S(1)} collective-permute-done((bf16[128,1024]{1,0:T(8,128)(2,1)S(1)}, bf16[128,1024]{1,0:T(8,128)(2,1)S(1)}, u32[]{:S(2)}, u32[]{:S(2)}) %collective-permute-start.1) | collective-permute-done | bytes 262176 | tf_op jit(solution)/shard_map/weight_gather/ppermute | solution.py:371
  47.3 9.9 %all-to-all-start.2 = ((bf16[8,2,128,128]{3,2,1,0:T(8,128)(2,1)}), bf16[8,2,128,128]{3,2,1,0:T(8,128)(2,1)S(1)}, u32[]{:S(2)}, u32[]{:S(2)}) async-start(bf16[8,2,128,128]{3,2,1,0:T(8,128)(2,1)} %projection.1), calls=%async_computation.2 | async-start | bytes 1048576 | tf_op jit(solution)/shard_map/kv_gather/all_to_all | solution.py:377
  61.8 5.5 %collective-permute-start.4 = (bf16[128,1024]{1,0:T(8,128)(2,1)}, bf16[128,1024]{1,0:T(8,128)(2,1)S(1)}, u32[]{:S(2)}, u32[]{:S(2)}) collective-permute-start(bf16[128,1024]{1,0:T(8,128)(2,1)} %copy-done.20), channel_id=1, source_target_pairs={{0,64},{1,65},{2,66},{3,67},{4,68},{5,69},{6,70},{7,71},{8,72},{9,... | collective-permute-start | bytes 786440 | tf_op jit(solution)/shard_map/kv_gather/ppermute | solution.py:371
  72.2 4.6 %collective-permute-done.4.q_ref = bf16[128,1024]{1,0:T(8,128)(2,1)S(1)} collective-permute-done((bf16[128,1024]{1,0:T(8,128)(2,1)}, bf16[128,1024]{1,0:T(8,128)(2,1)S(1)}, u32[]{:S(2)}, u32[]{:S(2)}) %collective-permute-start.4) | collective-permute-done | bytes 262176 | tf_op jit(solution)/shard_map/kv_gather/ppermute | solution.py:371
  76.8 4.7 %collective-permute-done.5.g_ref = bf16[128,1024]{1,0:T(8,128)(2,1)S(1)} collective-permute-done((bf16[128,1024]{1,0:T(8,128)(2,1)}, bf16[128,1024]{1,0:T(8,128)(2,1)S(1)}, u32[]{:S(2)}, u32[]{:S(2)}) %collective-permute-start.5) | collective-permute-done | bytes 262176 | tf_op jit(solution)/shard_map/kv_gather/ppermute | solution.py:371
  87.3 4.8 %attention_totals.1.own_ref = f32[2,3,1024]{2,1,0:T(4,128)S(1)} custom-call(s32[36]{0:T(128)S(1)} %copy-done.16, s32[1]{0:T(128)} %bitcast.core_ref, bf16[16,128,128]{2,1,0:T(8,128)(2,1)S(1)} %bitcast.36, bf16[16,128,128]{2,1,0:T(8,128)(2,1)S(1)} %collective-permute-done.8.far_ref, bf16[128,1024]{1,0:T(8,128)(2,1)S(1)} %get-tuple-element.82.rest_0_, ...), custom_call_target="tpu_custom_call" | custom-call | tf_op jit(solution)/shard_map/attention/attention_totals/pallas_call | solution.py:222
  92.1 4.8 %collective-permute-start.9 = (f32[2,3,1024]{2,1,0:T(4,128)S(1)}, f32[2,3,1024]{2,1,0:T(4,128)S(1)}, u32[]{:S(2)}, u32[]{:S(2)}) collective-permute-start(f32[2,3,1024]{2,1,0:T(4,128)S(1)} %attention_totals.1.own_ref), channel_id=1, source_target_pairs={{0,16},{1,17},{2,18},{3,19},{4,20},{5,21},{6,22},{7,23},{8,24},{9,... | collective-permute-start | bytes 73736 | tf_op jit(solution)/shard_map/attention/ppermute | solution.py:360
  100.7 8.7 %attention_grads.1 = (f32[128,1024]{1,0:T(8,128)S(1)}, bf16[128,1024]{1,0:T(8,128)(2,1)S(1)}, bf16[16,128,128]{2,1,0:T(8,128)(2,1)S(1)}, bf16[16,128,128]{2,1,0:T(8,128)(2,1)S(1)}) custom-call(s32[36]{0:T(128)S(1)} %copy-done.16, s32[1]{0:T(128)} %bitcast.core_ref, bf16[16,128,128]{2,1,0:T(8,128)(2,1)S(1)} %bitcast.37, ...), custom_call_target="tpu_custom_call" | custom-call | tf_op jit(solution)/shard_map/attention/attention_grads/pallas_call | solution.py:222
  114.3 10.0 %all-to-all-start.3 = ((bf16[8,2,128,128]{3,2,1,0:T(8,128)(2,1)}), bf16[8,2,128,128]{3,2,1,0:T(8,128)(2,1)S(1)}, u32[]{:S(2)}, u32[]{:S(2)}) async-start(bf16[8,2,128,128]{3,2,1,0:T(8,128)(2,1)} %bitcast.11), calls=%async_computation.3 | async-start | bytes 1048576 | tf_op jit(solution)/shard_map/kv_reduce/all_to_all | solution.py:377
  126.6 4.1 %collective-permute-start.13 = (bf16[128,1024]{1,0:T(8,128)(2,1)}, bf16[128,1024]{1,0:T(8,128)(2,1)S(1)}, u32[]{:S(2)}, u32[]{:S(2)}) collective-permute-start(bf16[128,1024]{1,0:T(8,128)(2,1)} %copy-done.18), channel_id=1, source_target_pairs={{0,64},{1,65},{2,66},{3,67},{4,68},{5,69},{6,70},{7,71},{8,72},{9,... | collective-permute-start | bytes 786440 | tf_op jit(solution)/shard_map/kv_reduce/ppermute | solution.py:371
  130.7 11.5 %all-to-all-done.3.arrived_ref = bf16[8,2,128,128]{3,2,1,0:T(8,128)(2,1)S(1)} async-done(((bf16[8,2,128,128]{3,2,1,0:T(8,128)(2,1)}), bf16[8,2,128,128]{3,2,1,0:T(8,128)(2,1)S(1)}, u32[]{:S(2)}, u32[]{:S(2)}) %all-to-all-start.3) | async-done | bytes 524320 | tf_op jit(solution)/shard_map/kv_reduce/all_to_all | solution.py:377
  153.6 3.9 %collective-permute-start.14 = (bf16[128,1024]{1,0:T(8,128)(2,1)S(1)}, bf16[128,1024]{1,0:T(8,128)(2,1)S(1)}, u32[]{:S(2)}, u32[]{:S(2)}) collective-permute-start(bf16[128,1024]{1,0:T(8,128)(2,1)S(1)} %collective-permute-done.13), channel_id=1, source_target_pairs={{0,64},{1,65},{2,66},{3,67},{4,68},{5,69},{6,70},{7,71},{8,72},{9,... | collective-permute-start | bytes 786440 | tf_op jit(solution)/shard_map/weight_grad/ppermute | solution.py:371
  157.5 3.8 %collective-permute-start.15 = (bf16[128,128]{1,0:T(8,128)(2,1)S(1)}, bf16[128,128]{1,0:T(8,128)(2,1)S(1)}, u32[]{:S(2)}, u32[]{:S(2)}) collective-permute-start(bf16[128,128]{1,0:T(8,128)(2,1)S(1)} %select_bitcast_fusion), channel_id=1, source_target_pairs={{0,1},{1,0},{2,3},{3,2},{4,5},{5,4},{6,7},{7,6},{8,9},{9,8},{10,11... | collective-permute-start | bytes 98312 | tf_op jit(solution)/shard_map/input_grad/ppermute | solution.py:357
  161.3 5.3 %collective-permute-done.14 = bf16[128,1024]{1,0:T(8,128)(2,1)S(1)} collective-permute-done((bf16[128,1024]{1,0:T(8,128)(2,1)S(1)}, bf16[128,1024]{1,0:T(8,128)(2,1)S(1)}, u32[]{:S(2)}, u32[]{:S(2)}) %collective-permute-start.14) | collective-permute-done | bytes 262176 | tf_op jit(solution)/shard_map/weight_grad/ppermute | solution.py:371
  169.0 10.4 %all-to-all-start.5 = ((bf16[16,32,128]{2,1,0:T(8,128)(2,1)}), bf16[16,32,128]{2,1,0:T(8,128)(2,1)S(1)}, u32[]{:S(2)}, u32[]{:S(2)}) async-start(bf16[16,32,128]{2,1,0:T(8,128)(2,1)} %bitcast.18), calls=%async_computation.5 | async-start | bytes 262144 | tf_op jit(solution)/shard_map/weight_grad/all_to_all | solution.py:377
  182.4 4.2 %all-to-all-done.5.parts_ref = bf16[16,32,128]{2,1,0:T(8,128)(2,1)S(1)} async-done(((bf16[16,32,128]{2,1,0:T(8,128)(2,1)}), bf16[16,32,128]{2,1,0:T(8,128)(2,1)S(1)}, u32[]{:S(2)}, u32[]{:S(2)}) %all-to-all-start.5) | async-done | bytes 131104 | tf_op jit(solution)/shard_map/weight_grad/all_to_all | solution.py:377
  195.8 4.3 %all-to-all-start.6 = ((bf16[8,32,128]{2,1,0:T(8,128)(2,1)}), bf16[8,32,128]{2,1,0:T(8,128)(2,1)S(1)}, u32[]{:S(2)}, u32[]{:S(2)}) async-start(bf16[8,32,128]{2,1,0:T(8,128)(2,1)} %whole_share.1), calls=%async_computation.6 | async-start | bytes 131072 | tf_op jit(solution)/shard_map/weight_grad/all_to_all | solution.py:377
  200.7 6.6 %all-to-all-done.6.near_ref = bf16[8,32,128]{2,1,0:T(8,128)(2,1)S(1)} async-done(((bf16[8,32,128]{2,1,0:T(8,128)(2,1)}), bf16[8,32,128]{2,1,0:T(8,128)(2,1)S(1)}, u32[]{:S(2)}, u32[]{:S(2)}) %all-to-all-start.6) | async-done | bytes 65568 | tf_op jit(solution)/shard_map/weight_grad/all_to_all | solution.py:377
  207.3 7.8 %collective-permute-start.17 = (bf16[8,32,128]{2,1,0:T(8,128)(2,1)S(1)}, bf16[8,32,128]{2,1,0:T(8,128)(2,1)S(1)}, u32[]{:S(2)}, u32[]{:S(2)}) collective-permute-start(bf16[8,32,128]{2,1,0:T(8,128)(2,1)S(1)} %all-to-all-done.6.near_ref), channel_id=1, source_target_pairs={{0,1},{1,0},{2,3},{3,2},{4,5},{5,4},{6,7},{7,6},{8,9},{9,8},{10,11... | collective-permute-start | bytes 196616 | tf_op jit(solution)/shard_map/weight_grad/ppermute | solution.py:357
  (98 shorter events, 69.6 us)
Async XLA Ops:
  2.3 12.3 %all-to-all-start = ((bf16[4,256,128]{2,1,0:T(8,128)(2,1)}), bf16[4,256,128]{2,1,0:T(8,128)(2,1)S(1)}, u32[]{:S(2)}, u32[]{:S(2)}) async-start(bf16[4,256,128]{2,1,0:T(8,128)(2,1)} %weight_copies.1), calls=%async_computation | async-start | bytes 524288 | tf_op jit(solution)/shard_map/weight_gather/all_to_all | solution.py:377
  7.9 33.2 %collective-permute-start.3 = (bf16[128,4096]{1,0:T(8,128)(2,1)}, bf16[128,4096]{1,0:T(8,128)(2,1)}, u32[]{:S(2)}, u32[]{:S(2)}) collective-permute-start(bf16[128,4096]{1,0:T(8,128)(2,1)} %bitcast.38), channel_id=1, source_target_pairs={{0,1},{1,0},{2,3},{3,2},{4,5},{5,4},{6,7},{7,6},{8,9},{9,8},{10,11... | collective-permute-start | bytes 3145736 | tf_op jit(solution)/shard_map/rotation/ppermute | solution.py:357
  15.8 25.3 %all-to-all-start.1 = ((bf16[4,4,256,128]{3,2,1,0:T(8,128)(2,1)}), bf16[4,4,256,128]{3,2,1,0:T(8,128)(2,1)S(1)}, u32[]{:S(2)}, u32[]{:S(2)}) async-start(bf16[4,4,256,128]{3,2,1,0:T(8,128)(2,1)} %broadcast_in_dim.8), calls=%async_computation.1 | async-start | bytes 2097152 | tf_op jit(solution)/shard_map/weight_gather/all_to_all | solution.py:377
  20.7 16.5 %collective-permute-start = (bf16[128,1024]{1,0:T(8,128)(2,1)S(1)}, bf16[128,1024]{1,0:T(8,128)(2,1)S(1)}, u32[]{:S(2)}, u32[]{:S(2)}) collective-permute-start(bf16[128,1024]{1,0:T(8,128)(2,1)S(1)} %bitcast.43), channel_id=1, source_target_pairs={{0,64},{1,65},{2,66},{3,67},{4,68},{5,69},{6,70},{7,71},{8,72},{9,... | collective-permute-start | bytes 786440 | tf_op jit(solution)/shard_map/weight_gather/ppermute | solution.py:371
  24.0 17.1 %collective-permute-start.1 = (bf16[128,1024]{1,0:T(8,128)(2,1)S(1)}, bf16[128,1024]{1,0:T(8,128)(2,1)S(1)}, u32[]{:S(2)}, u32[]{:S(2)}) collective-permute-start(bf16[128,1024]{1,0:T(8,128)(2,1)S(1)} %bitcast.45), channel_id=1, source_target_pairs={{0,80},{1,81},{2,82},{3,83},{4,84},{5,85},{6,86},{7,87},{8,88},{9,... | collective-permute-start | bytes 786440 | tf_op jit(solution)/shard_map/weight_gather/ppermute | solution.py:371
  30.3 6.9 %collective-permute-start.2 = (s32[2]{0:T(128)S(1)}, s32[2]{0:T(128)S(1)}, u32[]{:S(2)}, u32[]{:S(2)}) collective-permute-start(s32[2]{0:T(128)S(1)} %bitcast.49), channel_id=1, source_target_pairs={{0,1},{1,0},{2,3},{3,2},{4,5},{5,4},{6,7},{7,6},{8,9},{9,8},{10,11... | collective-permute-start | bytes 32 | tf_op jit(solution)/shard_map/weight_gather/ppermute | solution.py:357
  44.5 38.7 %collective-permute-start.7 = (bf16[4096,128]{1,0:T(8,128)(2,1)S(1)}, bf16[4096,128]{1,0:T(8,128)(2,1)}, u32[]{:S(2)}, u32[]{:S(2)}) collective-permute-start(bf16[4096,128]{1,0:T(8,128)(2,1)S(1)} %bitcast.33), channel_id=1, source_target_pairs={{0,1},{1,0},{2,3},{3,2},{4,5},{5,4},{6,7},{7,6},{8,9},{9,8},{10,11... | collective-permute-start | bytes 3145736 | tf_op jit(solution)/shard_map/kv_gather/ppermute | solution.py:357
  47.3 35.8 %all-to-all-start.2 = ((bf16[8,2,128,128]{3,2,1,0:T(8,128)(2,1)}), bf16[8,2,128,128]{3,2,1,0:T(8,128)(2,1)S(1)}, u32[]{:S(2)}, u32[]{:S(2)}) async-start(bf16[8,2,128,128]{3,2,1,0:T(8,128)(2,1)} %projection.1), calls=%async_computation.2 | async-start | bytes 1048576 | tf_op jit(solution)/shard_map/kv_gather/all_to_all | solution.py:377
  58.4 24.7 %collective-permute-start.6 = (bf16[2048,128]{1,0:T(8,128)(2,1)S(1)}, bf16[2048,128]{1,0:T(8,128)(2,1)}, u32[]{:S(2)}, u32[]{:S(2)}) collective-permute-start(bf16[2048,128]{1,0:T(8,128)(2,1)S(1)} %get-tuple-element.78), channel_id=1, source_target_pairs={{0,2},{1,3},{2,0},{3,1},{4,6},{5,7},{6,4},{7,5},{8,10},{9,11},{10,... | collective-permute-start | bytes 1572872 | tf_op jit(solution)/shard_map/kv_gather/ppermute | solution.py:374
  61.8 15.0 %collective-permute-start.4 = (bf16[128,1024]{1,0:T(8,128)(2,1)}, bf16[128,1024]{1,0:T(8,128)(2,1)S(1)}, u32[]{:S(2)}, u32[]{:S(2)}) collective-permute-start(bf16[128,1024]{1,0:T(8,128)(2,1)} %copy-done.20), channel_id=1, source_target_pairs={{0,64},{1,65},{2,66},{3,67},{4,68},{5,69},{6,70},{7,71},{8,72},{9,... | collective-permute-start | bytes 786440 | tf_op jit(solution)/shard_map/kv_gather/ppermute | solution.py:371
  67.3 14.3 %collective-permute-start.5 = (bf16[128,1024]{1,0:T(8,128)(2,1)}, bf16[128,1024]{1,0:T(8,128)(2,1)S(1)}, u32[]{:S(2)}, u32[]{:S(2)}) collective-permute-start(bf16[128,1024]{1,0:T(8,128)(2,1)} %copy-done.21), channel_id=1, source_target_pairs={{0,80},{1,81},{2,82},{3,83},{4,84},{5,85},{6,86},{7,87},{8,88},{9,... | collective-permute-start | bytes 786440 | tf_op jit(solution)/shard_map/kv_gather/ppermute | solution.py:371
  83.2 4.1 %collective-permute-start.8 = (bf16[16,128,128]{2,1,0:T(8,128)(2,1)S(1)}, bf16[16,128,128]{2,1,0:T(8,128)(2,1)S(1)}, u32[]{:S(2)}, u32[]{:S(2)}) collective-permute-start(bf16[16,128,128]{2,1,0:T(8,128)(2,1)S(1)} %bitcast.35), channel_id=1, source_target_pairs={{0,1},{1,0},{2,3},{3,2},{4,5},{5,4},{6,7},{7,6},{8,9},{9,8},{10,11... | collective-permute-start | bytes 1572872 | tf_op jit(solution)/shard_map/kv_gather/ppermute | solution.py:357
  92.1 8.6 %collective-permute-start.9 = (f32[2,3,1024]{2,1,0:T(4,128)S(1)}, f32[2,3,1024]{2,1,0:T(4,128)S(1)}, u32[]{:S(2)}, u32[]{:S(2)}) collective-permute-start(f32[2,3,1024]{2,1,0:T(4,128)S(1)} %attention_totals.1.own_ref), channel_id=1, source_target_pairs={{0,16},{1,17},{2,18},{3,19},{4,20},{5,21},{6,22},{7,23},{8,24},{9,... | collective-permute-start | bytes 73736 | tf_op jit(solution)/shard_map/attention/ppermute | solution.py:360
  114.3 28.0 %all-to-all-start.3 = ((bf16[8,2,128,128]{3,2,1,0:T(8,128)(2,1)}), bf16[8,2,128,128]{3,2,1,0:T(8,128)(2,1)S(1)}, u32[]{:S(2)}, u32[]{:S(2)}) async-start(bf16[8,2,128,128]{3,2,1,0:T(8,128)(2,1)} %bitcast.11), calls=%async_computation.3 | async-start | bytes 1048576 | tf_op jit(solution)/shard_map/kv_reduce/all_to_all | solution.py:377
  124.3 20.1 %collective-permute-start.12 = (bf16[2048,128]{1,0:T(8,128)(2,1)}, bf16[2048,128]{1,0:T(8,128)(2,1)}, u32[]{:S(2)}, u32[]{:S(2)}) collective-permute-start(bf16[2048,128]{1,0:T(8,128)(2,1)} %collective-permute-done.6.rest_2_), channel_id=1, source_target_pairs={{0,1},{1,0},{2,3},{3,2},{4,5},{5,4},{6,7},{7,6},{8,9},{9,8},{10,11... | collective-permute-start | bytes 1572872 | tf_op jit(solution)/shard_map/kv_reduce/ppermute | solution.py:357
  126.6 17.7 %collective-permute-start.13 = (bf16[128,1024]{1,0:T(8,128)(2,1)}, bf16[128,1024]{1,0:T(8,128)(2,1)S(1)}, u32[]{:S(2)}, u32[]{:S(2)}) collective-permute-start(bf16[128,1024]{1,0:T(8,128)(2,1)} %copy-done.18), channel_id=1, source_target_pairs={{0,64},{1,65},{2,66},{3,67},{4,68},{5,69},{6,70},{7,71},{8,72},{9,... | collective-permute-start | bytes 786440 | tf_op jit(solution)/shard_map/kv_reduce/ppermute | solution.py:371
  142.4 5.0 %collective-permute-start.11 = (bf16[2,128,128]{2,1,0:T(8,128)(2,1)S(1)}, bf16[2,128,128]{2,1,0:T(8,128)(2,1)S(1)}, u32[]{:S(2)}, u32[]{:S(2)}) collective-permute-start(bf16[2,128,128]{2,1,0:T(8,128)(2,1)S(1)} %bitcast.41), channel_id=1, source_target_pairs={{0,2},{1,3},{2,0},{3,1},{4,6},{5,7},{6,4},{7,5},{8,10},{9,11},{10,... | collective-permute-start | bytes 196616 | tf_op jit(solution)/shard_map/weight_grad/ppermute | solution.py:374
  150.1 18.2 %all-to-all-start.4 = ((bf16[4,16,32,128]{3,2,1,0:T(8,128)(2,1)}), bf16[4,16,32,128]{3,2,1,0:T(8,128)(2,1)S(1)}, u32[]{:S(2)}, u32[]{:S(2)}) async-start(bf16[4,16,32,128]{3,2,1,0:T(8,128)(2,1)} %weight_share.1), calls=%async_computation.4 | async-start | bytes 1048576 | tf_op jit(solution)/shard_map/weight_grad/all_to_all | solution.py:377
  153.6 13.0 %collective-permute-start.14 = (bf16[128,1024]{1,0:T(8,128)(2,1)S(1)}, bf16[128,1024]{1,0:T(8,128)(2,1)S(1)}, u32[]{:S(2)}, u32[]{:S(2)}) collective-permute-start(bf16[128,1024]{1,0:T(8,128)(2,1)S(1)} %collective-permute-done.13), channel_id=1, source_target_pairs={{0,64},{1,65},{2,66},{3,67},{4,68},{5,69},{6,70},{7,71},{8,72},{9,... | collective-permute-start | bytes 786440 | tf_op jit(solution)/shard_map/weight_grad/ppermute | solution.py:371
  157.5 21.9 %collective-permute-start.15 = (bf16[128,128]{1,0:T(8,128)(2,1)S(1)}, bf16[128,128]{1,0:T(8,128)(2,1)S(1)}, u32[]{:S(2)}, u32[]{:S(2)}) collective-permute-start(bf16[128,128]{1,0:T(8,128)(2,1)S(1)} %select_bitcast_fusion), channel_id=1, source_target_pairs={{0,1},{1,0},{2,3},{3,2},{4,5},{5,4},{6,7},{7,6},{8,9},{9,8},{10,11... | collective-permute-start | bytes 98312 | tf_op jit(solution)/shard_map/input_grad/ppermute | solution.py:357
  169.0 17.7 %all-to-all-start.5 = ((bf16[16,32,128]{2,1,0:T(8,128)(2,1)}), bf16[16,32,128]{2,1,0:T(8,128)(2,1)S(1)}, u32[]{:S(2)}, u32[]{:S(2)}) async-start(bf16[16,32,128]{2,1,0:T(8,128)(2,1)} %bitcast.18), calls=%async_computation.5 | async-start | bytes 262144 | tf_op jit(solution)/shard_map/weight_grad/all_to_all | solution.py:377
  186.7 8.4 %collective-permute-start.16 = (bf16[32,128]{1,0:T(8,128)(2,1)S(1)}, bf16[32,128]{1,0:T(8,128)(2,1)S(1)}, u32[]{:S(2)}, u32[]{:S(2)}) collective-permute-start(bf16[32,128]{1,0:T(8,128)(2,1)S(1)} %bitcast.47), channel_id=1, source_target_pairs={{0,16},{1,17},{2,18},{3,19},{4,20},{5,21},{6,22},{7,23},{8,24},{9,... | collective-permute-start | bytes 24584 | tf_op jit(solution)/shard_map/weight_grad/ppermute | solution.py:360
  195.8 11.5 %all-to-all-start.6 = ((bf16[8,32,128]{2,1,0:T(8,128)(2,1)}), bf16[8,32,128]{2,1,0:T(8,128)(2,1)S(1)}, u32[]{:S(2)}, u32[]{:S(2)}) async-start(bf16[8,32,128]{2,1,0:T(8,128)(2,1)} %whole_share.1), calls=%async_computation.6 | async-start | bytes 131072 | tf_op jit(solution)/shard_map/weight_grad/all_to_all | solution.py:377
  207.3 8.7 %collective-permute-start.17 = (bf16[8,32,128]{2,1,0:T(8,128)(2,1)S(1)}, bf16[8,32,128]{2,1,0:T(8,128)(2,1)S(1)}, u32[]{:S(2)}, u32[]{:S(2)}) collective-permute-start(bf16[8,32,128]{2,1,0:T(8,128)(2,1)S(1)} %all-to-all-done.6.near_ref), channel_id=1, source_target_pairs={{0,1},{1,0},{2,3},{3,2},{4,5},{5,4},{6,7},{7,6},{8,9},{9,8},{10,11... | collective-permute-start | bytes 196616 | tf_op jit(solution)/shard_map/weight_grad/ppermute | solution.py:357
  (24 other events, 356.6 us)

commit v10 on v8

--- a/solution.py
+++ b/solution.py
@@ -410,10 +410,8 @@
         copies = jnp.broadcast_to(run_weight[None], (dp_count // run, *run_weight.shape))
         copies = lax.optimization_barrier(copies)
         near_weight = exchanged(copies, "dp", strides).reshape(width, HD)
-        near_weight, q_middle, g_middle, plan, cosine, sine_part, far_bits, x_far = (
-            lax.optimization_barrier(
-                (near_weight, q_middle, g_middle, plan, cosine, sine_part, far_bits, x_far)
-            )
+        near_weight, plan, cosine, sine_part, far_bits, x_far = lax.optimization_barrier(
+            (near_weight, plan, cosine, sine_part, far_bits, x_far)
         )
     with jax.named_scope("projection"):
         stacked = local_call(
@@ -424,8 +422,8 @@
             "projection",
         )
     with jax.named_scope("kv_gather"):
-        stacked, x_late, x_far_late, late_weight = lax.optimization_barrier(
-            (stacked, x_rows, x_far, near_weight)
+        stacked, x_late, x_far_late, late_weight, q_middle, g_middle = lax.optimization_barrier(
+            (stacked, x_rows, x_far, near_weight, q_middle, g_middle)
         )
         far_weight = swapped(late_weight)
         near = exchanged(stacked, "seq", column_groups).reshape(half_count, tokens, HD)

time: 215 us -> 211 us (0.981)
  waiting for transfers between devices: 59 us -> 48.5 us
  starting transfers between devices: 108 us -> 111 us
  Pallas kernels: 27.4 us -> 29.7 us
    ppermute x6, waiting for transfers between devices: 18.6 us -> 9.08 us  [moved(): return lax.ppermute(value, ('dp', 'seq'), pairs)]
    ppermute x6, starting transfers between devices: 18.6 us -> 23 us  [moved(): return lax.ppermute(value, ('dp', 'seq'), pairs)]
    ppermute x7, starting transfers between devices: 30.6 us -> 26.6 us  [swapped(): return lax.ppermute(value, 'seq', swap)]
    ppermute x1, waiting for transfers between devices: 6.14 us -> 3.25 us  [crossed(): return lax.ppermute(value, 'seq', cross)]
    ppermute x1, starting transfers between devices: 2.46 us -> 5.31 us  [crossed(): return lax.ppermute(value, 'seq', cross)]
    pallas_call x13, Pallas kernels: 25.8 us -> 28.2 us  [local_call(): pl.pallas_call(kernel, out_shape=shapes, in_specs=[smem] * len(scalars) +...]
  transfers between devices with their start and end apart: 23 -> 23, of which waited for: 13 -> 13; matrix products, arithmetic and copies ran while one was open for 4% -> 5% of each run, Pallas kernels for 7% -> 9%
where the time goes in v10:
time: 211 us; the launch traced here: 207 us
  starting transfers between devices  111 us (53%)
  waiting for transfers between devices  48.5 us (23%)
  Pallas kernels  29.7 us (14%)
  local copies, waits for them, and re-layouts  7.68 us (4%)
  matrix products  6.08 us (3%)
  other arithmetic  3.03 us (1%)
    all_to_all x7, starting transfers between devices, exchanged(): return lax.all_to_all(value, axis, 0, 0, axis_index_groups=groups)  52.6 us
    all_to_all x7, waiting for transfers between devices, exchanged(): return lax.all_to_all(value, axis, 0, 0, axis_index_groups=groups)  29 us
    pallas_call x13, Pallas kernels, local_call(): pl.pallas_call(kernel, out_shape=shapes, in_specs=[smem] * len(scalars) +...  28.2 us
    ppermute x7, starting transfers between devices, swapped(): return lax.ppermute(value, 'seq', swap)  26.6 us
    ppermute x6, starting transfers between devices, moved(): return lax.ppermute(value, ('dp', 'seq'), pairs)  23 us
    ppermute x6, waiting for transfers between devices, moved(): return lax.ppermute(value, ('dp', 'seq'), pairs)  9.08 us
    unnamed x54, local copies, waits for them, and re-layouts  6.51 us
    dot_general x2, matrix products, dot_cols(): lax.dot_general(left, right, (((1,), (1,)), ((), ())), preferred_element_...  6.08 us
  transfers between devices with their start and end apart: 23, of which 13 were waited for; matrix products, arithmetic and copies ran while one was open for 5% of the time, Pallas kernels for 9%

profile of v10, /device:TPU:1, one launch (start us, length us, event | category | flops | bytes accessed | tf_op | source)
XLA Modules:
  0.0 207.4 jit_solution(4435229202096870217)
XLA Ops:
  2.3 5.6 %all-to-all-start = ((bf16[4,256,128]{2,1,0:T(8,128)(2,1)}), bf16[4,256,128]{2,1,0:T(8,128)(2,1)S(1)}, u32[]{:S(2)}, u32[]{:S(2)}) async-start(bf16[4,256,128]{2,1,0:T(8,128)(2,1)} %weight_copies.1), calls=%async_computation | async-start | bytes 524288 | tf_op jit(solution)/shard_map/weight_gather/all_to_all | solution.py:373
  7.9 6.8 %collective-permute-start.1 = (bf16[128,4096]{1,0:T(8,128)(2,1)}, bf16[128,4096]{1,0:T(8,128)(2,1)}, u32[]{:S(2)}, u32[]{:S(2)}) collective-permute-start(bf16[128,4096]{1,0:T(8,128)(2,1)} %bitcast.38), channel_id=1, source_target_pairs={{0,1},{1,0},{2,3},{3,2},{4,5},{5,4},{6,7},{7,6},{8,9},{9,8},{10,11... | collective-permute-start | bytes 3145736 | tf_op jit(solution)/shard_map/rotation/ppermute | solution.py:353
  15.8 4.8 %all-to-all-start.1 = ((bf16[4,4,256,128]{3,2,1,0:T(8,128)(2,1)}), bf16[4,4,256,128]{3,2,1,0:T(8,128)(2,1)S(1)}, u32[]{:S(2)}, u32[]{:S(2)}) async-start(bf16[4,4,256,128]{3,2,1,0:T(8,128)(2,1)} %broadcast_in_dim.8), calls=%async_computation.1 | async-start | bytes 2097152 | tf_op jit(solution)/shard_map/weight_gather/all_to_all | solution.py:373
  20.7 3.3 %collective-permute-start.2 = (bf16[128,1024]{1,0:T(8,128)(2,1)S(1)}, bf16[128,1024]{1,0:T(8,128)(2,1)}, u32[]{:S(2)}, u32[]{:S(2)}) collective-permute-start(bf16[128,1024]{1,0:T(8,128)(2,1)S(1)} %bitcast.44), channel_id=1, source_target_pairs={{0,64},{1,65},{2,66},{3,67},{4,68},{5,69},{6,70},{7,71},{8,72},{9,... | collective-permute-start | bytes 786440 | tf_op jit(solution)/shard_map/weight_gather/ppermute | solution.py:367
  24.0 4.1 %collective-permute-start.3 = (bf16[128,1024]{1,0:T(8,128)(2,1)S(1)}, bf16[128,1024]{1,0:T(8,128)(2,1)}, u32[]{:S(2)}, u32[]{:S(2)}) collective-permute-start(bf16[128,1024]{1,0:T(8,128)(2,1)S(1)} %bitcast.46), channel_id=1, source_target_pairs={{0,80},{1,81},{2,82},{3,83},{4,84},{5,85},{6,86},{7,87},{8,88},{9,... | collective-permute-start | bytes 786440 | tf_op jit(solution)/shard_map/weight_gather/ppermute | solution.py:367
  30.3 6.0 %collective-permute-start = (s32[2]{0:T(128)S(1)}, s32[2]{0:T(128)S(1)}, u32[]{:S(2)}, u32[]{:S(2)}) collective-permute-start(s32[2]{0:T(128)S(1)} %bitcast.48), channel_id=1, source_target_pairs={{0,1},{1,0},{2,3},{3,2},{4,5},{5,4},{6,7},{7,6},{8,9},{9,8},{10,11... | collective-permute-start | bytes 32 | tf_op jit(solution)/shard_map/weight_gather/ppermute | solution.py:353
  37.2 3.3 %projection.1 = bf16[8,2,128,128]{3,2,1,0:T(8,128)(2,1)} custom-call(s32[1]{0:T(128)} %bitcast.core_ref, s32[2]{0:T(128)S(1)} %bitcast.49, s32[2]{0:T(128)S(1)} %collective-permute-done.far_bits_ref, bf16[128,4096]{1,0:T(8,128)(2,1)S(1)} %bitcast.39, bf16[128,4096]{1,0:T(8,128)(2,1)} %collective-permute-done.1.far_ref.x_ref, bf16[4096,128]{1,0:T(8,128)(2,1)S(1)} %bitcast.32, ...), custom_call_target="tpu_custom_call" | custom-call | tf_op jit(solution)/shard_map/projection/projection/pallas_call | solution.py:222
  44.0 10.0 %all-to-all-start.2 = ((bf16[8,2,128,128]{3,2,1,0:T(8,128)(2,1)}), bf16[8,2,128,128]{3,2,1,0:T(8,128)(2,1)S(1)}, u32[]{:S(2)}, u32[]{:S(2)}) async-start(bf16[8,2,128,128]{3,2,1,0:T(8,128)(2,1)} %projection.1), calls=%async_computation.2 | async-start | bytes 1048576 | tf_op jit(solution)/shard_map/kv_gather/all_to_all | solution.py:373
  53.9 5.5 %collective-permute-start.4 = (bf16[128,1024]{1,0:T(8,128)(2,1)}, bf16[128,1024]{1,0:T(8,128)(2,1)}, u32[]{:S(2)}, u32[]{:S(2)}) collective-permute-start(bf16[128,1024]{1,0:T(8,128)(2,1)} %collective-permute-done.2), channel_id=1, source_target_pairs={{0,64},{1,65},{2,66},{3,67},{4,68},{5,69},{6,70},{7,71},{8,72},{9,... | collective-permute-start | bytes 786440 | tf_op jit(solution)/shard_map/kv_gather/ppermute | solution.py:367
  67.7 4.4 %collective-permute-done.4.q_ref = bf16[128,1024]{1,0:T(8,128)(2,1)} collective-permute-done((bf16[128,1024]{1,0:T(8,128)(2,1)}, bf16[128,1024]{1,0:T(8,128)(2,1)}, u32[]{:S(2)}, u32[]{:S(2)}) %collective-permute-start.4) | collective-permute-done | bytes 262176 | tf_op jit(solution)/shard_map/kv_gather/ppermute | solution.py:367
  80.7 5.6 %attention_totals.1.own_ref = f32[2,3,1024]{2,1,0:T(4,128)S(1)} custom-call(s32[36]{0:T(128)S(1)} %copy-done.20, s32[1]{0:T(128)} %bitcast.core_ref, bf16[16,128,128]{2,1,0:T(8,128)(2,1)S(1)} %bitcast.36, bf16[16,128,128]{2,1,0:T(8,128)(2,1)S(1)} %collective-permute-done.7.far_ref, bf16[128,1024]{1,0:T(8,128)(2,1)S(1)} %get-tuple-element.87.rest_0_, ...), custom_call_target="tpu_custom_call" | custom-call | tf_op jit(solution)/shard_map/attention/attention_totals/pallas_call | solution.py:222
  88.2 5.3 %collective-permute-start.8 = (f32[2,3,1024]{2,1,0:T(4,128)S(1)}, f32[2,3,1024]{2,1,0:T(4,128)S(1)}, u32[]{:S(2)}, u32[]{:S(2)}) collective-permute-start(f32[2,3,1024]{2,1,0:T(4,128)S(1)} %attention_totals.1.own_ref), channel_id=1, source_target_pairs={{0,16},{1,17},{2,18},{3,19},{4,20},{5,21},{6,22},{7,23},{8,24},{9,... | collective-permute-start | bytes 73736 | tf_op jit(solution)/shard_map/attention/ppermute | solution.py:356
  96.8 10.1 %attention_grads.1 = (f32[128,1024]{1,0:T(8,128)S(1)}, bf16[128,1024]{1,0:T(8,128)(2,1)S(1)}, bf16[16,128,128]{2,1,0:T(8,128)(2,1)S(1)}, bf16[16,128,128]{2,1,0:T(8,128)(2,1)S(1)}) custom-call(s32[36]{0:T(128)S(1)} %copy-done.20, s32[1]{0:T(128)} %bitcast.core_ref, bf16[16,128,128]{2,1,0:T(8,128)(2,1)S(1)} %bitcast.37, ...), custom_call_target="tpu_custom_call" | custom-call | tf_op jit(solution)/shard_map/attention/attention_grads/pallas_call | solution.py:222
  111.8 10.8 %all-to-all-start.3 = ((bf16[8,2,128,128]{3,2,1,0:T(8,128)(2,1)}), bf16[8,2,128,128]{3,2,1,0:T(8,128)(2,1)S(1)}, u32[]{:S(2)}, u32[]{:S(2)}) async-start(bf16[8,2,128,128]{3,2,1,0:T(8,128)(2,1)} %bitcast.50), calls=%async_computation.3 | async-start | bytes 1048576 | tf_op jit(solution)/shard_map/kv_reduce/all_to_all | solution.py:373
  125.2 4.0 %collective-permute-start.13 = (bf16[128,1024]{1,0:T(8,128)(2,1)}, bf16[128,1024]{1,0:T(8,128)(2,1)}, u32[]{:S(2)}, u32[]{:S(2)}) collective-permute-start(bf16[128,1024]{1,0:T(8,128)(2,1)} %copy-done.24), channel_id=1, source_target_pairs={{0,64},{1,65},{2,66},{3,67},{4,68},{5,69},{6,70},{7,71},{8,72},{9,... | collective-permute-start | bytes 786440 | tf_op jit(solution)/shard_map/kv_reduce/ppermute | solution.py:367
  129.1 11.4 %all-to-all-done.3.arrived_ref = bf16[8,2,128,128]{3,2,1,0:T(8,128)(2,1)S(1)} async-done(((bf16[8,2,128,128]{3,2,1,0:T(8,128)(2,1)}), bf16[8,2,128,128]{3,2,1,0:T(8,128)(2,1)S(1)}, u32[]{:S(2)}, u32[]{:S(2)}) %all-to-all-start.3) | async-done | bytes 524320 | tf_op jit(solution)/shard_map/kv_reduce/all_to_all | solution.py:373
  148.2 3.5 %all-to-all-start.4 = ((bf16[4,16,32,128]{3,2,1,0:T(8,128)(2,1)}), bf16[4,16,32,128]{3,2,1,0:T(8,128)(2,1)S(1)}, u32[]{:S(2)}, u32[]{:S(2)}) async-start(bf16[4,16,32,128]{3,2,1,0:T(8,128)(2,1)} %weight_share.1), calls=%async_computation.4 | async-start | bytes 1048576 | tf_op jit(solution)/shard_map/weight_grad/all_to_all | solution.py:373
  151.7 4.2 %collective-permute-start.14 = (bf16[128,1024]{1,0:T(8,128)(2,1)}, bf16[128,1024]{1,0:T(8,128)(2,1)S(1)}, u32[]{:S(2)}, u32[]{:S(2)}) collective-permute-start(bf16[128,1024]{1,0:T(8,128)(2,1)} %collective-permute-done.13), channel_id=1, source_target_pairs={{0,64},{1,65},{2,66},{3,67},{4,68},{5,69},{6,70},{7,71},{8,72},{9,... | collective-permute-start | bytes 786440 | tf_op jit(solution)/shard_map/weight_grad/ppermute | solution.py:367
  156.0 3.8 %collective-permute-start.15 = (bf16[128,128]{1,0:T(8,128)(2,1)S(1)}, bf16[128,128]{1,0:T(8,128)(2,1)S(1)}, u32[]{:S(2)}, u32[]{:S(2)}) collective-permute-start(bf16[128,128]{1,0:T(8,128)(2,1)S(1)} %select_bitcast_fusion), channel_id=1, source_target_pairs={{0,1},{1,0},{2,3},{3,2},{4,5},{5,4},{6,7},{7,6},{8,9},{9,8},{10,11... | collective-permute-start | bytes 98312 | tf_op jit(solution)/shard_map/input_grad/ppermute | solution.py:353
  162.1 4.3 %all-to-all-done.4.parts_ref = bf16[4,16,32,128]{3,2,1,0:T(8,128)(2,1)S(1)} async-done(((bf16[4,16,32,128]{3,2,1,0:T(8,128)(2,1)}), bf16[4,16,32,128]{3,2,1,0:T(8,128)(2,1)S(1)}, u32[]{:S(2)}, u32[]{:S(2)}) %all-to-all-start.4) | async-done | bytes 524320 | tf_op jit(solution)/shard_map/weight_grad/all_to_all | solution.py:373
  167.1 8.3 %all-to-all-start.5 = ((bf16[16,32,128]{2,1,0:T(8,128)(2,1)}), bf16[16,32,128]{2,1,0:T(8,128)(2,1)S(1)}, u32[]{:S(2)}, u32[]{:S(2)}) async-start(bf16[16,32,128]{2,1,0:T(8,128)(2,1)} %bitcast.18), calls=%async_computation.5 | async-start | bytes 262144 | tf_op jit(solution)/shard_map/weight_grad/all_to_all | solution.py:373
  178.5 4.2 %all-to-all-done.5.parts_ref = bf16[16,32,128]{2,1,0:T(8,128)(2,1)S(1)} async-done(((bf16[16,32,128]{2,1,0:T(8,128)(2,1)}), bf16[16,32,128]{2,1,0:T(8,128)(2,1)S(1)}, u32[]{:S(2)}, u32[]{:S(2)}) %all-to-all-start.5) | async-done | bytes 131104 | tf_op jit(solution)/shard_map/weight_grad/all_to_all | solution.py:373
  183.4 9.8 %all-to-all-start.6 = ((bf16[32,32,128]{2,1,0:T(8,128)(2,1)}), bf16[32,32,128]{2,1,0:T(8,128)(2,1)S(1)}, u32[]{:S(2)}, u32[]{:S(2)}) async-start(bf16[32,32,128]{2,1,0:T(8,128)(2,1)} %group_share.1), calls=%async_computation.6 | async-start | bytes 524288 | tf_op jit(solution)/shard_map/weight_grad/all_to_all | solution.py:373
  197.7 9.0 %all-to-all-done.6 = bf16[32,32,128]{2,1,0:T(8,128)(2,1)S(1)} async-done(((bf16[32,32,128]{2,1,0:T(8,128)(2,1)}), bf16[32,32,128]{2,1,0:T(8,128)(2,1)S(1)}, u32[]{:S(2)}, u32[]{:S(2)}) %all-to-all-start.6) | async-done | bytes 262176 | tf_op jit(solution)/shard_map/weight_grad/all_to_all | solution.py:373
  (101 shorter events, 58.4 us)
Async XLA Ops:
  2.3 12.3 %all-to-all-start = ((bf16[4,256,128]{2,1,0:T(8,128)(2,1)}), bf16[4,256,128]{2,1,0:T(8,128)(2,1)S(1)}, u32[]{:S(2)}, u32[]{:S(2)}) async-start(bf16[4,256,128]{2,1,0:T(8,128)(2,1)} %weight_copies.1), calls=%async_computation | async-start | bytes 524288 | tf_op jit(solution)/shard_map/weight_gather/all_to_all | solution.py:373
  7.9 29.3 %collective-permute-start.1 = (bf16[128,4096]{1,0:T(8,128)(2,1)}, bf16[128,4096]{1,0:T(8,128)(2,1)}, u32[]{:S(2)}, u32[]{:S(2)}) collective-permute-start(bf16[128,4096]{1,0:T(8,128)(2,1)} %bitcast.38), channel_id=1, source_target_pairs={{0,1},{1,0},{2,3},{3,2},{4,5},{5,4},{6,7},{7,6},{8,9},{9,8},{10,11... | collective-permute-start | bytes 3145736 | tf_op jit(solution)/shard_map/rotation/ppermute | solution.py:353
  15.8 21.3 %all-to-all-start.1 = ((bf16[4,4,256,128]{3,2,1,0:T(8,128)(2,1)}), bf16[4,4,256,128]{3,2,1,0:T(8,128)(2,1)S(1)}, u32[]{:S(2)}, u32[]{:S(2)}) async-start(bf16[4,4,256,128]{3,2,1,0:T(8,128)(2,1)} %broadcast_in_dim.8), calls=%async_computation.1 | async-start | bytes 2097152 | tf_op jit(solution)/shard_map/weight_gather/all_to_all | solution.py:373
  20.7 19.8 %collective-permute-start.2 = (bf16[128,1024]{1,0:T(8,128)(2,1)S(1)}, bf16[128,1024]{1,0:T(8,128)(2,1)}, u32[]{:S(2)}, u32[]{:S(2)}) collective-permute-start(bf16[128,1024]{1,0:T(8,128)(2,1)S(1)} %bitcast.44), channel_id=1, source_target_pairs={{0,64},{1,65},{2,66},{3,67},{4,68},{5,69},{6,70},{7,71},{8,72},{9,... | collective-permute-start | bytes 786440 | tf_op jit(solution)/shard_map/weight_gather/ppermute | solution.py:367
  24.0 17.2 %collective-permute-start.3 = (bf16[128,1024]{1,0:T(8,128)(2,1)S(1)}, bf16[128,1024]{1,0:T(8,128)(2,1)}, u32[]{:S(2)}, u32[]{:S(2)}) collective-permute-start(bf16[128,1024]{1,0:T(8,128)(2,1)S(1)} %bitcast.46), channel_id=1, source_target_pairs={{0,80},{1,81},{2,82},{3,83},{4,84},{5,85},{6,86},{7,87},{8,88},{9,... | collective-permute-start | bytes 786440 | tf_op jit(solution)/shard_map/weight_gather/ppermute | solution.py:367
  30.3 6.8 %collective-permute-start = (s32[2]{0:T(128)S(1)}, s32[2]{0:T(128)S(1)}, u32[]{:S(2)}, u32[]{:S(2)}) collective-permute-start(s32[2]{0:T(128)S(1)} %bitcast.48), channel_id=1, source_target_pairs={{0,1},{1,0},{2,3},{3,2},{4,5},{5,4},{6,7},{7,6},{8,9},{9,8},{10,11... | collective-permute-start | bytes 32 | tf_op jit(solution)/shard_map/weight_gather/ppermute | solution.py:353
  41.2 35.4 %collective-permute-start.6 = (bf16[4096,128]{1,0:T(8,128)(2,1)S(1)}, bf16[4096,128]{1,0:T(8,128)(2,1)}, u32[]{:S(2)}, u32[]{:S(2)}) collective-permute-start(bf16[4096,128]{1,0:T(8,128)(2,1)S(1)} %bitcast.33), channel_id=1, source_target_pairs={{0,1},{1,0},{2,3},{3,2},{4,5},{5,4},{6,7},{7,6},{8,9},{9,8},{10,11... | collective-permute-start | bytes 3145736 | tf_op jit(solution)/shard_map/kv_gather/ppermute | solution.py:353
  44.0 32.6 %all-to-all-start.2 = ((bf16[8,2,128,128]{3,2,1,0:T(8,128)(2,1)}), bf16[8,2,128,128]{3,2,1,0:T(8,128)(2,1)S(1)}, u32[]{:S(2)}, u32[]{:S(2)}) async-start(bf16[8,2,128,128]{3,2,1,0:T(8,128)(2,1)} %projection.1), calls=%async_computation.2 | async-start | bytes 1048576 | tf_op jit(solution)/shard_map/kv_gather/all_to_all | solution.py:373
  53.9 18.1 %collective-permute-start.4 = (bf16[128,1024]{1,0:T(8,128)(2,1)}, bf16[128,1024]{1,0:T(8,128)(2,1)}, u32[]{:S(2)}, u32[]{:S(2)}) collective-permute-start(bf16[128,1024]{1,0:T(8,128)(2,1)} %collective-permute-done.2), channel_id=1, source_target_pairs={{0,64},{1,65},{2,66},{3,67},{4,68},{5,69},{6,70},{7,71},{8,72},{9,... | collective-permute-start | bytes 786440 | tf_op jit(solution)/shard_map/kv_gather/ppermute | solution.py:367
  59.4 14.4 %collective-permute-start.5 = (bf16[128,1024]{1,0:T(8,128)(2,1)}, bf16[128,1024]{1,0:T(8,128)(2,1)}, u32[]{:S(2)}, u32[]{:S(2)}) collective-permute-start(bf16[128,1024]{1,0:T(8,128)(2,1)} %collective-permute-done.3), channel_id=1, source_target_pairs={{0,80},{1,81},{2,82},{3,83},{4,84},{5,85},{6,86},{7,87},{8,88},{9,... | collective-permute-start | bytes 786440 | tf_op jit(solution)/shard_map/kv_gather/ppermute | solution.py:367
  76.6 4.1 %collective-permute-start.7 = (bf16[16,128,128]{2,1,0:T(8,128)(2,1)S(1)}, bf16[16,128,128]{2,1,0:T(8,128)(2,1)S(1)}, u32[]{:S(2)}, u32[]{:S(2)}) collective-permute-start(bf16[16,128,128]{2,1,0:T(8,128)(2,1)S(1)} %bitcast.35), channel_id=1, source_target_pairs={{0,1},{1,0},{2,3},{3,2},{4,5},{5,4},{6,7},{7,6},{8,9},{9,8},{10,11... | collective-permute-start | bytes 1572872 | tf_op jit(solution)/shard_map/kv_gather/ppermute | solution.py:353
  86.3 20.7 %collective-permute-start.9 = (bf16[2048,128]{1,0:T(8,128)(2,1)S(1)}, bf16[2048,128]{1,0:T(8,128)(2,1)S(1)}, u32[]{:S(2)}, u32[]{:S(2)}) collective-permute-start(bf16[2048,128]{1,0:T(8,128)(2,1)S(1)} %copy-done.23), channel_id=1, source_target_pairs={{0,2},{1,3},{2,0},{3,1},{4,6},{5,7},{6,4},{7,5},{8,10},{9,11},{10,... | collective-permute-start | bytes 1572872 | tf_op jit(solution)/shard_map/attention/ppermute | solution.py:370
  88.2 8.6 %collective-permute-start.8 = (f32[2,3,1024]{2,1,0:T(4,128)S(1)}, f32[2,3,1024]{2,1,0:T(4,128)S(1)}, u32[]{:S(2)}, u32[]{:S(2)}) collective-permute-start(f32[2,3,1024]{2,1,0:T(4,128)S(1)} %attention_totals.1.own_ref), channel_id=1, source_target_pairs={{0,16},{1,17},{2,18},{3,19},{4,20},{5,21},{6,22},{7,23},{8,24},{9,... | collective-permute-start | bytes 73736 | tf_op jit(solution)/shard_map/attention/ppermute | solution.py:356
  106.9 38.8 %copy-start.4 = (bf16[2048,128]{1,0:T(8,128)(2,1)S(1)}, bf16[2048,128]{1,0:T(8,128)(2,1)}, u32[]{:S(2)}) copy-start(bf16[2048,128]{1,0:T(8,128)(2,1)} %copy-done.3) | copy-start | bytes 1572868
  107.0 3.9 %collective-permute-start.10 = (bf16[16,128,128]{2,1,0:T(8,128)(2,1)S(1)}, bf16[16,128,128]{2,1,0:T(8,128)(2,1)S(1)}, u32[]{:S(2)}, u32[]{:S(2)}) collective-permute-start(bf16[16,128,128]{2,1,0:T(8,128)(2,1)S(1)} %get-tuple-element.104), channel_id=1, source_target_pairs={{0,1},{1,0},{2,3},{3,2},{4,5},{5,4},{6,7},{7,6},{8,9},{9,8},{10,11... | collective-permute-start | bytes 1572872 | tf_op jit(solution)/shard_map/kv_reduce/ppermute | solution.py:353
  111.8 28.7 %all-to-all-start.3 = ((bf16[8,2,128,128]{3,2,1,0:T(8,128)(2,1)}), bf16[8,2,128,128]{3,2,1,0:T(8,128)(2,1)S(1)}, u32[]{:S(2)}, u32[]{:S(2)}) async-start(bf16[8,2,128,128]{3,2,1,0:T(8,128)(2,1)} %bitcast.50), calls=%async_computation.3 | async-start | bytes 1048576 | tf_op jit(solution)/shard_map/kv_reduce/all_to_all | solution.py:373
  122.6 20.0 %collective-permute-start.12 = (bf16[2048,128]{1,0:T(8,128)(2,1)}, bf16[2048,128]{1,0:T(8,128)(2,1)}, u32[]{:S(2)}, u32[]{:S(2)}) collective-permute-start(bf16[2048,128]{1,0:T(8,128)(2,1)} %copy-done.5), channel_id=1, source_target_pairs={{0,1},{1,0},{2,3},{3,2},{4,5},{5,4},{6,7},{7,6},{8,9},{9,8},{10,11... | collective-permute-start | bytes 1572872 | tf_op jit(solution)/shard_map/kv_reduce/ppermute | solution.py:353
  125.2 17.5 %collective-permute-start.13 = (bf16[128,1024]{1,0:T(8,128)(2,1)}, bf16[128,1024]{1,0:T(8,128)(2,1)}, u32[]{:S(2)}, u32[]{:S(2)}) collective-permute-start(bf16[128,1024]{1,0:T(8,128)(2,1)} %copy-done.24), channel_id=1, source_target_pairs={{0,64},{1,65},{2,66},{3,67},{4,68},{5,69},{6,70},{7,71},{8,72},{9,... | collective-permute-start | bytes 786440 | tf_op jit(solution)/shard_map/kv_reduce/ppermute | solution.py:367
  140.7 5.0 %collective-permute-start.11 = (bf16[2,128,128]{2,1,0:T(8,128)(2,1)S(1)}, bf16[2,128,128]{2,1,0:T(8,128)(2,1)S(1)}, u32[]{:S(2)}, u32[]{:S(2)}) collective-permute-start(bf16[2,128,128]{2,1,0:T(8,128)(2,1)S(1)} %bitcast.41), channel_id=1, source_target_pairs={{0,2},{1,3},{2,0},{3,1},{4,6},{5,7},{6,4},{7,5},{8,10},{9,11},{10,... | collective-permute-start | bytes 196616 | tf_op jit(solution)/shard_map/weight_grad/ppermute | solution.py:370
  148.2 18.2 %all-to-all-start.4 = ((bf16[4,16,32,128]{3,2,1,0:T(8,128)(2,1)}), bf16[4,16,32,128]{3,2,1,0:T(8,128)(2,1)S(1)}, u32[]{:S(2)}, u32[]{:S(2)}) async-start(bf16[4,16,32,128]{3,2,1,0:T(8,128)(2,1)} %weight_share.1), calls=%async_computation.4 | async-start | bytes 1048576 | tf_op jit(solution)/shard_map/weight_grad/all_to_all | solution.py:373
  151.7 10.4 %collective-permute-start.14 = (bf16[128,1024]{1,0:T(8,128)(2,1)}, bf16[128,1024]{1,0:T(8,128)(2,1)S(1)}, u32[]{:S(2)}, u32[]{:S(2)}) collective-permute-start(bf16[128,1024]{1,0:T(8,128)(2,1)} %collective-permute-done.13), channel_id=1, source_target_pairs={{0,64},{1,65},{2,66},{3,67},{4,68},{5,69},{6,70},{7,71},{8,72},{9,... | collective-permute-start | bytes 786440 | tf_op jit(solution)/shard_map/weight_grad/ppermute | solution.py:367
  156.0 19.5 %collective-permute-start.15 = (bf16[128,128]{1,0:T(8,128)(2,1)S(1)}, bf16[128,128]{1,0:T(8,128)(2,1)S(1)}, u32[]{:S(2)}, u32[]{:S(2)}) collective-permute-start(bf16[128,128]{1,0:T(8,128)(2,1)S(1)} %select_bitcast_fusion), channel_id=1, source_target_pairs={{0,1},{1,0},{2,3},{3,2},{4,5},{5,4},{6,7},{7,6},{8,9},{9,8},{10,11... | collective-permute-start | bytes 98312 | tf_op jit(solution)/shard_map/input_grad/ppermute | solution.py:353
  167.1 15.6 %all-to-all-start.5 = ((bf16[16,32,128]{2,1,0:T(8,128)(2,1)}), bf16[16,32,128]{2,1,0:T(8,128)(2,1)S(1)}, u32[]{:S(2)}, u32[]{:S(2)}) async-start(bf16[16,32,128]{2,1,0:T(8,128)(2,1)} %bitcast.18), calls=%async_computation.5 | async-start | bytes 262144 | tf_op jit(solution)/shard_map/weight_grad/all_to_all | solution.py:373
  183.4 23.2 %all-to-all-start.6 = ((bf16[32,32,128]{2,1,0:T(8,128)(2,1)}), bf16[32,32,128]{2,1,0:T(8,128)(2,1)S(1)}, u32[]{:S(2)}, u32[]{:S(2)}) async-start(bf16[32,32,128]{2,1,0:T(8,128)(2,1)} %group_share.1), calls=%async_computation.6 | async-start | bytes 524288 | tf_op jit(solution)/shard_map/weight_grad/all_to_all | solution.py:373
  (26 other events, 333.2 us)

commit v11 on v10

--- a/solution.py
+++ b/solution.py
@@ -439,10 +439,8 @@
         cross_forms = local_call(
             query_kernel, query_shapes, (), (q_cross, g_cross), "cross_query_forms"
         )
-        near, own_forms, cross_forms, own_half, given_half, far_half, far_weight = (
-            lax.optimization_barrier(
-                (near, own_forms, cross_forms, own_half, given_half, far_half, far_weight)
-            )
+        near, own_forms, cross_forms, own_half, given_half, far_half = lax.optimization_barrier(
+            (near, own_forms, cross_forms, own_half, given_half, far_half)
         )
         far = swapped(near)
     with jax.named_scope("attention"):

time: 211 us -> 209 us (level)
  Pallas kernels: 29.7 us -> 20.7 us
  starting transfers between devices: 111 us -> 120 us
    pallas_call x13, Pallas kernels: 28.2 us -> 19.1 us  [local_call(): pl.pallas_call(kernel, out_shape=shapes, in_specs=[smem] * len(scalars) +...]
    ppermute x2, starting transfers between devices: 3.84 us -> 10.4 us  [passed(): return lax.ppermute(value, 'seq', beside)]
    ppermute x7, starting transfers between devices: 26.6 us -> 33 us  [swapped(): return lax.ppermute(value, 'seq', swap)]
    all_to_all x7, waiting for transfers between devices: 29 us -> 25 us  [exchanged(): return lax.all_to_all(value, axis, 0, 0, axis_index_groups=groups)]
    ppermute x1, waiting for transfers between devices: 3.25 us -> 6.08 us  [crossed(): return lax.ppermute(value, 'seq', cross)]
    ppermute x1, starting transfers between devices: 5.31 us -> 2.83 us  [crossed(): return lax.ppermute(value, 'seq', cross)]
  transfers between devices with their start and end apart: 23 -> 23, of which waited for: 13 -> 13; matrix products, arithmetic and copies ran while one was open for 5% -> 5% of each run, Pallas kernels for 9% -> 8%
where the time goes in v11:
time: 209 us; the launch traced here: 206 us
  starting transfers between devices  120 us (57%)
  waiting for transfers between devices  47.4 us (23%)
  Pallas kernels  20.7 us (10%)
  local copies, waits for them, and re-layouts  7.68 us (4%)
  matrix products  6.08 us (3%)
  other arithmetic  3.03 us (1%)
    all_to_all x7, starting transfers between devices, exchanged(): return lax.all_to_all(value, axis, 0, 0, axis_index_groups=groups)  50.5 us
    ppermute x7, starting transfers between devices, swapped(): return lax.ppermute(value, 'seq', swap)  33 us
    all_to_all x7, waiting for transfers between devices, exchanged(): return lax.all_to_all(value, axis, 0, 0, axis_index_groups=groups)  25 us
    ppermute x6, starting transfers between devices, moved(): return lax.ppermute(value, ('dp', 'seq'), pairs)  23.2 us
    pallas_call x13, Pallas kernels, local_call(): pl.pallas_call(kernel, out_shape=shapes, in_specs=[smem] * len(scalars) +...  19.1 us
    ppermute x2, starting transfers between devices, passed(): return lax.ppermute(value, 'seq', beside)  10.4 us
    ppermute x6, waiting for transfers between devices, moved(): return lax.ppermute(value, ('dp', 'seq'), pairs)  9.44 us
    unnamed x54, local copies, waits for them, and re-layouts  6.51 us
  transfers between devices with their start and end apart: 23, of which 13 were waited for; matrix products, arithmetic and copies ran while one was open for 5% of the time, Pallas kernels for 8%

profile of v11, /device:TPU:1, one launch (start us, length us, event | category | flops | bytes accessed | tf_op | source)
XLA Modules:
  0.0 205.9 jit_solution(11913382459448592873)
XLA Ops:
  2.3 5.6 %all-to-all-start = ((bf16[4,256,128]{2,1,0:T(8,128)(2,1)}), bf16[4,256,128]{2,1,0:T(8,128)(2,1)S(1)}, u32[]{:S(2)}, u32[]{:S(2)}) async-start(bf16[4,256,128]{2,1,0:T(8,128)(2,1)} %weight_copies.1), calls=%async_computation | async-start | bytes 524288 | tf_op jit(solution)/shard_map/weight_gather/all_to_all | solution.py:373
  7.9 6.8 %collective-permute-start.1 = (bf16[128,4096]{1,0:T(8,128)(2,1)}, bf16[128,4096]{1,0:T(8,128)(2,1)}, u32[]{:S(2)}, u32[]{:S(2)}) collective-permute-start(bf16[128,4096]{1,0:T(8,128)(2,1)} %bitcast.38), channel_id=1, source_target_pairs={{0,1},{1,0},{2,3},{3,2},{4,5},{5,4},{6,7},{7,6},{8,9},{9,8},{10,11... | collective-permute-start | bytes 3145736 | tf_op jit(solution)/shard_map/rotation/ppermute | solution.py:353
  15.8 4.8 %all-to-all-start.1 = ((bf16[4,4,256,128]{3,2,1,0:T(8,128)(2,1)}), bf16[4,4,256,128]{3,2,1,0:T(8,128)(2,1)S(1)}, u32[]{:S(2)}, u32[]{:S(2)}) async-start(bf16[4,4,256,128]{3,2,1,0:T(8,128)(2,1)} %broadcast_in_dim.8), calls=%async_computation.1 | async-start | bytes 2097152 | tf_op jit(solution)/shard_map/weight_gather/all_to_all | solution.py:373
  24.0 4.1 %collective-permute-start.3 = (bf16[128,1024]{1,0:T(8,128)(2,1)S(1)}, bf16[128,1024]{1,0:T(8,128)(2,1)}, u32[]{:S(2)}, u32[]{:S(2)}) collective-permute-start(bf16[128,1024]{1,0:T(8,128)(2,1)S(1)} %bitcast.46), channel_id=1, source_target_pairs={{0,80},{1,81},{2,82},{3,83},{4,84},{5,85},{6,86},{7,87},{8,88},{9,... | collective-permute-start | bytes 786440 | tf_op jit(solution)/shard_map/weight_gather/ppermute | solution.py:367
  30.3 6.0 %collective-permute-start = (s32[2]{0:T(128)S(1)}, s32[2]{0:T(128)S(1)}, u32[]{:S(2)}, u32[]{:S(2)}) collective-permute-start(s32[2]{0:T(128)S(1)} %bitcast.48), channel_id=1, source_target_pairs={{0,1},{1,0},{2,3},{3,2},{4,5},{5,4},{6,7},{7,6},{8,9},{9,8},{10,11... | collective-permute-start | bytes 32 | tf_op jit(solution)/shard_map/weight_gather/ppermute | solution.py:353
  37.2 3.3 %projection.1 = bf16[8,2,128,128]{3,2,1,0:T(8,128)(2,1)} custom-call(s32[1]{0:T(128)} %bitcast.core_ref, s32[2]{0:T(128)S(1)} %bitcast.49, s32[2]{0:T(128)S(1)} %collective-permute-done.far_bits_ref, bf16[128,4096]{1,0:T(8,128)(2,1)S(1)} %bitcast.39, bf16[128,4096]{1,0:T(8,128)(2,1)} %collective-permute-done.1.far_ref.x_ref, bf16[4096,128]{1,0:T(8,128)(2,1)S(1)} %bitcast.32, ...), custom_call_target="tpu_custom_call" | custom-call | tf_op jit(solution)/shard_map/projection/projection/pallas_call | solution.py:222
  41.2 10.3 %all-to-all-start.2 = ((bf16[8,2,128,128]{3,2,1,0:T(8,128)(2,1)}), bf16[8,2,128,128]{3,2,1,0:T(8,128)(2,1)S(1)}, u32[]{:S(2)}, u32[]{:S(2)}) async-start(bf16[8,2,128,128]{3,2,1,0:T(8,128)(2,1)} %projection.1), calls=%async_computation.2 | async-start | bytes 1048576 | tf_op jit(solution)/shard_map/kv_gather/all_to_all | solution.py:373
  51.5 4.0 %collective-permute-start.4 = (bf16[128,1024]{1,0:T(8,128)(2,1)}, bf16[128,1024]{1,0:T(8,128)(2,1)}, u32[]{:S(2)}, u32[]{:S(2)}) collective-permute-start(bf16[128,1024]{1,0:T(8,128)(2,1)} %collective-permute-done.2), channel_id=1, source_target_pairs={{0,64},{1,65},{2,66},{3,67},{4,68},{5,69},{6,70},{7,71},{8,72},{9,... | collective-permute-start | bytes 786440 | tf_op jit(solution)/shard_map/kv_gather/ppermute | solution.py:367
  55.5 3.4 %collective-permute-start.5 = (bf16[128,1024]{1,0:T(8,128)(2,1)}, bf16[128,1024]{1,0:T(8,128)(2,1)}, u32[]{:S(2)}, u32[]{:S(2)}) collective-permute-start(bf16[128,1024]{1,0:T(8,128)(2,1)} %collective-permute-done.3), channel_id=1, source_target_pairs={{0,80},{1,81},{2,82},{3,83},{4,84},{5,85},{6,86},{7,87},{8,88},{9,... | collective-permute-start | bytes 786440 | tf_op jit(solution)/shard_map/kv_gather/ppermute | solution.py:367
  79.4 8.5 %collective-permute-start.8 = (bf16[2048,128]{1,0:T(8,128)(2,1)S(1)}, bf16[2048,128]{1,0:T(8,128)(2,1)S(1)}, u32[]{:S(2)}, u32[]{:S(2)}) collective-permute-start(bf16[2048,128]{1,0:T(8,128)(2,1)S(1)} %copy-done.23), channel_id=1, source_target_pairs={{0,2},{1,3},{2,0},{3,1},{4,6},{5,7},{6,4},{7,5},{8,10},{9,11},{10,... | collective-permute-start | bytes 1572872 | tf_op jit(solution)/shard_map/attention/ppermute | solution.py:370
  90.7 6.1 %collective-permute-done.7.other_ref = f32[2,3,1024]{2,1,0:T(4,128)S(1)} collective-permute-done((f32[2,3,1024]{2,1,0:T(4,128)S(1)}, f32[2,3,1024]{2,1,0:T(4,128)S(1)}, u32[]{:S(2)}, u32[]{:S(2)}) %collective-permute-start.7) | collective-permute-done | bytes 24608 | tf_op jit(solution)/shard_map/attention/ppermute | solution.py:356
  96.8 4.4 %attention_grads.1 = (f32[128,1024]{1,0:T(8,128)S(1)}, bf16[128,1024]{1,0:T(8,128)(2,1)S(1)}, bf16[16,128,128]{2,1,0:T(8,128)(2,1)S(1)}, bf16[16,128,128]{2,1,0:T(8,128)(2,1)S(1)}) custom-call(s32[36]{0:T(128)S(1)} %copy-done.20, s32[1]{0:T(128)} %bitcast.core_ref, bf16[16,128,128]{2,1,0:T(8,128)(2,1)S(1)} %bitcast.37, ...), custom_call_target="tpu_custom_call" | custom-call | tf_op jit(solution)/shard_map/attention/attention_grads/pallas_call | solution.py:222
  101.3 9.0 %collective-permute-start.9 = (bf16[16,128,128]{2,1,0:T(8,128)(2,1)S(1)}, bf16[16,128,128]{2,1,0:T(8,128)(2,1)S(1)}, u32[]{:S(2)}, u32[]{:S(2)}) collective-permute-start(bf16[16,128,128]{2,1,0:T(8,128)(2,1)S(1)} %get-tuple-element.102), channel_id=1, source_target_pairs={{0,1},{1,0},{2,3},{3,2},{4,5},{5,4},{6,7},{7,6},{8,9},{9,8},{10,11... | collective-permute-start | bytes 1572872 | tf_op jit(solution)/shard_map/kv_reduce/ppermute | solution.py:353
  112.7 7.1 %all-to-all-start.3 = ((bf16[8,2,128,128]{3,2,1,0:T(8,128)(2,1)}), bf16[8,2,128,128]{3,2,1,0:T(8,128)(2,1)S(1)}, u32[]{:S(2)}, u32[]{:S(2)}) async-start(bf16[8,2,128,128]{3,2,1,0:T(8,128)(2,1)} %bitcast.50), calls=%async_computation.3 | async-start | bytes 1048576 | tf_op jit(solution)/shard_map/kv_reduce/all_to_all | solution.py:373
  122.4 4.1 %collective-permute-start.12 = (bf16[128,1024]{1,0:T(8,128)(2,1)}, bf16[128,1024]{1,0:T(8,128)(2,1)}, u32[]{:S(2)}, u32[]{:S(2)}) collective-permute-start(bf16[128,1024]{1,0:T(8,128)(2,1)} %copy-done.24), channel_id=1, source_target_pairs={{0,64},{1,65},{2,66},{3,67},{4,68},{5,69},{6,70},{7,71},{8,72},{9,... | collective-permute-start | bytes 786440 | tf_op jit(solution)/shard_map/kv_reduce/ppermute | solution.py:367
  128.8 9.0 %all-to-all-done.3.arrived_ref = bf16[8,2,128,128]{3,2,1,0:T(8,128)(2,1)S(1)} async-done(((bf16[8,2,128,128]{3,2,1,0:T(8,128)(2,1)}), bf16[8,2,128,128]{3,2,1,0:T(8,128)(2,1)S(1)}, u32[]{:S(2)}, u32[]{:S(2)}) %all-to-all-start.3) | async-done | bytes 524320 | tf_op jit(solution)/shard_map/kv_reduce/all_to_all | solution.py:373
  145.5 3.5 %all-to-all-start.4 = ((bf16[4,16,32,128]{3,2,1,0:T(8,128)(2,1)}), bf16[4,16,32,128]{3,2,1,0:T(8,128)(2,1)S(1)}, u32[]{:S(2)}, u32[]{:S(2)}) async-start(bf16[4,16,32,128]{3,2,1,0:T(8,128)(2,1)} %weight_share.1), calls=%async_computation.4 | async-start | bytes 1048576 | tf_op jit(solution)/shard_map/weight_grad/all_to_all | solution.py:373
  149.0 4.3 %collective-permute-start.13 = (bf16[128,1024]{1,0:T(8,128)(2,1)}, bf16[128,1024]{1,0:T(8,128)(2,1)S(1)}, u32[]{:S(2)}, u32[]{:S(2)}) collective-permute-start(bf16[128,1024]{1,0:T(8,128)(2,1)} %collective-permute-done.12), channel_id=1, source_target_pairs={{0,64},{1,65},{2,66},{3,67},{4,68},{5,69},{6,70},{7,71},{8,72},{9,... | collective-permute-start | bytes 786440 | tf_op jit(solution)/shard_map/weight_grad/ppermute | solution.py:367
  153.3 3.8 %collective-permute-start.14 = (bf16[128,128]{1,0:T(8,128)(2,1)S(1)}, bf16[128,128]{1,0:T(8,128)(2,1)S(1)}, u32[]{:S(2)}, u32[]{:S(2)}) collective-permute-start(bf16[128,128]{1,0:T(8,128)(2,1)S(1)} %select_bitcast_fusion), channel_id=1, source_target_pairs={{0,1},{1,0},{2,3},{3,2},{4,5},{5,4},{6,7},{7,6},{8,9},{9,8},{10,11... | collective-permute-start | bytes 98312 | tf_op jit(solution)/shard_map/input_grad/ppermute | solution.py:353
  157.2 3.7 %collective-permute-done.13 = bf16[128,1024]{1,0:T(8,128)(2,1)S(1)} collective-permute-done((bf16[128,1024]{1,0:T(8,128)(2,1)}, bf16[128,1024]{1,0:T(8,128)(2,1)S(1)}, u32[]{:S(2)}, u32[]{:S(2)}) %collective-permute-start.13) | collective-permute-done | bytes 262176 | tf_op jit(solution)/shard_map/weight_grad/ppermute | solution.py:367
  164.4 8.9 %all-to-all-start.5 = ((bf16[16,32,128]{2,1,0:T(8,128)(2,1)}), bf16[16,32,128]{2,1,0:T(8,128)(2,1)S(1)}, u32[]{:S(2)}, u32[]{:S(2)}) async-start(bf16[16,32,128]{2,1,0:T(8,128)(2,1)} %bitcast.18), calls=%async_computation.5 | async-start | bytes 262144 | tf_op jit(solution)/shard_map/weight_grad/all_to_all | solution.py:373
  176.4 4.2 %all-to-all-done.5.parts_ref = bf16[16,32,128]{2,1,0:T(8,128)(2,1)S(1)} async-done(((bf16[16,32,128]{2,1,0:T(8,128)(2,1)}), bf16[16,32,128]{2,1,0:T(8,128)(2,1)S(1)}, u32[]{:S(2)}, u32[]{:S(2)}) %all-to-all-start.5) | async-done | bytes 131104 | tf_op jit(solution)/shard_map/weight_grad/all_to_all | solution.py:373
  181.3 10.4 %all-to-all-start.6 = ((bf16[32,32,128]{2,1,0:T(8,128)(2,1)}), bf16[32,32,128]{2,1,0:T(8,128)(2,1)S(1)}, u32[]{:S(2)}, u32[]{:S(2)}) async-start(bf16[32,32,128]{2,1,0:T(8,128)(2,1)} %group_share.1), calls=%async_computation.6 | async-start | bytes 524288 | tf_op jit(solution)/shard_map/weight_grad/all_to_all | solution.py:373
  196.2 9.0 %all-to-all-done.6 = bf16[32,32,128]{2,1,0:T(8,128)(2,1)S(1)} async-done(((bf16[32,32,128]{2,1,0:T(8,128)(2,1)}), bf16[32,32,128]{2,1,0:T(8,128)(2,1)S(1)}, u32[]{:S(2)}, u32[]{:S(2)}) %all-to-all-start.6) | async-done | bytes 262176 | tf_op jit(solution)/shard_map/weight_grad/all_to_all | solution.py:373
  (101 shorter events, 60.5 us)
Async XLA Ops:
  2.3 12.3 %all-to-all-start = ((bf16[4,256,128]{2,1,0:T(8,128)(2,1)}), bf16[4,256,128]{2,1,0:T(8,128)(2,1)S(1)}, u32[]{:S(2)}, u32[]{:S(2)}) async-start(bf16[4,256,128]{2,1,0:T(8,128)(2,1)} %weight_copies.1), calls=%async_computation | async-start | bytes 524288 | tf_op jit(solution)/shard_map/weight_gather/all_to_all | solution.py:373
  7.9 29.3 %collective-permute-start.1 = (bf16[128,4096]{1,0:T(8,128)(2,1)}, bf16[128,4096]{1,0:T(8,128)(2,1)}, u32[]{:S(2)}, u32[]{:S(2)}) collective-permute-start(bf16[128,4096]{1,0:T(8,128)(2,1)} %bitcast.38), channel_id=1, source_target_pairs={{0,1},{1,0},{2,3},{3,2},{4,5},{5,4},{6,7},{7,6},{8,9},{9,8},{10,11... | collective-permute-start | bytes 3145736 | tf_op jit(solution)/shard_map/rotation/ppermute | solution.py:353
  15.8 21.3 %all-to-all-start.1 = ((bf16[4,4,256,128]{3,2,1,0:T(8,128)(2,1)}), bf16[4,4,256,128]{3,2,1,0:T(8,128)(2,1)S(1)}, u32[]{:S(2)}, u32[]{:S(2)}) async-start(bf16[4,4,256,128]{3,2,1,0:T(8,128)(2,1)} %broadcast_in_dim.8), calls=%async_computation.1 | async-start | bytes 2097152 | tf_op jit(solution)/shard_map/weight_gather/all_to_all | solution.py:373
  20.7 19.8 %collective-permute-start.2 = (bf16[128,1024]{1,0:T(8,128)(2,1)S(1)}, bf16[128,1024]{1,0:T(8,128)(2,1)}, u32[]{:S(2)}, u32[]{:S(2)}) collective-permute-start(bf16[128,1024]{1,0:T(8,128)(2,1)S(1)} %bitcast.44), channel_id=1, source_target_pairs={{0,64},{1,65},{2,66},{3,67},{4,68},{5,69},{6,70},{7,71},{8,72},{9,... | collective-permute-start | bytes 786440 | tf_op jit(solution)/shard_map/weight_gather/ppermute | solution.py:367
  24.0 17.2 %collective-permute-start.3 = (bf16[128,1024]{1,0:T(8,128)(2,1)S(1)}, bf16[128,1024]{1,0:T(8,128)(2,1)}, u32[]{:S(2)}, u32[]{:S(2)}) collective-permute-start(bf16[128,1024]{1,0:T(8,128)(2,1)S(1)} %bitcast.46), channel_id=1, source_target_pairs={{0,80},{1,81},{2,82},{3,83},{4,84},{5,85},{6,86},{7,87},{8,88},{9,... | collective-permute-start | bytes 786440 | tf_op jit(solution)/shard_map/weight_gather/ppermute | solution.py:367
  30.3 6.8 %collective-permute-start = (s32[2]{0:T(128)S(1)}, s32[2]{0:T(128)S(1)}, u32[]{:S(2)}, u32[]{:S(2)}) collective-permute-start(s32[2]{0:T(128)S(1)} %bitcast.48), channel_id=1, source_target_pairs={{0,1},{1,0},{2,3},{3,2},{4,5},{5,4},{6,7},{7,6},{8,9},{9,8},{10,11... | collective-permute-start | bytes 32 | tf_op jit(solution)/shard_map/weight_gather/ppermute | solution.py:353
  41.2 31.8 %all-to-all-start.2 = ((bf16[8,2,128,128]{3,2,1,0:T(8,128)(2,1)}), bf16[8,2,128,128]{3,2,1,0:T(8,128)(2,1)S(1)}, u32[]{:S(2)}, u32[]{:S(2)}) async-start(bf16[8,2,128,128]{3,2,1,0:T(8,128)(2,1)} %projection.1), calls=%async_computation.2 | async-start | bytes 1048576 | tf_op jit(solution)/shard_map/kv_gather/all_to_all | solution.py:373
  51.5 15.7 %collective-permute-start.4 = (bf16[128,1024]{1,0:T(8,128)(2,1)}, bf16[128,1024]{1,0:T(8,128)(2,1)}, u32[]{:S(2)}, u32[]{:S(2)}) collective-permute-start(bf16[128,1024]{1,0:T(8,128)(2,1)} %collective-permute-done.2), channel_id=1, source_target_pairs={{0,64},{1,65},{2,66},{3,67},{4,68},{5,69},{6,70},{7,71},{8,72},{9,... | collective-permute-start | bytes 786440 | tf_op jit(solution)/shard_map/kv_gather/ppermute | solution.py:367
  55.5 14.8 %collective-permute-start.5 = (bf16[128,1024]{1,0:T(8,128)(2,1)}, bf16[128,1024]{1,0:T(8,128)(2,1)}, u32[]{:S(2)}, u32[]{:S(2)}) collective-permute-start(bf16[128,1024]{1,0:T(8,128)(2,1)} %collective-permute-done.3), channel_id=1, source_target_pairs={{0,80},{1,81},{2,82},{3,83},{4,84},{5,85},{6,86},{7,87},{8,88},{9,... | collective-permute-start | bytes 786440 | tf_op jit(solution)/shard_map/kv_gather/ppermute | solution.py:367
  73.1 4.1 %collective-permute-start.6 = (bf16[16,128,128]{2,1,0:T(8,128)(2,1)S(1)}, bf16[16,128,128]{2,1,0:T(8,128)(2,1)S(1)}, u32[]{:S(2)}, u32[]{:S(2)}) collective-permute-start(bf16[16,128,128]{2,1,0:T(8,128)(2,1)S(1)} %bitcast.35), channel_id=1, source_target_pairs={{0,1},{1,0},{2,3},{3,2},{4,5},{5,4},{6,7},{7,6},{8,9},{9,8},{10,11... | collective-permute-start | bytes 1572872 | tf_op jit(solution)/shard_map/kv_gather/ppermute | solution.py:353
  79.4 21.8 %collective-permute-start.8 = (bf16[2048,128]{1,0:T(8,128)(2,1)S(1)}, bf16[2048,128]{1,0:T(8,128)(2,1)S(1)}, u32[]{:S(2)}, u32[]{:S(2)}) collective-permute-start(bf16[2048,128]{1,0:T(8,128)(2,1)S(1)} %copy-done.23), channel_id=1, source_target_pairs={{0,2},{1,3},{2,0},{3,1},{4,6},{5,7},{6,4},{7,5},{8,10},{9,11},{10,... | collective-permute-start | bytes 1572872 | tf_op jit(solution)/shard_map/attention/ppermute | solution.py:370
  87.9 8.9 %collective-permute-start.7 = (f32[2,3,1024]{2,1,0:T(4,128)S(1)}, f32[2,3,1024]{2,1,0:T(4,128)S(1)}, u32[]{:S(2)}, u32[]{:S(2)}) collective-permute-start(f32[2,3,1024]{2,1,0:T(4,128)S(1)} %attention_totals.1.own_ref), channel_id=1, source_target_pairs={{0,16},{1,17},{2,18},{3,19},{4,20},{5,21},{6,22},{7,23},{8,24},{9,... | collective-permute-start | bytes 73736 | tf_op jit(solution)/shard_map/attention/ppermute | solution.py:356
  101.2 41.7 %copy-start.4 = (bf16[2048,128]{1,0:T(8,128)(2,1)S(1)}, bf16[2048,128]{1,0:T(8,128)(2,1)}, u32[]{:S(2)}) copy-start(bf16[2048,128]{1,0:T(8,128)(2,1)} %copy-done.3) | copy-start | bytes 1572868
  101.3 10.5 %collective-permute-start.9 = (bf16[16,128,128]{2,1,0:T(8,128)(2,1)S(1)}, bf16[16,128,128]{2,1,0:T(8,128)(2,1)S(1)}, u32[]{:S(2)}, u32[]{:S(2)}) collective-permute-start(bf16[16,128,128]{2,1,0:T(8,128)(2,1)S(1)} %get-tuple-element.102), channel_id=1, source_target_pairs={{0,1},{1,0},{2,3},{3,2},{4,5},{5,4},{6,7},{7,6},{8,9},{9,8},{10,11... | collective-permute-start | bytes 1572872 | tf_op jit(solution)/shard_map/kv_reduce/ppermute | solution.py:353
  112.7 25.1 %all-to-all-start.3 = ((bf16[8,2,128,128]{3,2,1,0:T(8,128)(2,1)}), bf16[8,2,128,128]{3,2,1,0:T(8,128)(2,1)S(1)}, u32[]{:S(2)}, u32[]{:S(2)}) async-start(bf16[8,2,128,128]{3,2,1,0:T(8,128)(2,1)} %bitcast.50), calls=%async_computation.3 | async-start | bytes 1048576 | tf_op jit(solution)/shard_map/kv_reduce/all_to_all | solution.py:373
  119.9 20.0 %collective-permute-start.11 = (bf16[2048,128]{1,0:T(8,128)(2,1)}, bf16[2048,128]{1,0:T(8,128)(2,1)}, u32[]{:S(2)}, u32[]{:S(2)}) collective-permute-start(bf16[2048,128]{1,0:T(8,128)(2,1)} %copy-done.5), channel_id=1, source_target_pairs={{0,1},{1,0},{2,3},{3,2},{4,5},{5,4},{6,7},{7,6},{8,9},{9,8},{10,11... | collective-permute-start | bytes 1572872 | tf_op jit(solution)/shard_map/kv_reduce/ppermute | solution.py:353
  122.4 17.5 %collective-permute-start.12 = (bf16[128,1024]{1,0:T(8,128)(2,1)}, bf16[128,1024]{1,0:T(8,128)(2,1)}, u32[]{:S(2)}, u32[]{:S(2)}) collective-permute-start(bf16[128,1024]{1,0:T(8,128)(2,1)} %copy-done.24), channel_id=1, source_target_pairs={{0,64},{1,65},{2,66},{3,67},{4,68},{5,69},{6,70},{7,71},{8,72},{9,... | collective-permute-start | bytes 786440 | tf_op jit(solution)/shard_map/kv_reduce/ppermute | solution.py:367
  126.5 46.8 %collective-permute-start.15 = (bf16[4096,128]{1,0:T(8,128)(2,1)S(1)}, bf16[4096,128]{1,0:T(8,128)(2,1)}, u32[]{:S(2)}, u32[]{:S(2)}) collective-permute-start(bf16[4096,128]{1,0:T(8,128)(2,1)S(1)} %bitcast.33), channel_id=1, source_target_pairs={{0,1},{1,0},{2,3},{3,2},{4,5},{5,4},{6,7},{7,6},{8,9},{9,8},{10,11... | collective-permute-start | bytes 3145736 | tf_op jit(solution)/shard_map/kv_gather/ppermute | solution.py:353
  138.0 5.0 %collective-permute-start.10 = (bf16[2,128,128]{2,1,0:T(8,128)(2,1)S(1)}, bf16[2,128,128]{2,1,0:T(8,128)(2,1)S(1)}, u32[]{:S(2)}, u32[]{:S(2)}) collective-permute-start(bf16[2,128,128]{2,1,0:T(8,128)(2,1)S(1)} %bitcast.41), channel_id=1, source_target_pairs={{0,2},{1,3},{2,0},{3,1},{4,6},{5,7},{6,4},{7,5},{8,10},{9,11},{10,... | collective-permute-start | bytes 196616 | tf_op jit(solution)/shard_map/weight_grad/ppermute | solution.py:370
  145.5 18.2 %all-to-all-start.4 = ((bf16[4,16,32,128]{3,2,1,0:T(8,128)(2,1)}), bf16[4,16,32,128]{3,2,1,0:T(8,128)(2,1)S(1)}, u32[]{:S(2)}, u32[]{:S(2)}) async-start(bf16[4,16,32,128]{3,2,1,0:T(8,128)(2,1)} %weight_share.1), calls=%async_computation.4 | async-start | bytes 1048576 | tf_op jit(solution)/shard_map/weight_grad/all_to_all | solution.py:373
  149.0 11.9 %collective-permute-start.13 = (bf16[128,1024]{1,0:T(8,128)(2,1)}, bf16[128,1024]{1,0:T(8,128)(2,1)S(1)}, u32[]{:S(2)}, u32[]{:S(2)}) collective-permute-start(bf16[128,1024]{1,0:T(8,128)(2,1)} %collective-permute-done.12), channel_id=1, source_target_pairs={{0,64},{1,65},{2,66},{3,67},{4,68},{5,69},{6,70},{7,71},{8,72},{9,... | collective-permute-start | bytes 786440 | tf_op jit(solution)/shard_map/weight_grad/ppermute | solution.py:367
  153.3 20.0 %collective-permute-start.14 = (bf16[128,128]{1,0:T(8,128)(2,1)S(1)}, bf16[128,128]{1,0:T(8,128)(2,1)S(1)}, u32[]{:S(2)}, u32[]{:S(2)}) collective-permute-start(bf16[128,128]{1,0:T(8,128)(2,1)S(1)} %select_bitcast_fusion), channel_id=1, source_target_pairs={{0,1},{1,0},{2,3},{3,2},{4,5},{5,4},{6,7},{7,6},{8,9},{9,8},{10,11... | collective-permute-start | bytes 98312 | tf_op jit(solution)/shard_map/input_grad/ppermute | solution.py:353
  164.4 16.2 %all-to-all-start.5 = ((bf16[16,32,128]{2,1,0:T(8,128)(2,1)}), bf16[16,32,128]{2,1,0:T(8,128)(2,1)S(1)}, u32[]{:S(2)}, u32[]{:S(2)}) async-start(bf16[16,32,128]{2,1,0:T(8,128)(2,1)} %bitcast.18), calls=%async_computation.5 | async-start | bytes 262144 | tf_op jit(solution)/shard_map/weight_grad/all_to_all | solution.py:373
  181.3 23.9 %all-to-all-start.6 = ((bf16[32,32,128]{2,1,0:T(8,128)(2,1)}), bf16[32,32,128]{2,1,0:T(8,128)(2,1)S(1)}, u32[]{:S(2)}, u32[]{:S(2)}) async-start(bf16[32,32,128]{2,1,0:T(8,128)(2,1)} %group_share.1), calls=%async_computation.6 | async-start | bytes 524288 | tf_op jit(solution)/shard_map/weight_grad/all_to_all | solution.py:373
  (26 other events, 356.7 us)
